TPU v7x, 32 devices: a whole 2x2x4 slice. The times are simulated.
32 devices in a mesh: seq: 8 (over y, x, core), head: 4 (over z).
Axes of the slice: x: 2, y: 2, z: 4, core: 2. Of those that a mesh axis runs over, the one named last changes fastest.
Arguments:
- inputs: bfloat16 [8192, 1024], P('seq', 'head'), may hold values from -6 to 6
- cotangent: bfloat16 [8192, 1024], P('seq', 'head'), may hold values from -6 to 6
- lengths: int32 [4], replicated, may hold values from 128 to 7424, as said below
- placement: int32 [64], replicated, may hold values from 0 to 63, as said below
- prenorm: float32 [1024], replicated, may hold values from 0.5 to 1.5
- gating: float32 [1024, 2048], P('seq', 'head'), may hold values from -0.1875 to 0.1875
- payload: float32 [1024, 2048], P('seq', 'head'), may hold values from -0.1875 to 0.1875
- address: float32 [1024, 256], P('seq'), may hold values from -0.1875 to 0.1875
- stepping: float32 [1024, 32], P('seq', 'head'), may hold values from -0.1875 to 0.1875
- kernels: float32 [4, 2048], P(None, 'head'), may hold values from -3 to 3
- offsets: float32 [2048], P('head'), may hold values from -3 to 3
- filters: float32 [4, 256], replicated, may hold values from -3 to 3
- shifts: float32 [256], replicated, may hold values from -3 to 3
- stepbias: float32 [32], P('head'), may hold values from -14 to -2.5
- decays: float32 [32], P('head'), may hold values from -0.7 to 0
- through: float32 [32], P('head'), may hold values from 0.1 to 1.9
- postnorm: float32 [2048], P('head'), may hold values from 0.5 to 1.5
- readout: float32 [2048, 1024], P('head', 'seq'), may hold values from -0.125 to 0.125
Outputs:
- outputs: bfloat16 [8192, 1024], P('seq', 'head')
- inputs_grad: bfloat16 [8192, 1024], P('seq', 'head')
- prenorm_grad: float32 [1024], P('head')
- gating_grad: float32 [1024, 2048], P('seq', 'head')
- payload_grad: float32 [1024, 2048], P('seq', 'head')
- address_grad: float32 [1024, 256], P('seq', 'head')
- stepping_grad: float32 [1024, 32], P('seq', 'head')
- kernels_grad: float32 [4, 2048], P(None, 'head')
- offsets_grad: float32 [2048], P('head')
- filters_grad: float32 [4, 256], P(None, 'head')
- shifts_grad: float32 [256], P('head')
- stepbias_grad: float32 [32], P('head')
- decays_grad: float32 [32], P('head')
- through_grad: float32 [32], P('head')
- postnorm_grad: float32 [2048], P('head')
- readout_grad: float32 [2048, 1024], P('head', 'seq')
Inputs may be any that keep to these rules, and one draw needn't show every extreme that they name: `lengths`: each length is a multiple of 128; they sum to 8192; exactly one sequence has the largest length. `placement`: A permutation of the blocks: block k of a device's working rows is block k of some device's given rows, and the blocks of one device's given rows go to different devices.
All inputs are finite; a program needn't handle non-finite values.
Results may differ from a plain program's by a relative error of at most 0.02.
Values may be sent and summed in bfloat16 or wider, within the bound.
A program may use at most 256 MiB of HBM per device.

v0:
```python
import jax
import jax.numpy as jnp
from jax import lax
from jax.sharding import PartitionSpec as P

D = 1024
GROUP = 256
BLOCK = 128
INNER = 2048


EPS = 1e-05


def from_behind(value, axis, steps):
    count = lax.axis_size(axis)
    leading, last = (max(0, -steps), min(count, count - steps))
    return lax.ppermute(value, axis, [(source, source + steps) for source in range(leading, last)])


def carried_in(x, axis, combine, identity):
    length, mine = (lax.axis_size(axis), lax.axis_index(axis))
    everything = jax.tree.map(
        lambda part, kind: lax.all_gather(part.astype(kind), axis),
        x,
        jax.tree.map(lambda a: jnp.bfloat16 if a.dtype == jnp.float32 else a.dtype, x),
    )
    start = jax.tree.map(
        lambda part, zero: jnp.broadcast_to(jnp.asarray(zero, part.dtype), part.shape), x, identity
    )

    def hop(k, before):
        reached = k < mine
        new = combine(
            before, jax.tree.map(lambda part, own: part[k].astype(own.dtype), everything, x)
        )
        return jax.tree.map(lambda a, b: jnp.where(reached, a, b), new, before)

    return lax.fori_loop(0, length, hop, start)


def prefix(part, axis, combine, identity):
    count = lax.axis_size(axis)
    place = lax.axis_index(axis)
    ahead = count - 1 - place
    gathered = jax.tree.map(lambda a: lax.all_gather(a, axis), part)
    state = jax.tree.map(lambda a, e: jnp.zeros_like(a) + jnp.asarray(e, a.dtype), part, identity)

    def one(hop, state):
        source = count - 1 - hop
        return combine(
            state, jax.tree.map(lambda a: lax.dynamic_index_in_dim(a, source, 0, False), gathered)
        )

    return lax.fori_loop(0, ahead, one, state)


def segment_of(position, seq_ends):
    counted = jnp.sum((position[:, None] >= seq_ends[None, :]).astype(jnp.int32), axis=1)
    return jnp.where(position < 0, -1, counted)


def conv_apply(extended, weights, bias, conv_mask):
    tap_count = weights.shape[0]
    row_count = extended.shape[0] - tap_count + 1
    total_sum = jnp.broadcast_to(bias[None, :], (row_count, extended.shape[1]))
    for tap_index in range(tap_count):
        total_sum = (
            total_sum
            + weights[tap_index][None, :]
            * extended[tap_index : tap_index + row_count]
            * conv_mask[:, tap_index : tap_index + 1]
        )
    return jax.nn.silu(total_sum)


def decay_terms(step_sizes, scale_rate, segment, previous):
    block_len = step_sizes.shape[0]
    cumul_rate = jnp.cumsum(step_sizes * scale_rate[None, :], axis=0)
    index_row = jnp.arange(block_len)
    causal = (index_row[:, None] >= index_row[None, :]) & (segment[:, None] == segment[None, :])
    spread = cumul_rate.T[:, :, None] - cumul_rate.T[:, None, :]
    inside = jnp.where(causal[None], spread, 0.0)
    lower_mask = jnp.where(causal[None], jnp.exp(inside), 0.0) * step_sizes.T[:, None, :]
    entry_decay = jnp.exp(cumul_rate) * (segment == previous).astype(cumul_rate.dtype)[:, None]
    final_mask = (segment == segment[block_len - 1]).astype(cumul_rate.dtype)
    weight = (
        step_sizes * jnp.exp(cumul_rate[block_len - 1][None, :] - cumul_rate) * final_mask[:, None]
    )
    carry_decay = jnp.exp(cumul_rate[block_len - 1]) * (segment[block_len - 1] == previous).astype(
        cumul_rate.dtype
    )
    return (lower_mask, entry_decay, weight, carry_decay)


def combine(earlier, subsequent):
    return (earlier[0] * subsequent[0], subsequent[0][:, None, None] * earlier[1] + subsequent[1])


def fold_block(summary, item):
    return (combine(summary, item), None)


def walk_blocks(state, item):
    return (item[0][:, None, None] * state + item[1], state)


def route_blocks(block_data, owners, devices, block_size):
    shaped = block_data.reshape(owners.shape[0], block_size, block_data.shape[1])
    onehot_table = (devices[:, None] == owners[None, :]).astype(jnp.bfloat16)
    return jnp.einsum(
        "nk,kbf->nbf", onehot_table, shaped, preferred_element_type=jnp.float32
    ).astype(jnp.bfloat16)


def pick_blocks(arrived, owners, devices):
    onehot_table = (owners[:, None] == devices[None, :]).astype(jnp.bfloat16)
    taken_rows = jnp.einsum(
        "kn,nbf->kbf", onehot_table, arrived, preferred_element_type=jnp.float32
    ).astype(jnp.bfloat16)
    return taken_rows.reshape(-1, arrived.shape[2])


def on_device(
    inputs,
    cotangent,
    lengths,
    placement,
    prenorm,
    gating,
    payload,
    address,
    stepping,
    kernels,
    offsets,
    filters,
    shifts,
    stepbias,
    decays,
    through,
    postnorm,
    readout,
):
    seq_count = lax.axis_size("seq")
    seq_index = lax.axis_index("seq")
    head_index = lax.axis_index("head")
    row_count = inputs.shape[0]
    per_dev = row_count // BLOCK
    block_ids = seq_index * per_dev + jnp.arange(per_dev, dtype=jnp.int32)
    every_block = jnp.arange(placement.shape[0], dtype=jnp.int32)
    target = jnp.sum(
        jnp.where(placement[None, :] == block_ids[:, None], every_block[None, :], 0), axis=1
    )
    target_dev = target // per_dev
    source_dev = lax.dynamic_slice_in_dim(placement, seq_index * per_dev, per_dev, 0) // per_dev
    devices = jnp.arange(seq_count, dtype=jnp.int32)
    moved_in = (
        lax.all_to_all(
            route_blocks(inputs, target_dev, devices, BLOCK),
            "seq",
            split_axis=0,
            concat_axis=0,
            tiled=True,
        ),
        lax.all_to_all(
            route_blocks(cotangent, target_dev, devices, BLOCK),
            "seq",
            split_axis=0,
            concat_axis=0,
            tiled=True,
        ),
    )
    x_local = pick_blocks(moved_in[0], source_dev, devices)
    g_local = pick_blocks(moved_in[1], source_dev, devices)
    x_full, g_full = (
        lax.all_gather(x_local, "head", axis=1, tiled=True),
        lax.all_gather(g_local, "head", axis=1, tiled=True),
    )
    u_full = x_full.astype(jnp.float32)
    inv_rms = lax.rsqrt(jnp.mean(u_full * u_full, axis=1, keepdims=True) + EPS)
    normed = (u_full * inv_rms * prenorm[None, :]).astype(jnp.bfloat16)
    w_gate, w_pay, w_addr, w_step, w_read = (
        lax.all_gather(gating.astype(jnp.bfloat16), "seq", axis=0, tiled=True),
        lax.all_gather(payload.astype(jnp.bfloat16), "seq", axis=0, tiled=True),
        lax.all_gather(address.astype(jnp.bfloat16), "seq", axis=0, tiled=True),
        lax.all_gather(stepping.astype(jnp.bfloat16), "seq", axis=0, tiled=True),
        lax.all_gather(readout.astype(jnp.bfloat16), "seq", axis=1, tiled=True),
    )
    gate_pre = jnp.dot(normed, w_gate, preferred_element_type=jnp.float32)
    value_pre = jnp.dot(normed, w_pay, preferred_element_type=jnp.float32).astype(jnp.bfloat16)
    addr_pre = jnp.dot(normed, w_addr, preferred_element_type=jnp.float32).astype(jnp.bfloat16)
    step_pre = jnp.dot(normed, w_step, preferred_element_type=jnp.float32)
    seq_ends = jnp.cumsum(lengths)
    tap_count = kernels.shape[0]
    position = seq_index * row_count + jnp.arange(-(tap_count - 1), row_count, dtype=jnp.int32)
    seg_ext = segment_of(position, seq_ends)
    segment = seg_ext[tap_count - 1 :]
    conv_mask = jnp.stack(
        [
            (seg_ext[tap_index : tap_index + row_count] == segment).astype(jnp.float32)
            for tap_index in range(tap_count)
        ],
        axis=1,
    )

    def conv_masked(extended, weights, bias):
        return conv_apply(extended, weights, bias, conv_mask)

    inner_local = value_pre.shape[1]
    rim_rows = jnp.concatenate(
        [value_pre[row_count - tap_count + 1 :], addr_pre[row_count - tap_count + 1 :]], axis=1
    )
    before = from_behind(rim_rows, "seq", 1)
    value_ext = jnp.concatenate([before[:, :inner_local], value_pre], axis=0).astype(jnp.float32)
    addr_ext = jnp.concatenate([before[:, inner_local:], addr_pre], axis=0).astype(jnp.float32)
    value_conv, value_back = jax.vjp(conv_masked, value_ext, kernels, offsets)
    values_all = value_conv.astype(jnp.bfloat16)
    addr_conv = conv_masked(addr_ext, filters, shifts).astype(jnp.bfloat16)
    block_len = min(GROUP, row_count)
    block_count = row_count // block_len
    heads_local = step_pre.shape[1]
    head_size = inner_local // heads_local
    state_size = addr_conv.shape[1] // 2
    values = values_all.reshape(block_count, block_len, heads_local, head_size)
    write_rows = addr_conv[:, :state_size].reshape(block_count, block_len, state_size)
    read_rows = addr_conv[:, state_size:].reshape(block_count, block_len, state_size)
    raw_steps = step_pre + stepbias[None, :]
    step_sizes = jax.nn.softplus(raw_steps).reshape(block_count, block_len, heads_local)
    scale_rate = -jnp.exp(decays)
    group_seg = segment.reshape(block_count, block_len)
    previous = seg_ext[tap_count - 2 : tap_count - 2 + row_count : block_len]

    def decay_all(step_arg, scale_arg):
        return jax.vmap(decay_terms, in_axes=(0, None, 0, 0))(
            step_arg, scale_arg, group_seg, previous
        )

    (lower_mask, entry_decay, weight, carry_decay), decay_back = jax.vjp(
        decay_all, step_sizes, scale_rate
    )
    scores = jnp.einsum("ctn,csn->cts", read_rows, write_rows, preferred_element_type=jnp.float32)
    mixing = (scores[:, None] * lower_mask).astype(jnp.bfloat16)
    intra_out = jnp.einsum("chts,cshp->cthp", mixing, values, preferred_element_type=jnp.float32)
    value_f = values.astype(jnp.float32)
    packed = (value_f * weight[..., None]).astype(jnp.bfloat16)
    local_state = jnp.einsum(
        "cshp,csn->chpn", packed, write_rows, preferred_element_type=jnp.float32
    )
    start_sum = (
        jnp.ones((heads_local,), jnp.float32),
        jnp.zeros((heads_local, head_size, state_size), jnp.float32),
    )
    summary, _ = lax.scan(fold_block, start_sum, (carry_decay, local_state))
    incoming = carried_in(summary, "seq", combine, start_sum)[1]
    _, starts = lax.scan(walk_blocks, incoming, (carry_decay, local_state))
    starts_low = starts.astype(jnp.bfloat16)
    queried = jnp.einsum(
        "ctn,chpn->cthp", read_rows, starts_low, preferred_element_type=jnp.float32
    )
    mixed_out = (
        intra_out + entry_decay[..., None] * queried + through[None, None, :, None] * value_f
    )
    ssd_out = mixed_out.reshape(row_count, inner_local)
    gate_act = jax.nn.silu(gate_pre)
    gated_rows = ssd_out * gate_act
    square_sum = lax.psum(jnp.sum(gated_rows * gated_rows, axis=1), "head")
    inv_inner = lax.rsqrt(square_sum / INNER + EPS)[:, None]
    normed_inner = (gated_rows * inv_inner * postnorm[None, :]).astype(jnp.bfloat16)
    out_part = jnp.dot(normed_inner, w_read, preferred_element_type=jnp.float32)
    trans_last = (((1,), (1,)), ((), ()))
    trans_first = (((0,), (0,)), ((), ()))
    grad_inner = lax.dot_general(g_full, w_read, trans_last, preferred_element_type=jnp.float32)
    grad_read = lax.dot_general(
        normed_inner, g_full, trans_first, preferred_element_type=jnp.float32
    )
    inner_dot = lax.psum(jnp.sum(gated_rows * postnorm[None, :] * grad_inner, axis=1), "head")
    cube_inner = inv_inner * inv_inner * inv_inner
    grad_gated = (
        inv_inner * postnorm[None, :] * grad_inner
        - gated_rows * cube_inner / INNER * inner_dot[:, None]
    )
    grad_post = jnp.sum(grad_inner * gated_rows * inv_inner, axis=0)
    grad_ssd = (grad_gated * gate_act).astype(jnp.bfloat16)
    gate_sigmoid = jax.nn.sigmoid(gate_pre)
    grad_gate_pre = (
        grad_gated * ssd_out * gate_sigmoid * (1.0 + gate_pre * (1.0 - gate_sigmoid))
    ).astype(jnp.bfloat16)
    grad_mixed = grad_ssd.reshape(block_count, block_len, heads_local, head_size)
    grad_mixed_f = grad_mixed.astype(jnp.float32)
    grad_query = (grad_mixed_f * entry_decay[..., None]).astype(jnp.bfloat16)
    grad_entry = jnp.sum(grad_mixed_f * queried, axis=3)
    grad_start_q = jnp.einsum(
        "cthp,ctn->chpn", grad_query, read_rows, preferred_element_type=jnp.float32
    )
    grad_read_rows = jnp.einsum(
        "cthp,chpn->ctn", grad_query, starts_low, preferred_element_type=jnp.float32
    )
    grad_mixing = jnp.einsum(
        "cthp,cshp->chts", grad_mixed, values, preferred_element_type=jnp.float32
    )
    grad_values = jnp.einsum(
        "chts,cthp->cshp", mixing, grad_mixed, preferred_element_type=jnp.float32
    )
    grad_scores = jnp.sum(grad_mixing * lower_mask, axis=1).astype(jnp.bfloat16)
    grad_lower = grad_mixing * scores[:, None]
    grad_read_rows = grad_read_rows + jnp.einsum(
        "cts,csn->ctn", grad_scores, write_rows, preferred_element_type=jnp.float32
    )
    grad_write_rows = jnp.einsum(
        "cts,ctn->csn", grad_scores, read_rows, preferred_element_type=jnp.float32
    )
    grad_through = jnp.sum(grad_mixed_f * value_f, axis=(0, 1, 3))
    grad_values = grad_values + through[None, None, :, None] * grad_mixed_f
    back_sum, _ = lax.scan(fold_block, start_sum, (carry_decay, grad_start_q), reverse=True)
    after = prefix(back_sum, "seq", combine, start_sum)[1]
    _, end_grads = lax.scan(walk_blocks, after, (carry_decay, grad_start_q), reverse=True)
    grad_carry = jnp.sum(end_grads * starts, axis=(2, 3))
    end_low = end_grads.astype(jnp.bfloat16)
    grad_packed = jnp.einsum(
        "csn,chpn->cshp", write_rows, end_low, preferred_element_type=jnp.float32
    )
    grad_write_rows = grad_write_rows + jnp.einsum(
        "cshp,chpn->csn", packed, end_low, preferred_element_type=jnp.float32
    )
    grad_values = grad_values + grad_packed * weight[..., None]
    grad_weight = jnp.sum(grad_packed * value_f, axis=3)
    grad_steps, grad_scale = decay_back((grad_lower, grad_entry, grad_weight, grad_carry))
    grad_decays = grad_scale * scale_rate
    grad_raw = grad_steps.reshape(row_count, heads_local) * jax.nn.sigmoid(raw_steps)
    grad_stepbias = jnp.sum(grad_raw, axis=0)
    grad_step_pre = grad_raw.astype(jnp.bfloat16)
    grad_addr_conv = jnp.concatenate(
        [
            grad_write_rows.reshape(row_count, state_size),
            grad_read_rows.reshape(row_count, state_size),
        ],
        axis=1,
    )
    grad_addr_share = lax.psum_scatter(
        grad_addr_conv.astype(jnp.bfloat16), "head", scatter_dimension=1, tiled=True
    ).astype(jnp.float32)
    col_count = grad_addr_share.shape[1]
    col_start = head_index * col_count
    addr_ext_share = lax.dynamic_slice_in_dim(addr_ext, col_start, col_count, 1)
    filter_share = lax.dynamic_slice_in_dim(filters, col_start, col_count, 1)
    shift_share = lax.dynamic_slice_in_dim(shifts, col_start, col_count, 0)
    _, addr_back = jax.vjp(conv_masked, addr_ext_share, filter_share, shift_share)
    grad_addr_ext, grad_filters, grad_shifts = addr_back(grad_addr_share)
    grad_value_ext, grad_kernels, grad_offsets = value_back(
        grad_values.reshape(row_count, inner_local)
    )
    head_rims = jnp.concatenate(
        [grad_value_ext[: tap_count - 1], grad_addr_ext[: tap_count - 1]], axis=1
    )
    after_rims = from_behind(head_rims, "seq", -1)
    tail_rows = jnp.concatenate(
        [jnp.zeros((row_count - tap_count + 1, after_rims.shape[1]), jnp.float32), after_rims],
        axis=0,
    )
    grad_value_pre = (grad_value_ext[tap_count - 1 :] + tail_rows[:, :inner_local]).astype(
        jnp.bfloat16
    )
    grad_addr_pre = (grad_addr_ext[tap_count - 1 :] + tail_rows[:, inner_local:]).astype(
        jnp.bfloat16
    )
    addr_share = lax.dynamic_slice_in_dim(w_addr, col_start, col_count, 1)
    grad_normed = lax.dot_general(
        grad_gate_pre, w_gate, trans_last, preferred_element_type=jnp.float32
    )
    grad_normed = grad_normed + lax.dot_general(
        grad_value_pre, w_pay, trans_last, preferred_element_type=jnp.float32
    )
    grad_normed = grad_normed + lax.dot_general(
        grad_addr_pre, addr_share, trans_last, preferred_element_type=jnp.float32
    )
    grad_normed = grad_normed + lax.dot_general(
        grad_step_pre, w_step, trans_last, preferred_element_type=jnp.float32
    )
    grad_gate_w = lax.dot_general(
        normed, grad_gate_pre, trans_first, preferred_element_type=jnp.float32
    )
    grad_pay_w = lax.dot_general(
        normed, grad_value_pre, trans_first, preferred_element_type=jnp.float32
    )
    grad_addr_w = lax.dot_general(
        normed, grad_addr_pre, trans_first, preferred_element_type=jnp.float32
    )
    grad_step_w = lax.dot_general(
        normed, grad_step_pre, trans_first, preferred_element_type=jnp.float32
    )
    cube_rms = inv_rms * inv_rms * inv_rms
    row_dot = jnp.sum(grad_normed * prenorm[None, :] * u_full, axis=1, keepdims=True)
    grad_part = inv_rms * prenorm[None, :] * grad_normed - u_full * cube_rms / D * row_dot
    extra_term = jnp.sum(grad_normed * u_full * inv_rms, axis=0)[None, :]
    out_sum, grad_sum, extra_sum = (
        lax.psum_scatter(
            out_part.astype(jnp.bfloat16), "head", scatter_dimension=1, tiled=True
        ).astype(jnp.float32),
        lax.psum_scatter(
            grad_part.astype(jnp.bfloat16), "head", scatter_dimension=1, tiled=True
        ).astype(jnp.float32),
        lax.psum_scatter(
            extra_term.astype(jnp.bfloat16), "head", scatter_dimension=1, tiled=True
        ).astype(jnp.float32),
    )
    u_local = x_local.astype(jnp.float32)
    input_grad = g_local.astype(jnp.float32) + grad_sum
    grad_prenorm = extra_sum[0]
    result = (u_local + out_sum).astype(jnp.bfloat16)
    grad_rows = input_grad.astype(jnp.bfloat16)
    moved_out = (
        lax.all_to_all(
            route_blocks(result, source_dev, devices, BLOCK),
            "seq",
            split_axis=0,
            concat_axis=0,
            tiled=True,
        ),
        lax.all_to_all(
            route_blocks(grad_rows, source_dev, devices, BLOCK),
            "seq",
            split_axis=0,
            concat_axis=0,
            tiled=True,
        ),
    )
    outputs = pick_blocks(moved_out[0], target_dev, devices)
    inputs_grad = pick_blocks(moved_out[1], target_dev, devices)
    gate_sum, pay_sum, addr_sum, step_sum, read_sum = (
        lax.psum_scatter(
            grad_gate_w.astype(jnp.bfloat16), "seq", scatter_dimension=0, tiled=True
        ).astype(jnp.float32),
        lax.psum_scatter(
            grad_pay_w.astype(jnp.bfloat16), "seq", scatter_dimension=0, tiled=True
        ).astype(jnp.float32),
        lax.psum_scatter(
            grad_addr_w.astype(jnp.bfloat16), "seq", scatter_dimension=0, tiled=True
        ).astype(jnp.float32),
        lax.psum_scatter(
            grad_step_w.astype(jnp.bfloat16), "seq", scatter_dimension=0, tiled=True
        ).astype(jnp.float32),
        lax.psum_scatter(
            grad_read.astype(jnp.bfloat16), "seq", scatter_dimension=1, tiled=True
        ).astype(jnp.float32),
    )
    smalls = lax.psum(
        (
            grad_prenorm,
            grad_kernels,
            grad_offsets,
            grad_filters,
            grad_shifts,
            grad_stepbias,
            grad_decays,
            grad_through,
            grad_post,
        ),
        "seq",
    )
    return (
        outputs,
        inputs_grad,
        smalls[0],
        gate_sum,
        pay_sum,
        addr_sum,
        step_sum,
        smalls[1],
        smalls[2],
        smalls[3],
        smalls[4],
        smalls[5],
        smalls[6],
        smalls[7],
        smalls[8],
        read_sum,
    )


def solution(mesh):
    in_specs = (
        P("seq", "head"),
        P("seq", "head"),
        P(),
        P(),
        P(),
        P("seq", "head"),
        P("seq", "head"),
        P("seq", None),
        P("seq", "head"),
        P(None, "head"),
        P("head"),
        P(),
        P(),
        P("head"),
        P("head"),
        P("head"),
        P("head"),
        P("head", "seq"),
    )
    out_specs = (
        P("seq", "head"),
        P("seq", "head"),
        P("head"),
        P("seq", "head"),
        P("seq", "head"),
        P("seq", "head"),
        P("seq", "head"),
        P(None, "head"),
        P("head"),
        P(None, "head"),
        P("head"),
        P("head"),
        P("head"),
        P("head"),
        P("head"),
        P("head", "seq"),
    )
    return jax.shard_map(
        on_device, mesh=mesh, in_specs=in_specs, out_specs=out_specs, check_vma=False
    )
```

profile of v0, /device:TPU:1, one launch (start us, length us, event | category | flops | bytes accessed | tf_op | source)
XLA Modules:
  0.0 678.3 jit_solution(3765709824932504975)
XLA Ops:
  9.7 5.4 all-to-all-start
  15.2 6.6 all-to-all-done
  25.3 10.8 %all_gather.48 = bf16[1024,8]{0,1:T(8,128)(2,1)S(1)} all-gather(bf16[128,8]{0,1:T(8,128)(2,1)S(1)} %convert_element_type.271), channel_id=1, replica_groups=mesh['seq'=8,'head'=4] {'seq'}, dimensions={0}, use_global_device_ids=true | all-gather | bytes 18432 | tf_op jit(solution)/shard_map/all_gather | solution.py:186
  37.6 9.8 %all_gather.47 = bf16[1024,256]{1,0:T(8,128)(2,1)S(1)} all-gather(bf16[128,256]{1,0:T(8,128)(2,1)S(1)} %convert_element_type.261), channel_id=1, replica_groups=mesh['seq'=8,'head'=4] {'seq'}, dimensions={0}, use_global_device_ids=true | all-gather | bytes 589824 | tf_op jit(solution)/shard_map/all_gather | solution.py:185
  49.4 21.2 %all-gather.12.cloned.1.call-done = bf16[1024,1024]{1,0:T(8,128)(2,1)} async-done(((bf16[1024,256]{1,0:T(8,128)(2,1)}), bf16[1024,1024]{1,0:T(8,128)(2,1)}) %all-gather.12.cloned.1.call-update) | async-done | bytes 2097168 | tf_op jit(solution)/shard_map/all_gather | solution.py:176
  76.1 19.8 %all-gather.14.cloned.1.call-done = bf16[1024,512]{1,0:T(8,128)(2,1)} async-done(((bf16[128,512]{1,0:T(8,128)(2,1)}), bf16[1024,512]{1,0:T(8,128)(2,1)}) %all-gather.14.cloned.1.call-update) | async-done | bytes 1048592 | tf_op jit(solution)/shard_map/all_gather | solution.py:184
  151.1 14.0 %all-reduce.19 = bf16[64]{0:T(256)(128)(2,1)S(1)} all-reduce(bf16[64]{0:T(256)(128)(2,1)S(1)} %dynamic-update-slice), channel_id=2, replica_groups=mesh['seq'=8,'head'=4] {'seq'}, use_global_device_ids=true, to_apply=%add.19 | all-reduce | flops 64 | bytes 256
  167.5 8.4 %while.90 = (s32[]{:T(128)}, f32[8,64,128]{2,1,0:T(8,128)S(1)}, s32[]{:T(128)}, bf16[8,8]{1,0:T(8,128)(2,1)S(1)}, bf16[8,8,64,128]{3,2,1,0:T(8,128)(2,1)}, /*index=5*/s32[]{:T(128)}, s32[]{:T(128)}) while((s32[]{:T(128)}, f32[8,64,128]{2,1,0:T(8,128)S(1)}, s32[]{:T(128)}, bf16[8,8]{1,0:T(8,128)(2,1)S(1)}, ...), condition=%wide.region_9.10_spmd.clone, body=%wide.region_8.9_spmd.clone.sunk | while | flops 327692 | bytes 655553 | solution.py:39
  177.1 7.2 %while.86 = (s32[]{:T(128)}, f32[8,64,128]{2,1,0:T(8,128)S(1)}, f32[4,8,64,128]{3,2,1,0:T(8,128)}, f32[4,8]{1,0:T(4,128)S(1)}, f32[4,8,64,128]{3,2,1,0:T(8,128)}, /*index=5*/s32[]{:T(128)}) while((s32[]{:T(128)}, f32[8,64,128]{2,1,0:T(8,128)S(1)}, f32[4,8,64,128]{3,2,1,0:T(8,128)}, f32[4,8]{1,0:T(4,128)S(1)}, f32[4,8,64,128]{3,2,1,0:T(8,128)}, ...), condition=%wide.region_11.12_spmd, body=%wide.region_10.11_spmd.sunk | while | flops 131074 | bytes 1310905 | solution.py:255
  195.7 4.8 reshape.484
  200.5 6.1 multiply_reduce_fusion.9
  206.7 9.7 %psum.77 = f32[1024]{0:T(1024)S(1)} all-reduce(f32[1024]{0:T(1024)S(1)} %get-tuple-element.615), channel_id=1, replica_groups=mesh['seq'=8,'head'=4] {'head'}, use_global_device_ids=true, to_apply=%region_13.14 | all-reduce | flops 1024 | bytes 8192 | tf_op jit(solution)/shard_map/psum | solution.py:266
  216.5 35.5 %all-gather.20.cloned.1.call-done = bf16[1024,1024]{1,0:T(8,128)(2,1)} async-done(((bf16[1024,256]{1,0:T(8,128)(2,1)}), bf16[1024,1024]{1,0:T(8,128)(2,1)}) %all-gather.20.cloned.1.call-update) | async-done | bytes 2097168 | tf_op jit(solution)/shard_map/all_gather | solution.py:177
  252.0 5.8 multiply_reduce_fusion.2
  257.8 8.0 %psum.78 = f32[1024]{0:T(1024)S(1)} all-reduce(f32[1024]{0:T(1024)S(1)} %get-tuple-element.529), channel_id=1, replica_groups=mesh['seq'=8,'head'=4] {'head'}, use_global_device_ids=true, to_apply=%region_16.17 | all-reduce | flops 1024 | bytes 8192 | tf_op jit(solution)/shard_map/psum | solution.py:276
  265.8 6.1 multiply_reduce_fusion.3
  281.5 8.7 %while.91 = (s32[]{:T(128)}, f32[8]{0:T(128)}, f32[8,64,128]{2,1,0:T(8,128)S(1)}, f32[4,8]{1,0:T(4,128)S(1)}, f32[4,8,64,128]{3,2,1,0:T(8,128)}, /*index=5*/s32[]{:T(128)}, s32[]{:T(128)}, s32[]{:T(128)}) while((s32[]{:T(128)}, f32[8]{0:T(128)}, f32[8,64,128]{2,1,0:T(8,128)S(1)}, f32[4,8]{1,0:T(4,128)S(1)}, ...), condition=%wide.region_18.19_spmd.clone, body=%wide.region_17.18_spmd.clone.sunk | while | flops 196628 | bytes 786716 | solution.py:314
  291.9 14.0 %all-reduce.20 = f32[64]{0:T(128)S(1)} all-reduce(f32[64]{0:T(128)S(1)} %dynamic-update-slice.1), channel_id=4, replica_groups=mesh['seq'=8,'head'=4] {'seq'}, use_global_device_ids=true, to_apply=%add.20 | all-reduce | flops 64 | bytes 512
  308.9 8.1 %fusion.8 = (f32[4,8,256]{2,1,0:T(8,128)}, f32[4,8,256]{2,1,0:T(8,128)S(1)}, f32[4,8,256]{2,1,0:T(8,128)}, bf16[4,256,256]{2,1,0:T(8,128)(2,1)S(1)}) fusion(f32[4,8,256]{2,1,0:T(8,128)S(1)} %bitcast.275, f32[4,8,256]{2,1,0:T(8,128)S(1)} %copy-done.58, f32[4,256,256]{2,1,0:T(8,128)} %fusion.114, pred[4,256,256]{2,1,0:T(8,128)(4,1)S(1)} %copy-done.47, ...), kind=kOutput, calls=%fused_computation.36 | convolution fusion | flops 299606016 | bytes 4096000 | tf_op jit(solution)/shard_map/cthp,cshp->chts/dot_general | solution.py:298
  320.2 10.6 %while.87 = (s32[]{:T(128)}, f32[8,64,128]{2,1,0:T(8,128)S(1)}, s32[]{:T(128)}, f32[8,8]{1,0:T(8,128)}, f32[8,8,64,128]{3,2,1,0:T(8,128)}, /*index=5*/s32[]{:T(128)}, s32[]{:T(128)}, s32[]{:T(128)}, s32[]{:T(128)}) while((s32[]{:T(128)}, f32[8,64,128]{2,1,0:T(8,128)S(1)}, s32[]{:T(128)}, f32[8,8]{1,0:T(8,128)}, ...), condition=%wide.region_20.21_spmd, body=%wide.region_19.20_spmd.sunk | while | flops 131078 | bytes 786683 | solution.py:55
  331.9 7.2 %while.88 = (s32[]{:T(128)}, f32[8,64,128]{2,1,0:T(8,128)S(1)}, f32[4,8,64,128]{3,2,1,0:T(8,128)}, f32[4,8]{1,0:T(4,128)S(1)}, f32[4,8,64,128]{3,2,1,0:T(8,128)}, /*index=5*/s32[]{:T(128)}, s32[]{:T(128)}) while((s32[]{:T(128)}, f32[8,64,128]{2,1,0:T(8,128)S(1)}, f32[4,8,64,128]{3,2,1,0:T(8,128)}, f32[4,8]{1,0:T(4,128)S(1)}, ...), condition=%wide.region_22.23_spmd, body=%wide.region_21.22_spmd.sunk | while | flops 131075 | bytes 1310925 | solution.py:316
  344.7 4.6 convolution_convert_fusion.1
  374.1 9.9 %reduce-window.31 = f32[4,8,2,128]{3,1,2,0:T(8,128)S(1)} reduce-window(f32[4,8,2,128]{3,1,2,0:T(8,128)S(1)} %copy.326, f32[]{:T(128)} %constant.225.clone.1), window={size=1x1x1x128 pad=0_0x0_0x0_0x0_127}, to_apply=%region_32.33 | reduce-window | flops 1040384 | bytes 65540 | tf_op jit(solution)/shard_map/reduce-window.3
  398.3 5.0 fusion.115
  411.2 4.8 reshape.486
  447.8 32.6 %reduce-scatter.34.cloned.1.call-done = bf16[128,8]{1,0:T(8,128)(2,1)} async-done(((bf16[1024,8]{1,0:T(8,128)(2,1)}), bf16[128,8]{1,0:T(8,128)(2,1)}) %reduce-scatter.34.cloned.1.call-update) | async-done | bytes 2064
  487.9 39.0 %reduce-scatter.20.cloned.1.call-done = bf16[1024,256]{1,0:T(8,128)(2,1)} async-done(((bf16[1024,1024]{1,0:T(8,128)(2,1)}), bf16[1024,256]{1,0:T(8,128)(2,1)}) %reduce-scatter.20.cloned.1.call-update) | async-done | bytes 524304 | tf_op jit(solution)/shard_map/reduce_scatter | solution.py:396
  533.8 38.5 %reduce-scatter.22.cloned.1.call-done = bf16[1024,256]{1,0:T(8,128)(2,1)} async-done(((bf16[1024,1024]{1,0:T(8,128)(2,1)}), bf16[1024,256]{1,0:T(8,128)(2,1)}) %reduce-scatter.22.cloned.1.call-update) | async-done | bytes 524304 | tf_op jit(solution)/shard_map/reduce_scatter | solution.py:399
  580.7 12.0 %reduce-scatter.30.cloned.1.call-done = bf16[256,1]{1,0:T(8,128)(2,1)} async-done(((bf16[1024,1]{1,0:T(8,128)(2,1)}), bf16[256,1]{1,0:T(8,128)(2,1)}) %reduce-scatter.30.cloned.1.call-update) | async-done | bytes 528
  593.6 22.0 %all-reduce.21 = (f32[256]{0:T(256)}, f32[4,512]{1,0:T(4,128)}, f32[512]{0:T(512)}, f32[4,64]{1,0:T(4,128)}, f32[64]{0:T(128)}, /*index=5*/f32[8]{0:T(128)}, f32[8]{0:T(128)}, f32[8]{0:T(128)}, f32[512]{0:T(512)}) all-reduce(f32[256]{0:T(256)S(1)} %bitcast.293, ...), channel_id=1, replica_groups=mesh['seq'=8,'head'=4] {'seq'}, use_global_device_ids=true, to_apply=%region_38.39 | all-reduce | flops 3672 | bytes 29376 | tf_op jit(solution)/shard_map/psum | solution.py:446
  615.6 13.0 %reduce-scatter.32.cloned.1.call-done = bf16[128,64]{1,0:T(8,128)(2,1)} async-done(((bf16[1024,64]{1,0:T(8,128)(2,1)}), bf16[128,64]{1,0:T(8,128)(2,1)}) %reduce-scatter.32.cloned.1.call-update) | async-done | bytes 16400
  630.1 38.3 %reduce-scatter.26.cloned.1.call-done = bf16[128,512]{1,0:T(8,128)(2,1)} async-done(((bf16[1024,512]{1,0:T(8,128)(2,1)}), bf16[128,512]{1,0:T(8,128)(2,1)}) %reduce-scatter.26.cloned.1.call-update) | async-done | bytes 131088 | tf_op jit(solution)/shard_map/reduce_scatter | solution.py:433
  (552 shorter events, 259.7 us)
Async XLA Ops:
  9.7 12.1 %all-to-all-start = ((bf16[8,128,256]{2,1,0:T(8,128)(2,1)}), bf16[8,128,256]{2,1,0:T(8,128)(2,1)S(1)}, u32[]{:S(2)}, u32[]{:S(2)}) async-start(bf16[8,128,256]{2,1,0:T(8,128)(2,1)} %copy.281), calls=%async_computation | async-start | bytes 1048576 | tf_op jit(solution)/shard_map/all_to_all | solution.py:158
  15.0 55.6 %all-gather.12.cloned.1.call-start = ((), (), s32[]{:S(2)}) async-start(), calls=%async_computation.13 | async-start | bytes 2621440 | tf_op jit(solution)/shard_map/all_gather | solution.py:176
  23.1 50.3 %copy-start.71 = (f32[1024]{0:T(1024)S(1)}, f32[1024]{0:T(1024)}, u32[]{:S(2)}) copy-start(f32[1024]{0:T(1024)} %param.34) | copy-start | bytes 12292
  23.1 72.8 %all-gather.14.cloned.1.call-start = ((), (), s32[]{:S(2)}) async-start(), calls=%async_computation.14 | async-start | bytes 1179648 | tf_op jit(solution)/shard_map/all_gather | solution.py:184
  23.9 143.6 %all-gather.22.cloned.1.call-start = ((), (), s32[]{:S(2)}) async-start(), calls=%async_computation.22 | async-start | bytes 1179648 | tf_op jit(solution)/shard_map/all_gather | solution.py:24
  36.1 66.2 %copy-start.52 = (bf16[1024,8]{0,1:T(8,128)(2,1)}, bf16[1024,8]{0,1:T(8,128)(2,1)S(1)}, u32[]{:S(2)}) copy-start(bf16[1024,8]{0,1:T(8,128)(2,1)S(1)} %all_gather.48) | copy-start | bytes 49156
  99.1 12.2 %collective-permute-start = (bf16[3,768]{1,0:T(4,128)(2,1)}, bf16[3,768]{1,0:T(4,128)(2,1)}, u32[]{:S(2)}, u32[]{:S(2)}) collective-permute-start(bf16[3,768]{1,0:T(4,128)(2,1)} %pad_maximum_fusion.2), channel_id=1, source_target_pairs={{0,4},{4,8},{8,12},{12,16},{16,20},{20,24},{24,28},{1,5},{5,9},{9,... | collective-permute-start | bytes 13832 | tf_op jit(solution)/shard_map/ppermute | solution.py:18
  130.7 69.9 %all-gather.16.cloned.1.call-start = ((), (), s32[]{:S(2)}) async-start(), calls=%async_computation.15 | async-start | bytes 1179648 | tf_op jit(solution)/shard_map/all_gather | solution.py:183
  132.4 84.1 %all-gather.18.cloned.1.call-start = ((), (), s32[]{:S(2)}) async-start(), calls=%async_computation.16 | async-start | bytes 1179648 | tf_op jit(solution)/shard_map/all_gather | solution.py:187
  136.4 10.6 %all-to-all-start.2 = ((bf16[8,128,256]{2,1,0:T(8,128)(2,1)}), bf16[8,128,256]{2,1,0:T(8,128)(2,1)}, u32[]{:S(2)}, u32[]{:S(2)}) async-start(bf16[8,128,256]{2,1,0:T(8,128)(2,1)} %copy.304), calls=%async_computation.3 | async-start | bytes 1048576 | tf_op jit(solution)/shard_map/all_to_all | solution.py:165
  140.5 111.4 %all-gather.20.cloned.1.call-start = ((), (), s32[]{:S(2)}) async-start(), calls=%async_computation.18 | async-start | bytes 2621440 | tf_op jit(solution)/shard_map/all_gather | solution.py:177
  149.6 170.5 %all-gather.24.cloned.1.call-start = ((), (), s32[]{:S(2)}) async-start(), calls=%async_computation.23 | async-start | bytes 2359296 | tf_op jit(solution)/shard_map/all_gather | solution.py:46
  200.5 51.4 %copy-start.111 = (f32[512]{0:T(512)S(1)}, f32[512]{0:T(512)}, u32[]{:S(2)}) copy-start(f32[512]{0:T(512)} %param.46) | copy-start | bytes 6148
  216.4 49.4 %copy-start.82 = (f32[1024]{0:T(1024)}, f32[1024]{0:T(1024)S(1)}, u32[]{:S(2)}) copy-start(f32[1024]{0:T(1024)S(1)} %get-tuple-element.644) | copy-start | bytes 12292
  291.0 135.1 %reduce-scatter.28.cloned.1.call-start = ((), (), s32[]{:S(2)}) async-start(), calls=%async_computation.24 | async-start | bytes 655360
  344.7 99.7 %reduce-scatter.36.cloned.1.call-start = ((), (), s32[]{:S(2)}) async-start(), calls=%async_computation.28 | async-start | bytes 1179648
  351.7 94.5 %reduce-scatter.24.cloned.1.call-start = ((), (), s32[]{:S(2)}) async-start(), calls=%async_computation.20 | async-start | bytes 1179648 | tf_op jit(solution)/shard_map/reduce_scatter | solution.py:430
  361.1 119.3 %reduce-scatter.34.cloned.1.call-start = ((), (), s32[]{:S(2)}) async-start(), calls=%async_computation.27 | async-start | bytes 294912
  393.4 133.4 %reduce-scatter.20.cloned.1.call-start = ((), (), s32[]{:S(2)}) async-start(), calls=%async_computation.17 | async-start | bytes 2621440 | tf_op jit(solution)/shard_map/reduce_scatter | solution.py:396
  398.2 174.2 %reduce-scatter.22.cloned.1.call-start = ((), (), s32[]{:S(2)}) async-start(), calls=%async_computation.19 | async-start | bytes 2621440 | tf_op jit(solution)/shard_map/reduce_scatter | solution.py:399
  428.9 5.4 collective-permute-start.1
  443.5 39.3 %copy-start.4 = (bf16[1024,1024]{1,0:T(8,128)(2,1)S(1)}, bf16[1024,1024]{1,0:T(8,128)(2,1)}, u32[]{:S(2)}) copy-start(bf16[1024,1024]{1,0:T(8,128)(2,1)} %copy-done.2) | copy-start | bytes 6291460
  443.5 149.2 %reduce-scatter.30.cloned.1.call-start = ((), (), s32[]{:S(2)}) async-start(), calls=%async_computation.25 | async-start | bytes 327680
  482.7 145.9 %reduce-scatter.32.cloned.1.call-start = ((), (), s32[]{:S(2)}) async-start(), calls=%async_computation.26 | async-start | bytes 294912
  484.2 42.7 %copy-start.31 = (bf16[8,128,256]{2,1,0:T(8,128)(2,1)S(1)}, bf16[8,128,256]{2,1,0:T(8,128)(2,1)}, u32[]{:S(2)}) copy-start(bf16[8,128,256]{2,1,0:T(8,128)(2,1)} %copy.283) | copy-start | bytes 1572868
  484.2 184.2 %reduce-scatter.26.cloned.1.call-start = ((), (), s32[]{:S(2)}) async-start(), calls=%async_computation.21 | async-start | bytes 1179648 | tf_op jit(solution)/shard_map/reduce_scatter | solution.py:433
  487.8 40.2 %copy-start.92 = (s32[8]{0:T(128)S(1)}, s32[8]{0:T(128)}, u32[]{:S(2)}) copy-start(s32[8]{0:T(128)} %copy-done.90) | copy-start | bytes 100
  487.8 84.5 %copy-start.32 = (bf16[8,128,256]{2,1,0:T(8,128)(2,1)S(1)}, bf16[8,128,256]{2,1,0:T(8,128)(2,1)}, u32[]{:S(2)}) copy-start(bf16[8,128,256]{2,1,0:T(8,128)(2,1)} %copy.306) | copy-start | bytes 1572868
  529.3 45.5 %all-to-all-start.1 = ((bf16[8,128,256]{2,1,0:T(8,128)(2,1)}), bf16[8,128,256]{2,1,0:T(8,128)(2,1)S(1)}, u32[]{:S(2)}, u32[]{:S(2)}) async-start(bf16[8,128,256]{2,1,0:T(8,128)(2,1)} %copy.300), calls=%async_computation.2 | async-start | bytes 1048576 | tf_op jit(solution)/shard_map/all_to_all | solution.py:412
  533.8 45.6 %copy-start.89 = (s32[8]{0:T(128)S(1)}, s32[8]{0:T(128)}, u32[]{:S(2)}) copy-start(s32[8]{0:T(128)} %copy-done.87) | copy-start | bytes 100
  574.9 95.2 %all-to-all-start.3 = ((bf16[8,128,256]{2,1,0:T(8,128)(2,1)}), bf16[8,128,256]{2,1,0:T(8,128)(2,1)S(1)}, u32[]{:S(2)}, u32[]{:S(2)}) async-start(bf16[8,128,256]{2,1,0:T(8,128)(2,1)} %copy.332), calls=%async_computation.5 | async-start | bytes 1048576 | tf_op jit(solution)/shard_map/all_to_all | solution.py:419
  579.4 92.0 %copy-start.1 = (bf16[1024,256]{1,0:T(8,128)(2,1)S(1)}, bf16[1024,256]{1,0:T(8,128)(2,1)}, u32[]{:S(2)}) copy-start(bf16[1024,256]{1,0:T(8,128)(2,1)} %param.30) | copy-start | bytes 1572868
  (117 other events, 661.3 us)
Sparse Core Ops, SparseCore 0:
  23.3 47.3 all-gather.11
  73.1 22.8 all-gather.13
  130.8 23.3 all-gather.21
  155.9 23.5 all-gather.15
  181.2 23.5 all-gather.17
  206.8 45.1 all-gather.19
  291.1 28.9 all-gather.23
  344.8 20.3 reduce-scatter.27
  368.4 35.9 reduce-scatter.35
  407.4 36.0 reduce-scatter.23
  447.1 33.2 reduce-scatter.33
  482.6 44.1 reduce-scatter.19
  529.1 43.1 reduce-scatter.21
  575.1 17.5 reduce-scatter.29
  595.6 32.9 reduce-scatter.31
  632.0 36.3 reduce-scatter.25
where the time goes:
time: 690 us; the launch traced here: 678 us
  waiting for transfers between devices  262 us (38%)
  other arithmetic  107 us (16%)
  local copies, waits for them, and re-layouts  92.2 us (13%)
  blocking collectives  88.3 us (13%)
  matrix products  84.4 us (12%)
  starting transfers between devices  27.3 us (4%)
  between operations  16.7 us (2%)
    unnamed x21, waiting for transfers between devices  57.8 us
    reduce_scatter x1, waiting for transfers between devices, on_device(): lax.psum_scatter(out_part.astype(jnp.bfloat16), 'head', scatter_dimension...  39 us
    reduce_scatter x1, waiting for transfers between devices, on_device(): lax.psum_scatter(grad_part.astype(jnp.bfloat16), 'head', scatter_dimensio...  38.5 us
    reduce_scatter x1, waiting for transfers between devices, on_device(): lax.psum_scatter(grad_pay_w.astype(jnp.bfloat16), 'seq', scatter_dimensio...  38.3 us
    all_gather x1, waiting for transfers between devices, on_device(): lax.all_gather(g_local, 'head', axis=1, tiled=True)  35.5 us
    unnamed x2, blocking collectives  28 us
    unnamed x270, local copies, waits for them, and re-layouts  25.4 us
    psum x1, blocking collectives, on_device(): lax.psum((grad_prenorm, grad_kernels, grad_offsets, grad_filters, grad_sh...  22 us
  transfers between devices with their start and end apart: 22, of which 12 were waited for; matrix products, arithmetic and copies ran while one was open for 28% of the time, Pallas kernels for 0%

commit v1 on v0

--- a/solution.py
+++ b/solution.py
@@ -1,12 +1,240 @@
+import functools
+
 import jax
 import jax.numpy as jnp
 from jax import lax
+from jax.experimental import pallas as pl
+from jax.experimental.pallas import tpu as pltpu
 from jax.sharding import PartitionSpec as P
 
 D = 1024
 GROUP = 256
 BLOCK = 128
 INNER = 2048
+HALO = 16
+LANES = 128
+MESH = pl.DeviceIdType.MESH
+VMEM = pltpu.MemorySpace.VMEM
+SMEM = pltpu.MemorySpace.SMEM
+DMA = pltpu.SemaphoreType.DMA
+MIB = 1 << 20
+
+
+def greet(seq_peers, head_peers):
+    barrier = pltpu.get_barrier_semaphore()
+    count = 0
+    if seq_peers > 1:
+        me = lax.axis_index("seq")
+
+        @pl.loop(1, seq_peers)
+        def _(i):
+            pl.semaphore_signal(
+                barrier, inc=1, device_id={"seq": lax.rem(me + i, seq_peers)}, device_id_type=MESH
+            )
+
+        count += seq_peers - 1
+    if head_peers > 1:
+        mine = lax.axis_index("head")
+
+        @pl.loop(1, head_peers)
+        def _(i):
+            pl.semaphore_signal(
+                barrier, inc=1, device_id={"head": lax.rem(mine + i, head_peers)}, device_id_type=MESH
+            )
+
+        count += head_peers - 1
+    pl.semaphore_wait(barrier, count)
+
+
+def remote(src, dst, send_sem, recv_sem, where):
+    return pltpu.make_async_remote_copy(
+        src_ref=src, dst_ref=dst, send_sem=send_sem, recv_sem=recv_sem, device_id=where, device_id_type=MESH
+    )
+
+
+class Line:
+    def __init__(self, count, out, width, send, recv):
+        self.count, self.out, self.width, self.send, self.recv = count, out, width, send, recv
+        self.me = lax.axis_index("head")
+
+    def view(self, shard):
+        return self.out.at[:, pl.ds(pl.multiple_of(shard * self.width, LANES), self.width)]
+
+    def copy(self, src, shard, way, step):
+        return remote(
+            src, self.view(shard), self.send.at[way, step], self.recv.at[shard], {"head": self.me + (1 - 2 * way)}
+        )
+
+    def first(self, own):
+        self.pass_on(own, self.me, 0, 0)
+        self.pass_on(own, self.me, 1, 0)
+
+    def pass_on(self, src, shard, way, step):
+        reach = (self.me < self.count - 1) if way == 0 else (self.me > 0)
+
+        @pl.when(reach)
+        def _():
+            self.copy(src, shard, way, step).start()
+
+    def hop(self, step):
+        for way in (0, 1):
+            shard = self.me - step if way == 0 else self.me + step
+            there = (shard >= 0) if way == 0 else (shard < self.count)
+
+            @pl.when(there)
+            def _():
+                self.copy(self.view(shard), shard, way, step).wait_recv()
+                if step < self.count - 1:
+                    self.pass_on(self.view(shard), shard, way, step)
+
+    def finish(self, own):
+        for way in (0, 1):
+            reach = (self.me < self.count - 1) if way == 0 else (self.me > 0)
+            for step in range(self.count - 1):
+                shard = self.me - step if way == 0 else self.me + step
+                there = (shard >= 0) if way == 0 else (shard < self.count)
+
+                @pl.when(reach & there)
+                def _():
+                    src = own if step == 0 else self.view(shard)
+                    self.copy(src, shard, way, step).wait_send()
+
+
+def spread_kernel(
+    seqs, heads, give, take, x, g, gating, payload, address, stepping, readout,
+    x_out, g_out, w_out, r_out,
+    send_x, send_g, recv_x, recv_g, work_x, work_g, w_own, r_own,
+    sent, got, w_sent, w_got, r_sent, r_got, rim_sent, rim_got, own_sem,
+    x_line_sent, x_line_got, g_line_sent, g_line_got,
+):
+    me, mine = lax.axis_index("seq"), lax.axis_index("head")
+    blocks, _, width = x.shape
+    rows = blocks * BLOCK
+    depth = gating.shape[0]
+    inner = gating.shape[1]
+    greet(seqs, heads)
+
+    @pl.loop(0, seqs)
+    def _(i):
+        to = lax.rem(me + i, seqs)
+        send_x[to] = x[give[to]]
+        send_g[to] = g[give[to]]
+
+        @pl.when(i == 0)
+        def _():
+            recv_x[to] = x[give[to]]
+            recv_g[to] = g[give[to]]
+
+        @pl.when(i > 0)
+        def _():
+            remote(send_x.at[to], recv_x.at[me], sent.at[0, to], got.at[0, me], {"seq": to}).start()
+
+    w_own[:, :inner] = gating[...].astype(jnp.bfloat16)
+    w_own[:, inner : 2 * inner] = payload[...].astype(jnp.bfloat16)
+    state2 = address.shape[1]
+    w_own[:, 2 * inner : 2 * inner + state2] = address[...].astype(jnp.bfloat16)
+    w_own[:, 2 * inner + state2 :] = jnp.zeros((depth, LANES), jnp.bfloat16)
+    w_own[:, 2 * inner + state2 : 2 * inner + state2 + stepping.shape[1]] = stepping[...].astype(jnp.bfloat16)
+    r_own[...] = readout[...].T.astype(jnp.bfloat16)
+
+    def rows_of(device):
+        return pl.ds(pl.multiple_of(device * depth, depth), depth)
+
+    def shard_copy(own, out, send, recv, to):
+        return remote(own, out.at[rows_of(me)], send.at[to], recv.at[me], {"seq": to})
+
+    own_w = pltpu.make_async_copy(w_own, w_out.at[rows_of(me)], own_sem.at[0])
+    own_r = pltpu.make_async_copy(r_own, r_out.at[rows_of(me)], own_sem.at[1])
+    own_w.start()
+    own_r.start()
+
+    @pl.loop(1, seqs)
+    def _(i):
+        to = lax.rem(me + i, seqs)
+        shard_copy(w_own, w_out, w_sent, w_got, to).start()
+        remote(send_g.at[to], recv_g.at[me], sent.at[1, to], got.at[1, me], {"seq": to}).start()
+
+    @pl.loop(1, seqs)
+    def _(i):
+        shard_copy(r_own, r_out, r_sent, r_got, lax.rem(me + i, seqs)).start()
+
+    def arrange(which, received, work):
+        @pl.loop(1, seqs)
+        def _(i):
+            source = lax.rem(me + i, seqs)
+            remote(received.at[source], received.at[source], sent.at[which, source], got.at[which, source], {"seq": source}).wait_recv()
+
+        for k in range(blocks):
+            work[pl.ds(k * BLOCK, BLOCK), :] = received[take[k]]
+
+    arrange(0, recv_x, work_x)
+    after = lax.rem(me + 1, seqs)
+    rim = remote(work_x.at[pl.ds(rows - HALO, HALO)], work_x.at[pl.ds(rows, HALO)], rim_sent, rim_got, {"seq": after})
+    rim.start()
+    rim.wait()
+    x_line = Line(heads, x_out, width, x_line_sent, x_line_got)
+    g_line = Line(heads, g_out, width, g_line_sent, g_line_got)
+    own_x = pltpu.make_async_copy(work_x, x_line.view(mine), own_sem.at[2])
+    own_x.start()
+    x_line.first(work_x)
+    arrange(1, recv_g, work_g)
+    own_g = pltpu.make_async_copy(work_g, g_line.view(mine), own_sem.at[3])
+    own_g.start()
+    for step in range(1, heads):
+        x_line.hop(step)
+        if step == 1:
+            g_line.first(work_g)
+    for step in range(1, heads):
+        g_line.hop(step)
+    x_line.finish(work_x)
+    g_line.finish(work_g)
+    for copy in (own_w, own_r, own_x, own_g):
+        copy.wait()
+
+    @pl.loop(1, seqs)
+    def _(i):
+        other = lax.rem(me + i, seqs)
+        for which, buffer in ((0, send_x), (1, send_g)):
+            remote(buffer.at[other], buffer.at[other], sent.at[which, other], got.at[which, other], {"seq": other}).wait_send()
+        for own, out, send, recv in ((w_own, w_out, w_sent, w_got), (r_own, r_out, r_sent, r_got)):
+            copy = remote(own, out.at[rows_of(other)], send.at[other], recv.at[other], {"seq": other})
+            copy.wait_send()
+            copy.wait_recv()
+
+
+def spread(give, take, x, g, gating, payload, address, stepping, readout):
+    seqs, heads = lax.axis_size("seq"), lax.axis_size("head")
+    rows, width = x.shape
+    depth, inner = gating.shape
+    total = depth * seqs
+    columns = 2 * inner + address.shape[1] + LANES
+    low = jnp.bfloat16
+    block = (seqs, BLOCK, width)
+    any_space = pl.BlockSpec(memory_space=pl.ANY)
+    vmem = pl.BlockSpec(memory_space=VMEM)
+    return pl.pallas_call(
+        functools.partial(spread_kernel, seqs, heads),
+        out_shape=(
+            jax.ShapeDtypeStruct((rows + HALO, total), low),
+            jax.ShapeDtypeStruct((rows, total), low),
+            jax.ShapeDtypeStruct((total, columns), low),
+            jax.ShapeDtypeStruct((total, inner), low),
+        ),
+        in_specs=[pl.BlockSpec(memory_space=SMEM)] * 2 + [vmem] * 7,
+        out_specs=(any_space,) * 4,
+        scratch_shapes=[
+            pltpu.VMEM(block, low), pltpu.VMEM(block, low), pltpu.VMEM(block, low), pltpu.VMEM(block, low),
+            pltpu.VMEM((rows + HALO, width), low), pltpu.VMEM((rows, width), low),
+            pltpu.VMEM((depth, columns), low), pltpu.VMEM((depth, inner), low),
+            DMA((2, seqs)), DMA((2, seqs)), DMA((seqs,)), DMA((seqs,)), DMA((seqs,)), DMA((seqs,)),
+            DMA, DMA, DMA((4,)),
+            DMA((2, heads)), DMA((heads,)), DMA((2, heads)), DMA((heads,)),
+        ],
+        compiler_params=pltpu.CompilerParams(
+            collective_id=0, has_side_effects=True, vmem_limit_bytes=48 * MIB
+        ),
+        name="spread",
+    )(give, take, x.reshape(-1, BLOCK, width), g.reshape(-1, BLOCK, width), gating, payload, address, stepping, readout)
 
 
 EPS = 1e-05
@@ -154,38 +382,23 @@
     target_dev = target // per_dev
     source_dev = lax.dynamic_slice_in_dim(placement, seq_index * per_dev, per_dev, 0) // per_dev
     devices = jnp.arange(seq_count, dtype=jnp.int32)
-    moved_in = (
-        lax.all_to_all(
-            route_blocks(inputs, target_dev, devices, BLOCK),
-            "seq",
-            split_axis=0,
-            concat_axis=0,
-            tiled=True,
-        ),
-        lax.all_to_all(
-            route_blocks(cotangent, target_dev, devices, BLOCK),
-            "seq",
-            split_axis=0,
-            concat_axis=0,
-            tiled=True,
-        ),
-    )
-    x_local = pick_blocks(moved_in[0], source_dev, devices)
-    g_local = pick_blocks(moved_in[1], source_dev, devices)
-    x_full, g_full = (
-        lax.all_gather(x_local, "head", axis=1, tiled=True),
-        lax.all_gather(g_local, "head", axis=1, tiled=True),
-    )
+    local_block = jnp.arange(per_dev, dtype=jnp.int32)
+    give = jnp.sum(jnp.where(target_dev[None, :] == devices[:, None], local_block[None, :], 0), axis=1)
+    x_rows, g_full, w_all, w_read_t = spread(
+        give, source_dev, inputs, cotangent, gating, payload, address, stepping, readout
+    )
+    x_full = x_rows[:row_count]
+    share = inputs.shape[1]
+    x_local = lax.dynamic_slice_in_dim(x_full, head_index * share, share, 1)
+    g_local = lax.dynamic_slice_in_dim(g_full, head_index * share, share, 1)
+    w_read = w_read_t.T
+    inner_width = gating.shape[1]
+    w_gate, w_pay = w_all[:, :inner_width], w_all[:, inner_width : 2 * inner_width]
+    addr_end = 2 * inner_width + address.shape[1]
+    w_addr, w_step = w_all[:, 2 * inner_width : addr_end], w_all[:, addr_end : addr_end + stepping.shape[1]]
     u_full = x_full.astype(jnp.float32)
     inv_rms = lax.rsqrt(jnp.mean(u_full * u_full, axis=1, keepdims=True) + EPS)
     normed = (u_full * inv_rms * prenorm[None, :]).astype(jnp.bfloat16)
-    w_gate, w_pay, w_addr, w_step, w_read = (
-        lax.all_gather(gating.astype(jnp.bfloat16), "seq", axis=0, tiled=True),
-        lax.all_gather(payload.astype(jnp.bfloat16), "seq", axis=0, tiled=True),
-        lax.all_gather(address.astype(jnp.bfloat16), "seq", axis=0, tiled=True),
-        lax.all_gather(stepping.astype(jnp.bfloat16), "seq", axis=0, tiled=True),
-        lax.all_gather(readout.astype(jnp.bfloat16), "seq", axis=1, tiled=True),
-    )
     gate_pre = jnp.dot(normed, w_gate, preferred_element_type=jnp.float32)
     value_pre = jnp.dot(normed, w_pay, preferred_element_type=jnp.float32).astype(jnp.bfloat16)
     addr_pre = jnp.dot(normed, w_addr, preferred_element_type=jnp.float32).astype(jnp.bfloat16)

time: 690 us -> 711 us (1.030)
  Pallas kernels: 0 us -> 128 us
  waiting for transfers between devices: 262 us -> 156 us
  blocking collectives: 88.3 us -> 64.5 us
  other arithmetic: 107 us -> 120 us
  local copies, waits for them, and re-layouts: 92.2 us -> 105 us
  starting transfers between devices: 27.3 us -> 18.9 us
    pallas_call x0 -> x1, Pallas kernels: none -> 128 us  [spread(): pl.pallas_call(functools.partial(spread_kernel, seqs, heads), out_shape=(...]
    all_gather x5 -> x0, waiting for transfers between devices: 76.6 us -> none  [the longest x1 35.5 us: on_device(): lax.all_gather(g_local, 'head', axis=1, tiled=True)]
    all_gather x2 -> x0, blocking collectives: 20.6 us -> none  [the longest x1 10.8 us: on_device(): lax.all_gather(stepping.astype(jnp.bfloat16), 'seq', axis=0, tiled=True)]
    unnamed x21 -> x16, waiting for transfers between devices: 57.8 us -> 41.9 us
    all_to_all x2 -> x0, waiting for transfers between devices: 10.3 us -> none  [the longest x1 6.61 us: on_device(): lax.all_to_all(route_blocks(inputs, target_dev, devices, BLOCK), 'seq', s...]
    all_to_all x2 -> x0, starting transfers between devices: 9.47 us -> none  [the longest x1 5.37 us: on_device(): lax.all_to_all(route_blocks(inputs, target_dev, devices, BLOCK), 'seq', s...]
    unnamed x270 -> x225, local copies, waits for them, and re-layouts: 25.4 us -> 33.7 us
  transfers between devices with their start and end apart: 22 -> 15, of which waited for: 12 -> 8; matrix products, arithmetic and copies ran while one was open for 28% -> 24% of each run, Pallas kernels for 0% -> 0%
where the time goes in v1:
time: 711 us; the launch traced here: 699 us
  waiting for transfers between devices  156 us (22%)
  Pallas kernels  128 us (18%)
  other arithmetic  120 us (17%)
  local copies, waits for them, and re-layouts  105 us (15%)
  matrix products  90 us (13%)
  blocking collectives  64.5 us (9%)
  starting transfers between devices  18.9 us (3%)
  between operations  16.3 us (2%)
    pallas_call x1, Pallas kernels, spread(): pl.pallas_call(functools.partial(spread_kernel, seqs, heads), out_shape=(...  128 us
    unnamed x16, waiting for transfers between devices  41.9 us
    reduce_scatter x1, waiting for transfers between devices, on_device(): lax.psum_scatter(grad_pay_w.astype(jnp.bfloat16), 'seq', scatter_dimensio...  38.5 us
    reduce_scatter x1, waiting for transfers between devices, on_device(): lax.psum_scatter(grad_part.astype(jnp.bfloat16), 'head', scatter_dimensio...  38.4 us
    reduce_scatter x1, waiting for transfers between devices, on_device(): lax.psum_scatter(out_part.astype(jnp.bfloat16), 'head', scatter_dimension...  35.9 us
    unnamed x225, local copies, waits for them, and re-layouts  33.7 us
    unnamed x2, blocking collectives  26.3 us
    psum x1, blocking collectives, on_device(): lax.psum((grad_prenorm, grad_kernels, grad_offsets, grad_filters, grad_sh...  22 us
  transfers between devices with their start and end apart: 15, of which 8 were waited for; matrix products, arithmetic and copies ran while one was open for 24% of the time, Pallas kernels for 0%

profile of v1, /device:TPU:1, one launch (start us, length us, event | category | flops | bytes accessed | tf_op | source)
XLA Modules:
  0.0 699.4 jit_solution(3202330592080159461)
XLA Ops:
  15.6 128.2 %spread.1 = (bf16[1040,1024]{1,0:T(8,128)(2,1)}, bf16[1024,1024]{1,0:T(8,128)(2,1)S(1)}, bf16[1024,1408]{1,0:T(8,128)(2,1)}, bf16[1024,512]{1,0:T(8,128)(2,1)S(1)}) custom-call(s32[8]{0:T(128)S(1)} %select_reduce_fusion.give, s32[8]{0:T(128)S(1)} %get-tuple-element.670.take, bf16[8,128,256]{2,1,0:T(8,128)(2,1)S(1)} %bitcast.218, ...), custom_call_target="tpu_custom_call" | custom-call | tf_op jit(solution)/shard_map/spread/pallas_call | solution.py:215
  152.9 4.7 collective-permute-start
  193.0 4.3 while.89
  204.6 10.9 %all-reduce.19 = bf16[64]{0:T(256)(128)(2,1)S(1)} all-reduce(bf16[64]{0:T(256)(128)(2,1)} %dynamic-update-slice), channel_id=2, replica_groups=mesh['seq'=8,'head'=4] {'seq'}, use_global_device_ids=true, to_apply=%add.19 | all-reduce | flops 64 | bytes 256
  219.9 13.7 %while.90 = (s32[]{:T(128)}, f32[8,64,128]{2,1,0:T(8,128)S(1)}, s32[]{:T(128)}, bf16[8,8]{1,0:T(8,128)(2,1)}, bf16[8,8,64,128]{3,2,1,0:T(8,128)(2,1)}, /*index=5*/s32[]{:T(128)}, s32[]{:T(128)}) while((s32[]{:T(128)}, f32[8,64,128]{2,1,0:T(8,128)S(1)}, s32[]{:T(128)}, bf16[8,8]{1,0:T(8,128)(2,1)}, ...), condition=%wide.region_10.11_spmd.clone, body=%wide.region_9.10_spmd.clone.sunk | while | flops 327692 | bytes 655553 | solution.py:267
  234.8 7.2 %while.86 = (s32[]{:T(128)}, f32[8,64,128]{2,1,0:T(8,128)S(1)}, f32[4,8,64,128]{3,2,1,0:T(8,128)}, f32[4,8]{1,0:T(4,128)S(1)}, f32[4,8,64,128]{3,2,1,0:T(8,128)}, /*index=5*/s32[]{:T(128)}) while((s32[]{:T(128)}, f32[8,64,128]{2,1,0:T(8,128)S(1)}, f32[4,8,64,128]{3,2,1,0:T(8,128)}, f32[4,8]{1,0:T(4,128)S(1)}, f32[4,8,64,128]{3,2,1,0:T(8,128)}, ...), condition=%wide.region_12.13_spmd, body=%wide.region_11.12_spmd.sunk | while | flops 131074 | bytes 1310905 | solution.py:468
  253.4 4.8 reshape.473
  258.2 6.1 multiply_reduce_fusion.9
  264.3 9.6 %psum.77 = f32[1024]{0:T(1024)S(1)} all-reduce(f32[1024]{0:T(1024)S(1)} %get-tuple-element.623), channel_id=1, replica_groups=mesh['seq'=8,'head'=4] {'head'}, use_global_device_ids=true, to_apply=%region_14.15 | all-reduce | flops 1024 | bytes 8192 | tf_op jit(solution)/shard_map/psum | solution.py:479
  273.9 4.8 multiply_reduce_fusion.2
  278.8 6.6 psum.78
  285.4 6.1 multiply_reduce_fusion.3
  301.1 8.5 %while.91 = (s32[]{:T(128)}, f32[8]{0:T(128)}, f32[8,64,128]{2,1,0:T(8,128)S(1)}, f32[4,8]{1,0:T(4,128)S(1)}, f32[4,8,64,128]{3,2,1,0:T(8,128)}, /*index=5*/s32[]{:T(128)}, s32[]{:T(128)}, s32[]{:T(128)}) while((s32[]{:T(128)}, f32[8]{0:T(128)}, f32[8,64,128]{2,1,0:T(8,128)S(1)}, f32[4,8]{1,0:T(4,128)S(1)}, ...), condition=%wide.region_19.20_spmd.clone, body=%wide.region_18.19_spmd.clone.sunk | while | flops 196628 | bytes 786716 | solution.py:527
  312.2 15.4 %all-reduce.20 = f32[64]{0:T(128)S(1)} all-reduce(f32[64]{0:T(128)} %dynamic-update-slice.1), channel_id=4, replica_groups=mesh['seq'=8,'head'=4] {'seq'}, use_global_device_ids=true, to_apply=%add.20 | all-reduce | flops 64 | bytes 512
  330.6 8.2 %fusion.8 = (f32[4,8,256]{2,1,0:T(8,128)}, f32[4,8,256]{2,1,0:T(8,128)S(1)}, f32[4,8,256]{2,1,0:T(8,128)}, bf16[4,256,256]{2,1,0:T(8,128)(2,1)S(1)}) fusion(f32[4,8,256]{2,1,0:T(8,128)S(1)} %bitcast.249, f32[4,8,256]{2,1,0:T(8,128)S(1)} %add_bitcast_fusion.1, f32[4,256,256]{2,1,0:T(8,128)} %fusion.118, pred[4,256,256]{2,1,0:T(8,128)(4,1)S(1)} %copy-done.44, ...), kind=kOutput, calls=%fused_computation.36 | convolution fusion | flops 299606016 | bytes 4096000 | tf_op jit(solution)/shard_map/cthp,cshp->chts/dot_general | solution.py:511
  340.9 10.8 %while.87 = (s32[]{:T(128)}, f32[8,64,128]{2,1,0:T(8,128)S(1)}, s32[]{:T(128)}, f32[8,8]{1,0:T(8,128)}, f32[8,8,64,128]{3,2,1,0:T(8,128)}, /*index=5*/s32[]{:T(128)}, s32[]{:T(128)}, s32[]{:T(128)}, s32[]{:T(128)}) while((s32[]{:T(128)}, f32[8,64,128]{2,1,0:T(8,128)S(1)}, s32[]{:T(128)}, f32[8,8]{1,0:T(8,128)}, ...), condition=%wide.region_21.22_spmd, body=%wide.region_20.21_spmd.sunk | while | flops 131078 | bytes 786683 | solution.py:283
  352.8 7.2 %while.88 = (s32[]{:T(128)}, f32[8,64,128]{2,1,0:T(8,128)S(1)}, f32[4,8,64,128]{3,2,1,0:T(8,128)}, f32[4,8]{1,0:T(4,128)S(1)}, f32[4,8,64,128]{3,2,1,0:T(8,128)}, /*index=5*/s32[]{:T(128)}, s32[]{:T(128)}) while((s32[]{:T(128)}, f32[8,64,128]{2,1,0:T(8,128)S(1)}, f32[4,8,64,128]{3,2,1,0:T(8,128)}, f32[4,8]{1,0:T(4,128)S(1)}, ...), condition=%wide.region_23.24_spmd, body=%wide.region_22.23_spmd.sunk | while | flops 131075 | bytes 1310925 | solution.py:529
  381.5 4.9 fusion.41
  400.5 9.9 %reduce-window.31 = f32[4,8,2,128]{3,1,2,0:T(8,128)S(1)} reduce-window(f32[4,8,2,128]{3,1,2,0:T(8,128)S(1)} %copy.288, f32[]{:T(128)} %constant.228.clone.1), window={size=1x1x1x128 pad=0_0x0_0x0_0x0_127}, to_apply=%region_33.34 | reduce-window | flops 1040384 | bytes 65540 | tf_op jit(solution)/shard_map/reduce-window.3
  420.2 4.3 convolution_convert_fusion
  425.7 5.7 fusion.24
  435.4 4.9 reshape.475
  440.3 7.4 %multiply_reduce_fusion.7 = (f32[512]{0:T(512)}, f32[512]{0:T(512)}, f32[512]{0:T(512)}, f32[512]{0:T(512)}, f32[512]{0:T(512)}, /*index=5*/f32[1024,512]{1,0:T(8,128)S(1)}) fusion(f32[1027,512]{1,0:T(8,128)} %copy-done.6, f32[1024]{0:T(1024)S(1)} %get-tuple-element.647, f32[1024]{0:T(1024)S(1)} %get-tuple-element.648, f32[1024]{0:T(1024)S(1)} %get-tuple-element.646, ...), kind=kLoop, calls=%fused_computation.76 | loop fusion | flops 11007488 | bytes 14702592 | tf_op jit(solution)/shard_map/transpose(jvp())/reduce_sum | solution.py:298
  484.3 16.7 %reduce-scatter.34.cloned.1.call-done = bf16[128,8]{1,0:T(8,128)(2,1)} async-done(((bf16[1024,8]{1,0:T(8,128)(2,1)}), bf16[128,8]{1,0:T(8,128)(2,1)}) %reduce-scatter.34.cloned.1.call-update) | async-done | bytes 2064
  511.7 35.9 %reduce-scatter.20.cloned.1.call-done = bf16[1024,256]{1,0:T(8,128)(2,1)} async-done(((bf16[1024,1024]{1,0:T(8,128)(2,1)}), bf16[1024,256]{1,0:T(8,128)(2,1)}) %reduce-scatter.20.cloned.1.call-update) | async-done | bytes 524304 | tf_op jit(solution)/shard_map/reduce_scatter | solution.py:609
  550.2 4.5 all-to-all-start
  554.7 38.4 %reduce-scatter.22.cloned.1.call-done = bf16[1024,256]{1,0:T(8,128)(2,1)} async-done(((bf16[1024,1024]{1,0:T(8,128)(2,1)}), bf16[1024,256]{1,0:T(8,128)(2,1)}) %reduce-scatter.22.cloned.1.call-update) | async-done | bytes 524304 | tf_op jit(solution)/shard_map/reduce_scatter | solution.py:612
  595.8 4.5 all-to-all-start.1
  601.6 12.0 %reduce-scatter.30.cloned.1.call-done = bf16[256,1]{1,0:T(8,128)(2,1)} async-done(((bf16[1024,1]{1,0:T(8,128)(2,1)}), bf16[256,1]{1,0:T(8,128)(2,1)}) %reduce-scatter.30.cloned.1.call-update) | async-done | bytes 528
  614.6 22.0 %all-reduce.21 = (f32[256]{0:T(256)}, f32[4,512]{1,0:T(4,128)}, f32[512]{0:T(512)}, f32[4,64]{1,0:T(4,128)}, f32[64]{0:T(128)}, /*index=5*/f32[8]{0:T(128)}, f32[8]{0:T(128)}, f32[8]{0:T(128)}, f32[512]{0:T(512)}) all-reduce(f32[256]{0:T(256)S(1)} %bitcast.264, ...), channel_id=1, replica_groups=mesh['seq'=8,'head'=4] {'seq'}, use_global_device_ids=true, to_apply=%region_39.40 | all-reduce | flops 3672 | bytes 29376 | tf_op jit(solution)/shard_map/psum | solution.py:659
  636.6 12.9 %reduce-scatter.32.cloned.1.call-done = bf16[128,64]{1,0:T(8,128)(2,1)} async-done(((bf16[1024,64]{1,0:T(8,128)(2,1)}), bf16[128,64]{1,0:T(8,128)(2,1)}) %reduce-scatter.32.cloned.1.call-update) | async-done | bytes 16400
  651.0 38.5 %reduce-scatter.26.cloned.1.call-done = bf16[128,512]{1,0:T(8,128)(2,1)} async-done(((bf16[1024,512]{1,0:T(8,128)(2,1)}), bf16[128,512]{1,0:T(8,128)(2,1)}) %reduce-scatter.26.cloned.1.call-update) | async-done | bytes 131088 | tf_op jit(solution)/shard_map/reduce_scatter | solution.py:646
  (476 shorter events, 254.3 us)
Async XLA Ops:
  7.2 212.7 %all-gather.7.cloned.1.call-start = ((), (), s32[]{:S(2)}) async-start(), calls=%async_computation.15 | async-start | bytes 1179648 | tf_op jit(solution)/shard_map/all_gather | solution.py:252
  8.9 137.6 %copy-start.57 = (f32[1024]{0:T(1024)S(1)}, f32[1024]{0:T(1024)}, u32[]{:S(2)}) copy-start(f32[1024]{0:T(1024)} %param.34) | copy-start | bytes 12292
  149.9 9.2 %copy-start.100 = (f32[8]{0:T(128)S(1)}, f32[8]{0:T(128)}, u32[]{:S(2)}) copy-start(f32[8]{0:T(128)} %param.43) | copy-start | bytes 100
  152.9 22.4 %collective-permute-start = (bf16[3,768]{1,0:T(4,128)(2,1)S(1)}, bf16[3,768]{1,0:T(4,128)(2,1)S(1)}, u32[]{:S(2)}, u32[]{:S(2)}) collective-permute-start(bf16[3,768]{1,0:T(4,128)(2,1)S(1)} %pad_maximum_fusion.2), channel_id=1, source_target_pairs={{0,4},{4,8},{8,12},{12,16},{16,20},{20,24},{24,28},{1,5},{5,9},{9,... | collective-permute-start | bytes 13832 | tf_op jit(solution)/shard_map/ppermute | solution.py:246
  158.4 15.0 %copy-start.91 = (f32[4]{0:T(128)}, f32[4]{0:T(128)S(1)}, u32[]{:S(2)}) copy-start(f32[4]{0:T(128)S(1)} %compare_convert_fusion.2) | copy-start | bytes 52
  158.5 18.4 %copy-start.53 = (f32[1,512]{1,0:T(1,128)}, f32[1,512]{1,0:T(1,128)S(1)}, u32[]{:S(2)}) copy-start(f32[1,512]{1,0:T(1,128)S(1)} %get-tuple-element.644) | copy-start | bytes 6148
  158.5 18.4 %copy-start.55 = (f32[1,512]{1,0:T(1,128)}, f32[1,512]{1,0:T(1,128)S(1)}, u32[]{:S(2)}) copy-start(f32[1,512]{1,0:T(1,128)S(1)} %get-tuple-element.645) | copy-start | bytes 6148
  198.0 142.9 %all-gather.9.cloned.1.call-start = ((), (), s32[]{:S(2)}) async-start(), calls=%async_computation.16 | async-start | bytes 2359296 | tf_op jit(solution)/shard_map/all_gather | solution.py:274
  258.2 15.7 %copy-start.93 = (f32[512]{0:T(512)S(1)}, f32[512]{0:T(512)}, u32[]{:S(2)}) copy-start(f32[512]{0:T(512)} %param.46) | copy-start | bytes 6148
  273.9 11.5 %copy-start.62 = (f32[1024]{0:T(1024)}, f32[1024]{0:T(1024)S(1)}, u32[]{:S(2)}) copy-start(f32[1024]{0:T(1024)S(1)} %get-tuple-element.652) | copy-start | bytes 12292
  310.4 20.2 %copy-start.44 = (pred[4,256,256]{2,1,0:T(8,128)(4,1)S(1)}, pred[4,256,256]{2,1,0:T(8,128)(4,1)}, u32[]{:S(2)}) copy-start(pred[4,256,256]{2,1,0:T(8,128)(4,1)} %compare_and_fusion) | copy-start | bytes 786436
  310.4 145.3 %reduce-scatter.28.cloned.1.call-start = ((), (), s32[]{:S(2)}) async-start(), calls=%async_computation.17 | async-start | bytes 655360
  330.6 9.0 %copy-start.31 = (bf16[1024,128]{1,0:T(8,128)(2,1)S(1)}, bf16[1024,128]{1,0:T(8,128)(2,1)}, u32[]{:S(2)}) copy-start(bf16[1024,128]{1,0:T(8,128)(2,1)} %copy-done.30) | copy-start | bytes 786436
  365.6 113.3 %reduce-scatter.36.cloned.1.call-start = ((), (), s32[]{:S(2)}) async-start(), calls=%async_computation.21 | async-start | bytes 1179648
  374.5 106.2 %reduce-scatter.24.cloned.1.call-start = ((), (), s32[]{:S(2)}) async-start(), calls=%async_computation.13 | async-start | bytes 1179648 | tf_op jit(solution)/shard_map/reduce_scatter | solution.py:643
  388.9 112.1 %reduce-scatter.34.cloned.1.call-start = ((), (), s32[]{:S(2)}) async-start(), calls=%async_computation.20 | async-start | bytes 294912
  396.2 15.5 %copy-start.82 = (f32[8]{0:T(128)S(1)}, f32[8]{0:T(128)}, u32[]{:S(2)}) copy-start(f32[8]{0:T(128)} %copy-done.81) | copy-start | bytes 100
  420.1 127.5 %reduce-scatter.20.cloned.1.call-start = ((), (), s32[]{:S(2)}) async-start(), calls=%async_computation.11 | async-start | bytes 2621440 | tf_op jit(solution)/shard_map/reduce_scatter | solution.py:609
  424.5 168.6 %reduce-scatter.22.cloned.1.call-start = ((), (), s32[]{:S(2)}) async-start(), calls=%async_computation.12 | async-start | bytes 2621440 | tf_op jit(solution)/shard_map/reduce_scatter | solution.py:612
  459.0 6.7 collective-permute-start.1
  475.1 138.6 %reduce-scatter.30.cloned.1.call-start = ((), (), s32[]{:S(2)}) async-start(), calls=%async_computation.18 | async-start | bytes 327680
  504.1 145.5 %reduce-scatter.32.cloned.1.call-start = ((), (), s32[]{:S(2)}) async-start(), calls=%async_computation.19 | async-start | bytes 294912
  507.6 181.8 %reduce-scatter.26.cloned.1.call-start = ((), (), s32[]{:S(2)}) async-start(), calls=%async_computation.14 | async-start | bytes 1179648 | tf_op jit(solution)/shard_map/reduce_scatter | solution.py:646
  550.2 45.5 %all-to-all-start = ((bf16[8,128,256]{2,1,0:T(8,128)(2,1)}), bf16[8,128,256]{2,1,0:T(8,128)(2,1)S(1)}, u32[]{:S(2)}, u32[]{:S(2)}) async-start(bf16[8,128,256]{2,1,0:T(8,128)(2,1)} %copy.266), calls=%async_computation.1 | async-start | bytes 1048576 | tf_op jit(solution)/shard_map/all_to_all | solution.py:625
  554.7 45.6 %copy-start.72 = (s32[8]{0:T(128)S(1)}, s32[8]{0:T(128)}, u32[]{:S(2)}) copy-start(s32[8]{0:T(128)} %copy-done.71) | copy-start | bytes 100
  594.8 19.8 %copy-start.68 = (f32[512]{0:T(512)S(1)}, f32[512]{0:T(512)}, u32[]{:S(2)}) copy-start(f32[512]{0:T(512)} %get-tuple-element.538) | copy-start | bytes 6148
  594.8 19.8 %copy-start.83 = (f32[8]{0:T(128)S(1)}, f32[8]{0:T(128)}, u32[]{:S(2)}) copy-start(f32[8]{0:T(128)} %get-tuple-element.619) | copy-start | bytes 100
  594.8 19.8 %copy-start.84 = (f32[64]{0:T(128)S(1)}, f32[64]{0:T(128)}, u32[]{:S(2)}) copy-start(f32[64]{0:T(128)} %get-tuple-element.543) | copy-start | bytes 772
  594.8 19.8 %copy-start.89 = (f32[512]{0:T(512)S(1)}, f32[512]{0:T(512)}, u32[]{:S(2)}) copy-start(f32[512]{0:T(512)} %get-tuple-element.536) | copy-start | bytes 6148
  594.8 19.8 %copy-start.90 = (f32[8]{0:T(128)S(1)}, f32[8]{0:T(128)}, u32[]{:S(2)}) copy-start(f32[8]{0:T(128)} %reduce_sum.374) | copy-start | bytes 100
  594.9 19.8 %copy-start.98 = (f32[8]{0:T(128)S(1)}, f32[8]{0:T(128)}, u32[]{:S(2)}) copy-start(f32[8]{0:T(128)} %fusion.101) | copy-start | bytes 100
  595.8 95.3 %all-to-all-start.1 = ((bf16[8,128,256]{2,1,0:T(8,128)(2,1)}), bf16[8,128,256]{2,1,0:T(8,128)(2,1)S(1)}, u32[]{:S(2)}, u32[]{:S(2)}) async-start(bf16[8,128,256]{2,1,0:T(8,128)(2,1)} %copy.294), calls=%async_computation.3 | async-start | bytes 1048576 | tf_op jit(solution)/shard_map/all_to_all | solution.py:632
  (87 other events, 318.0 us)
Sparse Core Ops, SparseCore 0:
  198.1 21.7 all-gather.6
  310.5 30.3 all-gather.8
  365.8 20.3 reduce-scatter.27
  389.2 35.9 reduce-scatter.35
  428.2 35.9 reduce-scatter.23
  467.7 33.2 reduce-scatter.33
  503.4 44.1 reduce-scatter.19
  549.9 43.1 reduce-scatter.21
  596.1 17.5 reduce-scatter.29
  616.5 32.9 reduce-scatter.31
  653.0 36.3 reduce-scatter.25

commit v2 on v1

v2 whole, which is shorter than its diff:
```python
import functools

import jax
import jax.numpy as jnp
from jax import lax
from jax.experimental import pallas as pl
from jax.experimental.pallas import tpu as pltpu
from jax.sharding import PartitionSpec as P

D = 1024
GROUP = 256
BLOCK = 128
INNER = 2048
HDIM = 64
STATE = 128
TAPS = 4
HALO = 16
EDGE = 8
LANES = 128
EPS = 1e-05
MESH = pl.DeviceIdType.MESH
VMEM = pltpu.MemorySpace.VMEM
SMEM = pltpu.MemorySpace.SMEM
DMA = pltpu.SemaphoreType.DMA
MIB = 1 << 20
LOW = jnp.bfloat16
WIDE = jnp.float32


def shape(dims, kind):
    return jax.ShapeDtypeStruct(dims, kind)


def nn(a, b):
    return jnp.dot(a, b, preferred_element_type=WIDE)


def nt(a, b):
    return lax.dot_general(a, b, (((1,), (1,)), ((), ())), preferred_element_type=WIDE)


def tn(a, b):
    return lax.dot_general(a, b, (((0,), (0,)), ((), ())), preferred_element_type=WIDE)


def halves(x):
    high = x.astype(LOW)
    return high, (x - high.astype(WIDE)).astype(LOW)


def thirds(x):
    high = x.astype(LOW)
    rest = x - high.astype(WIDE)
    middle = rest.astype(LOW)
    return high, middle, (rest - middle.astype(WIDE)).astype(LOW)


def head_rows(inner):
    row = lax.broadcasted_iota(jnp.int32, (LANES, inner), 0)
    column = lax.broadcasted_iota(jnp.int32, (LANES, inner), 1)
    return jnp.where(column // HDIM == row, 1.0, 0.0).astype(LOW)


def head_columns(inner):
    row = lax.broadcasted_iota(jnp.int32, (inner, LANES), 0)
    column = lax.broadcasted_iota(jnp.int32, (inner, LANES), 1)
    return jnp.where(row // HDIM == column, 1.0, 0.0).astype(LOW)


def to_columns(x, spread):
    high, rest = halves(x)
    return nn(high, spread) + nn(rest, spread)


def to_heads(x, collect):
    high, rest = halves(x)
    return nn(high, collect) + nn(rest, collect)


def ones_before(count):
    row = lax.broadcasted_iota(jnp.int32, (count, count), 0)
    column = lax.broadcasted_iota(jnp.int32, (count, count), 1)
    return row >= column


def sum_before(x):
    matrix = jnp.where(ones_before(x.shape[0]), 1.0, 0.0).astype(LOW)
    high, middle, low = thirds(x)
    return nn(matrix, high) + (nn(matrix, middle) + nn(matrix, low))


def sum_after(x):
    count = x.shape[0]
    row = lax.broadcasted_iota(jnp.int32, (count, count), 0)
    column = lax.broadcasted_iota(jnp.int32, (count, count), 1)
    matrix = jnp.where(row <= column, 1.0, 0.0).astype(LOW)
    high, middle, low = thirds(x)
    return nn(matrix, high) + (nn(matrix, middle) + nn(matrix, low))


def sigmoid(x):
    return 0.5 * jnp.tanh(0.5 * x) + 0.5


def step_terms(raw, heads):
    z = jnp.exp(-jnp.abs(raw))
    series = 1.0 - z * (0.5 - z * (1.0 / 3.0 - z * (0.25 - z * 0.2)))
    small = z < 0.03
    log1p = jnp.where(small, z * series, jnp.log(1.0 + z))
    soft = jnp.maximum(raw, 0.0) + log1p
    one = 1.0 / (1.0 + z)
    sig = jnp.where(raw >= 0, one, z * one)
    ratio = jnp.where(small & (raw < 0), one / series, sig / jnp.maximum(soft, 1e-20))
    lane = lax.broadcasted_iota(jnp.int32, raw.shape, 1)
    return jnp.where(lane < heads, soft, 0.0), sig, ratio


def greet(seq_peers, head_peers):
    barrier = pltpu.get_barrier_semaphore()
    count = 0
    if seq_peers > 1:
        me = lax.axis_index("seq")

        @pl.loop(1, seq_peers)
        def _(i):
            pl.semaphore_signal(
                barrier, inc=1, device_id={"seq": lax.rem(me + i, seq_peers)}, device_id_type=MESH
            )

        count += seq_peers - 1
    if head_peers > 1:
        mine = lax.axis_index("head")

        @pl.loop(1, head_peers)
        def _(i):
            pl.semaphore_signal(
                barrier, inc=1, device_id={"head": lax.rem(mine + i, head_peers)}, device_id_type=MESH
            )

        count += head_peers - 1
    pl.semaphore_wait(barrier, count)


def remote(src, dst, send_sem, recv_sem, where):
    return pltpu.make_async_remote_copy(
        src_ref=src, dst_ref=dst, send_sem=send_sem, recv_sem=recv_sem, device_id=where, device_id_type=MESH
    )


class Line:
    def __init__(self, count, out, width, send, recv):
        self.count, self.out, self.width, self.send, self.recv = count, out, width, send, recv
        self.me = lax.axis_index("head")

    def view(self, shard):
        return self.out.at[:, pl.ds(pl.multiple_of(shard * self.width, LANES), self.width)]

    def copy(self, src, shard, way, step):
        return remote(
            src, self.view(shard), self.send.at[way, step], self.recv.at[shard], {"head": self.me + (1 - 2 * way)}
        )

    def first(self, own):
        self.pass_on(own, self.me, 0, 0)
        self.pass_on(own, self.me, 1, 0)

    def pass_on(self, src, shard, way, step):
        reach = (self.me < self.count - 1) if way == 0 else (self.me > 0)

        @pl.when(reach)
        def _():
            self.copy(src, shard, way, step).start()

    def hop(self, step):
        for way in (0, 1):
            shard = self.me - step if way == 0 else self.me + step
            there = (shard >= 0) if way == 0 else (shard < self.count)

            @pl.when(there)
            def _():
                self.copy(self.view(shard), shard, way, step).wait_recv()
                if step < self.count - 1:
                    self.pass_on(self.view(shard), shard, way, step)

    def finish(self, own):
        for way in (0, 1):
            reach = (self.me < self.count - 1) if way == 0 else (self.me > 0)
            for step in range(self.count - 1):
                shard = self.me - step if way == 0 else self.me + step
                there = (shard >= 0) if way == 0 else (shard < self.count)

                @pl.when(reach & there)
                def _():
                    src = own if step == 0 else self.view(shard)
                    self.copy(src, shard, way, step).wait_send()


class Plane:
    def __init__(self, seqs, view, sent, got, passed, way=0):
        self.chips, self.view, self.sent, self.got, self.passed, self.way = seqs // 2, view, sent, got, passed, way
        self.me = lax.axis_index("seq")
        self.core = lax.rem(self.me, 2)
        self.chip = self.me // 2
        self.mate = self.me + 1 - 2 * self.core

    def forward(self, chip):
        return (chip > self.chip) if self.way == 1 else (chip < self.chip) if self.way == -1 else (chip >= 0)

    def backward(self, chip):
        return (chip < self.chip) if self.way == 1 else (chip > self.chip) if self.way == -1 else (chip >= 0)

    def each_chip(self, body):
        @pl.loop(1, self.chips)
        def _(i):
            body(lax.rem(self.chip + i, self.chips))

    def copy(self, src, source, to, sem):
        return remote(src, self.view(source), sem, self.got.at[source], {"seq": to})

    def start(self, own):
        def send(chip):
            to = 2 * chip + self.core

            @pl.when(self.forward(chip))
            def _():
                self.copy(own, self.me, to, self.sent.at[to]).start()

        self.each_chip(send)
        self.copy(own, self.me, self.mate, self.sent.at[self.mate]).start()

    def relay(self):
        def take(chip):
            source = 2 * chip + self.core

            @pl.when(self.backward(chip))
            def _():
                landed = self.view(source)
                self.copy(landed, source, self.mate, self.passed.at[source]).wait_recv()
                self.copy(landed, source, self.mate, self.passed.at[source]).start()

        self.each_chip(take)

    def finish(self, own):
        def take(chip):
            source = 2 * chip + 1 - self.core

            @pl.when(self.backward(chip))
            def _():
                self.copy(self.view(source), source, self.mate, self.passed.at[source]).wait_recv()

        self.each_chip(take)
        self.copy(self.view(self.mate), self.mate, self.mate, self.sent.at[self.mate]).wait_recv()
        self.copy(own, self.me, self.mate, self.sent.at[self.mate]).wait_send()

        def drain(chip):
            same = 2 * chip + self.core

            @pl.when(self.forward(chip))
            def _():
                self.copy(own, self.me, same, self.sent.at[same]).wait_send()

            @pl.when(self.backward(chip))
            def _():
                self.copy(self.view(same), same, self.mate, self.passed.at[same]).wait_send()

        self.each_chip(drain)


def spread_kernel(
    seqs, heads, give, take, x, g, gating, payload, address, stepping, readout,
    x_out, g_out, w_out, r_out, work_x, work_g,
    send_x, send_g, recv_x, recv_g, w_own, r_own,
    sent, got, w_sent, w_got, w_passed, r_sent, r_got, r_passed, rim_sent, rim_got, own_sem,
    x_line_sent, x_line_got, g_line_sent, g_line_got,
):
    me, mine = lax.axis_index("seq"), lax.axis_index("head")
    blocks, _, width = x.shape
    rows = blocks * BLOCK
    depth, inner = gating.shape
    greet(seqs, heads)

    def post(which, source, outgoing, incoming):
        @pl.loop(1, seqs)
        def _(i):
            to = lax.rem(me + i, seqs)
            outgoing[to] = source[give[to]]
            remote(outgoing.at[to], incoming.at[me], sent.at[which, to], got.at[which, me], {"seq": to}).start()

        incoming[me] = source[give[me]]

    post(0, x, send_x, recv_x)
    post(1, g, send_g, recv_g)

    w_own[:, :inner] = gating[...].astype(LOW)
    w_own[:, inner : 2 * inner] = payload[...].astype(LOW)
    state2 = address.shape[1]
    w_own[:, 2 * inner : 2 * inner + state2] = address[...].astype(LOW)
    w_own[:, 2 * inner + state2 :] = jnp.zeros((depth, LANES), LOW)
    w_own[:, 2 * inner + state2 : 2 * inner + state2 + stepping.shape[1]] = stepping[...].astype(LOW)
    r_own[...] = readout[...].T.astype(LOW)

    def rows_of(device):
        return pl.ds(pl.multiple_of(device * depth, depth), depth)

    own_w = pltpu.make_async_copy(w_own, w_out.at[rows_of(me)], own_sem.at[0])
    own_r = pltpu.make_async_copy(r_own, r_out.at[rows_of(me)], own_sem.at[1])
    own_w.start()
    own_r.start()
    w_plane = Plane(seqs, lambda s: w_out.at[rows_of(s)], w_sent, w_got, w_passed)
    r_plane = Plane(seqs, lambda s: r_out.at[rows_of(s)], r_sent, r_got, r_passed)
    w_plane.start(w_own)
    r_plane.start(r_own)

    def arrange(which, received, work):
        @pl.loop(1, seqs)
        def _(i):
            source = lax.rem(me + i, seqs)
            remote(
                received.at[source], received.at[source], sent.at[which, source], got.at[which, source], {"seq": source}
            ).wait_recv()

        for k in range(blocks):
            work[pl.ds(k * BLOCK, BLOCK), :] = received[take[k]]

    arrange(0, recv_x, work_x)
    after = lax.rem(me + 1, seqs)
    rim = remote(
        work_x.at[pl.ds(rows - HALO, HALO)], work_x.at[pl.ds(rows, HALO)], rim_sent, rim_got, {"seq": after}
    )
    rim.start()
    rim.wait()
    x_line = Line(heads, x_out, width, x_line_sent, x_line_got)
    g_line = Line(heads, g_out, width, g_line_sent, g_line_got)
    own_x = pltpu.make_async_copy(work_x, x_line.view(mine), own_sem.at[2])
    own_x.start()
    x_line.first(work_x)
    arrange(1, recv_g, work_g)
    own_g = pltpu.make_async_copy(work_g, g_line.view(mine), own_sem.at[3])
    own_g.start()
    for step in range(1, heads):
        x_line.hop(step)
        if step == 1:
            g_line.first(work_g)
            w_plane.relay()
    r_plane.relay()
    for step in range(1, heads):
        g_line.hop(step)
    x_line.finish(work_x)
    g_line.finish(work_g)
    w_plane.finish(w_own)
    r_plane.finish(r_own)
    for copy in (own_w, own_r, own_x, own_g):
        copy.wait()

    @pl.loop(1, seqs)
    def _(i):
        other = lax.rem(me + i, seqs)
        for which, buffer in ((0, send_x), (1, send_g)):
            remote(
                buffer.at[other], buffer.at[other], sent.at[which, other], got.at[which, other], {"seq": other}
            ).wait_send()


ANY_SPEC = pl.BlockSpec(memory_space=pl.ANY)
VMEM_SPEC = pl.BlockSpec(memory_space=VMEM)
SMEM_SPEC = pl.BlockSpec(memory_space=SMEM)


def spread(give, take, x, g, gating, payload, address, stepping, readout):
    seqs, heads = lax.axis_size("seq"), lax.axis_size("head")
    rows, width = x.shape
    depth, inner = gating.shape
    total = depth * seqs
    columns = 2 * inner + address.shape[1] + LANES
    block = (seqs, BLOCK, width)
    return pl.pallas_call(
        functools.partial(spread_kernel, seqs, heads),
        out_shape=(
            shape((rows + HALO, total), LOW),
            shape((rows, total), LOW),
            shape((total, columns), LOW),
            shape((total, inner), LOW),
            shape((rows + HALO, width), LOW),
            shape((rows, width), LOW),
        ),
        in_specs=[SMEM_SPEC] * 2 + [VMEM_SPEC] * 7,
        out_specs=(ANY_SPEC,) * 4 + (VMEM_SPEC,) * 2,
        scratch_shapes=[
            pltpu.VMEM(block, LOW), pltpu.VMEM(block, LOW), pltpu.VMEM(block, LOW), pltpu.VMEM(block, LOW),
            pltpu.VMEM((depth, columns), LOW), pltpu.VMEM((depth, inner), LOW),
            DMA((2, seqs)), DMA((2, seqs)),
            DMA((seqs,)), DMA((seqs,)), DMA((seqs,)), DMA((seqs,)), DMA((seqs,)), DMA((seqs,)),
            DMA, DMA, DMA((4,)),
            DMA((2, heads)), DMA((heads,)), DMA((2, heads)), DMA((heads,)),
        ],
        compiler_params=pltpu.CompilerParams(
            collective_id=0, has_side_effects=True, vmem_limit_bytes=48 * MIB
        ),
        name="spread",
    )(give, take, x.reshape(-1, BLOCK, width), g.reshape(-1, BLOCK, width), gating, payload, address, stepping, readout)


def blockwise(dims, index):
    return pl.BlockSpec(dims, index)


def fixed(dims):
    return pl.BlockSpec(dims, lambda i: (0,) * len(dims))


def carry_columns(carry_row_t, collect):
    high, middle, low = thirds(jnp.broadcast_to(carry_row_t, (LANES, LANES)))
    return nn(collect, high) + (nn(collect, middle) + nn(collect, low))


def pair_lanes(slab):
    lane = lax.broadcasted_iota(jnp.int32, slab.shape, 1)
    zero = jnp.zeros_like(slab)
    return jnp.where(lane < HDIM, slab, zero), jnp.where(lane >= HDIM, slab, zero)


def front_kernel(
    heads, flags, u, rim, w, vec, prenorm, kernels, filters, offsets, shifts,
    normed_o, gate_o, pre_o, conv_o, act_o, raw_o, cum_o, part_o, local_o, msg_o, rim_o,
    ext, prev, state, prod,
):
    i = pl.program_id(0)
    inner = gate_o.shape[1]
    wide = pre_o.shape[1]
    taps = jnp.concatenate([kernels[...], filters[...]], axis=1)
    bias = jnp.concatenate([offsets[...], shifts[...]], axis=1)
    spread_m, collect = head_rows(inner), head_columns(inner)

    def normalize(block):
        rows = block.astype(WIDE)
        scale = lax.rsqrt(jnp.mean(rows * rows, axis=1, keepdims=True) + EPS)
        return (rows * scale * prenorm[...]).astype(LOW)

    @pl.when(i == 0)
    def _():
        before = nn(normalize(rim[...]), w[:, inner : inner + wide]).astype(LOW).astype(WIDE)
        prev[...] = before[HALO - EDGE :]
        rim_o[...] = before[HALO - EDGE :]
        state[...] = jnp.zeros_like(state)
        prod[...] = jnp.ones_like(prod)

    normed = normalize(u[...])
    normed_o[...] = normed
    gate_o[...] = nn(normed, w[:, :inner])
    pre = nn(normed, w[:, inner : inner + wide]).astype(LOW)
    pre_o[...] = pre
    lane = lax.broadcasted_iota(jnp.int32, (GROUP, LANES), 1)
    raw = jnp.where(lane < heads, nn(normed, w[:, inner + wide :]) + vec[0:1, :], 0.0)
    raw_o[...] = raw
    first, second = flags[2 * i], flags[2 * i + 1]
    same = (first, second)
    for half in range(2):
        rows = pl.ds(half * BLOCK, BLOCK)
        ext[0:EDGE, :] = prev[...] * same[half]
        ext[EDGE:, :] = pre[half * BLOCK : (half + 1) * BLOCK].astype(WIDE)
        prev[...] = ext[BLOCK:, :]
        total = bias + taps[TAPS - 1 : TAPS] * ext[EDGE:, :]
        for tap in range(TAPS - 1):
            total = total + taps[tap : tap + 1] * ext[pl.ds(EDGE - (TAPS - 1) + tap, BLOCK), :]
        conv_o[rows, :] = total
        act_o[rows, :] = (total * sigmoid(total)).astype(LOW)

    steps, _, _ = step_terms(raw, heads)
    scale = -jnp.exp(vec[1:2, :])
    cum = sum_before(steps * scale)
    cum_o[...] = cum
    cum_t, steps_t = cum.T, steps.T
    write = act_o[:, inner : inner + STATE]
    read = act_o[:, inner + STATE :]
    lower = ones_before(BLOCK)
    top, low = slice(0, BLOCK), slice(BLOCK, GROUP)
    s00 = jnp.where(lower, nt(read[top], write[top]), 0.0)
    s10 = nt(read[low], write[top]) * second
    s11 = jnp.where(lower, nt(read[low], write[low]), 0.0)

    def mix(scores, head, t, s):
        decay = jnp.exp(jnp.minimum(cum[t, head : head + 1] - cum_t[head : head + 1, s], 0.0))
        return (scores * (decay * steps_t[head : head + 1, s])).astype(LOW)

    last = cum[GROUP - 1 : GROUP, :]
    row = lax.broadcasted_iota(jnp.int32, (GROUP, LANES), 0)
    weight = steps * jnp.exp(last - cum) * jnp.where(row < BLOCK, second, 1.0)
    weight_w = to_columns(weight, spread_m)
    packed = []
    for pair in range(inner // LANES):
        columns = slice(pair * LANES, (pair + 1) * LANES)
        slab = act_o[:, columns]
        slab_f = slab.astype(WIDE)
        ones = pair_lanes(slab)
        h0, h1 = 2 * pair, 2 * pair + 1
        y0 = nn(
            jnp.concatenate([mix(s00, h0, top, top), mix(s00, h1, top, top)], axis=1),
            jnp.concatenate([ones[0][top], ones[1][top]], axis=0),
        )
        y1 = nn(
            jnp.concatenate(
                [mix(s10, h0, low, top), mix(s11, h0, low, low), mix(s10, h1, low, top), mix(s11, h1, low, low)], axis=1
            ),
            jnp.concatenate([ones[0], ones[1]], axis=0),
        )
        skip = to_columns(jnp.broadcast_to(vec[2:3, :], (EDGE, LANES)), spread_m[:, columns])[0:1]
        part_o[top, columns] = y0 + skip * slab_f[top]
        part_o[low, columns] = y1 + skip * slab_f[low]
        packed.append((slab_f * weight_w[:, columns]).astype(LOW))
    local = tn(jnp.concatenate(packed, axis=1), write)
    local_o[0] = local
    carry = jnp.exp(cum_t[:, GROUP - 1 : GROUP]) * (first * second)
    state[...] = carry_columns(carry, collect) * state[...] + local
    prod[...] = jnp.broadcast_to(carry[:HALO], (HALO, STATE)) * prod[...]
    msg_o[:inner, :] = state[...].astype(LOW)
    msg_o[inner:, :] = prod[...].astype(LOW)


def front(flags, x_full, w_all, vec, prenorm, kernels, filters, offsets, shifts, heads):
    rows = x_full.shape[0] - HALO
    inner = kernels.shape[1]
    wide = inner + filters.shape[1]
    blocks = rows // GROUP
    total = x_full.shape[1]

    def by_rows(width):
        return blockwise((GROUP, width), lambda i: (i, 0))

    return pl.pallas_call(
        functools.partial(front_kernel, heads),
        grid=(blocks,),
        out_shape=(
            shape((rows, total), LOW), shape((rows, inner), WIDE), shape((rows, wide), LOW), shape((rows, wide), WIDE),
            shape((rows, wide), LOW), shape((rows, LANES), WIDE), shape((rows, LANES), WIDE), shape((rows, inner), WIDE),
            shape((blocks, inner, STATE), WIDE), shape((inner + HALO, STATE), LOW),
            shape((EDGE, wide), WIDE),
        ),
        in_specs=[
            SMEM_SPEC, by_rows(total), blockwise((HALO, total), lambda i: (rows // HALO, 0)), fixed(w_all.shape),
            fixed(vec.shape), fixed(prenorm.shape), fixed(kernels.shape), fixed(filters.shape), fixed(offsets.shape),
            fixed(shifts.shape),
        ],
        out_specs=(
            by_rows(total), by_rows(inner), by_rows(wide), by_rows(wide), by_rows(wide), by_rows(LANES), by_rows(LANES),
            by_rows(inner), blockwise((1, inner, STATE), lambda i: (i, 0, 0)), fixed((inner + HALO, STATE)),
            fixed((EDGE, wide)),
        ),
        scratch_shapes=[
            pltpu.VMEM((EDGE + BLOCK, wide), WIDE), pltpu.VMEM((EDGE, wide), WIDE),
            pltpu.VMEM((inner, STATE), WIDE), pltpu.VMEM((HALO, STATE), WIDE),
        ],
        compiler_params=pltpu.CompilerParams(vmem_limit_bytes=56 * MIB, dimension_semantics=("arbitrary",)),
        name="front",
    )(flags, x_full, x_full, w_all, vec, prenorm, kernels, filters, offsets, shifts)


def fold_states(slots, collect, inner, first, last, step, start):
    def hop(n, state):
        message = slots[first + n * step]
        carry = nn(collect[:, :HALO], message[inner:])
        return carry * state + message[:inner].astype(WIDE)

    return lax.fori_loop(0, (last - first) * step, hop, start)


def middle_kernel(
    seqs, line, blocks, flags, msg, gate, part, read, cum, local, g, normed, r_t, postnorm,
    ssd_o, starts_o, dssd_o, dgate_o, out_o, back_o, q_o, sums_o, gread_o, ggate_o, gpost_o,
    ssd_s, din_s, state, slots, sums, gread, ggate, prod,
    sent, got, passed, sum_sent, sum_got,
):
    i = pl.program_id(0)
    me, mine = lax.axis_index("seq"), lax.axis_index("head")
    inner = gate.shape[1]
    width = out_o.shape[2]
    spread_m, collect = head_rows(inner), head_columns(inner)
    first_phase = i < blocks
    block = lax.rem(i, blocks)
    here = pl.ds(pl.multiple_of(block * GROUP, GROUP), GROUP)
    first, second = flags[2 * block], flags[2 * block + 1]
    plane = Plane(seqs, lambda s: slots.at[s], sent, got, passed, way=1)

    @pl.when(i == 0)
    def _():
        greet(seqs, line)
        plane.start(msg)
        plane.relay()
        plane.finish(msg)
        state[...] = fold_states(slots, collect, inner, 0, me, 1, jnp.zeros((inner, STATE), WIDE))

    row = lax.broadcasted_iota(jnp.int32, (GROUP, LANES), 0)
    lane = lax.broadcasted_iota(jnp.int32, (GROUP, LANES), 1)
    entry = to_columns(jnp.exp(cum[...]) * (first * jnp.where(row < BLOCK, 1.0, second)), spread_m)
    gate_v = gate[...]
    sig = sigmoid(gate_v)
    act = gate_v * sig
    cum_t = cum[...].T
    carry = jnp.exp(cum_t[:, GROUP - 1 : GROUP]) * (first * second)

    @pl.when(first_phase)
    def _():
        start = state[...]
        starts_o[0] = start
        queried = nt(read[...], start.astype(LOW))
        ssd = part[...] + entry * queried
        ssd_s[here, :] = ssd
        ssd_o[...] = ssd
        state[...] = carry_columns(carry, collect) * start + local[0]
        gated = ssd * act
        scaled = gated * postnorm[...]
        d_inner = nn(g[...], r_t[...])
        din_s[here, :] = d_inner
        out = nt(scaled.astype(LOW), r_t[...])
        for z in range(line):
            out_o[z] = out[:, z * width : (z + 1) * width].astype(LOW)
        squares = jnp.sum(gated * gated, axis=1, keepdims=True)
        dots = jnp.sum(scaled * d_inner, axis=1, keepdims=True)
        both = jnp.where(lane == 0, squares, jnp.where(lane == 1, dots, 0.0)).T
        sums[mine, block] = both[:EDGE]

    def sum_copy(to, slot):
        return remote(sums.at[mine], sums.at[slot], sum_sent.at[to], sum_got.at[slot], {"head": to})

    @pl.when(i == blocks - 1)
    def _():
        if line > 1:

            @pl.loop(1, line)
            def _(n):
                sum_copy(lax.rem(mine + n, line), mine).start()

            @pl.loop(1, line)
            def _(n):
                other = lax.rem(mine + n, line)
                sum_copy(other, other).wait()

        sums_o[...] = jnp.sum(sums[...], axis=0)
        gread[...] = jnp.zeros_like(gread)
        ggate[...] = jnp.zeros_like(ggate)
        gpost_o[...] = jnp.zeros_like(gpost_o)
        state[...] = jnp.zeros_like(state)
        prod[...] = jnp.ones_like(prod)

    @pl.when(jnp.logical_not(first_phase))
    def _():
        total = sums_o[block]
        stats = jnp.concatenate([total, jnp.zeros((LANES - EDGE, GROUP), WIDE)], axis=0).T
        inv = lax.rsqrt(stats[:, 0:1] / INNER + EPS)
        dot = stats[:, 1:2]
        ssd = ssd_s[here, :]
        d_inner = din_s[here, :]
        gated = ssd * act
        gated_inv = gated * inv
        inner_normed = (gated_inv * postnorm[...]).astype(LOW)
        d_gated = (inv * postnorm[...]) * d_inner - gated * (inv * inv * inv / INNER * dot)
        gpost_o[...] += jnp.sum(d_inner * gated_inv, axis=0, keepdims=True)
        d_ssd = (d_gated * act).astype(LOW)
        d_gate = (d_gated * ssd * sig * (1.0 + gate_v * (1.0 - sig))).astype(LOW)
        dssd_o[...] = d_ssd
        dgate_o[...] = d_gate
        gread[...] += tn(g[...], inner_normed)
        ggate[...] += tn(normed[...], d_gate)
        query_grad = (d_ssd.astype(WIDE) * entry).astype(LOW)
        q = tn(query_grad, read[...])
        q_o[0] = q
        state[...] += carry_columns(prod[...], collect) * q
        prod[...] = prod[...] * carry

    @pl.when(i == 2 * blocks - 1)
    def _():
        gread_o[...] = gread[...].astype(LOW)
        ggate_o[...] = ggate[...].astype(LOW)
        back_o[:inner, :] = state[...].astype(LOW)
        back_o[inner:, :] = jnp.broadcast_to(prod[:HALO], (HALO, STATE)).astype(LOW)


def middle(flags, msg, gate, part, act, cum, local, g_full, normed, r_t, postnorm):
    seqs, line = lax.axis_size("seq"), lax.axis_size("head")
    rows, inner = gate.shape
    total = g_full.shape[1]
    width = total // line
    blocks = rows // GROUP

    def in_both(columns, at=0):
        return blockwise((GROUP, columns), lambda i: (lax.rem(i, blocks), at))

    def in_first(columns):
        return blockwise((GROUP, columns), lambda i: (jnp.minimum(i, blocks - 1), 0))

    def in_second(columns):
        return blockwise((GROUP, columns), lambda i: (jnp.maximum(i - blocks, 0), 0))

    state = (1, inner, STATE)
    return pl.pallas_call(
        functools.partial(middle_kernel, seqs, line, blocks),
        grid=(2 * blocks,),
        out_shape=(
            shape((rows, inner), WIDE), shape((blocks, inner, STATE), WIDE), shape((rows, inner), LOW),
            shape((rows, inner), LOW), shape((line, rows, width), LOW), shape((inner + HALO, STATE), LOW),
            shape((blocks, inner, STATE), WIDE), shape((blocks, EDGE, GROUP), WIDE), shape((total, inner), LOW),
            shape((total, inner), LOW), shape((1, inner), WIDE),
        ),
        in_specs=[
            SMEM_SPEC, VMEM_SPEC, in_both(inner), in_first(inner), in_both(STATE, (inner + STATE) // STATE),
            in_both(LANES), blockwise(state, lambda i: (jnp.minimum(i, blocks - 1), 0, 0)), in_both(total),
            in_second(total), fixed(r_t.shape), fixed(postnorm.shape),
        ],
        out_specs=(
            in_first(inner), blockwise(state, lambda i: (jnp.minimum(i, blocks - 1), 0, 0)), in_second(inner),
            in_second(inner), blockwise((line, GROUP, width), lambda i: (0, jnp.minimum(i, blocks - 1), 0)),
            fixed((inner + HALO, STATE)), blockwise(state, lambda i: (jnp.maximum(i - blocks, 0), 0, 0)),
            fixed((blocks, EDGE, GROUP)), fixed((total, inner)), fixed((total, inner)), fixed((1, inner)),
        ),
        scratch_shapes=[
            pltpu.VMEM((rows, inner), WIDE), pltpu.VMEM((rows, inner), WIDE), pltpu.VMEM((inner, STATE), WIDE),
            pltpu.VMEM((seqs, inner + HALO, STATE), LOW), pltpu.VMEM((line, blocks, EDGE, GROUP), WIDE),
            pltpu.VMEM((total, inner), WIDE), pltpu.VMEM((total, inner), WIDE), pltpu.VMEM((LANES, 1), WIDE),
            DMA((seqs,)), DMA((seqs,)), DMA((seqs,)), DMA((line,)), DMA((line,)),
        ],
        compiler_params=pltpu.CompilerParams(
            collective_id=1, has_side_effects=True, vmem_limit_bytes=60 * MIB, dimension_semantics=("arbitrary",)
        ),
        name="middle",
    )(flags, msg, gate, part, act, cum, local, g_full, normed, r_t, postnorm)


def chunk_lanes(x, count):
    size = x.shape[1] // count
    fold = LANES // size
    tall = GROUP // fold
    lane = lax.broadcasted_iota(jnp.int32, (tall, LANES), 1)
    out = []
    for chunk in range(count):
        slab, offset = chunk * size // LANES, chunk * size % LANES
        total = jnp.zeros((tall, LANES), WIDE)
        for group in range(fold):
            piece = x[group * tall : (group + 1) * tall, slab * LANES : (slab + 1) * LANES]
            shift = (group * size - offset) % LANES
            if shift:
                piece = pltpu.roll(piece, shift, 1)
            inside = (lane >= group * size) & (lane < (group + 1) * size)
            total = jnp.where(inside, piece, total)
        out.append(total)
    return out


def back_kernel(
    seqs, line, heads, blocks, flags, msg, d_ssd, ssd, act, cum, raw, starts, q, vec, out_part, gread, ggate,
    dval_o, daddr_o, dstep_o, tiny_o, out_got, gread_got, ggate_got,
    state, slots,
    sent, got, passed, out_sent, out_sem, w_sent, w_sem, own_sem,
):
    i = pl.program_id(0)
    me, mine = lax.axis_index("seq"), lax.axis_index("head")
    block = blocks - 1 - i
    inner = d_ssd.shape[1]
    depth = gread_got.shape[1]
    spread_m, collect = head_rows(inner), head_columns(inner)
    plane = Plane(seqs, lambda s: slots.at[s], sent, got, passed, way=-1)

    def out_copy(to, slot):
        return remote(out_part.at[to], out_got.at[slot], out_sent.at[to], out_sem.at[slot], {"head": to})

    def rows_of(device):
        return pl.ds(pl.multiple_of(device * depth, depth), depth)

    weights = ((gread, gread_got), (ggate, ggate_got))

    def w_copy(which, to, slot):
        src, dst = weights[which]
        return remote(
            src.at[rows_of(to)], dst.at[slot], w_sent.at[which, to], w_sem.at[which, slot], {"seq": to}
        )

    own_copies = [
        pltpu.make_async_copy(out_part.at[mine], out_got.at[mine], own_sem.at[0]),
        pltpu.make_async_copy(gread.at[rows_of(me)], gread_got.at[me], own_sem.at[1]),
        pltpu.make_async_copy(ggate.at[rows_of(me)], ggate_got.at[me], own_sem.at[2]),
    ]

    @pl.when(i == 0)
    def _():
        greet(seqs, line)
        plane.start(msg)
        plane.relay()
        plane.finish(msg)
        state[...] = fold_states(slots, collect, inner, seqs - 1, me, -1, jnp.zeros((inner, STATE), WIDE))
        tiny_o[...] = jnp.zeros_like(tiny_o)
        if line > 1:

            @pl.loop(1, line)
            def _(n):
                out_copy(lax.rem(mine + n, line), mine).start()

        for which in range(2):

            @pl.loop(1, seqs)
            def _(n):
                w_copy(which, lax.rem(me + n, seqs), me).start()

        for copy in own_copies:
            copy.start()

    first, second = flags[2 * block], flags[2 * block + 1]
    row = lax.broadcasted_iota(jnp.int32, (GROUP, LANES), 0)
    lower_mask = ones_before(BLOCK)
    top, low = slice(0, BLOCK), slice(BLOCK, GROUP)
    cum_v = cum[...]
    cum_t = cum_v.T
    steps, sig, ratio = step_terms(raw[...], heads)
    steps_t = steps.T
    scale = -jnp.exp(vec[1:2, :])
    last = cum_v[GROUP - 1 : GROUP, :]
    write = act[:, inner : inner + STATE]
    read = act[:, inner + STATE :]
    s00 = jnp.where(lower_mask, nt(read[top], write[top]), 0.0)
    s10 = nt(read[low], write[top]) * second
    s11 = jnp.where(lower_mask, nt(read[low], write[low]), 0.0)

    end = state[...]
    end_low = end.astype(LOW)
    start = starts[0]
    carry = jnp.exp(cum_t[:, GROUP - 1 : GROUP]) * (first * second)
    state[...] = carry_columns(carry, collect) * end + q[0]
    weight = steps * jnp.exp(last - cum_v) * jnp.where(row < BLOCK, second, 1.0)
    weight_w = to_columns(weight, spread_m)
    entry_w = to_columns(jnp.exp(cum_v) * (first * jnp.where(row < BLOCK, 1.0, second)), spread_m)
    d_query = (d_ssd[...].astype(WIDE) * entry_w).astype(LOW)
    through_w = to_columns(jnp.broadcast_to(vec[2:3, :], (EDGE, LANES)), spread_m)[0:1]

    def decay_of(head, t, s):
        decay = jnp.exp(jnp.minimum(cum_v[t, head : head + 1] - cum_t[head : head + 1, s], 0.0))
        return decay * steps_t[head : head + 1, s]

    ds00 = jnp.zeros((BLOCK, BLOCK), WIDE)
    ds10 = jnp.zeros((BLOCK, BLOCK), WIDE)
    ds11 = jnp.zeros((BLOCK, BLOCK), WIDE)
    packed, value_parts, tails = [], [], []
    d_packed = nt(write, end_low)
    for pair in range(inner // LANES):
        columns = slice(pair * LANES, (pair + 1) * LANES)
        values = act[:, columns]
        values_f = values.astype(WIDE)
        dy = d_ssd[:, columns]
        dys = pair_lanes(dy)
        m00, m10, m11 = [], [], []
        for k in range(2):
            head = 2 * pair + k
            l00, l10, l11 = decay_of(head, top, top), decay_of(head, low, top), decay_of(head, low, low)
            m00.append((s00 * l00).astype(LOW))
            m10.append((s10 * l10).astype(LOW))
            m11.append((s11 * l11).astype(LOW))
            ds00 = ds00 + nt(dys[k][top], values[top]) * l00
            ds10 = ds10 + nt(dys[k][low], values[top]) * l10
            ds11 = ds11 + nt(dys[k][low], values[low]) * l11
        v0 = tn(
            jnp.concatenate([m00[0], m10[0], m00[1], m10[1]], axis=0), jnp.concatenate([dys[0], dys[1]], axis=0)
        )
        v1 = tn(
            jnp.concatenate([m11[0], m11[1]], axis=0), jnp.concatenate([dys[0][low], dys[1][low]], axis=0)
        )
        tail = d_packed[:, columns] * weight_w[:, columns]
        part = jnp.concatenate([v0, v1], axis=0) + tail
        dval_o[:, columns] = part + through_w[:, columns] * dy.astype(WIDE)
        value_parts.append(values_f * part)
        tails.append(jnp.sum(tail * values_f, axis=0, keepdims=True))
        packed.append((values_f * weight_w[:, columns]).astype(LOW))

    ds = jnp.concatenate(
        [
            jnp.concatenate([jnp.where(lower_mask, ds00, 0.0), jnp.zeros((BLOCK, BLOCK), WIDE)], axis=1),
            jnp.concatenate([ds10 * second, jnp.where(lower_mask, ds11, 0.0)], axis=1),
        ],
        axis=0,
    ).astype(LOW)
    d_read = nn(ds, write) + nn(d_query, start.astype(LOW))
    d_write = tn(ds, read) + nn(jnp.concatenate(packed, axis=1), end_low)
    for z, chunk in enumerate(chunk_lanes(jnp.concatenate([d_write, d_read], axis=1), line)):
        daddr_o[z] = chunk.astype(LOW)

    dy_f = d_ssd[...].astype(WIDE)
    own = to_heads(dy_f * act[:, :inner].astype(WIDE), collect)
    r1 = to_heads(dy_f * ssd[...], collect) - vec[2:3, :] * own
    w = to_heads(jnp.concatenate(value_parts, axis=1), collect)
    tail_row = to_heads(jnp.broadcast_to(jnp.concatenate(tails, axis=1), (EDGE, inner)), collect)[0:1]
    high, rest = halves(end * start)
    ones = jnp.ones((EDGE, STATE), LOW)
    carry_grad = to_heads(nt(ones, high) + nt(ones, rest), collect)[0:1]
    d_last = tail_row + carry_grad * (jnp.exp(last) * (first * second))
    d_cum = r1 - w + jnp.where(row == GROUP - 1, d_last, 0.0)
    d_rate = sum_after(d_cum)
    d_raw = d_rate * scale * sig + w * ratio
    dstep_o[...] = d_raw.astype(LOW)
    tiny_o[0:1, :] += jnp.sum(d_raw, axis=0, keepdims=True)
    tiny_o[1:2, :] += jnp.sum(d_rate * steps, axis=0, keepdims=True) * scale
    tiny_o[2:3, :] += jnp.sum(own, axis=0, keepdims=True)

    @pl.when(i == blocks - 1)
    def _():
        if line > 1:

            @pl.loop(1, line)
            def _(n):
                other = lax.rem(mine + n, line)
                out_copy(other, other).wait()

        for which in range(2):

            @pl.loop(1, seqs)
            def _(n):
                other = lax.rem(me + n, seqs)
                w_copy(which, other, other).wait()

        for copy in own_copies:
            copy.wait()


def back(flags, msg, d_ssd, ssd, act, cum, raw, starts, q, vec, out_part, gread, ggate, heads):
    seqs, line = lax.axis_size("seq"), lax.axis_size("head")
    rows, inner = d_ssd.shape
    wide = act.shape[1]
    total = gread.shape[0]
    depth = total // seqs
    blocks = rows // GROUP
    fold = LANES * line // (2 * STATE)

    def by_rows(width):
        return blockwise((GROUP, width), lambda i: (blocks - 1 - i, 0))

    state = blockwise((1, inner, STATE), lambda i: (blocks - 1 - i, 0, 0))
    return pl.pallas_call(
        functools.partial(back_kernel, seqs, line, heads, blocks),
        grid=(blocks,),
        out_shape=(
            shape((rows, inner), WIDE), shape((line, rows // fold, LANES), LOW), shape((rows, LANES), LOW),
            shape((EDGE, LANES), WIDE), shape(out_part.shape, LOW), shape((seqs, depth, inner), LOW),
            shape((seqs, depth, inner), LOW),
        ),
        in_specs=[
            SMEM_SPEC, VMEM_SPEC, by_rows(inner), by_rows(inner), by_rows(wide), by_rows(LANES), by_rows(LANES),
            state, state, fixed(vec.shape), ANY_SPEC, ANY_SPEC, ANY_SPEC,
        ],
        out_specs=(
            by_rows(inner), blockwise((line, GROUP // fold, LANES), lambda i: (0, blocks - 1 - i, 0)), by_rows(LANES),
            fixed((EDGE, LANES)), ANY_SPEC, ANY_SPEC, ANY_SPEC,
        ),
        scratch_shapes=[
            pltpu.VMEM((inner, STATE), WIDE), pltpu.VMEM((seqs, inner + HALO, STATE), LOW),
            DMA((seqs,)), DMA((seqs,)), DMA((seqs,)), DMA((line,)), DMA((line,)), DMA((2, seqs)), DMA((2, seqs)),
            DMA((3,)),
        ],
        compiler_params=pltpu.CompilerParams(
            collective_id=2, has_side_effects=True, vmem_limit_bytes=56 * MIB, dimension_semantics=("arbitrary",)
        ),
        name="back",
    )(flags, msg, d_ssd, ssd, act, cum, raw, starts, q, vec, out_part, gread, ggate)


def conv_grad(d_act, conv):
    sig = sigmoid(conv)
    return d_act * (sig * (1.0 + conv * (1.0 - sig)))


def last_kernel(
    seqs, line, heads, blocks, flags, give, take,
    daddr, dval, dval_next, conv, conv_next, pre, normed, u, dgate, dstep, w, prenorm, kernels, filters, rim,
    out_got, work_x, work_g, sums, gread_got, ggate_got, tiny, gpost,
    out_o, dx_o, prenorm_o, gate_o, pay_o, addr_o, step_o, kernels_o, offsets_o, filters_o, shifts_o,
    tiny_o, post_o, read_o,
    d_addr, addr_got, edge_own, edge_got, ext, after, prev, taps_g, bias_g, dx_send, dx_got, dw, dw_low, dw_got,
    pn, pn_send, pn_got, small, small_got, result, fin_send, out_recv, grad_recv,
    addr_sent, addr_sem, edge_sent, edge_sem, dx_sent, dx_sem, dw_sent, dw_sem, pn_sent, pn_sem,
    small_sent, small_sem, fin_sent, fin_sem, own_sem,
):
    i = pl.program_id(0)
    me, mine = lax.axis_index("seq"), lax.axis_index("head")
    inner = dgate.shape[1]
    tiles = work_g.shape[0] // BLOCK
    rows = work_g.shape[0]
    width = work_g.shape[1]
    depth = dw_got.shape[1]
    size = 2 * STATE // line
    fold = LANES // size
    tall = GROUP // fold
    slab = mine * size // LANES
    offset = lax.rem(mine * size, LANES)
    here = pl.ds(pl.multiple_of(i * GROUP, GROUP), GROUP)
    wide = inner + LANES

    def slab_of(ref, at):
        return ref[:, pl.ds(pl.multiple_of(at + slab * LANES, LANES), LANES)]

    def addr_copy(to, slot):
        return remote(daddr.at[to], addr_got.at[slot], addr_sent.at[to], addr_sem.at[slot], {"head": to})

    def edge_copy(to):
        return remote(edge_own, edge_got, edge_sent, edge_sem, {"seq": to})

    def dx_copy(to, slot, block):
        part = pl.ds(pl.multiple_of(block * GROUP, GROUP), GROUP)
        return remote(
            dx_send.at[to, part], dx_got.at[slot, part], dx_sent.at[to, block], dx_sem.at[slot, block], {"head": to}
        )

    def rows_of(device):
        return pl.ds(pl.multiple_of(device * depth, depth), depth)

    def dw_copy(to, slot):
        return remote(dw_low.at[rows_of(to)], dw_got.at[slot], dw_sent.at[to], dw_sem.at[slot], {"seq": to})

    def pn_copy(to, slot):
        return remote(pn_send.at[to], pn_got.at[slot], pn_sent.at[to], pn_sem.at[slot], {"head": to})

    def small_copy(to, slot):
        return remote(small, small_got.at[slot], small_sent.at[to], small_sem.at[slot], {"seq": to})

    arrivals = (out_recv, grad_recv)

    def fin_copy(which, to, slot):
        return remote(
            fin_send.at[which, to], arrivals[which].at[slot], fin_sent.at[which, to], fin_sem.at[which, slot],
            {"seq": to},
        )

    def all_seq(body):
        @pl.loop(1, seqs)
        def _(n):
            body(lax.rem(me + n, seqs))

    def all_line(body):
        if line > 1:

            @pl.loop(1, line)
            def _(n):
                body(lax.rem(mine + n, line))

    def route(which):
        def send(to):
            fin_send[which, to] = result[which, give[to]]
            fin_copy(which, to, me).start()

        all_seq(send)
        arrivals[which][me] = result[which, give[me]]

    def land(which, out):
        all_seq(lambda other: fin_copy(which, other, other).wait())
        for k in range(tiles):
            out[k] = arrivals[which][take[k]]

    @pl.when(i == 0)
    def _():
        greet(seqs, line)
        all_line(lambda to: addr_copy(to, mine).start())
        own = pltpu.make_async_copy(daddr.at[mine], addr_got.at[mine], own_sem)
        own.start()

        @pl.loop(0, blocks)
        def _(b):
            part = pl.ds(pl.multiple_of(b * GROUP, GROUP), GROUP)
            stats = jnp.concatenate([sums[b], jnp.zeros((LANES - EDGE, GROUP), WIDE)], axis=0).T
            inv = lax.rsqrt(stats[:, 0:1] / INNER + EPS)
            total = out_got[0, part].astype(WIDE)
            for z in range(1, line):
                total = total + out_got[z, part].astype(WIDE)
            done = (work_x[part].astype(WIDE) + total * inv).astype(LOW)
            result[0, 2 * b] = done[:BLOCK]
            result[0, 2 * b + 1] = done[BLOCK:]

        route(0)
        all_line(lambda other: addr_copy(other, other).wait())
        own.wait()
        lane = lax.broadcasted_iota(jnp.int32, (tall, LANES), 1)
        inside = (lane >= offset) & (lane < offset + size)

        @pl.loop(0, blocks)
        def _(b):
            part = pl.ds(pl.multiple_of(b * tall, tall), tall)
            total = addr_got[0, part].astype(WIDE)
            for z in range(1, line):
                total = total + addr_got[z, part].astype(WIDE)
            for group in range(fold):
                turned = pltpu.roll(total, lax.rem(offset + (LANES - group * size), LANES), 1)
                at = pl.ds(pl.multiple_of(b * GROUP + group * tall, tall), tall)
                d_addr[at, :] = jnp.where(inside, turned, 0.0)

        edge_own[:, :inner] = conv_grad(dval[0:EDGE, :], conv[0:EDGE, :inner])
        edge_own[:, inner:] = conv_grad(d_addr[0:EDGE, :], slab_of(conv, inner)[0:EDGE])
        edge_copy(lax.rem(me + seqs - 1, seqs)).start()
        prev[:, :inner] = rim[:, :inner]
        prev[:, inner:] = slab_of(rim, inner)
        taps_g[...] = jnp.zeros_like(taps_g)
        bias_g[...] = jnp.zeros_like(bias_g)
        dw[...] = jnp.zeros_like(dw)
        pn[...] = jnp.zeros_like(pn)

    @pl.when(i < blocks - 1)
    def _():
        after[:, :inner] = conv_grad(dval_next[...], conv_next[:, :inner])
        following = pl.ds(pl.multiple_of((i + 1) * GROUP, GROUP), EDGE)
        after[:, inner:] = conv_grad(d_addr[following, :], slab_of(conv_next, inner))

    @pl.when(i == blocks - 1)
    def _():
        edge_copy(lax.rem(me + 1, seqs)).wait()
        after[...] = edge_got[...]

    taps = jnp.concatenate([kernels[...], slab_of(filters, 0)], axis=1)
    conv_v = jnp.concatenate([conv[:, :inner], slab_of(conv, inner)], axis=1)
    pre_v = jnp.concatenate([pre[:, :inner], slab_of(pre, inner)], axis=1).astype(WIDE)
    d_conv = conv_grad(jnp.concatenate([dval[...], d_addr[here, :]], axis=1), conv_v)
    bias_g[...] += jnp.sum(d_conv, axis=0, keepdims=True)
    d_pre = []
    for half in range(2):
        at = slice(half * BLOCK, (half + 1) * BLOCK)
        tile = d_conv[at]
        ext[0:EDGE, :] = prev[...] * flags[2 * i + half]
        ext[EDGE:, :] = pre_v[at]
        prev[...] = ext[BLOCK:, :]
        for tap in range(TAPS):
            taps_g[tap : tap + 1, :] += jnp.sum(
                tile * ext[pl.ds(EDGE - (TAPS - 1) + tap, BLOCK), :], axis=0, keepdims=True
            )
        ext[:BLOCK, :] = tile
        following = d_conv[BLOCK : BLOCK + EDGE] if half == 0 else after[...]
        ext[BLOCK:, :] = following * flags[2 * i + half + 1]
        total = taps[TAPS - 1 : TAPS] * ext[:BLOCK, :]
        for tap in range(TAPS - 1):
            total = total + taps[tap : tap + 1] * ext[pl.ds(TAPS - 1 - tap, BLOCK), :]
        d_pre.append(total.astype(LOW))
    d_pre = jnp.concatenate(d_pre, axis=0)
    d_value, d_slab = d_pre[:, :inner], d_pre[:, inner:]
    d_step = dstep[...]
    normed_v = normed[...]
    dw[:, :wide] += tn(normed_v, d_pre)
    dw[:, wide:] += tn(normed_v, d_step)
    d_normed = (
        nt(dgate[...], w[:, :inner])
        + nt(d_value, w[:, inner : 2 * inner])
        + nt(d_slab, slab_of(w, 2 * inner))
        + nt(d_step, w[:, 2 * inner + 2 * STATE :])
    )
    u_f = u[...].astype(WIDE)
    inv = lax.rsqrt(jnp.mean(u_f * u_f, axis=1, keepdims=True) + EPS)
    gained = d_normed * prenorm[...]
    dot = jnp.sum(gained * u_f, axis=1, keepdims=True)
    grad = gained * inv - u_f * (inv * inv * inv / D * dot)
    pn[...] += jnp.sum(d_normed * (u_f * inv), axis=0, keepdims=True)
    for z in range(line):
        dx_send[z, here] = grad[:, z * width : (z + 1) * width].astype(LOW)
    dx_got[mine, here] = dx_send[mine, here]
    all_line(lambda to: dx_copy(to, mine, i).start())

    @pl.when(i == blocks - 1)
    def _():
        dw_low[...] = dw[...].astype(LOW)
        all_seq(lambda to: dw_copy(to, me).start())
        for z in range(line):
            pn_send[z] = jnp.broadcast_to(pn[:, z * width : (z + 1) * width], (EDGE, width))
        pn_got[mine] = pn_send[mine]
        all_line(lambda to: pn_copy(to, mine).start())
        dw_got[me] = dw_low[rows_of(me), :]

        def summed(ref):
            total = ref[0].astype(WIDE)
            for n in range(1, seqs):
                total = total + ref[n].astype(WIDE)
            return total

        read_o[...] = summed(gread_got).T
        gate_o[...] = summed(ggate_got)
        all_line(lambda other: pn_copy(other, other).wait())
        small[...] = jnp.zeros_like(small)
        small[0:TAPS, :] = taps_g[0:TAPS, :]
        small[4:5, :] = bias_g[...]
        small[5:6, :inner] = gpost[...]
        small[6:7, :width] = jnp.sum(pn_got[...], axis=0)[0:1]
        for n in range(3):
            small[7:8, n * LANES : (n + 1) * LANES] = tiny[n : n + 1, :]
        small_got[me] = small[...]
        all_seq(lambda to: small_copy(to, me).start())

        @pl.loop(0, blocks)
        def _(b):
            all_line(lambda other: dx_copy(other, other, b).wait())
            part = pl.ds(pl.multiple_of(b * GROUP, GROUP), GROUP)
            total = dx_got[0, part].astype(WIDE)
            for z in range(1, line):
                total = total + dx_got[z, part].astype(WIDE)
            done = (work_g[part].astype(WIDE) + total).astype(LOW)
            result[1, 2 * b] = done[:BLOCK]
            result[1, 2 * b + 1] = done[BLOCK:]

        route(1)
        all_seq(lambda other: dw_copy(other, other).wait())
        grads = summed(dw_got)
        pay_o[...] = grads[:, :inner]
        back_turn = lax.rem(LANES - offset, LANES)
        addr_o[...] = pltpu.roll(grads[:, inner:wide], back_turn, 1)[:, :size]
        step_o[...] = grads[:, wide : wide + heads]
        all_seq(lambda other: small_copy(other, other).wait())
        totals = jnp.sum(small_got[...], axis=0)
        kernels_o[...] = totals[0:TAPS, :inner]
        offsets_o[...] = totals[4:5, :inner]
        turned = pltpu.roll(totals[:, inner:], back_turn, 1)
        filters_o[...] = turned[0:TAPS, :size]
        shifts_o[...] = turned[4:5, :size]
        post_o[...] = totals[5:6, :inner]
        prenorm_o[...] = totals[6:7, :width]
        for n in range(3):
            tiny_o[n : n + 1, :] = totals[7:8, n * LANES : n * LANES + heads]
        land(0, out_o)
        land(1, dx_o)


def last(
    flags, give, take, daddr, dval, conv, pre, normed, x_full, dgate, dstep, w_all, prenorm, kernels, filters, rim,
    out_got, work_x, work_g, sums, gread_got, ggate_got, tiny, gpost, heads,
):
    seqs, line = lax.axis_size("seq"), lax.axis_size("head")
    rows, width = work_g.shape
    inner = dgate.shape[1]
    wide = conv.shape[1]
    total = x_full.shape[1]
    depth = total // seqs
    blocks, tiles = rows // GROUP, rows // BLOCK
    size = 2 * STATE // line
    part = inner + LANES
    step = GROUP // EDGE

    def by_rows(columns):
        return blockwise((GROUP, columns), lambda i: (i, 0))

    def next_rows(columns):
        return blockwise((EDGE, columns), lambda i: (jnp.minimum((i + 1) * step, rows // EDGE - 1), 0))

    grid_whole = (VMEM_SPEC,)
    return pl.pallas_call(
        functools.partial(last_kernel, seqs, line, heads, blocks),
        grid=(blocks,),
        out_shape=(
            shape((tiles, BLOCK, width), LOW), shape((tiles, BLOCK, width), LOW), shape((1, width), WIDE),
            shape((depth, inner), WIDE), shape((depth, inner), WIDE), shape((depth, size), WIDE),
            shape((depth, heads), WIDE), shape((TAPS, inner), WIDE), shape((1, inner), WIDE),
            shape((TAPS, size), WIDE), shape((1, size), WIDE), shape((3, heads), WIDE), shape((1, inner), WIDE),
            shape((inner, depth), WIDE),
        ),
        in_specs=[SMEM_SPEC] * 3 + [
            ANY_SPEC, by_rows(inner), next_rows(inner), by_rows(wide), next_rows(wide), by_rows(wide), by_rows(total),
            by_rows(total), by_rows(inner), by_rows(LANES), VMEM_SPEC, VMEM_SPEC, VMEM_SPEC, VMEM_SPEC, VMEM_SPEC,
        ] + [VMEM_SPEC] * 8,
        out_specs=grid_whole * 14,
        scratch_shapes=[
            pltpu.VMEM((rows, LANES), WIDE), pltpu.VMEM(daddr.shape, LOW),
            pltpu.VMEM((EDGE, part), WIDE), pltpu.VMEM((EDGE, part), WIDE),
            pltpu.VMEM((BLOCK + EDGE, part), WIDE), pltpu.VMEM((EDGE, part), WIDE), pltpu.VMEM((EDGE, part), WIDE),
            pltpu.VMEM((EDGE, part), WIDE), pltpu.VMEM((1, part), WIDE),
            pltpu.VMEM((line, rows, width), LOW), pltpu.VMEM((line, rows, width), LOW),
            pltpu.VMEM((total, part + LANES), WIDE), pltpu.VMEM((total, part + LANES), LOW),
            pltpu.VMEM((seqs, depth, part + LANES), LOW),
            pltpu.VMEM((1, total), WIDE), pltpu.VMEM((line, EDGE, width), WIDE), pltpu.VMEM((line, EDGE, width), WIDE),
            pltpu.VMEM((EDGE, part), WIDE), pltpu.VMEM((seqs, EDGE, part), WIDE),
            pltpu.VMEM((2, tiles, BLOCK, width), LOW), pltpu.VMEM((2, seqs, BLOCK, width), LOW),
            pltpu.VMEM((seqs, BLOCK, width), LOW), pltpu.VMEM((seqs, BLOCK, width), LOW),
            DMA((line,)), DMA((line,)), DMA, DMA, DMA((line, blocks)), DMA((line, blocks)), DMA((seqs,)), DMA((seqs,)),
            DMA((line,)), DMA((line,)), DMA((seqs,)), DMA((seqs,)), DMA((2, seqs)), DMA((2, seqs)), DMA,
        ],
        compiler_params=pltpu.CompilerParams(
            collective_id=3, has_side_effects=True, vmem_limit_bytes=62 * MIB, dimension_semantics=("arbitrary",)
        ),
        name="last",
    )(
        flags, give, take, daddr, dval, dval, conv, conv, pre, normed, x_full, dgate, dstep, w_all, prenorm, kernels,
        filters, rim, out_got, work_x, work_g, sums, gread_got, ggate_got, tiny, gpost,
    )


def on_device(
    inputs,
    cotangent,
    lengths,
    placement,
    prenorm,
    gating,
    payload,
    address,
    stepping,
    kernels,
    offsets,
    filters,
    shifts,
    stepbias,
    decays,
    through,
    postnorm,
    readout,
):
    seq_count = lax.axis_size("seq")
    seq_index = lax.axis_index("seq")
    row_count, width = inputs.shape
    heads = stepbias.shape[0]
    per_dev = row_count // BLOCK
    devices = jnp.arange(seq_count, dtype=jnp.int32)
    slots = jnp.arange(per_dev, dtype=jnp.int32)
    block_ids = seq_index * per_dev + slots
    every_block = jnp.arange(placement.shape[0], dtype=jnp.int32)
    target = jnp.sum(
        jnp.where(placement[None, :] == block_ids[:, None], every_block[None, :], 0), axis=1
    )
    target_dev = target // per_dev
    source_dev = lax.dynamic_slice_in_dim(placement, seq_index * per_dev, per_dev, 0) // per_dev

    def block_for(owners):
        return jnp.sum(jnp.where(owners[None, :] == devices[:, None], slots[None, :], 0), axis=1)

    give_in, give_out = block_for(target_dev), block_for(source_dev)
    bounds = jnp.arange(per_dev + 1, dtype=jnp.int32) + seq_index * per_dev
    starts = bounds[:, None] * BLOCK == jnp.cumsum(lengths)[None, :]
    flags = jnp.where((bounds == 0) | jnp.any(starts, axis=1), 0.0, 1.0).astype(WIDE)

    x_full, g_full, w_all, r_t, work_x, work_g = spread(
        give_in, source_dev, inputs, cotangent, gating, payload, address, stepping, readout
    )
    vec = jnp.pad(jnp.stack([stepbias, decays, through]), ((0, EDGE - 3), (0, LANES - heads)))
    gain, post = prenorm[None, :], postnorm[None, :]
    normed, gate, pre, conv, act, raw, cum, part, local, msg, rim = front(
        flags, x_full, w_all, vec, gain, kernels, filters, offsets[None, :], shifts[None, :], heads
    )
    ssd, states, d_ssd, d_gate, out_part, back_msg, q, sums, gread, ggate, gpost = middle(
        flags, msg, gate, part, act, cum, local, g_full, normed, r_t, post
    )
    dval, daddr, dstep, tiny, out_got, gread_got, ggate_got = back(
        flags, back_msg, d_ssd, ssd, act, cum, raw, states, q, vec, out_part, gread, ggate, heads
    )
    (
        out, dx, prenorm_g, gate_g, pay_g, addr_g, step_g, kernels_g, offsets_g, filters_g, shifts_g, tiny_g,
        post_g, read_g,
    ) = last(
        flags, give_out, target_dev, daddr, dval, conv, pre, normed, x_full, d_gate, dstep, w_all, gain, kernels,
        filters, rim, out_got, work_x, work_g, sums, gread_got, ggate_got, tiny, gpost, heads
    )
    return (
        out.reshape(row_count, width),
        dx.reshape(row_count, width),
        prenorm_g[0],
        gate_g,
        pay_g,
        addr_g,
        step_g,
        kernels_g,
        offsets_g[0],
        filters_g,
        shifts_g[0],
        tiny_g[0],
        tiny_g[1],
        tiny_g[2],
        post_g[0],
        read_g,
    )


def solution(mesh):
    in_specs = (
        P("seq", "head"),
        P("seq", "head"),
        P(),
        P(),
        P(),
        P("seq", "head"),
        P("seq", "head"),
        P("seq", None),
        P("seq", "head"),
        P(None, "head"),
        P("head"),
        P(),
        P(),
        P("head"),
        P("head"),
        P("head"),
        P("head"),
        P("head", "seq"),
    )
    out_specs = (
        P("seq", "head"),
        P("seq", "head"),
        P("head"),
        P("seq", "head"),
        P("seq", "head"),
        P("seq", "head"),
        P("seq", "head"),
        P(None, "head"),
        P("head"),
        P(None, "head"),
        P("head"),
        P("head"),
        P("head"),
        P("head"),
        P("head"),
        P("head", "seq"),
    )
    return jax.shard_map(
        on_device, mesh=mesh, in_specs=in_specs, out_specs=out_specs, check_vma=False
    )
```

time: 711 us -> 331 us (0.47); the launches traced: 699 us -> 331 us
  Pallas kernels: 128 us -> 302 us
  waiting for transfers between devices: 156 us -> 0 us
  other arithmetic: 120 us -> 5.06 us
  matrix products: 90 us -> 0 us
  local copies, waits for them, and re-layouts: 105 us -> 22.8 us
  blocking collectives: 64.5 us -> 0 us
  starting transfers between devices: 18.9 us -> 0 us
  between operations: 16.3 us -> 0.81 us
    pallas_call x0 -> x4, Pallas kernels: none -> 194 us  [the longest x1 89.3 us: last(): pl.pallas_call(functools.partial(last_kernel, seqs, line, heads, blocks),...]
    reduce_scatter x4 -> x0, waiting for transfers between devices: 113 us -> none  [the longest x1 38.5 us: on_device(): lax.psum_scatter(grad_pay_w.astype(jnp.bfloat16), 'seq', scatter_dimensio...]
    dot_general x31 -> x0, matrix products: 90 us -> none  [the longest x1 8.2 us: on_device(): jnp.einsum('cthp,cshp->chts', grad_mixed, values, preferred_element_type=...]
    unnamed x16 -> x0, waiting for transfers between devices: 41.9 us -> none
    psum x3 -> x0, blocking collectives: 38.2 us -> none  [the longest x1 22 us: on_device(): lax.psum((grad_prenorm, grad_kernels, grad_offsets, grad_filters, grad_sh...]
    reshape x9 -> x0, local copies, waits for them, and re-layouts: 32.3 us -> none  [the longest x2 8.76 us: on_device(): grad_values.reshape(row_count, inner_local)]
    unnamed x2 -> x0, blocking collectives: 26.3 us -> none
    convert_element_type x27 -> x0, other arithmetic: 25.8 us -> none  [the longest x8 5.52 us: hop(): part[k].astype(own.dtype)]
  transfers between devices with their start and end apart: 15 -> 0, of which waited for: 8 -> 0; matrix products, arithmetic and copies ran while one was open for 24% -> 0% of each run, Pallas kernels for 0% -> 0%
where the time goes in v2:
time: 331 us
  Pallas kernels  302 us (91%)
  local copies, waits for them, and re-layouts  22.8 us (7%)
  other arithmetic  5.06 us (2%)
    pallas_call x1, Pallas kernels, spread(): pl.pallas_call(functools.partial(spread_kernel, seqs, heads), out_shape=(...  108 us
    pallas_call x1, Pallas kernels, last(): pl.pallas_call(functools.partial(last_kernel, seqs, line, heads, blocks),...  89.3 us
    pallas_call x1, Pallas kernels, back(): pl.pallas_call(functools.partial(back_kernel, seqs, line, heads, blocks),...  57.3 us
    pallas_call x1, Pallas kernels, middle(): pl.pallas_call(functools.partial(middle_kernel, seqs, line, blocks), grid...  32.5 us
    unnamed x52, local copies, waits for them, and re-layouts  21.5 us
    pallas_call x1, Pallas kernels, front(): pl.pallas_call(functools.partial(front_kernel, heads), grid=(blocks,), ou...  15 us

profile of v2, /device:TPU:1, one launch (start us, length us, event | category | flops | bytes accessed | tf_op | source)
XLA Modules:
  0.0 330.6 jit_solution(6908537825853322904)
XLA Ops:
  0.6 0.7 and_select_fusion.1.take
  1.4 0.8 reduce-window.8
  2.2 0.6 select_reduce_fusion.2.give
  3.5 0.8 select_reduce_fusion.1
  4.4 1.3 select_maximum_fusion.vec
  5.7 0.8 copy.37.stepping
  6.5 1.0 copy-done.2
  7.6 1.0 copy-done.3
  8.6 0.9 copy-done.5
  9.5 0.9 copy-done.6
  10.5 0.9 copy-done.7
  11.4 0.9 copy-done.8
  12.3 107.7 %spread.1 = (bf16[1040,1024]{1,0:T(8,128)(2,1)}, bf16[1024,1024]{1,0:T(8,128)(2,1)}, bf16[1024,1408]{1,0:T(8,128)(2,1)}, bf16[1024,512]{1,0:T(8,128)(2,1)S(1)}, ...) custom-call(s32[8]{0:T(128)S(1)} %select_reduce_fusion.give, s32[8]{0:T(128)S(1)} %and_select_fusion.1.take, ...), custom_call_target="tpu_custom_call" | custom-call | tf_op jit(solution)/shard_map/spread/pallas_call | solution.py:376
  120.1 1.0 copy-done
  121.1 0.8 copy-done.1
  121.9 0.8 copy-done.4
  122.7 15.0 %front.1 = (bf16[1024,1024]{1,0:T(8,128)(2,1)}, f32[1024,512]{1,0:T(8,128)}, bf16[1024,768]{1,0:T(8,128)(2,1)}, f32[1024,768]{1,0:T(8,128)}, bf16[1024,768]{1,0:...) custom-call(f32[9]{0:T(128)} %or_select_fusion.flags, ...), custom_call_target="tpu_custom_call" | custom-call | tf_op jit(solution)/shard_map/front/pallas_call | solution.py:529
  137.7 32.5 %middle.1 = (f32[1024,512]{1,0:T(8,128)}, f32[4,512,128]{2,1,0:T(8,128)}, bf16[1024,512]{1,0:T(8,128)(2,1)}, bf16[1024,512]{1,0:T(8,128)(2,1)}, bf16[4,1024,256]...) custom-call(f32[9]{0:T(128)} %or_select_fusion.flags, ...), custom_call_target="tpu_custom_call" | custom-call | tf_op jit(solution)/shard_map/middle/pallas_call | solution.py:694
  170.2 57.3 %back.1 = (f32[1024,512]{1,0:T(8,128)}, bf16[4,512,128]{2,1,0:T(8,128)(2,1)}, bf16[1024,128]{1,0:T(8,128)(2,1)}, f32[8,128]{1,0:T(8,128)}, bf16[4,1024,256]{2,1,...) custom-call(f32[9]{0:T(128)} %or_select_fusion.flags, ...), custom_call_target="tpu_custom_call" | custom-call | tf_op jit(solution)/shard_map/back/pallas_call | solution.py:931
  227.5 89.3 %last.1 = (bf16[8,128,256]{2,1,0:T(8,128)(2,1)}, bf16[8,128,256]{2,1,0:T(8,128)(2,1)}, f32[1,256]{1,0:T(1,128)}, f32[128,512]{1,0:T(8,128)}, f32[128,512]{1,0:T(...) custom-call(f32[9]{0:T(128)} %or_select_fusion.flags, ...), custom_call_target="tpu_custom_call" | custom-call | tf_op jit(solution)/shard_map/last/pallas_call | solution.py:1237
  317.0 1.3 slice_bitcast_fusion
  318.3 1.5 copy.39
  319.8 1.5 copy.38
  321.3 1.9 copy.51
  323.2 1.9 copy.52
  325.6 0.7 copy.54
  326.3 0.7 copy.55
  327.0 0.6 copy.56
  327.6 0.6 copy.57
  328.2 0.6 copy.58
  329.3 0.6 copy.60
  329.9 0.7 copy.61
  (37 shorter events, 1.9 us)
Async XLA Ops:
  4.3 133.4 %copy-start.17 = (s32[8]{0:T(128)}, s32[8]{0:T(128)S(1)}, u32[]{:S(2)}) copy-start(s32[8]{0:T(128)S(1)} %and_select_fusion.take) | copy-start | bytes 100
  6.5 1.0 copy-start.2
  7.6 1.0 copy-start.3
  8.6 0.9 copy-start.5
  9.5 0.9 copy-start.6
  10.5 0.9 copy-start.7
  11.4 0.9 copy-start.8
  120.1 1.0 copy-start
  121.1 0.8 copy-start.1
  121.9 0.8 copy-start.4
  316.9 8.1 %copy-start.16 = (f32[1,256]{1,0:T(1,128)S(1)}, f32[1,256]{1,0:T(1,128)}, u32[]{:S(2)}) copy-start(f32[1,256]{1,0:T(1,128)} %get-tuple-element.102) | copy-start | bytes 3076
  316.9 8.7 %copy-start.11 = (f32[128,512]{1,0:T(8,128)S(1)}, f32[128,512]{1,0:T(8,128)}, u32[]{:S(2)}) copy-start(f32[128,512]{1,0:T(8,128)} %get-tuple-element.168) | copy-start | bytes 786436
  316.9 9.4 %copy-start.10 = (f32[128,512]{1,0:T(8,128)S(1)}, f32[128,512]{1,0:T(8,128)}, u32[]{:S(2)}) copy-start(f32[128,512]{1,0:T(8,128)} %get-tuple-element.169) | copy-start | bytes 786436
  316.9 10.1 %copy-start.12 = (f32[4,512]{1,0:T(4,128)S(1)}, f32[4,512]{1,0:T(4,128)}, u32[]{:S(2)}) copy-start(f32[4,512]{1,0:T(4,128)} %get-tuple-element.172) | copy-start | bytes 24580
  316.9 10.7 %copy-start.15 = (f32[1,512]{1,0:T(1,128)S(1)}, f32[1,512]{1,0:T(1,128)}, u32[]{:S(2)}) copy-start(f32[1,512]{1,0:T(1,128)} %get-tuple-element.108) | copy-start | bytes 6148
  316.9 11.3 %copy-start.14 = (f32[4,64]{1,0:T(4,128)S(1)}, f32[4,64]{1,0:T(4,128)}, u32[]{:S(2)}) copy-start(f32[4,64]{1,0:T(4,128)} %get-tuple-element.174) | copy-start | bytes 3076
  316.9 11.8 %copy-start.18 = (f32[1,64]{1,0:T(1,128)S(1)}, f32[1,64]{1,0:T(1,128)}, u32[]{:S(2)}) copy-start(f32[1,64]{1,0:T(1,128)} %get-tuple-element.110) | copy-start | bytes 772
  316.9 12.3 %copy-start.13 = (f32[1,512]{1,0:T(1,128)S(1)}, f32[1,512]{1,0:T(1,128)}, u32[]{:S(2)}) copy-start(f32[1,512]{1,0:T(1,128)} %get-tuple-element.112) | copy-start | bytes 6148
  317.0 12.9 %copy-start.9 = (f32[512,128]{1,0:T(8,128)S(1)}, f32[512,128]{1,0:T(8,128)}, u32[]{:S(2)}) copy-start(f32[512,128]{1,0:T(8,128)} %get-tuple-element.180) | copy-start | bytes 786436

commit v3 on v2

v3 whole, which is shorter than its diff:
```python
import functools

import jax
import jax.numpy as jnp
from jax import lax
from jax.experimental import pallas as pl
from jax.experimental.pallas import tpu as pltpu
from jax.sharding import PartitionSpec as P

D = 1024
GROUP = 256
BLOCK = 128
INNER = 2048
HDIM = 64
STATE = 128
TAPS = 4
HALO = 16
EDGE = 8
LANES = 128
EPS = 1e-05
MESH = pl.DeviceIdType.MESH
VMEM = pltpu.MemorySpace.VMEM
SMEM = pltpu.MemorySpace.SMEM
DMA = pltpu.SemaphoreType.DMA
VMEM_LIMIT = 63 << 20
LOW = jnp.bfloat16
WIDE = jnp.float32


def shape(dims, kind):
    return jax.ShapeDtypeStruct(dims, kind)


def nn(a, b):
    return jnp.dot(a, b, preferred_element_type=WIDE)


def nt(a, b):
    return lax.dot_general(a, b, (((1,), (1,)), ((), ())), preferred_element_type=WIDE)


def tn(a, b):
    return lax.dot_general(a, b, (((0,), (0,)), ((), ())), preferred_element_type=WIDE)


def halves(x):
    high = x.astype(LOW)
    return high, (x - high.astype(WIDE)).astype(LOW)


def thirds(x):
    high = x.astype(LOW)
    rest = x - high.astype(WIDE)
    middle = rest.astype(LOW)
    return high, middle, (rest - middle.astype(WIDE)).astype(LOW)


def head_rows(inner):
    row = lax.broadcasted_iota(jnp.int32, (LANES, inner), 0)
    column = lax.broadcasted_iota(jnp.int32, (LANES, inner), 1)
    return jnp.where(column // HDIM == row, 1.0, 0.0).astype(LOW)


def head_columns(inner):
    row = lax.broadcasted_iota(jnp.int32, (inner, LANES), 0)
    column = lax.broadcasted_iota(jnp.int32, (inner, LANES), 1)
    return jnp.where(row // HDIM == column, 1.0, 0.0).astype(LOW)


def to_columns(x, spread):
    high, rest = halves(x)
    return nn(high, spread) + nn(rest, spread)


def to_heads(x, collect):
    high, rest = halves(x)
    return nn(high, collect) + nn(rest, collect)


def ones_before(count):
    row = lax.broadcasted_iota(jnp.int32, (count, count), 0)
    column = lax.broadcasted_iota(jnp.int32, (count, count), 1)
    return row >= column


def sum_before(x):
    matrix = jnp.where(ones_before(x.shape[0]), 1.0, 0.0).astype(LOW)
    high, middle, low = thirds(x)
    return nn(matrix, high) + (nn(matrix, middle) + nn(matrix, low))


def sum_after(x):
    count = x.shape[0]
    row = lax.broadcasted_iota(jnp.int32, (count, count), 0)
    column = lax.broadcasted_iota(jnp.int32, (count, count), 1)
    matrix = jnp.where(row <= column, 1.0, 0.0).astype(LOW)
    high, middle, low = thirds(x)
    return nn(matrix, high) + (nn(matrix, middle) + nn(matrix, low))


def sigmoid(x):
    return 0.5 * jnp.tanh(0.5 * x) + 0.5


def step_terms(raw, heads):
    z = jnp.exp(-jnp.abs(raw))
    series = 1.0 - z * (0.5 - z * (1.0 / 3.0 - z * (0.25 - z * 0.2)))
    small = z < 0.03
    log1p = jnp.where(small, z * series, jnp.log(1.0 + z))
    soft = jnp.maximum(raw, 0.0) + log1p
    one = 1.0 / (1.0 + z)
    sig = jnp.where(raw >= 0, one, z * one)
    ratio = jnp.where(small & (raw < 0), one / series, sig / jnp.maximum(soft, 1e-20))
    lane = lax.broadcasted_iota(jnp.int32, raw.shape, 1)
    return jnp.where(lane < heads, soft, 0.0), sig, ratio


def greet(seq_peers, head_peers):
    barrier = pltpu.get_barrier_semaphore()
    count = 0
    if seq_peers > 1:
        me = lax.axis_index("seq")

        @pl.loop(1, seq_peers)
        def _(i):
            pl.semaphore_signal(
                barrier, inc=1, device_id={"seq": lax.rem(me + i, seq_peers)}, device_id_type=MESH
            )

        count += seq_peers - 1
    if head_peers > 1:
        mine = lax.axis_index("head")

        @pl.loop(1, head_peers)
        def _(i):
            pl.semaphore_signal(
                barrier, inc=1, device_id={"head": lax.rem(mine + i, head_peers)}, device_id_type=MESH
            )

        count += head_peers - 1
    pl.semaphore_wait(barrier, count)


def remote(src, dst, send_sem, recv_sem, where):
    return pltpu.make_async_remote_copy(
        src_ref=src, dst_ref=dst, send_sem=send_sem, recv_sem=recv_sem, device_id=where, device_id_type=MESH
    )


class Line:
    def __init__(self, count, out, width, send, recv):
        self.count, self.out, self.width, self.send, self.recv = count, out, width, send, recv
        self.me = lax.axis_index("head")

    def view(self, shard):
        return self.out.at[:, pl.ds(pl.multiple_of(shard * self.width, LANES), self.width)]

    def copy(self, src, shard, way, step):
        return remote(
            src, self.view(shard), self.send.at[way, step], self.recv.at[shard], {"head": self.me + (1 - 2 * way)}
        )

    def first(self, own):
        self.pass_on(own, self.me, 0, 0)
        self.pass_on(own, self.me, 1, 0)

    def pass_on(self, src, shard, way, step):
        reach = (self.me < self.count - 1) if way == 0 else (self.me > 0)

        @pl.when(reach)
        def _():
            self.copy(src, shard, way, step).start()

    def hop(self, step, take=True, give=True, source=None):
        for way in (0, 1):
            shard = self.me - step if way == 0 else self.me + step
            there = (shard >= 0) if way == 0 else (shard < self.count)

            @pl.when(there)
            def _():
                if take:
                    self.copy(self.view(shard), shard, way, step).wait_recv()
                if give and step < self.count - 1:
                    self.pass_on(self.view(shard) if source is None else source(shard), shard, way, step)

    def finish(self, own, steps=None):
        for way in (0, 1):
            reach = (self.me < self.count - 1) if way == 0 else (self.me > 0)
            for step in range(self.count - 1) if steps is None else steps:
                shard = self.me - step if way == 0 else self.me + step
                there = (shard >= 0) if way == 0 else (shard < self.count)

                @pl.when(reach & there)
                def _():
                    src = own if step == 0 else self.view(shard)
                    self.copy(src, shard, way, step).wait_send()


class Plane:
    def __init__(self, seqs, view, sent, got, passed, way=0):
        self.chips, self.view, self.sent, self.got, self.passed, self.way = seqs // 2, view, sent, got, passed, way
        self.me = lax.axis_index("seq")
        self.core = lax.rem(self.me, 2)
        self.chip = self.me // 2
        self.mate = self.me + 1 - 2 * self.core

    def forward(self, chip):
        return (chip > self.chip) if self.way == 1 else (chip < self.chip) if self.way == -1 else (chip >= 0)

    def backward(self, chip):
        return (chip < self.chip) if self.way == 1 else (chip > self.chip) if self.way == -1 else (chip >= 0)

    def each_chip(self, body):
        @pl.loop(1, self.chips)
        def _(i):
            body(lax.rem(self.chip + i, self.chips))

    def copy(self, src, source, to, sem):
        return remote(src, self.view(source), sem, self.got.at[source], {"seq": to})

    def start(self, own):
        def send(chip):
            to = 2 * chip + self.core

            @pl.when(self.forward(chip))
            def _():
                self.copy(own, self.me, to, self.sent.at[to]).start()

        self.each_chip(send)
        self.copy(own, self.me, self.mate, self.sent.at[self.mate]).start()

    def relay(self):
        def take(chip):
            source = 2 * chip + self.core

            @pl.when(self.backward(chip))
            def _():
                landed = self.view(source)
                self.copy(landed, source, self.mate, self.passed.at[source]).wait_recv()
                self.copy(landed, source, self.mate, self.passed.at[source]).start()

        self.each_chip(take)

    def finish(self, own):
        def take(chip):
            source = 2 * chip + 1 - self.core

            @pl.when(self.backward(chip))
            def _():
                self.copy(self.view(source), source, self.mate, self.passed.at[source]).wait_recv()

        self.each_chip(take)
        self.copy(self.view(self.mate), self.mate, self.mate, self.sent.at[self.mate]).wait_recv()
        self.copy(own, self.me, self.mate, self.sent.at[self.mate]).wait_send()

        def drain(chip):
            same = 2 * chip + self.core

            @pl.when(self.forward(chip))
            def _():
                self.copy(own, self.me, same, self.sent.at[same]).wait_send()

            @pl.when(self.backward(chip))
            def _():
                self.copy(self.view(same), same, self.mate, self.passed.at[same]).wait_send()

        self.each_chip(drain)


ANY_SPEC = pl.BlockSpec(memory_space=pl.ANY)
VMEM_SPEC = pl.BlockSpec(memory_space=VMEM)
SMEM_SPEC = pl.BlockSpec(memory_space=SMEM)


def index_kernel(
    seqs, tiles, place, lengths, stepbias, decays, through, give_in, take_in, give_out, take_out, flags, vec
):
    me = lax.axis_index("seq")

    @pl.loop(0, seqs * tiles)
    def _(j):
        block = place[j]

        @pl.when(lax.div(block, tiles) == me)
        def _():
            to = lax.div(j, tiles)
            give_in[to] = lax.rem(block, tiles)
            take_out[lax.rem(block, tiles)] = to

    @pl.loop(0, tiles)
    def _(k):
        source = lax.div(place[me * tiles + k], tiles)
        take_in[k] = source
        give_out[source] = k

    @pl.loop(0, tiles + 1)
    def _(k):
        position = (me * tiles + k) * BLOCK
        end = jnp.int32(0)
        border = position == 0
        for n in range(lengths.shape[0]):
            end = end + lengths[n]
            border = border | (position == end)
        flags[k] = jnp.where(border, 0.0, 1.0)

    heads = stepbias.shape[1]
    vec[...] = jnp.zeros_like(vec)
    vec[0:1, :heads] = stepbias[...]
    vec[1:2, :heads] = decays[...]
    vec[2:3, :heads] = through[...]


def index(place, lengths, stepbias, decays, through, tiles):
    seqs = lax.axis_size("seq")
    whole = jnp.int32
    return pl.pallas_call(
        functools.partial(index_kernel, seqs, tiles),
        out_shape=(
            shape((seqs,), whole), shape((tiles,), whole), shape((seqs,), whole), shape((tiles,), whole),
            shape((tiles + 1,), WIDE), shape((EDGE, LANES), WIDE),
        ),
        in_specs=[SMEM_SPEC] * 2 + [VMEM_SPEC] * 3,
        out_specs=(SMEM_SPEC,) * 5 + (VMEM_SPEC,),
        compiler_params=pltpu.CompilerParams(vmem_limit_bytes=VMEM_LIMIT),
        name="index",
    )(place, lengths, stepbias[None, :], decays[None, :], through[None, :])


def spread_kernel(
    seqs, heads, chunks, give, take, x_in, g_in, gating_in, payload_in, address_in, stepping_in, readout_in,
    x_out, w_out, r_out, work_x, work_g,
    x, g, gating, payload, address, stepping, readout, square,
    send_x, send_g, recv_x, recv_g, w_own, r_own,
    sent, got, w_sent, w_got, w_passed, r_sent, r_got, r_passed, rim_sent, rim_got, own_sem, load_sem,
    line_sent, line_got,
):
    me, mine = lax.axis_index("seq"), lax.axis_index("head")
    blocks, _, width = x.shape
    rows = blocks * BLOCK
    depth, inner = gating.shape
    pairs = (
        (x_in, x), (g_in, g), (gating_in, gating), (payload_in, payload), (address_in, address),
        (stepping_in, stepping), (readout_in, readout),
    )
    loads = [pltpu.make_async_copy(src, dst, load_sem.at[n]) for n, (src, dst) in enumerate(pairs)]
    for load in loads:
        load.start()
    greet(seqs, heads)

    def post(which, source, outgoing, incoming):
        @pl.loop(1, seqs)
        def _(i):
            to = lax.rem(me + i, seqs)
            outgoing[to] = source[give[to]]
            remote(outgoing.at[to], incoming.at[me], sent.at[which, to], got.at[which, me], {"seq": to}).start()

        incoming[me] = source[give[me]]

    loads[0].wait()
    post(0, x, send_x, recv_x)
    for load in loads[1:]:
        load.wait()

    w_own[:, :inner] = gating[...].astype(LOW)
    w_own[:, inner : 2 * inner] = payload[...].astype(LOW)
    state2 = address.shape[1]
    w_own[:, 2 * inner : 2 * inner + state2] = address[...].astype(LOW)
    square[...] = jnp.zeros_like(square)
    square[: stepping.shape[0], :depth] = stepping[...]
    w_own[:, 2 * inner + state2 :] = square[...].T[:depth].astype(LOW)
    r_own[...] = readout[...].T.astype(LOW)

    def rows_of(device):
        return pl.ds(pl.multiple_of(device * depth, depth), depth)

    own_w = pltpu.make_async_copy(w_own, w_out.at[rows_of(me)], own_sem.at[0])
    own_r = pltpu.make_async_copy(r_own, r_out.at[rows_of(me)], own_sem.at[1])
    own_w.start()
    own_r.start()
    w_plane = Plane(seqs, lambda s: w_out.at[rows_of(s)], w_sent, w_got, w_passed)
    r_plane = Plane(seqs, lambda s: r_out.at[rows_of(s)], r_sent, r_got, r_passed)

    def arrange(which, received, work):
        @pl.loop(1, seqs)
        def _(i):
            source = lax.rem(me + i, seqs)
            remote(
                received.at[source], received.at[source], sent.at[which, source], got.at[which, source], {"seq": source}
            ).wait_recv()

        for k in range(blocks):
            work[pl.ds(k * BLOCK, BLOCK), :] = received[take[k]]

    arrange(0, recv_x, work_x)
    part = rows // chunks
    pieces = [(n * part, part) for n in range(chunks)] + [(rows, HALO)]
    lines = [
        Line(heads, x_out.at[pl.ds(at, size)], width, line_sent.at[n], line_got.at[n])
        for n, (at, size) in enumerate(pieces)
    ]
    owns = [work_x.at[pl.ds(at, size)] for at, size in pieces]
    after = lax.rem(me + 1, seqs)
    rim = remote(
        work_x.at[pl.ds(rows - HALO, HALO)], work_x.at[pl.ds(rows, HALO)], rim_sent, rim_got, {"seq": after}
    )
    rim.start()
    for line, own in zip(lines[:-1], owns[:-1]):
        line.first(own)
    w_plane.start(w_own)
    own_columns = x_out.at[pl.ds(0, rows), pl.ds(pl.multiple_of(mine * width, LANES), width)]
    own_x = pltpu.make_async_copy(work_x.at[pl.ds(0, rows)], own_columns, own_sem.at[2])
    own_x.start()
    rim.wait()
    lines[-1].first(owns[-1])
    own_rim = pltpu.make_async_copy(owns[-1], lines[-1].view(mine), own_sem.at[3])
    own_rim.start()
    post(1, g, send_g, recv_g)
    r_plane.start(r_own)
    for step in range(1, heads):
        for line in lines:
            line.hop(step)
        if step == 1:
            w_plane.relay()
    arrange(1, recv_g, work_g)
    r_plane.relay()
    for line, own in zip(lines, owns):
        line.finish(own)
    w_plane.finish(w_own)
    r_plane.finish(r_own)
    for copy in (own_w, own_r, own_x, own_rim):
        copy.wait()

    @pl.loop(1, seqs)
    def _(i):
        other = lax.rem(me + i, seqs)
        for which, buffer in ((0, send_x), (1, send_g)):
            remote(
                buffer.at[other], buffer.at[other], sent.at[which, other], got.at[which, other], {"seq": other}
            ).wait_send()


def spread(give, take, x, g, gating, payload, address, stepping, readout):
    seqs, heads = lax.axis_size("seq"), lax.axis_size("head")
    rows, width = x.shape
    depth, inner = gating.shape
    total = depth * seqs
    columns = 2 * inner + address.shape[1] + LANES
    block = (seqs, BLOCK, width)
    given = (rows // BLOCK, BLOCK, width)
    chunks = 4
    operands = (x.reshape(given), g.reshape(given), gating, payload, address, stepping.T, readout)
    return pl.pallas_call(
        functools.partial(spread_kernel, seqs, heads, chunks),
        out_shape=(
            shape((rows + HALO, total), LOW),
            shape((total, columns), LOW),
            shape((total, inner), LOW),
            shape((rows + HALO, width), LOW),
            shape((rows, width), LOW),
        ),
        in_specs=[SMEM_SPEC] * 2 + [ANY_SPEC] * 7,
        out_specs=(ANY_SPEC,) * 3 + (VMEM_SPEC,) * 2,
        scratch_shapes=[pltpu.VMEM(a.shape, a.dtype) for a in operands] + [
            pltpu.VMEM((LANES, LANES), WIDE),
            pltpu.VMEM(block, LOW), pltpu.VMEM(block, LOW), pltpu.VMEM(block, LOW), pltpu.VMEM(block, LOW),
            pltpu.VMEM((depth, columns), LOW), pltpu.VMEM((depth, inner), LOW),
            DMA((2, seqs)), DMA((2, seqs)),
            DMA((seqs,)), DMA((seqs,)), DMA((seqs,)), DMA((seqs,)), DMA((seqs,)), DMA((seqs,)),
            DMA, DMA, DMA((4,)), DMA((7,)),
            DMA((chunks + 1, 2, heads)), DMA((chunks + 1, heads)),
        ],
        compiler_params=pltpu.CompilerParams(
            collective_id=0, has_side_effects=True, vmem_limit_bytes=VMEM_LIMIT
        ),
        name="spread",
    )(give, take, *operands)


def blockwise(dims, index):
    return pl.BlockSpec(dims, index)


def fixed(dims):
    return pl.BlockSpec(dims, lambda i: (0,) * len(dims), pipeline_mode=pl.Buffered(1))


def carry_columns(carry_row_t, collect):
    high, middle, low = thirds(jnp.broadcast_to(carry_row_t, (LANES, LANES)))
    return nn(collect, high) + (nn(collect, middle) + nn(collect, low))


def pair_lanes(slab):
    lane = lax.broadcasted_iota(jnp.int32, slab.shape, 1)
    zero = jnp.zeros_like(slab)
    return jnp.where(lane < HDIM, slab, zero), jnp.where(lane >= HDIM, slab, zero)


def front_kernel(
    heads, line, flags, u, rim, w, vec, prenorm, kernels, filters, offsets, shifts, g,
    normed_o, gate_o, pre_o, conv_o, act_o, raw_o, cum_o, part_o, local_o, msg_o, rim_o, g_o,
    ext, prev, state, prod, line_sent, line_got, own_sem,
):
    i = pl.program_id(0)
    g_line = Line(line, g_o, g.shape[1], line_sent, line_got)
    own_g = pltpu.make_async_copy(g, g_line.view(g_line.me), own_sem)
    inner = gate_o.shape[1]
    wide = pre_o.shape[1]
    taps = jnp.concatenate([kernels[...], filters[...]], axis=1)
    bias = jnp.concatenate([offsets[...], shifts[...]], axis=1)
    spread_m, collect = head_rows(inner), head_columns(inner)

    def normalize(block):
        rows = block.astype(WIDE)
        scale = lax.rsqrt(jnp.mean(rows * rows, axis=1, keepdims=True) + EPS)
        return (rows * scale * prenorm[...]).astype(LOW)

    @pl.when(i == 0)
    def _():
        greet(1, line)
        g_line.first(g)
        own_g.start()
        before = nn(normalize(rim[...]), w[:, inner : inner + wide]).astype(LOW).astype(WIDE)
        prev[...] = before[HALO - EDGE :]
        rim_o[...] = before[HALO - EDGE :]
        state[...] = jnp.zeros_like(state)
        prod[...] = jnp.ones_like(prod)

    normed = normalize(u[...])
    normed_o[...] = normed
    gate_o[...] = nn(normed, w[:, :inner])
    pre = nn(normed, w[:, inner : inner + wide]).astype(LOW)
    pre_o[...] = pre
    lane = lax.broadcasted_iota(jnp.int32, (GROUP, LANES), 1)
    raw = jnp.where(lane < heads, nn(normed, w[:, inner + wide :]) + vec[0:1, :], 0.0)
    raw_o[...] = raw
    first, second = flags[2 * i], flags[2 * i + 1]
    same = (first, second)
    for half in range(2):
        rows = pl.ds(half * BLOCK, BLOCK)
        ext[0:EDGE, :] = prev[...] * same[half]
        ext[EDGE:, :] = pre[half * BLOCK : (half + 1) * BLOCK].astype(WIDE)
        prev[...] = ext[BLOCK:, :]
        total = bias + taps[TAPS - 1 : TAPS] * ext[EDGE:, :]
        for tap in range(TAPS - 1):
            total = total + taps[tap : tap + 1] * ext[pl.ds(EDGE - (TAPS - 1) + tap, BLOCK), :]
        conv_o[rows, :] = total
        act_o[rows, :] = (total * sigmoid(total)).astype(LOW)

    steps, _, _ = step_terms(raw, heads)
    scale = -jnp.exp(vec[1:2, :])
    cum = sum_before(steps * scale)
    cum_o[...] = cum
    cum_t, steps_t = cum.T, steps.T
    write = act_o[:, inner : inner + STATE]
    read = act_o[:, inner + STATE :]
    lower = ones_before(BLOCK)
    top, low = slice(0, BLOCK), slice(BLOCK, GROUP)
    s00 = jnp.where(lower, nt(read[top], write[top]), 0.0)
    s10 = nt(read[low], write[top]) * second
    s11 = jnp.where(lower, nt(read[low], write[low]), 0.0)

    def mix(scores, head, t, s):
        decay = jnp.exp(jnp.minimum(cum[t, head : head + 1] - cum_t[head : head + 1, s], 0.0))
        return (scores * (decay * steps_t[head : head + 1, s])).astype(LOW)

    last = cum[GROUP - 1 : GROUP, :]
    row = lax.broadcasted_iota(jnp.int32, (GROUP, LANES), 0)
    weight = steps * jnp.exp(last - cum) * jnp.where(row < BLOCK, second, 1.0)
    weight_w = to_columns(weight, spread_m)
    packed = []
    for pair in range(inner // LANES):
        columns = slice(pair * LANES, (pair + 1) * LANES)
        slab = act_o[:, columns]
        slab_f = slab.astype(WIDE)
        ones = pair_lanes(slab)
        h0, h1 = 2 * pair, 2 * pair + 1
        y0 = nn(
            jnp.concatenate([mix(s00, h0, top, top), mix(s00, h1, top, top)], axis=1),
            jnp.concatenate([ones[0][top], ones[1][top]], axis=0),
        )
        y1 = nn(
            jnp.concatenate(
                [mix(s10, h0, low, top), mix(s11, h0, low, low), mix(s10, h1, low, top), mix(s11, h1, low, low)], axis=1
            ),
            jnp.concatenate([ones[0], ones[1]], axis=0),
        )
        skip = to_columns(jnp.broadcast_to(vec[2:3, :], (EDGE, LANES)), spread_m[:, columns])[0:1]
        part_o[top, columns] = y0 + skip * slab_f[top]
        part_o[low, columns] = y1 + skip * slab_f[low]
        packed.append((slab_f * weight_w[:, columns]).astype(LOW))
    local = tn(jnp.concatenate(packed, axis=1), write)
    local_o[0] = local
    carry = jnp.exp(cum_t[:, GROUP - 1 : GROUP]) * (first * second)
    state[...] = carry_columns(carry, collect) * state[...] + local
    prod[...] = jnp.broadcast_to(carry[:HALO], (HALO, STATE)) * prod[...]
    msg_o[:inner, :] = state[...].astype(LOW)
    msg_o[inner:, :] = prod[...].astype(LOW)

    @pl.when(i == pl.num_programs(0) - 1)
    def _():
        if line > 1:
            g_line.hop(1, give=False)
        g_line.finish(g, (0,))
        own_g.wait()


def front(flags, x_full, w_all, vec, prenorm, kernels, filters, offsets, shifts, g, heads):
    line = lax.axis_size("head")
    rows = x_full.shape[0] - HALO
    inner = kernels.shape[1]
    wide = inner + filters.shape[1]
    blocks = rows // GROUP
    total = x_full.shape[1]

    def by_rows(width):
        return blockwise((GROUP, width), lambda i: (i, 0))

    return pl.pallas_call(
        functools.partial(front_kernel, heads, line),
        grid=(blocks,),
        out_shape=(
            shape((rows, total), LOW), shape((rows, inner), WIDE), shape((rows, wide), LOW), shape((rows, wide), WIDE),
            shape((rows, wide), LOW), shape((rows, LANES), WIDE), shape((rows, LANES), WIDE), shape((rows, inner), WIDE),
            shape((blocks, inner, STATE), WIDE), shape((inner + HALO, STATE), LOW),
            shape((EDGE, wide), WIDE), shape((rows, total), LOW),
        ),
        in_specs=[
            SMEM_SPEC, by_rows(total), blockwise((HALO, total), lambda i: (rows // HALO, 0)), fixed(w_all.shape),
            fixed(vec.shape), fixed(prenorm.shape), fixed(kernels.shape), fixed(filters.shape), fixed(offsets.shape),
            fixed(shifts.shape), ANY_SPEC,
        ],
        out_specs=(
            by_rows(total), by_rows(inner), by_rows(wide), by_rows(wide), by_rows(wide), by_rows(LANES), by_rows(LANES),
            by_rows(inner), blockwise((1, inner, STATE), lambda i: (i, 0, 0)), fixed((inner + HALO, STATE)),
            fixed((EDGE, wide)), ANY_SPEC,
        ),
        scratch_shapes=[
            pltpu.VMEM((EDGE + BLOCK, wide), WIDE), pltpu.VMEM((EDGE, wide), WIDE),
            pltpu.VMEM((inner, STATE), WIDE), pltpu.VMEM((HALO, STATE), WIDE),
            DMA((2, line)), DMA((line,)), DMA,
        ],
        compiler_params=pltpu.CompilerParams(
            collective_id=1, has_side_effects=True, vmem_limit_bytes=VMEM_LIMIT, dimension_semantics=("arbitrary",)
        ),
        name="front",
    )(flags, x_full, x_full, w_all, vec, prenorm, kernels, filters, offsets, shifts, g)


def fold_states(slots, collect, inner, first, last, step, start):
    def hop(n, state):
        message = slots[first + n * step]
        carry = nn(collect[:, :HALO], message[inner:])
        return carry * state + message[:inner].astype(WIDE)

    return lax.fori_loop(0, (last - first) * step, hop, start)


def chunk_lanes(x, count):
    size = x.shape[1] // count
    fold = LANES // size
    tall = GROUP // fold
    lane = lax.broadcasted_iota(jnp.int32, (tall, LANES), 1)
    out = []
    for chunk in range(count):
        slab, offset = chunk * size // LANES, chunk * size % LANES
        total = jnp.zeros((tall, LANES), WIDE)
        for group in range(fold):
            piece = x[group * tall : (group + 1) * tall, slab * LANES : (slab + 1) * LANES]
            shift = (group * size - offset) % LANES
            if shift:
                piece = pltpu.roll(piece, shift, 1)
            inside = (lane >= group * size) & (lane < (group + 1) * size)
            total = jnp.where(inside, piece, total)
        out.append(total)
    return out


def core_kernel(
    seqs, line, heads, blocks, flags, msg, gate, part, read, act, cum, raw, local, g_part, normed, r_t, postnorm, vec,
    dgate_o, dval_o, daddr_o, dstep_o, tiny_o, gpost_o, sums_o, out_got, gread_got, ggate_got,
    ssd_s, gated_s, din_s, dssd_s, starts, q, state, prod, g_buf, out_part, slots, back_slots, back_msg, sums,
    gread, ggate, gread_low, ggate_low,
    sent, got, passed, back_sent, back_got, back_passed, sum_sent, sum_got, line_sent, line_got, load_sem,
    out_sent, out_sem, w_sent, w_sem, own_sem,
):
    i = pl.program_id(0)
    me, mine = lax.axis_index("seq"), lax.axis_index("head")
    inner = gate.shape[1]
    width = out_part.shape[2]
    depth = gread_got.shape[1]
    phase = i // blocks
    block = jnp.where(phase == 3, 4 * blocks - 1 - i, lax.rem(i, blocks))
    here = pl.ds(pl.multiple_of(block * GROUP, GROUP), GROUP)
    first, second = flags[2 * block], flags[2 * block + 1]
    plane = Plane(seqs, lambda s: slots.at[s], sent, got, passed, way=1)
    back_plane = Plane(seqs, lambda s: back_slots.at[s], back_sent, back_got, back_passed, way=-1)
    g_line = Line(line, g_buf, width, line_sent, line_got)

    def shard_of(ref, shard):
        return ref.at[:, pl.ds(pl.multiple_of(shard * width, LANES), width)]

    def load_copy(shard, n):
        return pltpu.make_async_copy(shard_of(g_part, shard), shard_of(g_buf, shard), load_sem.at[n])

    def each_load(body):
        body(load_copy(mine, 0))
        if line > 1:
            pl.when(mine > 0)(lambda: body(load_copy(mine - 1, 1)))
            pl.when(mine < line - 1)(lambda: body(load_copy(mine + 1, 2)))

    def sum_copy(to, slot):
        return remote(sums.at[mine], sums.at[slot], sum_sent.at[to], sum_got.at[slot], {"head": to})

    def out_copy(to, slot):
        return remote(out_part.at[to], out_got.at[slot], out_sent.at[to], out_sem.at[slot], {"head": to})

    def rows_of(device):
        return pl.ds(pl.multiple_of(device * depth, depth), depth)

    weights = ((gread_low, gread_got), (ggate_low, ggate_got))

    def w_copy(which, to, slot):
        src, dst = weights[which]
        return remote(
            src.at[rows_of(to)], dst.at[slot], w_sent.at[which, to], w_sem.at[which, slot], {"seq": to}
        )

    own_copies = [
        pltpu.make_async_copy(out_part.at[mine], out_got.at[mine], own_sem.at[0]),
        pltpu.make_async_copy(gread_low.at[rows_of(me)], gread_got.at[me], own_sem.at[1]),
        pltpu.make_async_copy(ggate_low.at[rows_of(me)], ggate_got.at[me], own_sem.at[2]),
    ]

    def all_line(body):
        if line > 1:

            @pl.loop(1, line)
            def _(n):
                body(lax.rem(mine + n, line))

    def all_seq(body):
        @pl.loop(1, seqs)
        def _(n):
            body(lax.rem(me + n, seqs))

    row = lax.broadcasted_iota(jnp.int32, (GROUP, LANES), 0)
    lane = lax.broadcasted_iota(jnp.int32, (GROUP, LANES), 1)

    def entry_of(cum_v, spread_m):
        return to_columns(jnp.exp(cum_v) * (first * jnp.where(row < BLOCK, 1.0, second)), spread_m)

    @pl.when(i == 0)
    def _():
        greet(seqs, line)
        g_line.hop(1, take=False, source=lambda shard: shard_of(g_part, shard))
        plane.start(msg)
        each_load(lambda copy: copy.start())
        plane.relay()
        plane.finish(msg)
        state[...] = fold_states(
            slots, head_columns(inner), inner, 0, me, 1, jnp.zeros((inner, STATE), WIDE)
        )

    @pl.when(phase == 0)
    def _():
        spread_m, collect = head_rows(inner), head_columns(inner)
        cum_v = cum[...]
        carry = jnp.exp(cum_v.T[:, GROUP - 1 : GROUP]) * (first * second)
        start = state[...]
        starts[block] = start
        ssd = part[...] + entry_of(cum_v, spread_m) * nt(read[...], start.astype(LOW))
        ssd_s[here, :] = ssd
        state[...] = carry_columns(carry, collect) * start + local[0]
        gate_v = gate[...]
        gated = ssd * (gate_v * sigmoid(gate_v))
        gated_s[here, :] = gated
        out = nt((gated * postnorm[...]).astype(LOW), r_t[...])
        for z in range(line):
            out_part[z, here] = out[:, z * width : (z + 1) * width].astype(LOW)

    @pl.when(i == blocks - 1)
    def _():
        for step in range(2, line):
            g_line.hop(step)
        each_load(lambda copy: copy.wait())
        g_line.finish(None, range(1, line - 1))

    @pl.when(phase == 1)
    def _():
        gated = gated_s[here, :]
        d_inner = nn(g_buf[here, :], r_t[...])
        din_s[here, :] = d_inner
        squares = jnp.sum(gated * gated, axis=1, keepdims=True)
        dots = jnp.sum(gated * postnorm[...] * d_inner, axis=1, keepdims=True)
        both = jnp.where(lane == 0, squares, jnp.where(lane == 1, dots, 0.0)).T
        sums[mine, block] = both[:EDGE]

    @pl.when(i == 2 * blocks - 1)
    def _():
        all_line(lambda to: sum_copy(to, mine).start())
        gread[...] = jnp.zeros_like(gread)
        ggate[...] = jnp.zeros_like(ggate)
        gpost_o[...] = jnp.zeros_like(gpost_o)
        state[...] = jnp.zeros_like(state)
        prod[...] = jnp.ones_like(prod)
        all_line(lambda other: sum_copy(other, other).wait())
        sums_o[...] = jnp.sum(sums[...], axis=0)
        all_line(lambda to: out_copy(to, mine).start())
        own_copies[0].start()

    @pl.when(phase == 2)
    def _():
        spread_m, collect = head_rows(inner), head_columns(inner)
        cum_v = cum[...]
        carry = jnp.exp(cum_v.T[:, GROUP - 1 : GROUP]) * (first * second)
        stats = jnp.concatenate([sums_o[block], jnp.zeros((LANES - EDGE, GROUP), WIDE)], axis=0).T
        inv = lax.rsqrt(stats[:, 0:1] / INNER + EPS)
        dot = stats[:, 1:2]
        gate_v = gate[...]
        sig = sigmoid(gate_v)
        ssd = ssd_s[here, :]
        d_inner = din_s[here, :]
        gated = gated_s[here, :]
        gated_inv = gated * inv
        inner_normed = (gated_inv * postnorm[...]).astype(LOW)
        d_gated = (inv * postnorm[...]) * d_inner - gated * (inv * inv * inv / INNER * dot)
        gpost_o[...] += jnp.sum(d_inner * gated_inv, axis=0, keepdims=True)
        d_ssd = (d_gated * (gate_v * sig)).astype(LOW)
        d_gate = (d_gated * ssd * sig * (1.0 + gate_v * (1.0 - sig))).astype(LOW)
        dssd_s[here, :] = d_ssd
        dgate_o[...] = d_gate
        gread[...] += tn(g_buf[here, :], inner_normed)
        ggate[...] += tn(normed[...], d_gate)
        query_grad = (d_ssd.astype(WIDE) * entry_of(cum_v, spread_m)).astype(LOW)
        found = tn(query_grad, read[...])
        q[block] = found
        state[...] += carry_columns(prod[...], collect) * found
        prod[...] = prod[...] * carry

    @pl.when(i == 3 * blocks - 1)
    def _():
        back_msg[:inner, :] = state[...].astype(LOW)
        back_msg[inner:, :] = jnp.broadcast_to(prod[:HALO], (HALO, STATE)).astype(LOW)
        back_plane.start(back_msg)
        gread_low[...] = gread[...].astype(LOW)
        ggate_low[...] = ggate[...].astype(LOW)
        tiny_o[...] = jnp.zeros_like(tiny_o)
        back_plane.relay()
        back_plane.finish(back_msg)
        for which in range(2):
            all_seq(lambda to: w_copy(which, to, me).start())
        own_copies[1].start()
        own_copies[2].start()
        state[...] = fold_states(
            back_slots, head_columns(inner), inner, seqs - 1, me, -1, jnp.zeros((inner, STATE), WIDE)
        )

    @pl.when(phase == 3)
    def _():
        spread_m, collect = head_rows(inner), head_columns(inner)
        lower_mask = ones_before(BLOCK)
        top, low = slice(0, BLOCK), slice(BLOCK, GROUP)
        cum_v = cum[...]
        cum_t = cum_v.T
        steps, sig, ratio = step_terms(raw[...], heads)
        steps_t = steps.T
        scale = -jnp.exp(vec[1:2, :])
        last = cum_v[GROUP - 1 : GROUP, :]
        write = act[:, inner : inner + STATE]
        read_v = act[:, inner + STATE :]
        s00 = jnp.where(lower_mask, nt(read_v[top], write[top]), 0.0)
        s10 = nt(read_v[low], write[top]) * second
        s11 = jnp.where(lower_mask, nt(read_v[low], write[low]), 0.0)

        end = state[...]
        end_low = end.astype(LOW)
        start = starts[block]
        carry = jnp.exp(cum_t[:, GROUP - 1 : GROUP]) * (first * second)
        state[...] = carry_columns(carry, collect) * end + q[block]
        weight = steps * jnp.exp(last - cum_v) * jnp.where(row < BLOCK, second, 1.0)
        weight_w = to_columns(weight, spread_m)
        d_ssd = dssd_s[here, :]
        d_query = (d_ssd.astype(WIDE) * entry_of(cum_v, spread_m)).astype(LOW)
        through_w = to_columns(jnp.broadcast_to(vec[2:3, :], (EDGE, LANES)), spread_m)[0:1]

        def decay_of(head, t, s):
            decay = jnp.exp(jnp.minimum(cum_v[t, head : head + 1] - cum_t[head : head + 1, s], 0.0))
            return decay * steps_t[head : head + 1, s]

        ds00 = jnp.zeros((BLOCK, BLOCK), WIDE)
        ds10 = jnp.zeros((BLOCK, BLOCK), WIDE)
        ds11 = jnp.zeros((BLOCK, BLOCK), WIDE)
        packed, value_parts, tails = [], [], []
        d_packed = nt(write, end_low)
        for pair in range(inner // LANES):
            columns = slice(pair * LANES, (pair + 1) * LANES)
            values = act[:, columns]
            values_f = values.astype(WIDE)
            dy = d_ssd[:, columns]
            dys = pair_lanes(dy)
            m00, m10, m11 = [], [], []
            for k in range(2):
                head = 2 * pair + k
                l00, l10, l11 = decay_of(head, top, top), decay_of(head, low, top), decay_of(head, low, low)
                m00.append((s00 * l00).astype(LOW))
                m10.append((s10 * l10).astype(LOW))
                m11.append((s11 * l11).astype(LOW))
                ds00 = ds00 + nt(dys[k][top], values[top]) * l00
                ds10 = ds10 + nt(dys[k][low], values[top]) * l10
                ds11 = ds11 + nt(dys[k][low], values[low]) * l11
            v0 = tn(
                jnp.concatenate([m00[0], m10[0], m00[1], m10[1]], axis=0), jnp.concatenate([dys[0], dys[1]], axis=0)
            )
            v1 = tn(
                jnp.concatenate([m11[0], m11[1]], axis=0), jnp.concatenate([dys[0][low], dys[1][low]], axis=0)
            )
            tail = d_packed[:, columns] * weight_w[:, columns]
            whole = jnp.concatenate([v0, v1], axis=0) + tail
            dval_o[:, columns] = whole + through_w[:, columns] * dy.astype(WIDE)
            value_parts.append(values_f * whole)
            tails.append(jnp.sum(tail * values_f, axis=0, keepdims=True))
            packed.append((values_f * weight_w[:, columns]).astype(LOW))

        ds = jnp.concatenate(
            [
                jnp.concatenate([jnp.where(lower_mask, ds00, 0.0), jnp.zeros((BLOCK, BLOCK), WIDE)], axis=1),
                jnp.concatenate([ds10 * second, jnp.where(lower_mask, ds11, 0.0)], axis=1),
            ],
            axis=0,
        ).astype(LOW)
        d_read = nn(ds, write) + nn(d_query, start.astype(LOW))
        d_write = tn(ds, read_v) + nn(jnp.concatenate(packed, axis=1), end_low)
        for z, chunk in enumerate(chunk_lanes(jnp.concatenate([d_write, d_read], axis=1), line)):
            daddr_o[z] = chunk.astype(LOW)

        dy_f = d_ssd.astype(WIDE)
        own = to_heads(dy_f * act[:, :inner].astype(WIDE), collect)
        r1 = to_heads(dy_f * ssd_s[here, :], collect) - vec[2:3, :] * own
        w = to_heads(jnp.concatenate(value_parts, axis=1), collect)
        tail_row = to_heads(jnp.broadcast_to(jnp.concatenate(tails, axis=1), (EDGE, inner)), collect)[0:1]
        high, rest = halves(end * start)
        ones = jnp.ones((EDGE, STATE), LOW)
        carry_grad = to_heads(nt(ones, high) + nt(ones, rest), collect)[0:1]
        d_last = tail_row + carry_grad * (jnp.exp(last) * (first * second))
        d_cum = r1 - w + jnp.where(row == GROUP - 1, d_last, 0.0)
        d_rate = sum_after(d_cum)
        d_raw = d_rate * scale * sig + w * ratio
        dstep_o[...] = d_raw.astype(LOW)
        tiny_o[0:1, :] += jnp.sum(d_raw, axis=0, keepdims=True)
        tiny_o[1:2, :] += jnp.sum(d_rate * steps, axis=0, keepdims=True) * scale
        tiny_o[2:3, :] += jnp.sum(own, axis=0, keepdims=True)

    @pl.when(i == 4 * blocks - 1)
    def _():
        all_line(lambda other: out_copy(other, other).wait())
        for which in range(2):
            all_seq(lambda other: w_copy(which, other, other).wait())
        for copy in own_copies:
            copy.wait()


def core(flags, msg, gate, part, act, cum, raw, local, g_part, normed, r_t, postnorm, vec, heads):
    seqs, line = lax.axis_size("seq"), lax.axis_size("head")
    rows, inner = gate.shape
    wide = act.shape[1]
    total = g_part.shape[1]
    width = total // line
    depth = total // seqs
    blocks = rows // GROUP
    fold = LANES * line // (2 * STATE)

    def place(phases):
        def at(i):
            phase = i // blocks
            index = jnp.int32(0)
            held = jnp.int32(0)
            for n in range(4):
                if n in phases:
                    now = (4 * blocks - 1 - i) if n == 3 else i - n * blocks
                    held = jnp.int32(0 if n == 3 else blocks - 1)
                else:
                    later = [m for m in phases if m > n]
                    now = held if not later else jnp.int32(blocks - 1 if later[0] == 3 else 0)
                index = jnp.where(phase == n, now, index)
            return index

        return at

    def by_rows(columns, phases, column=0):
        at = place(phases)
        return blockwise((GROUP, columns), lambda i: (at(i), column))

    at_first, at_last = place((0,)), place((3,))
    message = (inner + HALO, STATE)
    return pl.pallas_call(
        functools.partial(core_kernel, seqs, line, heads, blocks),
        grid=(4 * blocks,),
        out_shape=(
            shape((rows, inner), LOW), shape((rows, inner), WIDE), shape((line, rows // fold, LANES), LOW),
            shape((rows, LANES), LOW), shape((EDGE, LANES), WIDE), shape((1, inner), WIDE),
            shape((blocks, EDGE, GROUP), WIDE), shape((line, rows, width), LOW), shape((seqs, depth, inner), LOW),
            shape((seqs, depth, inner), LOW),
        ),
        in_specs=[
            SMEM_SPEC, ANY_SPEC, by_rows(inner, (0, 2)), by_rows(inner, (0,)),
            by_rows(STATE, (0, 2), (inner + STATE) // STATE), by_rows(wide, (3,)), by_rows(LANES, (0, 2, 3)),
            by_rows(LANES, (3,)), blockwise((1, inner, STATE), lambda i: (at_first(i), 0, 0)), ANY_SPEC,
            by_rows(total, (2,)), fixed(r_t.shape), fixed(postnorm.shape), fixed(vec.shape),
        ],
        out_specs=(
            by_rows(inner, (2,)), by_rows(inner, (3,)),
            blockwise((line, GROUP // fold, LANES), lambda i: (0, at_last(i), 0)), by_rows(LANES, (3,)),
            fixed((EDGE, LANES)), fixed((1, inner)), fixed((blocks, EDGE, GROUP)), ANY_SPEC, ANY_SPEC, ANY_SPEC,
        ),
        scratch_shapes=[
            pltpu.VMEM((rows, inner), WIDE), pltpu.VMEM((rows, inner), WIDE), pltpu.VMEM((rows, inner), WIDE),
            pltpu.VMEM((rows, inner), LOW), pltpu.VMEM((blocks, inner, STATE), WIDE),
            pltpu.VMEM((blocks, inner, STATE), WIDE), pltpu.VMEM((inner, STATE), WIDE), pltpu.VMEM((LANES, 1), WIDE),
            pltpu.VMEM((rows, total), LOW), pltpu.VMEM((line, rows, width), LOW), pltpu.VMEM((seqs,) + message, LOW),
            pltpu.VMEM((seqs,) + message, LOW), pltpu.VMEM(message, LOW), pltpu.VMEM((line, blocks, EDGE, GROUP), WIDE),
            pltpu.VMEM((total, inner), WIDE), pltpu.VMEM((total, inner), WIDE), pltpu.VMEM((total, inner), LOW),
            pltpu.VMEM((total, inner), LOW),
            DMA((seqs,)), DMA((seqs,)), DMA((seqs,)), DMA((seqs,)), DMA((seqs,)), DMA((seqs,)), DMA((line,)),
            DMA((line,)), DMA((2, line)), DMA((line,)), DMA((3,)), DMA((line,)), DMA((line,)), DMA((2, seqs)),
            DMA((2, seqs)), DMA((3,)),
        ],
        compiler_params=pltpu.CompilerParams(
            collective_id=2, has_side_effects=True, vmem_limit_bytes=VMEM_LIMIT, dimension_semantics=("arbitrary",)
        ),
        name="core",
    )(flags, msg, gate, part, act, act, cum, raw, local, g_part, normed, r_t, postnorm, vec)


def conv_grad(d_act, conv):
    sig = sigmoid(conv)
    return d_act * (sig * (1.0 + conv * (1.0 - sig)))


def last_kernel(
    seqs, line, blocks, flags, give,
    daddr, dval, dval_next, conv, conv_next, pre, normed, u, dgate, dstep, w, prenorm, kernels, filters, rim,
    out_got, work_x, work_g, sums, tiny, gpost,
    out_recv, grad_recv, dw_got, small_got,
    d_addr, addr_got, edge_own, edge_got, ext, after, prev, taps_g, bias_g, dx_send, dx_got, dw, dw_low,
    pn, pn_send, pn_got, small, result, fin_send,
    addr_sent, addr_sem, edge_sent, edge_sem, dx_sent, dx_sem, dw_sent, dw_sem, pn_sent, pn_sem,
    small_sent, small_sem, fin_sent, fin_sem, own_sem,
):
    i = pl.program_id(0)
    me, mine = lax.axis_index("seq"), lax.axis_index("head")
    inner = dgate.shape[1]
    tiles = work_g.shape[0] // BLOCK
    rows = work_g.shape[0]
    width = work_g.shape[1]
    depth = dw_got.shape[1]
    size = 2 * STATE // line
    fold = LANES // size
    tall = GROUP // fold
    slab = mine * size // LANES
    offset = lax.rem(mine * size, LANES)
    here = pl.ds(pl.multiple_of(i * GROUP, GROUP), GROUP)
    wide = inner + LANES

    def slab_of(ref, at):
        return ref[:, pl.ds(pl.multiple_of(at + slab * LANES, LANES), LANES)]

    def addr_copy(to, slot):
        return remote(daddr.at[to], addr_got.at[slot], addr_sent.at[to], addr_sem.at[slot], {"head": to})

    def edge_copy(to):
        return remote(edge_own, edge_got, edge_sent, edge_sem, {"seq": to})

    def dx_copy(to, slot, block):
        part = pl.ds(pl.multiple_of(block * GROUP, GROUP), GROUP)
        return remote(
            dx_send.at[to, part], dx_got.at[slot, part], dx_sent.at[to, block], dx_sem.at[slot, block], {"head": to}
        )

    def rows_of(device):
        return pl.ds(pl.multiple_of(device * depth, depth), depth)

    def dw_copy(to, slot):
        return remote(dw_low.at[rows_of(to)], dw_got.at[slot], dw_sent.at[to], dw_sem.at[slot], {"seq": to})

    def pn_copy(to, slot):
        return remote(pn_send.at[to], pn_got.at[slot], pn_sent.at[to], pn_sem.at[slot], {"head": to})

    def small_copy(to, slot):
        return remote(small, small_got.at[slot], small_sent.at[to], small_sem.at[slot], {"seq": to})

    arrivals = (out_recv, grad_recv)

    def fin_copy(which, to, slot):
        return remote(
            fin_send.at[which, to], arrivals[which].at[slot], fin_sent.at[which, to], fin_sem.at[which, slot],
            {"seq": to},
        )

    def all_seq(body):
        @pl.loop(1, seqs)
        def _(n):
            body(lax.rem(me + n, seqs))

    def all_line(body):
        if line > 1:

            @pl.loop(1, line)
            def _(n):
                body(lax.rem(mine + n, line))

    def kept(which):
        return pltpu.make_async_copy(fin_send.at[which, me], arrivals[which].at[me], own_sem.at[which])

    def route(which):
        def send(to):
            fin_send[which, to] = result[which, give[to]]
            fin_copy(which, to, me).start()

        all_seq(send)
        fin_send[which, me] = result[which, give[me]]
        kept(which).start()

    def land(which):
        all_seq(lambda other: fin_copy(which, other, other).wait())
        kept(which).wait()

    own_dw = pltpu.make_async_copy(dw_low.at[rows_of(me)], dw_got.at[me], own_sem.at[3])
    own_small = pltpu.make_async_copy(small, small_got.at[me], own_sem.at[4])

    @pl.when(i == 0)
    def _():
        greet(seqs, line)
        all_line(lambda to: addr_copy(to, mine).start())
        own = pltpu.make_async_copy(daddr.at[mine], addr_got.at[mine], own_sem.at[2])
        own.start()

        @pl.loop(0, blocks)
        def _(b):
            part = pl.ds(pl.multiple_of(b * GROUP, GROUP), GROUP)
            stats = jnp.concatenate([sums[b], jnp.zeros((LANES - EDGE, GROUP), WIDE)], axis=0).T
            inv = lax.rsqrt(stats[:, 0:1] / INNER + EPS)
            total = out_got[0, part].astype(WIDE)
            for z in range(1, line):
                total = total + out_got[z, part].astype(WIDE)
            done = (work_x[part].astype(WIDE) + total * inv).astype(LOW)
            result[0, 2 * b] = done[:BLOCK]
            result[0, 2 * b + 1] = done[BLOCK:]

        route(0)
        all_line(lambda other: addr_copy(other, other).wait())
        own.wait()
        lane = lax.broadcasted_iota(jnp.int32, (tall, LANES), 1)
        inside = (lane >= offset) & (lane < offset + size)

        @pl.loop(0, blocks)
        def _(b):
            part = pl.ds(pl.multiple_of(b * tall, tall), tall)
            total = addr_got[0, part].astype(WIDE)
            for z in range(1, line):
                total = total + addr_got[z, part].astype(WIDE)
            for group in range(fold):
                turned = pltpu.roll(total, lax.rem(offset + (LANES - group * size), LANES), 1)
                at = pl.ds(pl.multiple_of(b * GROUP + group * tall, tall), tall)
                d_addr[at, :] = jnp.where(inside, turned, 0.0)

        edge_own[:, :inner] = conv_grad(dval[0:EDGE, :], conv[0:EDGE, :inner])
        edge_own[:, inner:] = conv_grad(d_addr[0:EDGE, :], slab_of(conv, inner)[0:EDGE])
        edge_copy(lax.rem(me + seqs - 1, seqs)).start()
        prev[:, :inner] = rim[:, :inner]
        prev[:, inner:] = slab_of(rim, inner)
        taps_g[...] = jnp.zeros_like(taps_g)
        bias_g[...] = jnp.zeros_like(bias_g)
        dw[...] = jnp.zeros_like(dw)
        pn[...] = jnp.zeros_like(pn)

    @pl.when(i < blocks - 1)
    def _():
        after[:, :inner] = conv_grad(dval_next[...], conv_next[:, :inner])
        following = pl.ds(pl.multiple_of((i + 1) * GROUP, GROUP), EDGE)
        after[:, inner:] = conv_grad(d_addr[following, :], slab_of(conv_next, inner))

    @pl.when(i == blocks - 1)
    def _():
        edge_copy(lax.rem(me + 1, seqs)).wait()
        after[...] = edge_got[...]

    taps = jnp.concatenate([kernels[...], slab_of(filters, 0)], axis=1)
    conv_v = jnp.concatenate([conv[:, :inner], slab_of(conv, inner)], axis=1)
    pre_v = jnp.concatenate([pre[:, :inner], slab_of(pre, inner)], axis=1).astype(WIDE)
    d_conv = conv_grad(jnp.concatenate([dval[...], d_addr[here, :]], axis=1), conv_v)
    bias_g[...] += jnp.sum(d_conv, axis=0, keepdims=True)
    d_pre = []
    for half in range(2):
        at = slice(half * BLOCK, (half + 1) * BLOCK)
        tile = d_conv[at]
        ext[0:EDGE, :] = prev[...] * flags[2 * i + half]
        ext[EDGE:, :] = pre_v[at]
        prev[...] = ext[BLOCK:, :]
        for tap in range(TAPS):
            taps_g[tap : tap + 1, :] += jnp.sum(
                tile * ext[pl.ds(EDGE - (TAPS - 1) + tap, BLOCK), :], axis=0, keepdims=True
            )
        ext[:BLOCK, :] = tile
        following = d_conv[BLOCK : BLOCK + EDGE] if half == 0 else after[...]
        ext[BLOCK:, :] = following * flags[2 * i + half + 1]
        total = taps[TAPS - 1 : TAPS] * ext[:BLOCK, :]
        for tap in range(TAPS - 1):
            total = total + taps[tap : tap + 1] * ext[pl.ds(TAPS - 1 - tap, BLOCK), :]
        d_pre.append(total.astype(LOW))
    d_pre = jnp.concatenate(d_pre, axis=0)
    d_value, d_slab = d_pre[:, :inner], d_pre[:, inner:]
    d_step = dstep[...]
    normed_v = normed[...]
    dw[:, :wide] += tn(normed_v, d_pre)
    dw[:, wide:] += tn(normed_v, d_step)
    d_normed = (
        nt(dgate[...], w[:, :inner])
        + nt(d_value, w[:, inner : 2 * inner])
        + nt(d_slab, slab_of(w, 2 * inner))
        + nt(d_step, w[:, 2 * inner + 2 * STATE :])
    )
    u_f = u[...].astype(WIDE)
    inv = lax.rsqrt(jnp.mean(u_f * u_f, axis=1, keepdims=True) + EPS)
    gained = d_normed * prenorm[...]
    dot = jnp.sum(gained * u_f, axis=1, keepdims=True)
    grad = gained * inv - u_f * (inv * inv * inv / D * dot)
    pn[...] += jnp.sum(d_normed * (u_f * inv), axis=0, keepdims=True)
    for z in range(line):
        dx_send[z, here] = grad[:, z * width : (z + 1) * width].astype(LOW)
    dx_got[mine, here] = dx_send[mine, here]
    all_line(lambda to: dx_copy(to, mine, i).start())

    @pl.when(i == blocks - 1)
    def _():
        dw_low[...] = dw[...].astype(LOW)
        all_seq(lambda to: dw_copy(to, me).start())
        for z in range(line):
            pn_send[z] = jnp.broadcast_to(pn[:, z * width : (z + 1) * width], (EDGE, width))
        pn_got[mine] = pn_send[mine]
        all_line(lambda to: pn_copy(to, mine).start())
        own_dw.start()
        all_line(lambda other: pn_copy(other, other).wait())
        small[...] = jnp.zeros_like(small)
        small[0:TAPS, :] = taps_g[0:TAPS, :]
        small[4:5, :] = bias_g[...]
        small[5:6, :inner] = gpost[...]
        small[6:7, :width] = jnp.sum(pn_got[...], axis=0)[0:1]
        for n in range(3):
            small[7:8, n * LANES : (n + 1) * LANES] = tiny[n : n + 1, :]
        own_small.start()
        all_seq(lambda to: small_copy(to, me).start())

        @pl.loop(0, blocks)
        def _(b):
            all_line(lambda other: dx_copy(other, other, b).wait())
            part = pl.ds(pl.multiple_of(b * GROUP, GROUP), GROUP)
            total = dx_got[0, part].astype(WIDE)
            for z in range(1, line):
                total = total + dx_got[z, part].astype(WIDE)
            done = (work_g[part].astype(WIDE) + total).astype(LOW)
            result[1, 2 * b] = done[:BLOCK]
            result[1, 2 * b + 1] = done[BLOCK:]

        route(1)
        all_seq(lambda other: dw_copy(other, other).wait())
        all_seq(lambda other: small_copy(other, other).wait())
        land(0)
        land(1)
        own_dw.wait()
        own_small.wait()


def finish_kernel(
    take, out_recv, grad_recv, gread_got, ggate_got, dw_got, small_got,
    out_o, dx_o, prenorm_o, gate_o, pay_o, addr_o, step_o, kernels_o, offsets_o, filters_o, shifts_o,
    stepbias_o, decays_o, through_o, post_o, read_o,
):
    inner, size, heads, width = gate_o.shape[1], addr_o.shape[1], step_o.shape[0], prenorm_o.shape[1]
    wide = inner + LANES
    offset = lax.rem(lax.axis_index("head") * size, LANES)
    back_turn = lax.rem(LANES - offset, LANES)
    for k in range(out_o.shape[0]):
        out_o[k] = out_recv[take[k]]
        dx_o[k] = grad_recv[take[k]]

    def summed(ref):
        total = ref[0].astype(WIDE)
        for n in range(1, ref.shape[0]):
            total = total + ref[n].astype(WIDE)
        return total

    read_o[...] = summed(gread_got).T
    gate_o[...] = summed(ggate_got)
    grads = summed(dw_got)
    pay_o[...] = grads[:, :inner]
    addr_o[...] = pltpu.roll(grads[:, inner:wide], back_turn, 1)[:, :size]
    step_o[...] = grads[:, wide:].T[:heads]
    totals = jnp.sum(small_got[...], axis=0)
    kernels_o[...] = totals[0:TAPS, :inner]
    offsets_o[...] = totals[4:5, :inner]
    turned = pltpu.roll(totals[:, inner:], back_turn, 1)
    filters_o[...] = turned[0:TAPS, :size]
    shifts_o[...] = turned[4:5, :size]
    post_o[...] = totals[5:6, :inner]
    prenorm_o[...] = totals[6:7, :width]
    for n, ref in enumerate((stepbias_o, decays_o, through_o)):
        ref[...] = totals[7:8, n * LANES : n * LANES + heads]


def finish(take, out_recv, grad_recv, gread_got, ggate_got, dw_got, small_got, heads, line):
    seqs, _, width = out_recv.shape
    tiles = take.shape[0]
    _, depth, inner = gread_got.shape
    size = 2 * STATE // line
    operands = (out_recv, grad_recv, gread_got, ggate_got, dw_got, small_got)
    outs = (
        shape((tiles, BLOCK, width), LOW), shape((tiles, BLOCK, width), LOW), shape((1, width), WIDE),
        shape((depth, inner), WIDE), shape((depth, inner), WIDE), shape((depth, size), WIDE),
        shape((heads, depth), WIDE), shape((TAPS, inner), WIDE), shape((1, inner), WIDE),
        shape((TAPS, size), WIDE), shape((1, size), WIDE), shape((1, heads), WIDE), shape((1, heads), WIDE),
        shape((1, heads), WIDE), shape((1, inner), WIDE), shape((inner, depth), WIDE),
    )
    return pl.pallas_call(
        finish_kernel,
        grid=(1,),
        out_shape=outs,
        in_specs=[SMEM_SPEC] + [fixed(a.shape) for a in operands],
        out_specs=tuple(fixed(a.shape) for a in outs),
        compiler_params=pltpu.CompilerParams(vmem_limit_bytes=VMEM_LIMIT, dimension_semantics=("arbitrary",)),
        name="finish",
    )(take, *operands)


def last(
    flags, give, daddr, dval, conv, pre, normed, x_full, dgate, dstep, w_all, prenorm, kernels, filters, rim,
    out_got, work_x, work_g, sums, tiny, gpost,
):
    seqs, line = lax.axis_size("seq"), lax.axis_size("head")
    rows, width = work_g.shape
    inner = dgate.shape[1]
    wide = conv.shape[1]
    total = x_full.shape[1]
    depth = total // seqs
    blocks, tiles = rows // GROUP, rows // BLOCK
    part = inner + LANES
    step = GROUP // EDGE

    def by_rows(columns):
        return blockwise((GROUP, columns), lambda i: (i, 0))

    def next_rows(columns):
        return blockwise((EDGE, columns), lambda i: (jnp.minimum((i + 1) * step, rows // EDGE - 1), 0))

    whole = (w_all, prenorm, kernels, filters, rim, out_got, work_x, work_g, sums, tiny, gpost)
    return pl.pallas_call(
        functools.partial(last_kernel, seqs, line, blocks),
        grid=(blocks,),
        out_shape=(
            shape((seqs, BLOCK, width), LOW), shape((seqs, BLOCK, width), LOW),
            shape((seqs, depth, part + LANES), LOW), shape((seqs, EDGE, part), WIDE),
        ),
        in_specs=[SMEM_SPEC] * 2 + [
            ANY_SPEC, by_rows(inner), next_rows(inner), by_rows(wide), next_rows(wide), by_rows(wide), by_rows(total),
            by_rows(total), by_rows(inner), by_rows(LANES),
        ] + [fixed(a.shape) for a in whole],
        out_specs=(ANY_SPEC,) * 4,
        scratch_shapes=[
            pltpu.VMEM((rows, LANES), WIDE), pltpu.VMEM(daddr.shape, LOW),
            pltpu.VMEM((EDGE, part), WIDE), pltpu.VMEM((EDGE, part), WIDE),
            pltpu.VMEM((BLOCK + EDGE, part), WIDE), pltpu.VMEM((EDGE, part), WIDE), pltpu.VMEM((EDGE, part), WIDE),
            pltpu.VMEM((EDGE, part), WIDE), pltpu.VMEM((1, part), WIDE),
            pltpu.VMEM((line, rows, width), LOW), pltpu.VMEM((line, rows, width), LOW),
            pltpu.VMEM((total, part + LANES), WIDE), pltpu.VMEM((total, part + LANES), LOW),
            pltpu.VMEM((1, total), WIDE), pltpu.VMEM((line, EDGE, width), WIDE), pltpu.VMEM((line, EDGE, width), WIDE),
            pltpu.VMEM((EDGE, part), WIDE),
            pltpu.VMEM((2, tiles, BLOCK, width), LOW), pltpu.VMEM((2, seqs, BLOCK, width), LOW),
            DMA((line,)), DMA((line,)), DMA, DMA, DMA((line, blocks)), DMA((line, blocks)), DMA((seqs,)), DMA((seqs,)),
            DMA((line,)), DMA((line,)), DMA((seqs,)), DMA((seqs,)), DMA((2, seqs)), DMA((2, seqs)), DMA((5,)),
        ],
        compiler_params=pltpu.CompilerParams(
            collective_id=3, has_side_effects=True, vmem_limit_bytes=VMEM_LIMIT, dimension_semantics=("arbitrary",)
        ),
        name="last",
    )(
        flags, give, daddr, dval, dval, conv, conv, pre, normed, x_full, dgate, dstep, *whole
    )


def on_device(
    inputs,
    cotangent,
    lengths,
    placement,
    prenorm,
    gating,
    payload,
    address,
    stepping,
    kernels,
    offsets,
    filters,
    shifts,
    stepbias,
    decays,
    through,
    postnorm,
    readout,
):
    rows, width = inputs.shape
    heads = stepbias.shape[0]
    tiles = rows // BLOCK
    give_in, take_in, give_out, take_out, flags, vec = index(placement, lengths, stepbias, decays, through, tiles)
    x_full, w_all, r_t, work_x, work_g = spread(
        give_in, take_in, inputs, cotangent, gating, payload, address, stepping, readout
    )
    gain, post = prenorm[None, :], postnorm[None, :]
    normed, gate, pre, conv, act, raw, cum, part, local, msg, rim, g_part = front(
        flags, x_full, w_all, vec, gain, kernels, filters, offsets[None, :], shifts[None, :], work_g, heads
    )
    d_gate, dval, daddr, dstep, tiny, gpost, sums, out_got, gread_got, ggate_got = core(
        flags, msg, gate, part, act, cum, raw, local, g_part, normed, r_t, post, vec, heads
    )
    out_recv, grad_recv, dw_got, small_got = last(
        flags, give_out, daddr, dval, conv, pre, normed, x_full, d_gate, dstep, w_all, gain, kernels, filters, rim,
        out_got, work_x, work_g, sums, tiny, gpost
    )
    (
        out, dx, prenorm_g, gate_g, pay_g, addr_g, step_g, kernels_g, offsets_g, filters_g, shifts_g, stepbias_g,
        decays_g, through_g, post_g, read_g,
    ) = finish(take_out, out_recv, grad_recv, gread_got, ggate_got, dw_got, small_got, heads, lax.axis_size("head"))
    return (
        out.reshape(rows, width),
        dx.reshape(rows, width),
        prenorm_g.reshape(-1),
        gate_g,
        pay_g,
        addr_g,
        step_g.T,
        kernels_g,
        offsets_g.reshape(-1),
        filters_g,
        shifts_g.reshape(-1),
        stepbias_g.reshape(-1),
        decays_g.reshape(-1),
        through_g.reshape(-1),
        post_g.reshape(-1),
        read_g,
    )


def solution(mesh):
    in_specs = (
        P("seq", "head"),
        P("seq", "head"),
        P(),
        P(),
        P(),
        P("seq", "head"),
        P("seq", "head"),
        P("seq", None),
        P("seq", "head"),
        P(None, "head"),
        P("head"),
        P(),
        P(),
        P("head"),
        P("head"),
        P("head"),
        P("head"),
        P("head", "seq"),
    )
    out_specs = (
        P("seq", "head"),
        P("seq", "head"),
        P("head"),
        P("seq", "head"),
        P("seq", "head"),
        P("seq", "head"),
        P("seq", "head"),
        P(None, "head"),
        P("head"),
        P(None, "head"),
        P("head"),
        P("head"),
        P("head"),
        P("head"),
        P("head"),
        P("head", "seq"),
    )
    return jax.shard_map(
        on_device, mesh=mesh, in_specs=in_specs, out_specs=out_specs, check_vma=False
    )
```

time: 331 us -> 248 us (0.75)
  Pallas kernels: 302 us -> 246 us
  local copies, waits for them, and re-layouts: 22.8 us -> 1.54 us
  other arithmetic: 5.06 us -> 0 us
    pallas_call x5 -> x6, Pallas kernels: 302 us -> 246 us  [the longest x1 81.9 us: last(): pl.pallas_call(functools.partial(last_kernel, seqs, line, blocks), grid=(...]
    unnamed x52 -> x1, local copies, waits for them, and re-layouts: 21.5 us -> 1.54 us
where the time goes in v3:
time: 248 us
  Pallas kernels  246 us (99%)
    pallas_call x1, Pallas kernels, last(): pl.pallas_call(functools.partial(last_kernel, seqs, line, blocks), grid=(...  81.9 us
    pallas_call x1, Pallas kernels, core(): pl.pallas_call(functools.partial(core_kernel, seqs, line, heads, blocks),...  81.7 us
    pallas_call x1, Pallas kernels, spread(): pl.pallas_call(functools.partial(spread_kernel, seqs, heads, chunks), out...  53.2 us
    pallas_call x1, Pallas kernels, front(): pl.pallas_call(functools.partial(front_kernel, heads, line), grid=(blocks...  22.8 us

profile of v3, /device:TPU:1, one launch (start us, length us, event | category | flops | bytes accessed | tf_op | source)
XLA Modules:
  0.0 248.1 jit_solution(7395344276847366994)
XLA Ops:
  0.6 2.3 index.1
  2.9 53.2 %spread.1 = (bf16[1040,1024]{1,0:T(8,128)(2,1)}, bf16[1024,1408]{1,0:T(8,128)(2,1)}, bf16[1024,512]{1,0:T(8,128)(2,1)}, bf16[1040,256]{1,0:T(8,128)(2,1)}, bf16[1024,256]{1,0:T(8,128)(2,1)}) custom-call(s32[8]{0:T(128)} %get-tuple-element.72.give, s32[8]{0:T(128)} %get-tuple-element.73.take, bf16[8,128,256]{2,1,0:T(8,128)(2,1)} %bitcast.20, ...), custom_call_target="tpu_custom_call" | custom-call | tf_op jit(solution)/shard_map/spread/pallas_call | solution.py:452
  56.2 22.8 %front.1 = (bf16[1024,1024]{1,0:T(8,128)(2,1)}, f32[1024,512]{1,0:T(8,128)}, bf16[1024,768]{1,0:T(8,128)(2,1)}, f32[1024,768]{1,0:T(8,128)}, bf16[1024,768]{1,0:...) custom-call(f32[9]{0:T(128)} %get-tuple-element.70.flags, ...), custom_call_target="tpu_custom_call" | custom-call | tf_op jit(solution)/shard_map/front/pallas_call | solution.py:618
  79.0 81.7 %core.1 = (bf16[1024,512]{1,0:T(8,128)(2,1)}, f32[1024,512]{1,0:T(8,128)}, bf16[4,512,128]{2,1,0:T(8,128)(2,1)}, bf16[1024,128]{1,0:T(8,128)(2,1)}, f32[8,128]{1...) custom-call(f32[9]{0:T(128)} %get-tuple-element.70.flags, ...), custom_call_target="tpu_custom_call" | custom-call | tf_op jit(solution)/shard_map/core/pallas_call | solution.py:995
  160.8 81.9 %last.1 = (bf16[8,128,256]{2,1,0:T(8,128)(2,1)}, bf16[8,128,256]{2,1,0:T(8,128)(2,1)}, bf16[8,128,768]{2,1,0:T(8,128)(2,1)}, f32[8,8,640]{2,1,0:T(8,128)}) custom-call(f32[9]{0:T(128)} %get-tuple-element.70.flags, s32[8]{0:T(128)} %get-tuple-element.71.give, bf16[4,512,128]{2,1,0:T(8,128)(2,1)} %get-tuple-element.88.daddr, ...), custom_call_target="tpu_custom_call" | custom-call | tf_op jit(solution)/shard_map/last/pallas_call | solution.py:1355
  242.7 3.9 %finish.1 = (bf16[8,128,256]{2,1,0:T(8,128)(2,1)}, bf16[8,128,256]{2,1,0:T(8,128)(2,1)}, f32[1,256]{1,0:T(1,128)}, f32[128,512]{1,0:T(8,128)}, f32[128,512]{1,0:...) custom-call(s32[8]{0:T(128)} %get-tuple-element.69.take, ...), custom_call_target="tpu_custom_call" | custom-call | tf_op jit(solution)/shard_map/finish/pallas_call | solution.py:1323
  246.6 1.5 copy.34

commit v4 on v3

v4 whole, which is shorter than its diff:
```python
import functools

import jax
import jax.numpy as jnp
from jax import lax
from jax.experimental import pallas as pl
from jax.experimental.pallas import tpu as pltpu
from jax.sharding import PartitionSpec as P

D = 1024
GROUP = 256
BLOCK = 128
INNER = 2048
HDIM = 64
STATE = 128
TAPS = 4
HALO = 16
EDGE = 8
LANES = 128
EPS = 1e-05
MESH = pl.DeviceIdType.MESH
VMEM = pltpu.MemorySpace.VMEM
SMEM = pltpu.MemorySpace.SMEM
DMA = pltpu.SemaphoreType.DMA
VMEM_LIMIT = 63 << 20
LOW = jnp.bfloat16
WIDE = jnp.float32


def shape(dims, kind):
    return jax.ShapeDtypeStruct(dims, kind)


def nn(a, b):
    return jnp.dot(a, b, preferred_element_type=WIDE)


def nt(a, b):
    return lax.dot_general(a, b, (((1,), (1,)), ((), ())), preferred_element_type=WIDE)


def tn(a, b):
    return lax.dot_general(a, b, (((0,), (0,)), ((), ())), preferred_element_type=WIDE)


def halves(x):
    high = x.astype(LOW)
    return high, (x - high.astype(WIDE)).astype(LOW)


def thirds(x):
    high = x.astype(LOW)
    rest = x - high.astype(WIDE)
    middle = rest.astype(LOW)
    return high, middle, (rest - middle.astype(WIDE)).astype(LOW)


def head_rows(inner):
    row = lax.broadcasted_iota(jnp.int32, (LANES, inner), 0)
    column = lax.broadcasted_iota(jnp.int32, (LANES, inner), 1)
    return jnp.where(column // HDIM == row, 1.0, 0.0).astype(LOW)


def head_columns(inner):
    row = lax.broadcasted_iota(jnp.int32, (inner, LANES), 0)
    column = lax.broadcasted_iota(jnp.int32, (inner, LANES), 1)
    return jnp.where(row // HDIM == column, 1.0, 0.0).astype(LOW)


def to_columns(x, spread):
    high, rest = halves(x)
    return nn(high, spread) + nn(rest, spread)


def to_heads(x, collect):
    high, rest = halves(x)
    return nn(high, collect) + nn(rest, collect)


def ones_before(count):
    row = lax.broadcasted_iota(jnp.int32, (count, count), 0)
    column = lax.broadcasted_iota(jnp.int32, (count, count), 1)
    return row >= column


def sum_before(x):
    matrix = jnp.where(ones_before(x.shape[0]), 1.0, 0.0).astype(LOW)
    high, middle, low = thirds(x)
    return nn(matrix, high) + (nn(matrix, middle) + nn(matrix, low))


def sum_after(x):
    count = x.shape[0]
    row = lax.broadcasted_iota(jnp.int32, (count, count), 0)
    column = lax.broadcasted_iota(jnp.int32, (count, count), 1)
    matrix = jnp.where(row <= column, 1.0, 0.0).astype(LOW)
    high, middle, low = thirds(x)
    return nn(matrix, high) + (nn(matrix, middle) + nn(matrix, low))


def sigmoid(x):
    return 0.5 * jnp.tanh(0.5 * x) + 0.5


def step_terms(raw, heads):
    z = jnp.exp(-jnp.abs(raw))
    series = 1.0 - z * (0.5 - z * (1.0 / 3.0 - z * (0.25 - z * 0.2)))
    small = z < 0.03
    log1p = jnp.where(small, z * series, jnp.log(1.0 + z))
    soft = jnp.maximum(raw, 0.0) + log1p
    one = 1.0 / (1.0 + z)
    sig = jnp.where(raw >= 0, one, z * one)
    ratio = jnp.where(small & (raw < 0), one / series, sig / jnp.maximum(soft, 1e-20))
    lane = lax.broadcasted_iota(jnp.int32, raw.shape, 1)
    return jnp.where(lane < heads, soft, 0.0), sig, ratio


def greet(seq_peers, head_peers):
    barrier = pltpu.get_barrier_semaphore()
    count = 0
    if seq_peers > 1:
        me = lax.axis_index("seq")

        @pl.loop(1, seq_peers)
        def _(i):
            pl.semaphore_signal(
                barrier, inc=1, device_id={"seq": lax.rem(me + i, seq_peers)}, device_id_type=MESH
            )

        count += seq_peers - 1
    if head_peers > 1:
        mine = lax.axis_index("head")

        @pl.loop(1, head_peers)
        def _(i):
            pl.semaphore_signal(
                barrier, inc=1, device_id={"head": lax.rem(mine + i, head_peers)}, device_id_type=MESH
            )

        count += head_peers - 1
    pl.semaphore_wait(barrier, count)


def remote(src, dst, send_sem, recv_sem, where):
    return pltpu.make_async_remote_copy(
        src_ref=src, dst_ref=dst, send_sem=send_sem, recv_sem=recv_sem, device_id=where, device_id_type=MESH
    )


class Line:
    def __init__(self, count, out, width, send, recv):
        self.count, self.out, self.width, self.send, self.recv = count, out, width, send, recv
        self.me = lax.axis_index("head")

    def view(self, shard):
        return self.out.at[:, pl.ds(pl.multiple_of(shard * self.width, LANES), self.width)]

    def copy(self, src, shard, way, step):
        return remote(
            src, self.view(shard), self.send.at[way, step], self.recv.at[shard], {"head": self.me + (1 - 2 * way)}
        )

    def first(self, own):
        self.pass_on(own, self.me, 0, 0)
        self.pass_on(own, self.me, 1, 0)

    def pass_on(self, src, shard, way, step):
        reach = (self.me < self.count - 1) if way == 0 else (self.me > 0)

        @pl.when(reach)
        def _():
            self.copy(src, shard, way, step).start()

    def hop(self, step, take=True, give=True, source=None):
        for way in (0, 1):
            shard = self.me - step if way == 0 else self.me + step
            there = (shard >= 0) if way == 0 else (shard < self.count)

            @pl.when(there)
            def _():
                if take:
                    self.copy(self.view(shard), shard, way, step).wait_recv()
                if give and step < self.count - 1:
                    self.pass_on(self.view(shard) if source is None else source(shard), shard, way, step)

    def finish(self, own, steps=None):
        for way in (0, 1):
            reach = (self.me < self.count - 1) if way == 0 else (self.me > 0)
            for step in range(self.count - 1) if steps is None else steps:
                shard = self.me - step if way == 0 else self.me + step
                there = (shard >= 0) if way == 0 else (shard < self.count)

                @pl.when(reach & there)
                def _():
                    src = own if step == 0 else self.view(shard)
                    self.copy(src, shard, way, step).wait_send()


class Plane:
    def __init__(self, seqs, view, sent, got, passed, way=0):
        self.chips, self.view, self.sent, self.got, self.passed, self.way = seqs // 2, view, sent, got, passed, way
        self.me = lax.axis_index("seq")
        self.core = lax.rem(self.me, 2)
        self.chip = self.me // 2
        self.mate = self.me + 1 - 2 * self.core

    def forward(self, chip):
        return (chip > self.chip) if self.way == 1 else (chip < self.chip) if self.way == -1 else (chip >= 0)

    def backward(self, chip):
        return (chip < self.chip) if self.way == 1 else (chip > self.chip) if self.way == -1 else (chip >= 0)

    def each_chip(self, body):
        @pl.loop(1, self.chips)
        def _(i):
            body(lax.rem(self.chip + i, self.chips))

    def copy(self, src, source, to, sem):
        return remote(src, self.view(source), sem, self.got.at[source], {"seq": to})

    def start(self, own):
        def send(chip):
            to = 2 * chip + self.core

            @pl.when(self.forward(chip))
            def _():
                self.copy(own, self.me, to, self.sent.at[to]).start()

        self.each_chip(send)
        self.copy(own, self.me, self.mate, self.sent.at[self.mate]).start()

    def relay(self):
        def take(chip):
            source = 2 * chip + self.core

            @pl.when(self.backward(chip))
            def _():
                landed = self.view(source)
                self.copy(landed, source, self.mate, self.passed.at[source]).wait_recv()
                self.copy(landed, source, self.mate, self.passed.at[source]).start()

        self.each_chip(take)

    def finish(self, own):
        def take(chip):
            source = 2 * chip + 1 - self.core

            @pl.when(self.backward(chip))
            def _():
                self.copy(self.view(source), source, self.mate, self.passed.at[source]).wait_recv()

        self.each_chip(take)
        self.copy(self.view(self.mate), self.mate, self.mate, self.sent.at[self.mate]).wait_recv()
        self.copy(own, self.me, self.mate, self.sent.at[self.mate]).wait_send()

        def drain(chip):
            same = 2 * chip + self.core

            @pl.when(self.forward(chip))
            def _():
                self.copy(own, self.me, same, self.sent.at[same]).wait_send()

            @pl.when(self.backward(chip))
            def _():
                self.copy(self.view(same), same, self.mate, self.passed.at[same]).wait_send()

        self.each_chip(drain)


ANY_SPEC = pl.BlockSpec(memory_space=pl.ANY)
VMEM_SPEC = pl.BlockSpec(memory_space=VMEM)
SMEM_SPEC = pl.BlockSpec(memory_space=SMEM)


def index_kernel(
    seqs, tiles, place, lengths, stepbias, decays, through, give_in, take_in, give_out, take_out, flags, vec
):
    me = lax.axis_index("seq")

    @pl.loop(0, seqs * tiles)
    def _(j):
        block = place[j]

        @pl.when(lax.div(block, tiles) == me)
        def _():
            to = lax.div(j, tiles)
            give_in[to] = lax.rem(block, tiles)
            take_out[lax.rem(block, tiles)] = to

    @pl.loop(0, tiles)
    def _(k):
        source = lax.div(place[me * tiles + k], tiles)
        take_in[k] = source
        give_out[source] = k

    @pl.loop(0, tiles + 1)
    def _(k):
        position = (me * tiles + k) * BLOCK
        end = jnp.int32(0)
        border = position == 0
        for n in range(lengths.shape[0]):
            end = end + lengths[n]
            border = border | (position == end)
        flags[k] = jnp.where(border, 0.0, 1.0)

    heads = stepbias.shape[1]
    vec[...] = jnp.zeros_like(vec)
    vec[0:1, :heads] = stepbias[...]
    vec[1:2, :heads] = decays[...]
    vec[2:3, :heads] = through[...]


def index(place, lengths, stepbias, decays, through, tiles):
    seqs = lax.axis_size("seq")
    whole = jnp.int32
    return pl.pallas_call(
        functools.partial(index_kernel, seqs, tiles),
        out_shape=(
            shape((seqs,), whole), shape((tiles,), whole), shape((seqs,), whole), shape((tiles,), whole),
            shape((tiles + 1,), WIDE), shape((EDGE, LANES), WIDE),
        ),
        in_specs=[SMEM_SPEC] * 2 + [VMEM_SPEC] * 3,
        out_specs=(SMEM_SPEC,) * 5 + (VMEM_SPEC,),
        compiler_params=pltpu.CompilerParams(vmem_limit_bytes=VMEM_LIMIT),
        name="index",
    )(place, lengths, stepbias[None, :], decays[None, :], through[None, :])


def blockwise(dims, index):
    return pl.BlockSpec(dims, index)


def fixed(dims):
    return pl.BlockSpec(dims, lambda i: (0,) * len(dims), pipeline_mode=pl.Buffered(1))


def carry_columns(carry_row_t, collect):
    high, middle, low = thirds(jnp.broadcast_to(carry_row_t, (LANES, LANES)))
    return nn(collect, high) + (nn(collect, middle) + nn(collect, low))


def pair_lanes(slab):
    lane = lax.broadcasted_iota(jnp.int32, slab.shape, 1)
    zero = jnp.zeros_like(slab)
    return jnp.where(lane < HDIM, slab, zero), jnp.where(lane >= HDIM, slab, zero)


def fold_states(slots, collect, inner, first, last, step, start):
    def hop(n, state):
        message = slots[first + n * step]
        carry = nn(collect[:, :HALO], message[inner:])
        return carry * state + message[:inner].astype(WIDE)

    return lax.fori_loop(0, (last - first) * step, hop, start)


def front_kernel(
    seqs, line, heads, blocks, chunks, give, take, flags,
    x_in, g_in, gating_in, payload_in, address_in, stepping_in, readout_in,
    vec, prenorm, kernels, filters, offsets, shifts,
    u_o, normed_o, gate_o, pre_o, conv_o, act_o, raw_o, cum_o, part_o, local_o, state_o, rim_o, g_o, w_o, r_o,
    x, g, gating, payload, address, stepping, readout, square,
    send_x, send_g, recv_x, recv_g, work_x, work_g, w_own, r_own, u, w, msg, slots,
    ext, prev, state, prod,
    sent, got, w_sent, w_got, w_passed, r_sent, r_got, r_passed, s_sent, s_got, s_passed, rim_sent, rim_got, own_sem,
    load_sem, line_sent, line_got, g_sent, g_got,
):
    i = pl.program_id(0)
    me, mine = lax.axis_index("seq"), lax.axis_index("head")
    tiles, _, width = x.shape
    rows = tiles * BLOCK
    depth, inner = gating.shape
    wide = pre_o.shape[1]
    part = rows // chunks
    per = blocks // chunks

    def rows_of(device):
        return pl.ds(pl.multiple_of(device * depth, depth), depth)

    def piece(n):
        if isinstance(n, int):
            return pl.ds(rows, HALO) if n == chunks else pl.ds(n * part, part)
        return pl.ds(pl.multiple_of(n * part, part), part)

    def u_line(n):
        return Line(line, u.at[piece(n)], width, line_sent.at[n], line_got.at[n])

    def own_columns(ref):
        return ref.at[:, pl.ds(pl.multiple_of(mine * width, LANES), width)]

    w_plane = Plane(seqs, lambda s: w.at[rows_of(s)], w_sent, w_got, w_passed)
    r_plane = Plane(seqs, lambda s: r_o.at[rows_of(s)], r_sent, r_got, r_passed)
    s_plane = Plane(seqs, lambda s: slots.at[s], s_sent, s_got, s_passed, way=1)
    g_line = Line(line, g_o, width, g_sent, g_got)
    own_r = pltpu.make_async_copy(r_own, r_o.at[rows_of(me)], own_sem.at[0])
    own_g = pltpu.make_async_copy(work_g, g_line.view(mine), own_sem.at[1])
    save_w = pltpu.make_async_copy(w, w_o, own_sem.at[2])

    def arrange(which, received, work):
        @pl.loop(1, seqs)
        def _(n):
            source = lax.rem(me + n, seqs)
            remote(
                received.at[source], received.at[source], sent.at[which, source], got.at[which, source], {"seq": source}
            ).wait_recv()

        for k in range(tiles):
            work[pl.ds(k * BLOCK, BLOCK), :] = received[take[k]]

    @pl.when(i == 0)
    def _():
        pairs = (
            (x_in, x), (g_in, g), (gating_in, gating), (payload_in, payload), (address_in, address),
            (stepping_in, stepping), (readout_in, readout),
        )
        loads = [pltpu.make_async_copy(src, dst, load_sem.at[n]) for n, (src, dst) in enumerate(pairs)]
        for load in loads:
            load.start()
        greet(seqs, line)

        def post(which, source, outgoing, incoming):
            @pl.loop(1, seqs)
            def _(n):
                to = lax.rem(me + n, seqs)
                outgoing[to] = source[give[to]]
                remote(outgoing.at[to], incoming.at[me], sent.at[which, to], got.at[which, me], {"seq": to}).start()

            incoming[me] = source[give[me]]

        loads[0].wait()
        post(0, x, send_x, recv_x)
        for load in loads[1:]:
            load.wait()

        w_own[:, :inner] = gating[...].astype(LOW)
        w_own[:, inner : 2 * inner] = payload[...].astype(LOW)
        state2 = address.shape[1]
        w_own[:, 2 * inner : 2 * inner + state2] = address[...].astype(LOW)
        square[...] = jnp.zeros_like(square)
        square[: stepping.shape[0], :depth] = stepping[...]
        w_own[:, 2 * inner + state2 :] = square[...].T[:depth].astype(LOW)
        r_own[...] = readout[...].T.astype(LOW)
        w[rows_of(me), :] = w_own[...]
        own_r.start()

        arrange(0, recv_x, work_x)
        after = lax.rem(me + 1, seqs)
        rim = remote(
            work_x.at[pl.ds(rows - HALO, HALO)], work_x.at[pl.ds(rows, HALO)], rim_sent, rim_got, {"seq": after}
        )
        rim.start()
        for n in range(chunks):
            u_line(n).first(work_x.at[piece(n)])
        w_plane.start(w_own)
        rim.wait()
        u_line(chunks).first(work_x.at[piece(chunks)])
        own = pltpu.make_async_copy(work_x, own_columns(u), own_sem.at[3])
        own.start()
        post(1, g, send_g, recv_g)
        r_plane.start(r_own)
        for step in range(1, line - 1):
            for n in range(chunks + 1):
                u_line(n).hop(step)
            if step == 1:
                w_plane.relay()
        if line > 1:
            u_line(chunks).hop(line - 1)
        own.wait()
        w_plane.finish(w_own)
        save_w.start()

    if line > 1:

        @pl.when(lax.rem(i, per) == 0)
        def _():
            u_line(lax.div(i, per)).hop(line - 1)

    @pl.when(i == blocks - 1)
    def _():
        arrange(1, recv_g, work_g)
        g_line.first(work_g)
        own_g.start()

    taps = jnp.concatenate([kernels[...], filters[...]], axis=1)
    bias = jnp.concatenate([offsets[...], shifts[...]], axis=1)
    spread_m, collect = head_rows(inner), head_columns(inner)

    def normalize(block):
        wide_rows = block.astype(WIDE)
        scale = lax.rsqrt(jnp.mean(wide_rows * wide_rows, axis=1, keepdims=True) + EPS)
        return (wide_rows * scale * prenorm[...]).astype(LOW)

    @pl.when(i == 0)
    def _():
        before = nn(normalize(u[pl.ds(rows, HALO), :]), w[:, inner : inner + wide]).astype(LOW).astype(WIDE)
        prev[...] = before[HALO - EDGE :]
        rim_o[...] = before[HALO - EDGE :]
        state[...] = jnp.zeros_like(state)
        prod[...] = jnp.ones_like(prod)

    u_v = u[pl.ds(pl.multiple_of(i * GROUP, GROUP), GROUP), :]
    u_o[...] = u_v
    normed = normalize(u_v)
    normed_o[...] = normed
    gate_o[...] = nn(normed, w[:, :inner])
    pre = nn(normed, w[:, inner : inner + wide]).astype(LOW)
    pre_o[...] = pre
    lane = lax.broadcasted_iota(jnp.int32, (GROUP, LANES), 1)
    raw = jnp.where(lane < heads, nn(normed, w[:, inner + wide :]) + vec[0:1, :], 0.0)
    raw_o[...] = raw
    first, second = flags[2 * i], flags[2 * i + 1]
    same = (first, second)
    for half in range(2):
        at = pl.ds(half * BLOCK, BLOCK)
        ext[0:EDGE, :] = prev[...] * same[half]
        ext[EDGE:, :] = pre[half * BLOCK : (half + 1) * BLOCK].astype(WIDE)
        prev[...] = ext[BLOCK:, :]
        total = bias + taps[TAPS - 1 : TAPS] * ext[EDGE:, :]
        for tap in range(TAPS - 1):
            total = total + taps[tap : tap + 1] * ext[pl.ds(EDGE - (TAPS - 1) + tap, BLOCK), :]
        conv_o[at, :] = total
        act_o[at, :] = (total * sigmoid(total)).astype(LOW)

    steps, _, _ = step_terms(raw, heads)
    scale = -jnp.exp(vec[1:2, :])
    cum = sum_before(steps * scale)
    cum_o[...] = cum
    cum_t, steps_t = cum.T, steps.T
    write = act_o[:, inner : inner + STATE]
    read = act_o[:, inner + STATE :]
    lower = ones_before(BLOCK)
    top, low = slice(0, BLOCK), slice(BLOCK, GROUP)
    s00 = jnp.where(lower, nt(read[top], write[top]), 0.0)
    s10 = nt(read[low], write[top]) * second
    s11 = jnp.where(lower, nt(read[low], write[low]), 0.0)

    def mix(scores, head, t, s):
        decay = jnp.exp(jnp.minimum(cum[t, head : head + 1] - cum_t[head : head + 1, s], 0.0))
        return (scores * (decay * steps_t[head : head + 1, s])).astype(LOW)

    last = cum[GROUP - 1 : GROUP, :]
    row = lax.broadcasted_iota(jnp.int32, (GROUP, LANES), 0)
    weight = steps * jnp.exp(last - cum) * jnp.where(row < BLOCK, second, 1.0)
    weight_w = to_columns(weight, spread_m)
    skip = to_columns(jnp.broadcast_to(vec[2:3, :], (EDGE, LANES)), spread_m)[0:1]
    packed = []
    for pair in range(inner // LANES):
        columns = slice(pair * LANES, (pair + 1) * LANES)
        slab = act_o[:, columns]
        slab_f = slab.astype(WIDE)
        ones = pair_lanes(slab)
        h0, h1 = 2 * pair, 2 * pair + 1
        y0 = nn(
            jnp.concatenate([mix(s00, h0, top, top), mix(s00, h1, top, top)], axis=1),
            jnp.concatenate([ones[0][top], ones[1][top]], axis=0),
        )
        y1 = nn(
            jnp.concatenate(
                [mix(s10, h0, low, top), mix(s11, h0, low, low), mix(s10, h1, low, top), mix(s11, h1, low, low)], axis=1
            ),
            jnp.concatenate([ones[0], ones[1]], axis=0),
        )
        part_o[top, columns] = y0 + skip[:, columns] * slab_f[top]
        part_o[low, columns] = y1 + skip[:, columns] * slab_f[low]
        packed.append((slab_f * weight_w[:, columns]).astype(LOW))
    local = tn(jnp.concatenate(packed, axis=1), write)
    local_o[0] = local
    carry = jnp.exp(cum_t[:, GROUP - 1 : GROUP]) * (first * second)
    state[...] = carry_columns(carry, collect) * state[...] + local
    prod[...] = jnp.broadcast_to(carry[:HALO], (HALO, STATE)) * prod[...]

    @pl.when(i == blocks - 1)
    def _():
        msg[:inner, :] = state[...].astype(LOW)
        msg[inner:, :] = prod[...].astype(LOW)
        s_plane.start(msg)
        s_plane.relay()
        s_plane.finish(msg)
        state_o[...] = fold_states(slots, collect, inner, 0, me, 1, jnp.zeros((inner, STATE), WIDE))
        r_plane.relay()
        r_plane.finish(r_own)
        if line > 1:
            g_line.hop(1, give=False)
        g_line.finish(work_g, (0,))
        for n in range(chunks + 1):
            u_line(n).finish(work_x.at[piece(n)])

        @pl.loop(1, seqs)
        def _(n):
            other = lax.rem(me + n, seqs)
            for which, buffer in ((0, send_x), (1, send_g)):
                remote(
                    buffer.at[other], buffer.at[other], sent.at[which, other], got.at[which, other], {"seq": other}
                ).wait_send()

        own_r.wait()
        own_g.wait()
        save_w.wait()


def front(give, take, flags, x, g, gating, payload, address, stepping, readout, vec, prenorm, kernels, filters, offsets, shifts):
    seqs, line = lax.axis_size("seq"), lax.axis_size("head")
    rows, width = x.shape
    depth, inner = gating.shape
    total = depth * seqs
    wide = inner + address.shape[1]
    columns = inner + wide + LANES
    blocks = rows // GROUP
    chunks = min(blocks, 4)
    heads = stepping.shape[1]
    routed = (seqs, BLOCK, width)
    given = (rows // BLOCK, BLOCK, width)
    message = (inner + HALO, STATE)
    operands = (x.reshape(given), g.reshape(given), gating, payload, address, stepping.T, readout)
    small = (vec, prenorm, kernels, filters, offsets, shifts)

    def by_rows(size):
        return blockwise((GROUP, size), lambda i: (i, 0))

    return pl.pallas_call(
        functools.partial(front_kernel, seqs, line, heads, blocks, chunks),
        grid=(blocks,),
        out_shape=(
            shape((rows, total), LOW), shape((rows, total), LOW), shape((rows, inner), WIDE), shape((rows, wide), LOW),
            shape((rows, wide), WIDE), shape((rows, wide), LOW), shape((rows, LANES), WIDE), shape((rows, LANES), WIDE),
            shape((rows, inner), WIDE), shape((blocks, inner, STATE), WIDE), shape((inner, STATE), WIDE),
            shape((EDGE, wide), WIDE), shape((rows, total), LOW), shape((total, columns), LOW),
            shape((total, inner), LOW),
        ),
        in_specs=[SMEM_SPEC] * 3 + [ANY_SPEC] * 7 + [fixed(a.shape) for a in small],
        out_specs=(
            by_rows(total), by_rows(total), by_rows(inner), by_rows(wide), by_rows(wide), by_rows(wide), by_rows(LANES),
            by_rows(LANES), by_rows(inner), blockwise((1, inner, STATE), lambda i: (i, 0, 0)), fixed((inner, STATE)),
            fixed((EDGE, wide)), ANY_SPEC, ANY_SPEC, ANY_SPEC,
        ),
        scratch_shapes=[pltpu.VMEM(a.shape, a.dtype) for a in operands] + [
            pltpu.VMEM((LANES, LANES), WIDE),
            pltpu.VMEM(routed, LOW), pltpu.VMEM(routed, LOW), pltpu.VMEM(routed, LOW), pltpu.VMEM(routed, LOW),
            pltpu.VMEM((rows + HALO, width), LOW), pltpu.VMEM((rows, width), LOW),
            pltpu.VMEM((depth, columns), LOW), pltpu.VMEM((depth, inner), LOW),
            pltpu.VMEM((rows + HALO, total), LOW), pltpu.VMEM((total, columns), LOW),
            pltpu.VMEM(message, LOW), pltpu.VMEM((seqs,) + message, LOW),
            pltpu.VMEM((EDGE + BLOCK, wide), WIDE), pltpu.VMEM((EDGE, wide), WIDE),
            pltpu.VMEM((inner, STATE), WIDE), pltpu.VMEM((HALO, STATE), WIDE),
            DMA((2, seqs)), DMA((2, seqs)),
            DMA((seqs,)), DMA((seqs,)), DMA((seqs,)), DMA((seqs,)), DMA((seqs,)), DMA((seqs,)),
            DMA((seqs,)), DMA((seqs,)), DMA((seqs,)), DMA, DMA, DMA((4,)), DMA((7,)),
            DMA((chunks + 1, 2, line)), DMA((chunks + 1, line)), DMA((2, line)), DMA((line,)),
        ],
        compiler_params=pltpu.CompilerParams(
            collective_id=0, has_side_effects=True, vmem_limit_bytes=VMEM_LIMIT, dimension_semantics=("arbitrary",)
        ),
        name="front",
    )(give, take, flags, *operands, *small)


def conv_grad(d_act, conv):
    sig = sigmoid(conv)
    return d_act * (sig * (1.0 + conv * (1.0 - sig)))


def core_kernel(
    seqs, line, heads, blocks, flags, give,
    gate, part, read, act, cum, raw, local, conv, pre, pre_before, normed, u, g_part,
    state_in, r_t, w, postnorm, vec, prenorm, kernels, filters, rim,
    out_recv, grad_recv, out_got, dx_got, gread_got, ggate_got, dw_got, addr_got, small_got,
    ssd_s, din_s, dssd_s, dgate_s, starts, q, state, prod, g_buf, g_own, out_part, back_slots, back_msg, sums,
    totals, gread, ggate, gread_low, ggate_low, gpost, tiny, d_conv, d_step, after, edge_own, edge_got, ext,
    taps_g, bias_g, dw, dw_low, da_low, da_got, da_send, pn, zs_send, zs_got, small, result, fin_send,
    back_sent, back_sem, back_passed, sum_sent, sum_sem, line_sent, line_sem, load_sem, out_sent, out_sem,
    w_sent, w_sem, dx_sent, dx_sem, edge_sent, edge_sem, zs_sent, zs_sem, da_sent, da_sem, small_sent, small_sem,
    fin_sent, fin_sem, own_sem,
):
    i = pl.program_id(0)
    me, mine = lax.axis_index("seq"), lax.axis_index("head")
    inner = gate.shape[1]
    wide = act.shape[1]
    width = out_part.shape[2]
    depth = gread_got.shape[1]
    size = 2 * STATE // line
    phase = jnp.minimum(lax.div(i, blocks), 3)
    turn = i - 3 * blocks
    block = jnp.where(phase == 3, jnp.maximum(blocks - 1 - turn, 0), lax.rem(i, blocks))
    first, second = flags[2 * block], flags[2 * block + 1]
    g_line = Line(line, g_buf, width, line_sent, line_sem)
    back_plane = Plane(seqs, lambda s: back_slots.at[s], back_sent, back_sem, back_passed, way=-1)

    def group_rows(b):
        return pl.ds(pl.multiple_of(b * GROUP, GROUP), GROUP)

    here = group_rows(block)

    def rows_of(device):
        return pl.ds(pl.multiple_of(device * depth, depth), depth)

    def shard_of(ref, shard):
        return ref.at[:, pl.ds(pl.multiple_of(shard * width, LANES), width)]

    def all_line(body):
        if line > 1:

            @pl.loop(1, line)
            def _(n):
                body(lax.rem(mine + n, line))

    def all_seq(body):
        @pl.loop(1, seqs)
        def _(n):
            body(lax.rem(me + n, seqs))

    def each_load(body):
        def load(shard, n):
            return pltpu.make_async_copy(shard_of(g_part, shard), shard_of(g_buf, shard), load_sem.at[n])

        body(load(mine, 0))
        body(pltpu.make_async_copy(shard_of(g_part, mine), g_own, load_sem.at[3]))
        if line > 1:
            pl.when(mine > 0)(lambda: body(load(mine - 1, 1)))
            pl.when(mine < line - 1)(lambda: body(load(mine + 1, 2)))

    def sum_copy(to, slot):
        return remote(sums.at[mine], sums.at[slot], sum_sent.at[to], sum_sem.at[slot], {"head": to})

    def out_copy(to, slot):
        return remote(out_part.at[to], out_got.at[slot], out_sent.at[to], out_sem.at[slot], {"head": to})

    weights = ((gread_low, gread_got), (ggate_low, ggate_got), (dw_low, dw_got), (da_low, da_got))

    def w_copy(which, to, slot):
        src, dst = weights[which]
        return remote(src.at[rows_of(to)], dst.at[slot], w_sent.at[which, to], w_sem.at[which, slot], {"seq": to})

    def w_start(which):
        all_seq(lambda to: w_copy(which, to, me).start())

    def w_wait(which):
        all_seq(lambda other: w_copy(which, other, other).wait())

    def dx_copy(to, slot, b):
        return remote(
            shard_of(g_buf.at[group_rows(b)], to), dx_got.at[slot, group_rows(b)], dx_sent.at[to, b],
            dx_sem.at[slot, b], {"head": to},
        )

    def edge_copy(to):
        return remote(edge_own, edge_got, edge_sent, edge_sem, {"seq": to})

    def zs_copy(to, slot):
        return remote(zs_send.at[to], zs_got.at[slot], zs_sent.at[to], zs_sem.at[slot], {"head": to})

    def da_copy(to, slot):
        return remote(da_send.at[to], addr_got.at[slot], da_sent.at[to], da_sem.at[slot], {"head": to})

    def small_copy(to, slot):
        return remote(small, small_got.at[slot], small_sent.at[to], small_sem.at[slot], {"seq": to})

    arrivals = (out_recv, grad_recv)

    def fin_copy(which, to, slot):
        return remote(
            fin_send.at[which, to], arrivals[which].at[slot], fin_sent.at[which, to], fin_sem.at[which, slot],
            {"seq": to},
        )

    own_copies = {
        "out": pltpu.make_async_copy(out_part.at[mine], out_got.at[mine], own_sem.at[0]),
        "gread": pltpu.make_async_copy(gread_low.at[rows_of(me)], gread_got.at[me], own_sem.at[1]),
        "ggate": pltpu.make_async_copy(ggate_low.at[rows_of(me)], ggate_got.at[me], own_sem.at[2]),
        "dw": pltpu.make_async_copy(dw_low.at[rows_of(me)], dw_got.at[me], own_sem.at[3]),
        "dx": pltpu.make_async_copy(shard_of(g_buf, mine), dx_got.at[mine], own_sem.at[4]),
        "addr": pltpu.make_async_copy(da_send.at[mine], addr_got.at[mine], own_sem.at[5]),
        "small": pltpu.make_async_copy(small, small_got.at[me], own_sem.at[6]),
        "fin0": pltpu.make_async_copy(fin_send.at[0, me], out_recv.at[me], own_sem.at[7]),
        "fin1": pltpu.make_async_copy(fin_send.at[1, me], grad_recv.at[me], own_sem.at[8]),
    }

    def route(which):
        def send(to):
            fin_send[which, to] = result[which, give[to]]
            fin_copy(which, to, me).start()

        all_seq(send)
        fin_send[which, me] = result[which, give[me]]
        own_copies["fin%d" % which].start()

    row = lax.broadcasted_iota(jnp.int32, (GROUP, LANES), 0)
    lane = lax.broadcasted_iota(jnp.int32, (GROUP, LANES), 1)

    def entry_of(cum_v, spread_m):
        return to_columns(jnp.exp(cum_v) * (first * jnp.where(row < BLOCK, 1.0, second)), spread_m)

    def row_stats(b):
        stats = jnp.concatenate([totals[b], jnp.zeros((LANES - EDGE, GROUP), WIDE)], axis=0).T
        return lax.rsqrt(stats[:, 0:1] / INNER + EPS), stats[:, 1:2]

    def gated_of(ssd):
        gate_v = gate[...]
        return ssd * (gate_v * sigmoid(gate_v))

    @pl.when(i == 0)
    def _():
        greet(seqs, line)
        g_line.hop(1, take=False, source=lambda shard: shard_of(g_part, shard))
        each_load(lambda copy: copy.start())
        state[...] = state_in[...]

    @pl.when(phase == 0)
    def _():
        spread_m, collect = head_rows(inner), head_columns(inner)
        cum_v = cum[...]
        carry = jnp.exp(cum_v.T[:, GROUP - 1 : GROUP]) * (first * second)
        start = state[...]
        starts[block] = start
        ssd = part[...] + entry_of(cum_v, spread_m) * nt(read[...], start.astype(LOW))
        ssd_s[here, :] = ssd
        state[...] = carry_columns(carry, collect) * start + local[0]
        out = nt((gated_of(ssd) * postnorm[...]).astype(LOW), r_t[...])
        for z in range(line):
            out_part[z, here] = out[:, z * width : (z + 1) * width].astype(LOW)

    @pl.when(i == blocks - 1)
    def _():
        for step in range(2, line):
            g_line.hop(step)
        each_load(lambda copy: copy.wait())
        g_line.finish(None, range(1, line - 1))

    @pl.when(phase == 1)
    def _():
        gated = gated_of(ssd_s[here, :])
        d_inner = nn(g_buf[here, :], r_t[...])
        din_s[here, :] = d_inner
        squares = jnp.sum(gated * gated, axis=1, keepdims=True)
        dots = jnp.sum(gated * postnorm[...] * d_inner, axis=1, keepdims=True)
        both = jnp.where(lane == 0, squares, jnp.where(lane == 1, dots, 0.0)).T
        sums[mine, block] = both[:EDGE]

    @pl.when(i == 2 * blocks - 1)
    def _():
        all_line(lambda to: sum_copy(to, mine).start())
        gread[...] = jnp.zeros_like(gread)
        ggate[...] = jnp.zeros_like(ggate)
        gpost[...] = jnp.zeros_like(gpost)
        state[...] = jnp.zeros_like(state)
        prod[...] = jnp.ones_like(prod)
        all_line(lambda other: sum_copy(other, other).wait())
        totals[...] = jnp.sum(sums[...], axis=0)
        all_line(lambda to: out_copy(to, mine).start())
        own_copies["out"].start()

    @pl.when(phase == 2)
    def _():
        spread_m, collect = head_rows(inner), head_columns(inner)
        cum_v = cum[...]
        carry = jnp.exp(cum_v.T[:, GROUP - 1 : GROUP]) * (first * second)
        inv, dot = row_stats(block)
        gate_v = gate[...]
        sig = sigmoid(gate_v)
        ssd = ssd_s[here, :]
        d_inner = din_s[here, :]
        gated = ssd * (gate_v * sig)
        gated_inv = gated * inv
        inner_normed = (gated_inv * postnorm[...]).astype(LOW)
        d_gated = (inv * postnorm[...]) * d_inner - gated * (inv * inv * inv / INNER * dot)
        gpost[...] += jnp.sum(d_inner * gated_inv, axis=0, keepdims=True)
        d_ssd = (d_gated * (gate_v * sig)).astype(LOW)
        d_gate = (d_gated * ssd * sig * (1.0 + gate_v * (1.0 - sig))).astype(LOW)
        dssd_s[here, :] = d_ssd
        dgate_s[here, :] = d_gate
        gread[...] += tn(g_buf[here, :], inner_normed)
        ggate[...] += tn(normed[...], d_gate)
        query_grad = (d_ssd.astype(WIDE) * entry_of(cum_v, spread_m)).astype(LOW)
        found = tn(query_grad, read[...])
        q[block] = found
        state[...] += carry_columns(prod[...], collect) * found
        prod[...] = prod[...] * carry

    @pl.when(i == 3 * blocks - 1)
    def _():
        back_msg[:inner, :] = state[...].astype(LOW)
        back_msg[inner:, :] = jnp.broadcast_to(prod[:HALO], (HALO, STATE)).astype(LOW)
        back_plane.start(back_msg)
        gread_low[...] = gread[...].astype(LOW)
        ggate_low[...] = ggate[...].astype(LOW)
        for ref in (tiny, taps_g, bias_g, dw, pn):
            ref[...] = jnp.zeros_like(ref)
        back_plane.relay()
        back_plane.finish(back_msg)
        w_start(0)
        w_start(1)
        own_copies["gread"].start()
        own_copies["ggate"].start()
        state[...] = fold_states(
            back_slots, head_columns(inner), inner, seqs - 1, me, -1, jnp.zeros((inner, STATE), WIDE)
        )

    @pl.when((phase == 3) & (turn < blocks))
    def _():
        slot = jnp.where(turn == 0, 1, 0)
        spread_m, collect = head_rows(inner), head_columns(inner)
        lower_mask = ones_before(BLOCK)
        top, low = slice(0, BLOCK), slice(BLOCK, GROUP)
        cum_v = cum[...]
        cum_t = cum_v.T
        steps, sig, ratio = step_terms(raw[...], heads)
        steps_t = steps.T
        scale = -jnp.exp(vec[1:2, :])
        last = cum_v[GROUP - 1 : GROUP, :]
        write = act[:, inner : inner + STATE]
        read_v = act[:, inner + STATE :]
        s00 = jnp.where(lower_mask, nt(read_v[top], write[top]), 0.0)
        s10 = nt(read_v[low], write[top]) * second
        s11 = jnp.where(lower_mask, nt(read_v[low], write[low]), 0.0)

        end = state[...]
        end_low = end.astype(LOW)
        start = starts[block]
        carry = jnp.exp(cum_t[:, GROUP - 1 : GROUP]) * (first * second)
        state[...] = carry_columns(carry, collect) * end + q[block]
        weight = steps * jnp.exp(last - cum_v) * jnp.where(row < BLOCK, second, 1.0)
        weight_w = to_columns(weight, spread_m)
        d_ssd = dssd_s[here, :]
        d_query = (d_ssd.astype(WIDE) * entry_of(cum_v, spread_m)).astype(LOW)
        through_w = to_columns(jnp.broadcast_to(vec[2:3, :], (EDGE, LANES)), spread_m)[0:1]

        def decay_of(head, t, s):
            decay = jnp.exp(jnp.minimum(cum_v[t, head : head + 1] - cum_t[head : head + 1, s], 0.0))
            return decay * steps_t[head : head + 1, s]

        ds00 = jnp.zeros((BLOCK, BLOCK), WIDE)
        ds10 = jnp.zeros((BLOCK, BLOCK), WIDE)
        ds11 = jnp.zeros((BLOCK, BLOCK), WIDE)
        packed, value_parts, tails = [], [], []
        d_packed = nt(write, end_low)
        for pair in range(inner // LANES):
            columns = slice(pair * LANES, (pair + 1) * LANES)
            values = act[:, columns]
            values_f = values.astype(WIDE)
            dy = d_ssd[:, columns]
            dys = pair_lanes(dy)
            m00, m10, m11 = [], [], []
            for k in range(2):
                head = 2 * pair + k
                l00, l10, l11 = decay_of(head, top, top), decay_of(head, low, top), decay_of(head, low, low)
                m00.append((s00 * l00).astype(LOW))
                m10.append((s10 * l10).astype(LOW))
                m11.append((s11 * l11).astype(LOW))
                ds00 = ds00 + nt(dys[k][top], values[top]) * l00
                ds10 = ds10 + nt(dys[k][low], values[top]) * l10
                ds11 = ds11 + nt(dys[k][low], values[low]) * l11
            v0 = tn(
                jnp.concatenate([m00[0], m10[0], m00[1], m10[1]], axis=0), jnp.concatenate([dys[0], dys[1]], axis=0)
            )
            v1 = tn(
                jnp.concatenate([m11[0], m11[1]], axis=0), jnp.concatenate([dys[0][low], dys[1][low]], axis=0)
            )
            tail = d_packed[:, columns] * weight_w[:, columns]
            whole = jnp.concatenate([v0, v1], axis=0) + tail
            d_conv[slot, :, columns] = conv_grad(
                whole + through_w[:, columns] * dy.astype(WIDE), conv[:, columns]
            )
            value_parts.append(values_f * whole)
            tails.append(jnp.sum(tail * values_f, axis=0, keepdims=True))
            packed.append((values_f * weight_w[:, columns]).astype(LOW))

        ds = jnp.concatenate(
            [
                jnp.concatenate([jnp.where(lower_mask, ds00, 0.0), jnp.zeros((BLOCK, BLOCK), WIDE)], axis=1),
                jnp.concatenate([ds10 * second, jnp.where(lower_mask, ds11, 0.0)], axis=1),
            ],
            axis=0,
        ).astype(LOW)
        d_read = nn(ds, write) + nn(d_query, start.astype(LOW))
        d_write = tn(ds, read_v) + nn(jnp.concatenate(packed, axis=1), end_low)
        d_conv[slot, :, inner : inner + STATE] = conv_grad(d_write, conv[:, inner : inner + STATE])
        d_conv[slot, :, inner + STATE :] = conv_grad(d_read, conv[:, inner + STATE :])

        dy_f = d_ssd.astype(WIDE)
        own = to_heads(dy_f * act[:, :inner].astype(WIDE), collect)
        r1 = to_heads(dy_f * ssd_s[here, :], collect) - vec[2:3, :] * own
        by_value = to_heads(jnp.concatenate(value_parts, axis=1), collect)
        tail_row = to_heads(jnp.broadcast_to(jnp.concatenate(tails, axis=1), (EDGE, inner)), collect)[0:1]
        high, rest = halves(end * start)
        ones = jnp.ones((EDGE, STATE), LOW)
        carry_grad = to_heads(nt(ones, high) + nt(ones, rest), collect)[0:1]
        d_last = tail_row + carry_grad * (jnp.exp(last) * (first * second))
        d_cum = r1 - by_value + jnp.where(row == GROUP - 1, d_last, 0.0)
        d_rate = sum_after(d_cum)
        d_raw = d_rate * scale * sig + by_value * ratio
        d_step[slot] = d_raw.astype(LOW)
        tiny[0:1, :] += jnp.sum(d_raw, axis=0, keepdims=True)
        tiny[1:2, :] += jnp.sum(d_rate * steps, axis=0, keepdims=True) * scale
        tiny[2:3, :] += jnp.sum(own, axis=0, keepdims=True)

    @pl.when(turn == blocks - 1)
    def _():
        edge_own[...] = d_conv[jnp.where(turn == 0, 1, 0), 0:EDGE, :]
        edge_copy(lax.rem(me + seqs - 1, seqs)).start()

    @pl.when(turn == blocks)
    def _():
        edge_copy(lax.rem(me + 1, seqs)).wait()
        after[...] = edge_got[...]

    @pl.when(turn >= 1)
    def _():
        final = turn == blocks
        slot = jnp.where(final, 1, 0)
        b = jnp.where(final, blocks - 1, blocks - 1 - turn)
        at_b = group_rows(b)
        taps = jnp.concatenate([kernels[...], filters[...]], axis=1)
        grad_c = d_conv[slot]
        pre_v = pre[...].astype(WIDE)
        before = jnp.where(b == 0, rim[...], pre_before[HALO - EDGE :, :].astype(WIDE))
        bias_g[...] += jnp.sum(grad_c, axis=0, keepdims=True)
        d_pre = []
        for half in range(2):
            part_rows = slice(half * BLOCK, (half + 1) * BLOCK)
            tile = grad_c[part_rows]
            ext[0:EDGE, :] = (before if half == 0 else pre_v[BLOCK - EDGE : BLOCK]) * flags[2 * b + half]
            ext[EDGE:, :] = pre_v[part_rows]
            for tap in range(TAPS):
                taps_g[tap : tap + 1, :] += jnp.sum(
                    tile * ext[pl.ds(EDGE - (TAPS - 1) + tap, BLOCK), :], axis=0, keepdims=True
                )
            ext[:BLOCK, :] = tile
            ext[BLOCK:, :] = (grad_c[BLOCK : BLOCK + EDGE] if half == 0 else after[...]) * flags[2 * b + half + 1]
            total = taps[TAPS - 1 : TAPS] * ext[:BLOCK, :]
            for tap in range(TAPS - 1):
                total = total + taps[tap : tap + 1] * ext[pl.ds(TAPS - 1 - tap, BLOCK), :]
            d_pre.append(total.astype(LOW))
        d_pre = jnp.concatenate(d_pre, axis=0)
        step_grad = d_step[slot]
        normed_v = normed[...]
        dw[:, :wide] += tn(normed_v, d_pre)
        dw[:, wide:] += tn(normed_v, step_grad)
        d_normed = (
            nt(dgate_s[at_b, :], w[:, :inner])
            + nt(d_pre, w[:, inner : inner + wide])
            + nt(step_grad, w[:, inner + wide :])
        )
        u_f = u[...].astype(WIDE)
        inv = lax.rsqrt(jnp.mean(u_f * u_f, axis=1, keepdims=True) + EPS)
        gained = d_normed * prenorm[...]
        dot = jnp.sum(gained * u_f, axis=1, keepdims=True)
        grad = gained * inv - u_f * (inv * inv * inv / D * dot)
        pn[...] += jnp.sum(d_normed * (u_f * inv), axis=0, keepdims=True)
        g_buf[at_b, :] = grad.astype(LOW)
        all_line(lambda to: dx_copy(to, mine, b).start())
        result[0, 2 * b] = u[0:BLOCK, pl.ds(pl.multiple_of(mine * width, LANES), width)]
        result[0, 2 * b + 1] = u[BLOCK:, pl.ds(pl.multiple_of(mine * width, LANES), width)]

    @pl.when((turn >= 0) & (turn < blocks))
    def _():
        after[...] = d_conv[jnp.where(turn == 0, 1, 0), 0:EDGE, :]

    @pl.when(turn == blocks)
    def _():
        own_copies["dx"].start()
        dw_low[:, :inner] = dw[:, :inner].astype(LOW)
        dw_low[:, inner:] = dw[:, wide:].astype(LOW)
        da_low[...] = dw[:, inner:wide].astype(LOW)
        w_start(3)
        w_start(2)
        own_copies["dw"].start()
        da_got[me] = da_low[rows_of(me), :]

        for z in range(line):
            slab = z * size // LANES * LANES
            zs_send[z] = jnp.zeros(zs_send.shape[1:], WIDE)
            zs_send[z, 0:1, :] = pn[:, z * width : (z + 1) * width]
            zs_send[z, EDGE : EDGE + TAPS, :LANES] = taps_g[0:TAPS, inner + slab : inner + slab + LANES]
            zs_send[z, EDGE + TAPS : EDGE + TAPS + 1, :LANES] = bias_g[:, inner + slab : inner + slab + LANES]
        zs_got[mine] = zs_send[mine]
        all_line(lambda to: zs_copy(to, mine).start())

        all_line(lambda other: out_copy(other, other).wait())
        own_copies["out"].wait()

        def fetch(src, n):
            return pltpu.make_async_copy(src, out_part, load_sem.at[n])

        fetch(out_got, 0).start()
        fetch(out_got, 0).wait()

        @pl.loop(0, blocks)
        def _(b):
            inv, _ = row_stats(b)
            total = out_part[0, group_rows(b)].astype(WIDE)
            for z in range(1, line):
                total = total + out_part[z, group_rows(b)].astype(WIDE)
            total = total * inv
            result[0, 2 * b] = (result[0, 2 * b].astype(WIDE) + total[:BLOCK]).astype(LOW)
            result[0, 2 * b + 1] = (result[0, 2 * b + 1].astype(WIDE) + total[BLOCK:]).astype(LOW)

        route(0)
        all_line(lambda other: zs_copy(other, other).wait())
        from_line = jnp.sum(zs_got[...], axis=0)
        small[...] = jnp.zeros_like(small)
        small[0:TAPS, :inner] = taps_g[0:TAPS, :inner]
        small[0:TAPS, inner:] = from_line[EDGE : EDGE + TAPS, :LANES]
        small[4:5, :inner] = bias_g[:, :inner]
        small[4:5, inner:] = from_line[EDGE + TAPS : EDGE + TAPS + 1, :LANES]
        small[5:6, :inner] = gpost[...]
        small[6:7, :width] = from_line[0:1]
        for n in range(3):
            small[7:8, n * LANES : (n + 1) * LANES] = tiny[n : n + 1, :]
        own_copies["small"].start()
        all_seq(lambda to: small_copy(to, me).start())

        w_wait(3)
        from_plane = da_got[0].astype(WIDE)
        for n in range(1, seqs):
            from_plane = from_plane + da_got[n].astype(WIDE)
        for z in range(line):
            slab = z * size // LANES * LANES
            da_send[z] = from_plane[:, slab : slab + LANES]
        own_copies["addr"].start()
        all_line(lambda to: da_copy(to, mine).start())

        @pl.loop(0, blocks)
        def _(b):
            all_line(lambda other: dx_copy(other, other, b).wait())

        own_copies["dx"].wait()
        fetch(dx_got, 1).start()
        fetch(dx_got, 1).wait()

        @pl.loop(0, blocks)
        def _(b):
            total = out_part[0, group_rows(b)].astype(WIDE)
            for z in range(1, line):
                total = total + out_part[z, group_rows(b)].astype(WIDE)
            done = (g_own[group_rows(b), :].astype(WIDE) + total).astype(LOW)
            result[1, 2 * b] = done[:BLOCK]
            result[1, 2 * b + 1] = done[BLOCK:]

        route(1)
        for which in range(3):
            w_wait(which)
        all_line(lambda other: da_copy(other, other).wait())
        all_seq(lambda other: small_copy(other, other).wait())
        all_seq(lambda other: fin_copy(0, other, other).wait())
        all_seq(lambda other: fin_copy(1, other, other).wait())
        for name in ("gread", "ggate", "dw", "addr", "small", "fin0", "fin1"):
            own_copies[name].wait()


def core(
    flags, give, gate, part, act, cum, raw, local, conv, pre, normed, u, g_part, state_in, r_t, w_all, postnorm, vec,
    prenorm, kernels, filters, rim,
):
    seqs, line = lax.axis_size("seq"), lax.axis_size("head")
    rows, inner = gate.shape
    wide = act.shape[1]
    total = g_part.shape[1]
    width = total // line
    depth = total // seqs
    blocks, tiles = rows // GROUP, rows // BLOCK
    heads = inner // HDIM
    steps = 4 * blocks + 1

    def scan_block(i):
        return jnp.clip(4 * blocks - 1 - i, 0, blocks - 1)

    def late_block(i):
        return jnp.where(i == steps - 1, blocks - 1, jnp.clip(4 * blocks - 1 - i, 0, max(blocks - 2, 0)))

    def place(early, late=None):
        def at(i):
            index = jnp.int32(0)
            for n in range(3):
                if n in early:
                    now = i - n * blocks
                elif any(m > n for m in early):
                    now = jnp.int32(0)
                elif late is not None:
                    now = late(jnp.int32(3 * blocks))
                else:
                    now = jnp.int32(blocks - 1)
                index = jnp.where((i >= n * blocks) & (i < (n + 1) * blocks), now, index)
            return jnp.where(i >= 3 * blocks, late(i) if late is not None else blocks - 1, index)

        return at

    def by_rows(columns, at, column=0):
        return blockwise((GROUP, columns), lambda i: (at(i), column))

    local_at = place((0,))
    pre_at = place((), late_block)
    message = (inner + HALO, STATE)
    sums = (blocks, EDGE, GROUP)
    whole = (state_in, r_t, w_all, postnorm, vec, prenorm, kernels, filters, rim)
    gather = (line, rows, width)
    small = (EDGE, inner + LANES)
    return pl.pallas_call(
        functools.partial(core_kernel, seqs, line, heads, blocks),
        grid=(steps,),
        out_shape=(
            shape((seqs, BLOCK, width), LOW), shape((seqs, BLOCK, width), LOW), shape(gather, LOW), shape(gather, LOW),
            shape((seqs, depth, inner), LOW), shape((seqs, depth, inner), LOW), shape((seqs, depth, inner + LANES), LOW),
            shape((line, depth, LANES), WIDE), shape((seqs,) + small, WIDE),
        ),
        in_specs=[
            SMEM_SPEC, SMEM_SPEC,
            by_rows(inner, place((0, 1, 2))), by_rows(inner, place((0,))),
            by_rows(STATE, place((0, 2)), (inner + STATE) // STATE), by_rows(wide, place((), scan_block)),
            by_rows(LANES, place((0, 2), scan_block)), by_rows(LANES, place((), scan_block)),
            blockwise((1, inner, STATE), lambda i: (local_at(i), 0, 0)), by_rows(wide, place((), scan_block)),
            by_rows(wide, pre_at),
            blockwise((HALO, wide), lambda i: (jnp.maximum(pre_at(i) * (GROUP // HALO) - 1, 0), 0)),
            by_rows(total, place((2,), late_block)), by_rows(total, pre_at), ANY_SPEC,
        ] + [fixed(a.shape) for a in whole],
        out_specs=(ANY_SPEC,) * 9,
        scratch_shapes=[
            pltpu.VMEM((rows, inner), WIDE), pltpu.VMEM((rows, inner), WIDE), pltpu.VMEM((rows, inner), LOW),
            pltpu.VMEM((rows, inner), LOW), pltpu.VMEM((blocks, inner, STATE), WIDE),
            pltpu.VMEM((blocks, inner, STATE), WIDE), pltpu.VMEM((inner, STATE), WIDE), pltpu.VMEM((LANES, 1), WIDE),
            pltpu.VMEM((rows, total), LOW), pltpu.VMEM((rows, width), LOW), pltpu.VMEM(gather, LOW),
            pltpu.VMEM((seqs,) + message, LOW), pltpu.VMEM(message, LOW),
            pltpu.VMEM((line,) + sums, WIDE), pltpu.VMEM(sums, WIDE),
            pltpu.VMEM((total, inner), WIDE), pltpu.VMEM((total, inner), WIDE), pltpu.VMEM((total, inner), LOW),
            pltpu.VMEM((total, inner), LOW), pltpu.VMEM((1, inner), WIDE), pltpu.VMEM((EDGE, LANES), WIDE),
            pltpu.VMEM((2, GROUP, wide), WIDE), pltpu.VMEM((2, GROUP, LANES), LOW), pltpu.VMEM((EDGE, wide), WIDE),
            pltpu.VMEM((EDGE, wide), WIDE), pltpu.VMEM((EDGE, wide), WIDE), pltpu.VMEM((BLOCK + EDGE, wide), WIDE),
            pltpu.VMEM((EDGE, wide), WIDE), pltpu.VMEM((1, wide), WIDE), pltpu.VMEM((total, wide + LANES), WIDE),
            pltpu.VMEM((total, inner + LANES), LOW), pltpu.VMEM((total, wide - inner), LOW),
            pltpu.VMEM((seqs, depth, wide - inner), LOW), pltpu.VMEM((line, depth, LANES), WIDE),
            pltpu.VMEM((1, total), WIDE), pltpu.VMEM((line, 2 * EDGE, width), WIDE),
            pltpu.VMEM((line, 2 * EDGE, width), WIDE), pltpu.VMEM(small, WIDE),
            pltpu.VMEM((2, tiles, BLOCK, width), LOW), pltpu.VMEM((2, seqs, BLOCK, width), LOW),
            DMA((seqs,)), DMA((seqs,)), DMA((seqs,)), DMA((line,)), DMA((line,)), DMA((2, line)), DMA((line,)), DMA((4,)),
            DMA((line,)), DMA((line,)), DMA((4, seqs)), DMA((4, seqs)), DMA((line, blocks)), DMA((line, blocks)), DMA, DMA,
            DMA((line,)), DMA((line,)), DMA((line,)), DMA((line,)), DMA((seqs,)), DMA((seqs,)), DMA((2, seqs)),
            DMA((2, seqs)), DMA((9,)),
        ],
        compiler_params=pltpu.CompilerParams(
            collective_id=1, has_side_effects=True, vmem_limit_bytes=VMEM_LIMIT, dimension_semantics=("arbitrary",)
        ),
        name="core",
    )(
        flags, give, gate, part, act, act, cum, raw, local, conv, pre, pre, normed, u, g_part, *whole
    )


def finish_kernel(
    take, out_recv, grad_recv, gread_got, ggate_got, dw_got, addr_got, small_got,
    out_o, dx_o, prenorm_o, gate_o, pay_o, addr_o, step_o, kernels_o, offsets_o, filters_o, shifts_o,
    stepbias_o, decays_o, through_o, post_o, read_o,
):
    inner, size, heads, width = gate_o.shape[1], addr_o.shape[1], step_o.shape[0], prenorm_o.shape[1]
    offset = lax.rem(lax.axis_index("head") * size, LANES)
    back_turn = lax.rem(LANES - offset, LANES)
    for k in range(out_o.shape[0]):
        out_o[k] = out_recv[take[k]]
        dx_o[k] = grad_recv[take[k]]

    def summed(ref):
        total = ref[0].astype(WIDE)
        for n in range(1, ref.shape[0]):
            total = total + ref[n].astype(WIDE)
        return total

    read_o[...] = summed(gread_got).T
    gate_o[...] = summed(ggate_got)
    grads = summed(dw_got)
    pay_o[...] = grads[:, :inner]
    step_o[...] = grads[:, inner:].T[:heads]
    addr_o[...] = pltpu.roll(summed(addr_got), back_turn, 1)[:, :size]
    totals = jnp.sum(small_got[...], axis=0)
    kernels_o[...] = totals[0:TAPS, :inner]
    offsets_o[...] = totals[4:5, :inner]
    turned = pltpu.roll(totals[:, inner:], back_turn, 1)
    filters_o[...] = turned[0:TAPS, :size]
    shifts_o[...] = turned[4:5, :size]
    post_o[...] = totals[5:6, :inner]
    prenorm_o[...] = totals[6:7, :width]
    for n, ref in enumerate((stepbias_o, decays_o, through_o)):
        ref[...] = totals[7:8, n * LANES : n * LANES + heads]


def finish(take, out_recv, grad_recv, gread_got, ggate_got, dw_got, addr_got, small_got):
    seqs, _, width = out_recv.shape
    tiles = take.shape[0]
    _, depth, inner = gread_got.shape
    heads = inner // HDIM
    size = 2 * STATE // addr_got.shape[0]
    operands = (out_recv, grad_recv, gread_got, ggate_got, dw_got, addr_got, small_got)
    outs = (
        shape((tiles, BLOCK, width), LOW), shape((tiles, BLOCK, width), LOW), shape((1, width), WIDE),
        shape((depth, inner), WIDE), shape((depth, inner), WIDE), shape((depth, size), WIDE),
        shape((heads, depth), WIDE), shape((TAPS, inner), WIDE), shape((1, inner), WIDE),
        shape((TAPS, size), WIDE), shape((1, size), WIDE), shape((1, heads), WIDE), shape((1, heads), WIDE),
        shape((1, heads), WIDE), shape((1, inner), WIDE), shape((inner, depth), WIDE),
    )
    return pl.pallas_call(
        finish_kernel,
        grid=(1,),
        out_shape=outs,
        in_specs=[SMEM_SPEC] + [fixed(a.shape) for a in operands],
        out_specs=tuple(fixed(a.shape) for a in outs),
        compiler_params=pltpu.CompilerParams(vmem_limit_bytes=VMEM_LIMIT, dimension_semantics=("arbitrary",)),
        name="finish",
    )(take, *operands)


def on_device(
    inputs,
    cotangent,
    lengths,
    placement,
    prenorm,
    gating,
    payload,
    address,
    stepping,
    kernels,
    offsets,
    filters,
    shifts,
    stepbias,
    decays,
    through,
    postnorm,
    readout,
):
    rows, width = inputs.shape
    heads = stepbias.shape[0]
    tiles = rows // BLOCK
    give_in, take_in, give_out, take_out, flags, vec = index(placement, lengths, stepbias, decays, through, tiles)
    gain, post = prenorm[None, :], postnorm[None, :]
    (
        u, normed, gate, pre, conv, act, raw, cum, part, local, state_in, rim, g_part, w_all, r_t
    ) = front(
        give_in, take_in, flags, inputs, cotangent, gating, payload, address, stepping, readout, vec, gain, kernels,
        filters, offsets[None, :], shifts[None, :]
    )
    out_recv, grad_recv, _, _, gread_got, ggate_got, dw_got, addr_got, small_got = core(
        flags, give_out, gate, part, act, cum, raw, local, conv, pre, normed, u, g_part, state_in, r_t, w_all, post, vec,
        gain, kernels, filters, rim
    )
    (
        out, dx, prenorm_g, gate_g, pay_g, addr_g, step_g, kernels_g, offsets_g, filters_g, shifts_g, stepbias_g,
        decays_g, through_g, post_g, read_g,
    ) = finish(take_out, out_recv, grad_recv, gread_got, ggate_got, dw_got, addr_got, small_got)
    return (
        out.reshape(rows, width),
        dx.reshape(rows, width),
        prenorm_g.reshape(-1),
        gate_g,
        pay_g,
        addr_g,
        step_g.T,
        kernels_g,
        offsets_g.reshape(-1),
        filters_g,
        shifts_g.reshape(-1),
        stepbias_g.reshape(-1),
        decays_g.reshape(-1),
        through_g.reshape(-1),
        post_g.reshape(-1),
        read_g,
    )


def solution(mesh):
    in_specs = (
        P("seq", "head"),
        P("seq", "head"),
        P(),
        P(),
        P(),
        P("seq", "head"),
        P("seq", "head"),
        P("seq", None),
        P("seq", "head"),
        P(None, "head"),
        P("head"),
        P(),
        P(),
        P("head"),
        P("head"),
        P("head"),
        P("head"),
        P("head", "seq"),
    )
    out_specs = (
        P("seq", "head"),
        P("seq", "head"),
        P("head"),
        P("seq", "head"),
        P("seq", "head"),
        P("seq", "head"),
        P("seq", "head"),
        P(None, "head"),
        P("head"),
        P(None, "head"),
        P("head"),
        P("head"),
        P("head"),
        P("head"),
        P("head"),
        P("head", "seq"),
    )
    return jax.shard_map(
        on_device, mesh=mesh, in_specs=in_specs, out_specs=out_specs, check_vma=False
    )
```

time: 248 us -> 226 us (0.911)
  Pallas kernels: 246 us -> 224 us
    pallas_call x3 -> x1, Pallas kernels: 158 us -> 73 us  [front(): pl.pallas_call(functools.partial(front_kernel, seqs, line, heads, blocks,...]
    pallas_call x1, Pallas kernels: 81.7 us -> 145 us  [core(): pl.pallas_call(functools.partial(core_kernel, seqs, line, heads, blocks),...]
where the time goes in v4:
time: 226 us
  Pallas kernels  224 us (99%)
    pallas_call x1, Pallas kernels, core(): pl.pallas_call(functools.partial(core_kernel, seqs, line, heads, blocks),...  145 us
    pallas_call x1, Pallas kernels, front(): pl.pallas_call(functools.partial(front_kernel, seqs, line, heads, blocks,...  73 us

profile of v4, /device:TPU:1, one launch (start us, length us, event | category | flops | bytes accessed | tf_op | source)
XLA Modules:
  0.0 226.0 jit_solution(10977873338690857496)
XLA Ops:
  0.6 2.3 %index.1 = (s32[8]{0:T(128)}, s32[8]{0:T(128)}, s32[8]{0:T(128)}, s32[8]{0:T(128)}, f32[9]{0:T(128)}, /*index=5*/f32[8,128]{1,0:T(8,128)}) custom-call(s32[64]{0:T(128)} %place.1, s32[4]{0:T(128)} %lengths.1, f32[1,8]{1,0:T(1,128)} %bitcast.28, f32[1,8]{1,0:T(1,128)} %bitcast.29, f32[1,8]{1,0:T(1,128)} %bitcast.30), custom_call_target="tpu_custom_call" | custom-call | tf_op jit(solution)/shard_map/index/pallas_call | solution.py:316
  2.9 73.0 %front.1 = (bf16[1024,1024]{1,0:T(8,128)(2,1)}, bf16[1024,1024]{1,0:T(8,128)(2,1)}, f32[1024,512]{1,0:T(8,128)}, bf16[1024,768]{1,0:T(8,128)(2,1)}, f32[1024,768...) custom-call(s32[8]{0:T(128)} %get-tuple-element.63.give, ...), custom_call_target="tpu_custom_call" | custom-call | tf_op jit(solution)/shard_map/front/pallas_call | solution.py:620
  75.9 144.6 %core.1 = (bf16[8,128,256]{2,1,0:T(8,128)(2,1)}, bf16[8,128,256]{2,1,0:T(8,128)(2,1)}, bf16[4,1024,256]{2,1,0:T(8,128)(2,1)}, bf16[4,1024,256]{2,1,0:T(8,128)(2,...) custom-call(f32[9]{0:T(128)} %get-tuple-element.61.flags, ...), custom_call_target="tpu_custom_call" | custom-call | tf_op jit(solution)/shard_map/core/pallas_call | solution.py:1196
  220.6 3.9 %finish.1 = (bf16[8,128,256]{2,1,0:T(8,128)(2,1)}, bf16[8,128,256]{2,1,0:T(8,128)(2,1)}, f32[1,256]{1,0:T(1,128)}, f32[128,512]{1,0:T(8,128)}, f32[128,512]{1,0:...) custom-call(s32[8]{0:T(128)} %get-tuple-element.60.take, ...), custom_call_target="tpu_custom_call" | custom-call | tf_op jit(solution)/shard_map/finish/pallas_call | solution.py:1296
  224.4 1.5 copy.34

commit v5 on v4

--- a/solution.py
+++ b/solution.py
@@ -115,7 +115,7 @@
     return jnp.where(lane < heads, soft, 0.0), sig, ratio
 
 
-def greet(seq_peers, head_peers):
+def greet(seq_peers, head_peers, corners=False):
     barrier = pltpu.get_barrier_semaphore()
     count = 0
     if seq_peers > 1:
@@ -138,6 +138,16 @@
             )
 
         count += head_peers - 1
+    if corners and head_peers > 1:
+        me, mine = lax.axis_index("seq"), lax.axis_index("head")
+        for side in (1, seq_peers - 1):
+
+            @pl.loop(1, head_peers)
+            def _(i):
+                where = {"seq": lax.rem(me + side, seq_peers), "head": lax.rem(mine + i, head_peers)}
+                pl.semaphore_signal(barrier, inc=1, device_id=where, device_id_type=MESH)
+
+        count += 2 * (head_peers - 1)
     pl.semaphore_wait(barrier, count)
 
 
@@ -379,7 +389,7 @@
 
     def piece(n):
         if isinstance(n, int):
-            return pl.ds(rows, HALO) if n == chunks else pl.ds(n * part, part)
+            return pl.ds(n * part, part)
         return pl.ds(pl.multiple_of(n * part, part), part)
 
     def u_line(n):
@@ -396,6 +406,13 @@
     own_g = pltpu.make_async_copy(work_g, g_line.view(mine), own_sem.at[1])
     save_w = pltpu.make_async_copy(w, w_o, own_sem.at[2])
 
+    def rim_copy(to, shard):
+        columns = pl.ds(pl.multiple_of(shard * width, LANES), width)
+        return remote(
+            work_x.at[pl.ds(rows - HALO, HALO)], u.at[pl.ds(rows, HALO), columns], rim_sent.at[to], rim_got.at[shard],
+            {"seq": lax.rem(me + 1, seqs), "head": to},
+        )
+
     def arrange(which, received, work):
         @pl.loop(1, seqs)
         def _(n):
@@ -416,7 +433,7 @@
         loads = [pltpu.make_async_copy(src, dst, load_sem.at[n]) for n, (src, dst) in enumerate(pairs)]
         for load in loads:
             load.start()
-        greet(seqs, line)
+        greet(seqs, line, corners=True)
 
         def post(which, source, outgoing, incoming):
             @pl.loop(1, seqs)
@@ -444,28 +461,29 @@
         own_r.start()
 
         arrange(0, recv_x, work_x)
-        after = lax.rem(me + 1, seqs)
-        rim = remote(
-            work_x.at[pl.ds(rows - HALO, HALO)], work_x.at[pl.ds(rows, HALO)], rim_sent, rim_got, {"seq": after}
-        )
-        rim.start()
+
+        @pl.loop(0, line)
+        def _(n):
+            rim_copy(lax.rem(mine + n, line), mine).start()
+
         for n in range(chunks):
             u_line(n).first(work_x.at[piece(n)])
         w_plane.start(w_own)
-        rim.wait()
-        u_line(chunks).first(work_x.at[piece(chunks)])
-        own = pltpu.make_async_copy(work_x, own_columns(u), own_sem.at[3])
+        own = pltpu.make_async_copy(work_x, own_columns(u.at[pl.ds(0, rows)]), own_sem.at[3])
         own.start()
         post(1, g, send_g, recv_g)
         r_plane.start(r_own)
         for step in range(1, line - 1):
-            for n in range(chunks + 1):
+            for n in range(chunks):
                 u_line(n).hop(step)
             if step == 1:
                 w_plane.relay()
-        if line > 1:
-            u_line(chunks).hop(line - 1)
         own.wait()
+
+        @pl.loop(0, line)
+        def _(n):
+            rim_copy(n, n).wait_recv()
+
         w_plane.finish(w_own)
         save_w.start()
 
@@ -582,8 +600,13 @@
         if line > 1:
             g_line.hop(1, give=False)
         g_line.finish(work_g, (0,))
-        for n in range(chunks + 1):
+        for n in range(chunks):
             u_line(n).finish(work_x.at[piece(n)])
+
+        @pl.loop(0, line)
+        def _(n):
+            rim_copy(n, mine).wait_send()
+
 
         @pl.loop(1, seqs)
         def _(n):
@@ -636,7 +659,7 @@
         scratch_shapes=[pltpu.VMEM(a.shape, a.dtype) for a in operands] + [
             pltpu.VMEM((LANES, LANES), WIDE),
             pltpu.VMEM(routed, LOW), pltpu.VMEM(routed, LOW), pltpu.VMEM(routed, LOW), pltpu.VMEM(routed, LOW),
-            pltpu.VMEM((rows + HALO, width), LOW), pltpu.VMEM((rows, width), LOW),
+            pltpu.VMEM((rows, width), LOW), pltpu.VMEM((rows, width), LOW),
             pltpu.VMEM((depth, columns), LOW), pltpu.VMEM((depth, inner), LOW),
             pltpu.VMEM((rows + HALO, total), LOW), pltpu.VMEM((total, columns), LOW),
             pltpu.VMEM(message, LOW), pltpu.VMEM((seqs,) + message, LOW),
@@ -644,8 +667,8 @@
             pltpu.VMEM((inner, STATE), WIDE), pltpu.VMEM((HALO, STATE), WIDE),
             DMA((2, seqs)), DMA((2, seqs)),
             DMA((seqs,)), DMA((seqs,)), DMA((seqs,)), DMA((seqs,)), DMA((seqs,)), DMA((seqs,)),
-            DMA((seqs,)), DMA((seqs,)), DMA((seqs,)), DMA, DMA, DMA((4,)), DMA((7,)),
-            DMA((chunks + 1, 2, line)), DMA((chunks + 1, line)), DMA((2, line)), DMA((line,)),
+            DMA((seqs,)), DMA((seqs,)), DMA((seqs,)), DMA((line,)), DMA((line,)), DMA((4,)), DMA((7,)),
+            DMA((chunks, 2, line)), DMA((chunks, line)), DMA((2, line)), DMA((line,)),
         ],
         compiler_params=pltpu.CompilerParams(
             collective_id=0, has_side_effects=True, vmem_limit_bytes=VMEM_LIMIT, dimension_semantics=("arbitrary",)
@@ -662,14 +685,14 @@
 def core_kernel(
     seqs, line, heads, blocks, flags, give,
     gate, part, read, act, cum, raw, local, conv, pre, pre_before, normed, u, g_part,
-    state_in, r_t, w, postnorm, vec, prenorm, kernels, filters, rim,
+    r_in, w_in, state_in, postnorm, vec, prenorm, kernels, filters, rim,
     out_recv, grad_recv, out_got, dx_got, gread_got, ggate_got, dw_got, addr_got, small_got,
-    ssd_s, din_s, dssd_s, dgate_s, starts, q, state, prod, g_buf, g_own, out_part, back_slots, back_msg, sums,
+    r_t, w, ssd_s, din_s, dssd_s, dgate_s, starts, q, state, prod, g_buf, g_own, out_part, back_slots, back_msg, relay, dx_relay, sums,
     totals, gread, ggate, gread_low, ggate_low, gpost, tiny, d_conv, d_step, after, edge_own, edge_got, ext,
     taps_g, bias_g, dw, dw_low, da_low, da_got, da_send, pn, zs_send, zs_got, small, result, fin_send,
     back_sent, back_sem, back_passed, sum_sent, sum_sem, line_sent, line_sem, load_sem, out_sent, out_sem,
     w_sent, w_sem, dx_sent, dx_sem, edge_sent, edge_sem, zs_sent, zs_sem, da_sent, da_sem, small_sent, small_sem,
-    fin_sent, fin_sem, own_sem,
+    fin_sent, fin_sem, own_sem, weight_sem, relay_sent, relay_sem, dx_relay_sent, dx_relay_sem,
 ):
     i = pl.program_id(0)
     me, mine = lax.axis_index("seq"), lax.axis_index("head")
@@ -742,6 +765,88 @@
             dx_sem.at[slot, b], {"head": to},
         )
 
+    merge = line == 4
+    is_end = (mine == 0) | (mine == line - 1)
+    low_side = mine < 2
+    mid = jnp.where(low_side, 1, 2)
+    far = jnp.where(low_side, 3, 0)
+
+    def relay_copy():
+        return remote(out_part.at[far], relay, relay_sent, relay_sem, {"head": mid})
+
+    def dx_relay_copy(b):
+        return remote(
+            shard_of(g_buf.at[group_rows(b)], far), dx_relay.at[group_rows(b)], dx_relay_sent.at[b],
+            dx_relay_sem.at[b], {"head": mid},
+        )
+
+    def all_direct(body, received=False):
+        if not merge:
+            all_line(body)
+            return
+
+        @pl.loop(1, line)
+        def _(n):
+            other = lax.rem(mine + n, line)
+            skipped = (is_end & (other == far)) if received else (other == far)
+            pl.when(jnp.logical_not(skipped))(lambda: body(other))
+
+    def send_out():
+        if merge:
+            pl.when(is_end)(lambda: relay_copy().start())
+        all_direct(lambda to: out_copy(to, mine).start())
+
+    def merge_out():
+        if merge:
+
+            @pl.when(jnp.logical_not(is_end))
+            def _():
+                relay_copy().wait_recv()
+
+                @pl.loop(0, blocks)
+                def _(b):
+                    at = group_rows(b)
+                    out_part[far, at] = (out_part[far, at].astype(WIDE) + relay[at].astype(WIDE)).astype(LOW)
+
+                out_copy(far, mine).start()
+
+    def wait_out():
+        all_direct(lambda other: out_copy(other, mine).wait_send())
+        all_direct(lambda other: out_copy(other, other).wait_recv(), received=True)
+        if merge:
+            pl.when(is_end)(lambda: relay_copy().wait_send())
+            pl.when(jnp.logical_not(is_end))(lambda: out_copy(far, mine).wait_send())
+
+    def send_dx(b):
+        if merge:
+            pl.when(is_end)(lambda: dx_relay_copy(b).start())
+        all_direct(lambda to: dx_copy(to, mine, b).start())
+
+    def merge_dx(b):
+        if merge:
+
+            @pl.when(jnp.logical_not(is_end))
+            def _():
+                at = group_rows(b)
+                columns = pl.ds(pl.multiple_of(far * width, LANES), width)
+                dx_relay_copy(b).wait_recv()
+                g_buf[at, columns] = (g_buf[at, columns].astype(WIDE) + dx_relay[at].astype(WIDE)).astype(LOW)
+                dx_copy(far, mine, b).start()
+
+    def wait_dx(b):
+        all_direct(lambda other: dx_copy(other, mine, b).wait_send())
+        all_direct(lambda other: dx_copy(other, other, b).wait_recv(), received=True)
+        if merge:
+            pl.when(is_end)(lambda: dx_relay_copy(b).wait_send())
+            pl.when(jnp.logical_not(is_end))(lambda: dx_copy(far, mine, b).wait_send())
+
+    def from_line_of(b):
+        total = jnp.zeros((GROUP, width), WIDE)
+        for z in range(line):
+            block_z = out_part[z, group_rows(b)].astype(WIDE)
+            total = total + (jnp.where(is_end & (far == z), 0.0, block_z) if merge else block_z)
+        return total
+
     def edge_copy(to):
         return remote(edge_own, edge_got, edge_sent, edge_sem, {"seq": to})
 
@@ -797,12 +902,18 @@
         gate_v = gate[...]
         return ssd * (gate_v * sigmoid(gate_v))
 
+    fetch_r = pltpu.make_async_copy(r_in, r_t, weight_sem.at[0])
+    fetch_w = pltpu.make_async_copy(w_in, w, weight_sem.at[1])
+
     @pl.when(i == 0)
     def _():
+        fetch_r.start()
         greet(seqs, line)
         g_line.hop(1, take=False, source=lambda shard: shard_of(g_part, shard))
         each_load(lambda copy: copy.start())
+        fetch_w.start()
         state[...] = state_in[...]
+        fetch_r.wait()
 
     @pl.when(phase == 0)
     def _():
@@ -824,7 +935,7 @@
             g_line.hop(step)
         each_load(lambda copy: copy.wait())
         g_line.finish(None, range(1, line - 1))
-
+        fetch_w.wait()
     @pl.when(phase == 1)
     def _():
         gated = gated_of(ssd_s[here, :])
@@ -845,7 +956,7 @@
         prod[...] = jnp.ones_like(prod)
         all_line(lambda other: sum_copy(other, other).wait())
         totals[...] = jnp.sum(sums[...], axis=0)
-        all_line(lambda to: out_copy(to, mine).start())
+        send_out()
         own_copies["out"].start()
 
     @pl.when(phase == 2)
@@ -893,6 +1004,7 @@
         state[...] = fold_states(
             back_slots, head_columns(inner), inner, seqs - 1, me, -1, jnp.zeros((inner, STATE), WIDE)
         )
+        merge_out()
 
     @pl.when((phase == 3) & (turn < blocks))
     def _():
@@ -1046,9 +1158,13 @@
         grad = gained * inv - u_f * (inv * inv * inv / D * dot)
         pn[...] += jnp.sum(d_normed * (u_f * inv), axis=0, keepdims=True)
         g_buf[at_b, :] = grad.astype(LOW)
-        all_line(lambda to: dx_copy(to, mine, b).start())
+        send_dx(b)
         result[0, 2 * b] = u[0:BLOCK, pl.ds(pl.multiple_of(mine * width, LANES), width)]
         result[0, 2 * b + 1] = u[BLOCK:, pl.ds(pl.multiple_of(mine * width, LANES), width)]
+
+    @pl.when((turn >= 2) & (turn < blocks))
+    def _():
+        merge_dx(blocks - turn)
 
     @pl.when((turn >= 0) & (turn < blocks))
     def _():
@@ -1065,6 +1181,9 @@
         own_copies["dw"].start()
         da_got[me] = da_low[rows_of(me), :]
 
+        if blocks > 1:
+            merge_dx(0)
+
         for z in range(line):
             slab = z * size // LANES * LANES
             zs_send[z] = jnp.zeros(zs_send.shape[1:], WIDE)
@@ -1074,7 +1193,7 @@
         zs_got[mine] = zs_send[mine]
         all_line(lambda to: zs_copy(to, mine).start())
 
-        all_line(lambda other: out_copy(other, other).wait())
+        wait_out()
         own_copies["out"].wait()
 
         def fetch(src, n):
@@ -1086,14 +1205,12 @@
         @pl.loop(0, blocks)
         def _(b):
             inv, _ = row_stats(b)
-            total = out_part[0, group_rows(b)].astype(WIDE)
-            for z in range(1, line):
-                total = total + out_part[z, group_rows(b)].astype(WIDE)
-            total = total * inv
+            total = from_line_of(b) * inv
             result[0, 2 * b] = (result[0, 2 * b].astype(WIDE) + total[:BLOCK]).astype(LOW)
             result[0, 2 * b + 1] = (result[0, 2 * b + 1].astype(WIDE) + total[BLOCK:]).astype(LOW)
 
         route(0)
+        merge_dx(blocks - 1)
         all_line(lambda other: zs_copy(other, other).wait())
         from_line = jnp.sum(zs_got[...], axis=0)
         small[...] = jnp.zeros_like(small)
@@ -1120,7 +1237,7 @@
 
         @pl.loop(0, blocks)
         def _(b):
-            all_line(lambda other: dx_copy(other, other, b).wait())
+            wait_dx(b)
 
         own_copies["dx"].wait()
         fetch(dx_got, 1).start()
@@ -1128,10 +1245,7 @@
 
         @pl.loop(0, blocks)
         def _(b):
-            total = out_part[0, group_rows(b)].astype(WIDE)
-            for z in range(1, line):
-                total = total + out_part[z, group_rows(b)].astype(WIDE)
-            done = (g_own[group_rows(b), :].astype(WIDE) + total).astype(LOW)
+            done = (g_own[group_rows(b), :].astype(WIDE) + from_line_of(b)).astype(LOW)
             result[1, 2 * b] = done[:BLOCK]
             result[1, 2 * b + 1] = done[BLOCK:]
 
@@ -1190,7 +1304,7 @@
     pre_at = place((), late_block)
     message = (inner + HALO, STATE)
     sums = (blocks, EDGE, GROUP)
-    whole = (state_in, r_t, w_all, postnorm, vec, prenorm, kernels, filters, rim)
+    whole = (state_in, postnorm, vec, prenorm, kernels, filters, rim)
     gather = (line, rows, width)
     small = (EDGE, inner + LANES)
     return pl.pallas_call(
@@ -1209,15 +1323,17 @@
             blockwise((1, inner, STATE), lambda i: (local_at(i), 0, 0)), by_rows(wide, place((), scan_block)),
             by_rows(wide, pre_at),
             blockwise((HALO, wide), lambda i: (jnp.maximum(pre_at(i) * (GROUP // HALO) - 1, 0), 0)),
-            by_rows(total, place((2,), late_block)), by_rows(total, pre_at), ANY_SPEC,
+            by_rows(total, place((2,), late_block)), by_rows(total, pre_at), ANY_SPEC, ANY_SPEC, ANY_SPEC,
         ] + [fixed(a.shape) for a in whole],
         out_specs=(ANY_SPEC,) * 9,
         scratch_shapes=[
+            pltpu.VMEM(r_t.shape, LOW), pltpu.VMEM(w_all.shape, LOW),
             pltpu.VMEM((rows, inner), WIDE), pltpu.VMEM((rows, inner), WIDE), pltpu.VMEM((rows, inner), LOW),
             pltpu.VMEM((rows, inner), LOW), pltpu.VMEM((blocks, inner, STATE), WIDE),
             pltpu.VMEM((blocks, inner, STATE), WIDE), pltpu.VMEM((inner, STATE), WIDE), pltpu.VMEM((LANES, 1), WIDE),
             pltpu.VMEM((rows, total), LOW), pltpu.VMEM((rows, width), LOW), pltpu.VMEM(gather, LOW),
             pltpu.VMEM((seqs,) + message, LOW), pltpu.VMEM(message, LOW),
+            pltpu.VMEM((rows if line == 4 else GROUP, width), LOW), pltpu.VMEM((rows if line == 4 else GROUP, width), LOW),
             pltpu.VMEM((line,) + sums, WIDE), pltpu.VMEM(sums, WIDE),
             pltpu.VMEM((total, inner), WIDE), pltpu.VMEM((total, inner), WIDE), pltpu.VMEM((total, inner), LOW),
             pltpu.VMEM((total, inner), LOW), pltpu.VMEM((1, inner), WIDE), pltpu.VMEM((EDGE, LANES), WIDE),
@@ -1232,14 +1348,14 @@
             DMA((seqs,)), DMA((seqs,)), DMA((seqs,)), DMA((line,)), DMA((line,)), DMA((2, line)), DMA((line,)), DMA((4,)),
             DMA((line,)), DMA((line,)), DMA((4, seqs)), DMA((4, seqs)), DMA((line, blocks)), DMA((line, blocks)), DMA, DMA,
             DMA((line,)), DMA((line,)), DMA((line,)), DMA((line,)), DMA((seqs,)), DMA((seqs,)), DMA((2, seqs)),
-            DMA((2, seqs)), DMA((9,)),
+            DMA((2, seqs)), DMA((9,)), DMA((2,)), DMA, DMA, DMA((blocks,)), DMA((blocks,)),
         ],
         compiler_params=pltpu.CompilerParams(
             collective_id=1, has_side_effects=True, vmem_limit_bytes=VMEM_LIMIT, dimension_semantics=("arbitrary",)
         ),
         name="core",
     )(
-        flags, give, gate, part, act, act, cum, raw, local, conv, pre, pre, normed, u, g_part, *whole
+        flags, give, gate, part, act, act, cum, raw, local, conv, pre, pre, normed, u, g_part, r_t, w_all, *whole
     )
 
 

time: 226 us -> 206 us (0.912)
  the two profiles are of different devices: /device:TPU:1 before, /device:TPU:27 now
where the time goes in v5:
time: 206 us; the launch traced here: 205 us
  Pallas kernels  203 us (99%)
    pallas_call x1, Pallas kernels, core(): pl.pallas_call(functools.partial(core_kernel, seqs, line, heads, blocks),...  133 us
    pallas_call x1, Pallas kernels, front(): pl.pallas_call(functools.partial(front_kernel, seqs, line, heads, blocks,...  63.6 us

profile of v5, /device:TPU:27, one launch (start us, length us, event | category | flops | bytes accessed | tf_op | source)
XLA Modules:
  0.0 205.4 jit_solution(4919367777811154579)
XLA Ops:
  0.6 2.3 %index.1 = (s32[8]{0:T(128)}, s32[8]{0:T(128)}, s32[8]{0:T(128)}, s32[8]{0:T(128)}, f32[9]{0:T(128)}, /*index=5*/f32[8,128]{1,0:T(8,128)}) custom-call(s32[64]{0:T(128)} %place.1, s32[4]{0:T(128)} %lengths.1, f32[1,8]{1,0:T(1,128)} %bitcast.28, f32[1,8]{1,0:T(1,128)} %bitcast.29, f32[1,8]{1,0:T(1,128)} %bitcast.30), custom_call_target="tpu_custom_call" | custom-call | tf_op jit(solution)/shard_map/index/pallas_call | solution.py:326
  2.9 63.6 %front.1 = (bf16[1024,1024]{1,0:T(8,128)(2,1)}, bf16[1024,1024]{1,0:T(8,128)(2,1)}, f32[1024,512]{1,0:T(8,128)}, bf16[1024,768]{1,0:T(8,128)(2,1)}, f32[1024,768...) custom-call(s32[8]{0:T(128)} %get-tuple-element.63.give, ...), custom_call_target="tpu_custom_call" | custom-call | tf_op jit(solution)/shard_map/front/pallas_call | solution.py:643
  66.6 133.4 %core.1 = (bf16[8,128,256]{2,1,0:T(8,128)(2,1)}, bf16[8,128,256]{2,1,0:T(8,128)(2,1)}, bf16[4,1024,256]{2,1,0:T(8,128)(2,1)}, bf16[4,1024,256]{2,1,0:T(8,128)(2,...) custom-call(f32[9]{0:T(128)} %get-tuple-element.61.flags, ...), custom_call_target="tpu_custom_call" | custom-call | tf_op jit(solution)/shard_map/core/pallas_call | solution.py:1310
  199.9 3.9 %finish.1 = (bf16[8,128,256]{2,1,0:T(8,128)(2,1)}, bf16[8,128,256]{2,1,0:T(8,128)(2,1)}, f32[1,256]{1,0:T(1,128)}, f32[128,512]{1,0:T(8,128)}, f32[128,512]{1,0:...) custom-call(s32[8]{0:T(128)} %get-tuple-element.60.take, ...), custom_call_target="tpu_custom_call" | custom-call | tf_op jit(solution)/shard_map/finish/pallas_call | solution.py:1412
  203.8 1.5 copy.34

commit v6 on v4

--- a/solution.py
+++ b/solution.py
@@ -115,7 +115,7 @@
     return jnp.where(lane < heads, soft, 0.0), sig, ratio
 
 
-def greet(seq_peers, head_peers):
+def greet(seq_peers, head_peers, corners=False):
     barrier = pltpu.get_barrier_semaphore()
     count = 0
     if seq_peers > 1:
@@ -138,6 +138,16 @@
             )
 
         count += head_peers - 1
+    if corners and head_peers > 1:
+        me, mine = lax.axis_index("seq"), lax.axis_index("head")
+        for side in (1, seq_peers - 1):
+
+            @pl.loop(1, head_peers)
+            def _(i):
+                where = {"seq": lax.rem(me + side, seq_peers), "head": lax.rem(mine + i, head_peers)}
+                pl.semaphore_signal(barrier, inc=1, device_id=where, device_id_type=MESH)
+
+        count += 2 * (head_peers - 1)
     pl.semaphore_wait(barrier, count)
 
 
@@ -379,7 +389,7 @@
 
     def piece(n):
         if isinstance(n, int):
-            return pl.ds(rows, HALO) if n == chunks else pl.ds(n * part, part)
+            return pl.ds(n * part, part)
         return pl.ds(pl.multiple_of(n * part, part), part)
 
     def u_line(n):
@@ -395,6 +405,13 @@
     own_r = pltpu.make_async_copy(r_own, r_o.at[rows_of(me)], own_sem.at[0])
     own_g = pltpu.make_async_copy(work_g, g_line.view(mine), own_sem.at[1])
     save_w = pltpu.make_async_copy(w, w_o, own_sem.at[2])
+
+    def rim_copy(to, shard):
+        columns = pl.ds(pl.multiple_of(shard * width, LANES), width)
+        return remote(
+            work_x.at[pl.ds(rows - HALO, HALO)], u.at[pl.ds(rows, HALO), columns], rim_sent.at[to], rim_got.at[shard],
+            {"seq": lax.rem(me + 1, seqs), "head": to},
+        )
 
     def arrange(which, received, work):
         @pl.loop(1, seqs)
@@ -416,7 +433,7 @@
         loads = [pltpu.make_async_copy(src, dst, load_sem.at[n]) for n, (src, dst) in enumerate(pairs)]
         for load in loads:
             load.start()
-        greet(seqs, line)
+        greet(seqs, line, corners=True)
 
         def post(which, source, outgoing, incoming):
             @pl.loop(1, seqs)
@@ -444,28 +461,29 @@
         own_r.start()
 
         arrange(0, recv_x, work_x)
-        after = lax.rem(me + 1, seqs)
-        rim = remote(
-            work_x.at[pl.ds(rows - HALO, HALO)], work_x.at[pl.ds(rows, HALO)], rim_sent, rim_got, {"seq": after}
-        )
-        rim.start()
+
+        @pl.loop(0, line)
+        def _(n):
+            rim_copy(lax.rem(mine + n, line), mine).start()
+
         for n in range(chunks):
             u_line(n).first(work_x.at[piece(n)])
         w_plane.start(w_own)
-        rim.wait()
-        u_line(chunks).first(work_x.at[piece(chunks)])
-        own = pltpu.make_async_copy(work_x, own_columns(u), own_sem.at[3])
+        own = pltpu.make_async_copy(work_x, own_columns(u.at[pl.ds(0, rows)]), own_sem.at[3])
         own.start()
         post(1, g, send_g, recv_g)
         r_plane.start(r_own)
         for step in range(1, line - 1):
-            for n in range(chunks + 1):
+            for n in range(chunks):
                 u_line(n).hop(step)
             if step == 1:
                 w_plane.relay()
-        if line > 1:
-            u_line(chunks).hop(line - 1)
         own.wait()
+
+        @pl.loop(0, line)
+        def _(n):
+            rim_copy(n, n).wait_recv()
+
         w_plane.finish(w_own)
         save_w.start()
 
@@ -582,8 +600,13 @@
         if line > 1:
             g_line.hop(1, give=False)
         g_line.finish(work_g, (0,))
-        for n in range(chunks + 1):
+        for n in range(chunks):
             u_line(n).finish(work_x.at[piece(n)])
+
+        @pl.loop(0, line)
+        def _(n):
+            rim_copy(n, mine).wait_send()
+
 
         @pl.loop(1, seqs)
         def _(n):
@@ -636,7 +659,7 @@
         scratch_shapes=[pltpu.VMEM(a.shape, a.dtype) for a in operands] + [
             pltpu.VMEM((LANES, LANES), WIDE),
             pltpu.VMEM(routed, LOW), pltpu.VMEM(routed, LOW), pltpu.VMEM(routed, LOW), pltpu.VMEM(routed, LOW),
-            pltpu.VMEM((rows + HALO, width), LOW), pltpu.VMEM((rows, width), LOW),
+            pltpu.VMEM((rows, width), LOW), pltpu.VMEM((rows, width), LOW),
             pltpu.VMEM((depth, columns), LOW), pltpu.VMEM((depth, inner), LOW),
             pltpu.VMEM((rows + HALO, total), LOW), pltpu.VMEM((total, columns), LOW),
             pltpu.VMEM(message, LOW), pltpu.VMEM((seqs,) + message, LOW),
@@ -644,8 +667,8 @@
             pltpu.VMEM((inner, STATE), WIDE), pltpu.VMEM((HALO, STATE), WIDE),
             DMA((2, seqs)), DMA((2, seqs)),
             DMA((seqs,)), DMA((seqs,)), DMA((seqs,)), DMA((seqs,)), DMA((seqs,)), DMA((seqs,)),
-            DMA((seqs,)), DMA((seqs,)), DMA((seqs,)), DMA, DMA, DMA((4,)), DMA((7,)),
-            DMA((chunks + 1, 2, line)), DMA((chunks + 1, line)), DMA((2, line)), DMA((line,)),
+            DMA((seqs,)), DMA((seqs,)), DMA((seqs,)), DMA((line,)), DMA((line,)), DMA((4,)), DMA((7,)),
+            DMA((chunks, 2, line)), DMA((chunks, line)), DMA((2, line)), DMA((line,)),
         ],
         compiler_params=pltpu.CompilerParams(
             collective_id=0, has_side_effects=True, vmem_limit_bytes=VMEM_LIMIT, dimension_semantics=("arbitrary",)
@@ -659,42 +682,143 @@
     return d_act * (sig * (1.0 + conv * (1.0 - sig)))
 
 
+class Stream:
+    def __init__(self, view, slots, sems):
+        self.view, self.slots, self.sems = view, slots, sems
+
+    def copy(self, block, turn):
+        slot = lax.rem(turn, 2)
+        return pltpu.make_async_copy(self.view(block), self.slots.at[slot], self.sems.at[slot])
+
+    def start(self, block, turn):
+        self.copy(block, turn).start()
+
+    def wait(self, block, turn):
+        self.copy(block, turn).wait()
+
+    def at(self, turn):
+        return self.slots.at[lax.rem(turn, 2)]
+
+
+class Fold:
+    def __init__(self, line, part, got, relay, sent, arrived, relayed):
+        self.line, self.part, self.got, self.relay = line, part, got, relay
+        self.sent, self.arrived, self.relayed = sent, arrived, relayed
+        self.mine = mine = lax.axis_index("head")
+        self.merges = line == 4
+        low = mine < 2
+        self.is_end = (mine == 0) | (mine == line - 1)
+        self.end, self.mid = jnp.where(low, 0, 3), jnp.where(low, 1, 2)
+        self.next, self.far = jnp.where(low, 2, 1), jnp.where(low, 3, 0)
+
+    def others(self, body):
+        @pl.loop(1, self.line)
+        def _(n):
+            body(lax.rem(self.mine + n, self.line))
+
+    def chunk(self, rows, piece, chunk, to, way):
+        return remote(
+            self.part(chunk, rows), self.got.at[self.mine, rows], self.sent.at[way, piece],
+            self.arrived.at[self.mine, piece], {"head": to},
+        )
+
+    def hand(self, rows, piece, chunk, which):
+        return remote(
+            self.part(chunk, rows), self.relay.at[which, rows], self.sent.at[1 + which, piece],
+            self.relayed.at[which, piece], {"head": self.mid},
+        )
+
+    def landed(self, rows, piece, source):
+        slot = self.got.at[source, rows]
+        return remote(slot, slot, self.sent.at[0, piece], self.arrived.at[source, piece], {"head": source})
+
+    def send(self, rows, piece):
+        if not self.merges:
+            if self.line > 1:
+                self.others(lambda to: self.chunk(rows, piece, to, to, to).start())
+            return
+
+        @pl.when(self.is_end)
+        def _():
+            self.hand(rows, piece, self.far, 1).start()
+            self.hand(rows, piece, self.next, 0).start()
+            self.chunk(rows, piece, self.mid, self.mid, 0).start()
+
+        @pl.when(jnp.logical_not(self.is_end))
+        def _():
+            self.chunk(rows, piece, self.end, self.end, 0).start()
+
+    def merge(self, rows, piece):
+        if self.merges:
+
+            @pl.when(jnp.logical_not(self.is_end))
+            def _():
+                for which, chunk in ((1, self.far), (0, self.next)):
+                    self.hand(rows, piece, chunk, which).wait_recv()
+                    own = self.part(chunk, rows)
+                    own[...] = (own[...].astype(WIDE) + self.relay[which, rows].astype(WIDE)).astype(LOW)
+                    self.chunk(rows, piece, chunk, chunk, 1 + which).start()
+
+    def drain(self, rows, piece):
+        if not self.merges:
+            if self.line > 1:
+                self.others(lambda to: self.chunk(rows, piece, to, to, to).wait_send())
+                self.others(lambda source: self.landed(rows, piece, source).wait_recv())
+            return
+        for way in range(3):
+            self.chunk(rows, piece, self.mid, self.mid, way).wait_send()
+        for source in (jnp.where(self.is_end, self.mid, self.end), self.next):
+            self.landed(rows, piece, source).wait_recv()
+
+    def total(self, rows, ref):
+        sum_ = self.part(self.mine, rows)[...].astype(WIDE)
+        if self.merges:
+            first = jnp.where(self.is_end, self.mid, self.end)
+            return sum_ + ref[first, rows].astype(WIDE) + ref[self.next, rows].astype(WIDE)
+        for n in range(1, self.line):
+            sum_ = sum_ + ref[lax.rem(self.mine + n, self.line), rows].astype(WIDE)
+        return sum_
+
+
 def core_kernel(
-    seqs, line, heads, blocks, flags, give,
-    gate, part, read, act, cum, raw, local, conv, pre, pre_before, normed, u, g_part,
-    state_in, r_t, w, postnorm, vec, prenorm, kernels, filters, rim,
-    out_recv, grad_recv, out_got, dx_got, gread_got, ggate_got, dw_got, addr_got, small_got,
-    ssd_s, din_s, dssd_s, dgate_s, starts, q, state, prod, g_buf, g_own, out_part, back_slots, back_msg, sums,
+    seqs, line, heads, blocks, roomy, flags, give,
+    gate_in, part_in, act_in, cum_in, raw_in, local_in, conv_in, pre_in, normed_in, u_in, g_part, r_in, w_in,
+    state_in, postnorm, vec, prenorm, kernels, filters, rim,
+    out_recv, grad_recv, out_far, dx_far, gread_got, ggate_got, dw_got, addr_got, small_got,
+    gate_b, part_b, read_b, cum_b, local_b, normed_b, act_b, raw_b, conv_b, pre_b, before_b, u_b, stream_sems,
+    r_t, w, ssd_s, din_s, dssd_s, dgate_s, ds_s, starts, q, state, prod, g_buf, out_part, back_slots, back_msg,
+    relay, dx_relay, out_near, dx_near, sums,
     totals, gread, ggate, gread_low, ggate_low, gpost, tiny, d_conv, d_step, after, edge_own, edge_got, ext,
+    keep_conv, keep_step, keep_normed, keep_u,
     taps_g, bias_g, dw, dw_low, da_low, da_got, da_send, pn, zs_send, zs_got, small, result, fin_send,
-    back_sent, back_sem, back_passed, sum_sent, sum_sem, line_sent, line_sem, load_sem, out_sent, out_sem,
-    w_sent, w_sem, dx_sent, dx_sem, edge_sent, edge_sem, zs_sent, zs_sem, da_sent, da_sem, small_sent, small_sem,
-    fin_sent, fin_sem, own_sem,
+    back_sent, back_sem, back_passed, sum_sent, sum_sem, line_sent, line_sem, load_sem, out_sent, out_sem, out_relayed,
+    w_sent, w_sem, dx_sent, dx_sem, dx_relayed, edge_sent, edge_sem, zs_sent, zs_sem, da_sent, da_sem, small_sent,
+    small_sem, fin_sent, fin_sem, own_sem, weight_sem,
 ):
-    i = pl.program_id(0)
     me, mine = lax.axis_index("seq"), lax.axis_index("head")
-    inner = gate.shape[1]
-    wide = act.shape[1]
+    inner = r_t.shape[1]
+    wide = act_b.shape[2]
     width = out_part.shape[2]
     depth = gread_got.shape[1]
+    rows = ssd_s.shape[0]
     size = 2 * STATE // line
-    phase = jnp.minimum(lax.div(i, blocks), 3)
-    turn = i - 3 * blocks
-    block = jnp.where(phase == 3, jnp.maximum(blocks - 1 - turn, 0), lax.rem(i, blocks))
-    first, second = flags[2 * block], flags[2 * block + 1]
     g_line = Line(line, g_buf, width, line_sent, line_sem)
     back_plane = Plane(seqs, lambda s: back_slots.at[s], back_sent, back_sem, back_passed, way=-1)
+    out_got, dx_got = (out_near, dx_near) if roomy else (out_far, dx_far)
 
     def group_rows(b):
         return pl.ds(pl.multiple_of(b * GROUP, GROUP), GROUP)
 
-    here = group_rows(block)
-
     def rows_of(device):
         return pl.ds(pl.multiple_of(device * depth, depth), depth)
 
     def shard_of(ref, shard):
         return ref.at[:, pl.ds(pl.multiple_of(shard * width, LANES), width)]
+
+    def by_group(ref, first=0, columns=None):
+        if columns is None:
+            return lambda b: ref.at[group_rows(b)]
+        return lambda b: ref.at[group_rows(b), pl.ds(first, columns)]
 
     def all_line(body):
         if line > 1:
@@ -708,12 +832,52 @@
         def _(n):
             body(lax.rem(me + n, seqs))
 
+    def before_rows(b):
+        start = jnp.maximum(b * GROUP - HALO, 0)
+        return pre_in.at[pl.ds(pl.multiple_of(start, HALO), HALO)]
+
+    views = (
+        (by_group(gate_in), gate_b), (by_group(part_in), part_b), (by_group(act_in, inner + STATE, STATE), read_b),
+        (by_group(cum_in), cum_b), (lambda b: local_in.at[b], local_b), (by_group(normed_in), normed_b),
+        (by_group(act_in), act_b), (by_group(raw_in), raw_b), (by_group(conv_in), conv_b), (by_group(pre_in), pre_b),
+        (before_rows, before_b), (by_group(u_in), u_b),
+    )
+    gate_f, part_f, read_f, cum_f, local_f, normed_f, act_f, raw_f, conv_f, pre_f, before_f, u_f = [
+        Stream(view, slots, stream_sems.at[n]) for n, (view, slots) in enumerate(views)
+    ]
+
+    def forwards(turn):
+        return turn
+
+    def backwards(turn):
+        return blocks - 1 - turn
+
+    def begin(streams, order):
+        for stream in streams:
+            stream.start(order(0), 0)
+
+    def step(streams, order, turn, following):
+        @pl.when(turn + 1 < blocks)
+        def _():
+            for stream in streams:
+                stream.start(order(turn + 1), turn + 1)
+
+        if following is not None:
+            pl.when(turn + 1 == blocks)(lambda: begin(*following))
+        for stream in streams:
+            stream.wait(order(turn), turn)
+
+    first_phase = ((gate_f, part_f, read_f, cum_f, local_f), forwards)
+    norm_phase = ((gate_f,), forwards)
+    gate_phase = ((gate_f, normed_f, read_f, cum_f), forwards)
+    scan_phase = ((act_f, cum_f, raw_f), forwards)
+    last_phase = ((act_f, cum_f, raw_f, conv_f, pre_f, before_f, normed_f, u_f), backwards)
+
     def each_load(body):
         def load(shard, n):
             return pltpu.make_async_copy(shard_of(g_part, shard), shard_of(g_buf, shard), load_sem.at[n])
 
         body(load(mine, 0))
-        body(pltpu.make_async_copy(shard_of(g_part, mine), g_own, load_sem.at[3]))
         if line > 1:
             pl.when(mine > 0)(lambda: body(load(mine - 1, 1)))
             pl.when(mine < line - 1)(lambda: body(load(mine + 1, 2)))
@@ -721,9 +885,6 @@
     def sum_copy(to, slot):
         return remote(sums.at[mine], sums.at[slot], sum_sent.at[to], sum_sem.at[slot], {"head": to})
 
-    def out_copy(to, slot):
-        return remote(out_part.at[to], out_got.at[slot], out_sent.at[to], out_sem.at[slot], {"head": to})
-
     weights = ((gread_low, gread_got), (ggate_low, ggate_got), (dw_low, dw_got), (da_low, da_got))
 
     def w_copy(which, to, slot):
@@ -736,11 +897,24 @@
     def w_wait(which):
         all_seq(lambda other: w_copy(which, other, other).wait())
 
-    def dx_copy(to, slot, b):
-        return remote(
-            shard_of(g_buf.at[group_rows(b)], to), dx_got.at[slot, group_rows(b)], dx_sent.at[to, b],
-            dx_sem.at[slot, b], {"head": to},
-        )
+    out_fold = Fold(
+        line, lambda z, at: out_part.at[z, at], out_got, relay, out_sent, out_sem, out_relayed
+    )
+    dx_fold = Fold(
+        line, lambda z, at: shard_of(g_buf.at[at], z), dx_got, dx_relay, dx_sent, dx_sem, dx_relayed
+    )
+    short_piece = (pl.ds(rows - GROUP, GROUP - HALO), blocks - 1)
+    edge_piece = (pl.ds(rows - HALO, HALO), blocks)
+
+    def each_piece(body):
+        body(*short_piece)
+
+        @pl.loop(1, blocks)
+        def _(turn):
+            b = blocks - 1 - turn
+            body(group_rows(b), b)
+
+        body(*edge_piece)
 
     def edge_copy(to):
         return remote(edge_own, edge_got, edge_sent, edge_sem, {"seq": to})
@@ -763,15 +937,13 @@
         )
 
     own_copies = {
-        "out": pltpu.make_async_copy(out_part.at[mine], out_got.at[mine], own_sem.at[0]),
-        "gread": pltpu.make_async_copy(gread_low.at[rows_of(me)], gread_got.at[me], own_sem.at[1]),
-        "ggate": pltpu.make_async_copy(ggate_low.at[rows_of(me)], ggate_got.at[me], own_sem.at[2]),
-        "dw": pltpu.make_async_copy(dw_low.at[rows_of(me)], dw_got.at[me], own_sem.at[3]),
-        "dx": pltpu.make_async_copy(shard_of(g_buf, mine), dx_got.at[mine], own_sem.at[4]),
-        "addr": pltpu.make_async_copy(da_send.at[mine], addr_got.at[mine], own_sem.at[5]),
-        "small": pltpu.make_async_copy(small, small_got.at[me], own_sem.at[6]),
-        "fin0": pltpu.make_async_copy(fin_send.at[0, me], out_recv.at[me], own_sem.at[7]),
-        "fin1": pltpu.make_async_copy(fin_send.at[1, me], grad_recv.at[me], own_sem.at[8]),
+        "gread": pltpu.make_async_copy(gread_low.at[rows_of(me)], gread_got.at[me], own_sem.at[0]),
+        "ggate": pltpu.make_async_copy(ggate_low.at[rows_of(me)], ggate_got.at[me], own_sem.at[1]),
+        "dw": pltpu.make_async_copy(dw_low.at[rows_of(me)], dw_got.at[me], own_sem.at[2]),
+        "addr": pltpu.make_async_copy(da_send.at[mine], addr_got.at[mine], own_sem.at[3]),
+        "small": pltpu.make_async_copy(small, small_got.at[me], own_sem.at[4]),
+        "fin0": pltpu.make_async_copy(fin_send.at[0, me], out_recv.at[me], own_sem.at[5]),
+        "fin1": pltpu.make_async_copy(fin_send.at[1, me], grad_recv.at[me], own_sem.at[6]),
     }
 
     def route(which):
@@ -783,78 +955,100 @@
         fin_send[which, me] = result[which, give[me]]
         own_copies["fin%d" % which].start()
 
+    def fetch(src):
+        if not roomy:
+            all_line(lambda z: pltpu.make_async_copy(src.at[z], out_part.at[z], load_sem.at[0]).start())
+            all_line(lambda z: pltpu.make_async_copy(src.at[z], out_part.at[z], load_sem.at[0]).wait())
+
     row = lax.broadcasted_iota(jnp.int32, (GROUP, LANES), 0)
     lane = lax.broadcasted_iota(jnp.int32, (GROUP, LANES), 1)
-
-    def entry_of(cum_v, spread_m):
-        return to_columns(jnp.exp(cum_v) * (first * jnp.where(row < BLOCK, 1.0, second)), spread_m)
+    spread_m, collect = head_rows(inner), head_columns(inner)
+    lower_mask = ones_before(BLOCK)
+    top, low = slice(0, BLOCK), slice(BLOCK, GROUP)
+
+    def entry_of(b, cum_v):
+        gone_on = flags[2 * b] * jnp.where(row < BLOCK, 1.0, flags[2 * b + 1])
+        return to_columns(jnp.exp(cum_v) * gone_on, spread_m)
+
+    def carry_of(b, cum_t):
+        return jnp.exp(cum_t[:, GROUP - 1 : GROUP]) * (flags[2 * b] * flags[2 * b + 1])
 
     def row_stats(b):
         stats = jnp.concatenate([totals[b], jnp.zeros((LANES - EDGE, GROUP), WIDE)], axis=0).T
         return lax.rsqrt(stats[:, 0:1] / INNER + EPS), stats[:, 1:2]
 
-    def gated_of(ssd):
-        gate_v = gate[...]
+    def gated_of(ssd, turn):
+        gate_v = gate_f.at(turn)[...]
         return ssd * (gate_v * sigmoid(gate_v))
 
-    @pl.when(i == 0)
-    def _():
-        greet(seqs, line)
-        g_line.hop(1, take=False, source=lambda shard: shard_of(g_part, shard))
-        each_load(lambda copy: copy.start())
-        state[...] = state_in[...]
-
-    @pl.when(phase == 0)
-    def _():
-        spread_m, collect = head_rows(inner), head_columns(inner)
-        cum_v = cum[...]
-        carry = jnp.exp(cum_v.T[:, GROUP - 1 : GROUP]) * (first * second)
+    begin(*first_phase)
+    fetch_r = pltpu.make_async_copy(r_in, r_t, weight_sem.at[0])
+    fetch_w = pltpu.make_async_copy(w_in, w, weight_sem.at[1])
+    fetch_r.start()
+    greet(seqs, line)
+    g_line.hop(1, take=False, source=lambda shard: shard_of(g_part, shard))
+    each_load(lambda copy: copy.start())
+    fetch_w.start()
+    state[...] = state_in[...]
+    fetch_r.wait()
+
+    @pl.loop(0, blocks)
+    def _(b):
+        step(*first_phase, b, norm_phase)
+        here = group_rows(b)
+        cum_v = cum_f.at(b)[...]
         start = state[...]
-        starts[block] = start
-        ssd = part[...] + entry_of(cum_v, spread_m) * nt(read[...], start.astype(LOW))
+        starts[b] = start
+        ssd = part_f.at(b)[...] + entry_of(b, cum_v) * nt(read_f.at(b)[...], start.astype(LOW))
         ssd_s[here, :] = ssd
-        state[...] = carry_columns(carry, collect) * start + local[0]
-        out = nt((gated_of(ssd) * postnorm[...]).astype(LOW), r_t[...])
+        state[...] = carry_columns(carry_of(b, cum_v.T), collect) * start + local_f.at(b)[...]
+        out = nt((gated_of(ssd, b) * postnorm[...]).astype(LOW), r_t[...])
         for z in range(line):
             out_part[z, here] = out[:, z * width : (z + 1) * width].astype(LOW)
-
-    @pl.when(i == blocks - 1)
-    def _():
-        for step in range(2, line):
-            g_line.hop(step)
-        each_load(lambda copy: copy.wait())
-        g_line.finish(None, range(1, line - 1))
-
-    @pl.when(phase == 1)
-    def _():
-        gated = gated_of(ssd_s[here, :])
+        if out_fold.merges:
+            pl.when(out_fold.is_end)(lambda: out_fold.send(here, b))
+
+    for hop in range(2, line):
+        g_line.hop(hop)
+    each_load(lambda copy: copy.wait())
+    g_line.finish(None, range(1, line - 1))
+    fetch_w.wait()
+
+    @pl.loop(0, blocks)
+    def _(b):
+        step(*norm_phase, b, gate_phase)
+        here = group_rows(b)
+        gated = gated_of(ssd_s[here, :], b)
         d_inner = nn(g_buf[here, :], r_t[...])
         din_s[here, :] = d_inner
         squares = jnp.sum(gated * gated, axis=1, keepdims=True)
         dots = jnp.sum(gated * postnorm[...] * d_inner, axis=1, keepdims=True)
         both = jnp.where(lane == 0, squares, jnp.where(lane == 1, dots, 0.0)).T
-        sums[mine, block] = both[:EDGE]
-
-    @pl.when(i == 2 * blocks - 1)
-    def _():
-        all_line(lambda to: sum_copy(to, mine).start())
-        gread[...] = jnp.zeros_like(gread)
-        ggate[...] = jnp.zeros_like(ggate)
-        gpost[...] = jnp.zeros_like(gpost)
-        state[...] = jnp.zeros_like(state)
-        prod[...] = jnp.ones_like(prod)
-        all_line(lambda other: sum_copy(other, other).wait())
-        totals[...] = jnp.sum(sums[...], axis=0)
-        all_line(lambda to: out_copy(to, mine).start())
-        own_copies["out"].start()
-
-    @pl.when(phase == 2)
-    def _():
-        spread_m, collect = head_rows(inner), head_columns(inner)
-        cum_v = cum[...]
-        carry = jnp.exp(cum_v.T[:, GROUP - 1 : GROUP]) * (first * second)
-        inv, dot = row_stats(block)
-        gate_v = gate[...]
+        sums[mine, b] = both[:EDGE]
+
+    all_line(lambda to: sum_copy(to, mine).start())
+    for ref in (gread, ggate, gpost, state, tiny, taps_g, bias_g, dw, pn):
+        ref[...] = jnp.zeros_like(ref)
+    prod[...] = jnp.ones_like(prod)
+    all_line(lambda other: sum_copy(other, other).wait())
+    totals[...] = jnp.sum(sums[...], axis=0)
+
+    @pl.loop(0, blocks)
+    def _(b):
+        here = group_rows(b)
+        if out_fold.merges:
+            pl.when(jnp.logical_not(out_fold.is_end))(lambda: out_fold.send(here, b))
+        else:
+            out_fold.send(here, b)
+        out_fold.merge(here, b)
+
+    @pl.loop(0, blocks)
+    def _(b):
+        step(*gate_phase, b, scan_phase)
+        here = group_rows(b)
+        cum_v = cum_f.at(b)[...]
+        inv, dot = row_stats(b)
+        gate_v = gate_f.at(b)[...]
         sig = sigmoid(gate_v)
         ssd = ssd_s[here, :]
         d_inner = din_s[here, :]
@@ -868,61 +1062,39 @@
         dssd_s[here, :] = d_ssd
         dgate_s[here, :] = d_gate
         gread[...] += tn(g_buf[here, :], inner_normed)
-        ggate[...] += tn(normed[...], d_gate)
-        query_grad = (d_ssd.astype(WIDE) * entry_of(cum_v, spread_m)).astype(LOW)
-        found = tn(query_grad, read[...])
-        q[block] = found
+        ggate[...] += tn(normed_f.at(b)[...], d_gate)
+        query_grad = (d_ssd.astype(WIDE) * entry_of(b, cum_v)).astype(LOW)
+        found = tn(query_grad, read_f.at(b)[...])
+        q[b] = found
         state[...] += carry_columns(prod[...], collect) * found
-        prod[...] = prod[...] * carry
-
-    @pl.when(i == 3 * blocks - 1)
-    def _():
-        back_msg[:inner, :] = state[...].astype(LOW)
-        back_msg[inner:, :] = jnp.broadcast_to(prod[:HALO], (HALO, STATE)).astype(LOW)
-        back_plane.start(back_msg)
-        gread_low[...] = gread[...].astype(LOW)
-        ggate_low[...] = ggate[...].astype(LOW)
-        for ref in (tiny, taps_g, bias_g, dw, pn):
-            ref[...] = jnp.zeros_like(ref)
-        back_plane.relay()
-        back_plane.finish(back_msg)
-        w_start(0)
-        w_start(1)
-        own_copies["gread"].start()
-        own_copies["ggate"].start()
-        state[...] = fold_states(
-            back_slots, head_columns(inner), inner, seqs - 1, me, -1, jnp.zeros((inner, STATE), WIDE)
-        )
-
-    @pl.when((phase == 3) & (turn < blocks))
-    def _():
-        slot = jnp.where(turn == 0, 1, 0)
-        spread_m, collect = head_rows(inner), head_columns(inner)
-        lower_mask = ones_before(BLOCK)
-        top, low = slice(0, BLOCK), slice(BLOCK, GROUP)
-        cum_v = cum[...]
+        prod[...] = prod[...] * carry_of(b, cum_v.T)
+
+    back_msg[:inner, :] = state[...].astype(LOW)
+    back_msg[inner:, :] = jnp.broadcast_to(prod[:HALO], (HALO, STATE)).astype(LOW)
+    back_plane.start(back_msg)
+    gread_low[...] = gread[...].astype(LOW)
+    ggate_low[...] = ggate[...].astype(LOW)
+    w_start(0)
+    w_start(1)
+    own_copies["gread"].start()
+    own_copies["ggate"].start()
+
+    @pl.loop(0, blocks)
+    def _(b):
+        step(*scan_phase, b, last_phase)
+        here = group_rows(b)
+        second = flags[2 * b + 1]
+        act = act_f.at(b)
+        cum_v = cum_f.at(b)[...]
         cum_t = cum_v.T
-        steps, sig, ratio = step_terms(raw[...], heads)
+        steps, _, _ = step_terms(raw_f.at(b)[...], heads)
         steps_t = steps.T
-        scale = -jnp.exp(vec[1:2, :])
-        last = cum_v[GROUP - 1 : GROUP, :]
         write = act[:, inner : inner + STATE]
         read_v = act[:, inner + STATE :]
         s00 = jnp.where(lower_mask, nt(read_v[top], write[top]), 0.0)
         s10 = nt(read_v[low], write[top]) * second
         s11 = jnp.where(lower_mask, nt(read_v[low], write[low]), 0.0)
 
-        end = state[...]
-        end_low = end.astype(LOW)
-        start = starts[block]
-        carry = jnp.exp(cum_t[:, GROUP - 1 : GROUP]) * (first * second)
-        state[...] = carry_columns(carry, collect) * end + q[block]
-        weight = steps * jnp.exp(last - cum_v) * jnp.where(row < BLOCK, second, 1.0)
-        weight_w = to_columns(weight, spread_m)
-        d_ssd = dssd_s[here, :]
-        d_query = (d_ssd.astype(WIDE) * entry_of(cum_v, spread_m)).astype(LOW)
-        through_w = to_columns(jnp.broadcast_to(vec[2:3, :], (EDGE, LANES)), spread_m)[0:1]
-
         def decay_of(head, t, s):
             decay = jnp.exp(jnp.minimum(cum_v[t, head : head + 1] - cum_t[head : head + 1, s], 0.0))
             return decay * steps_t[head : head + 1, s]
@@ -930,14 +1102,10 @@
         ds00 = jnp.zeros((BLOCK, BLOCK), WIDE)
         ds10 = jnp.zeros((BLOCK, BLOCK), WIDE)
         ds11 = jnp.zeros((BLOCK, BLOCK), WIDE)
-        packed, value_parts, tails = [], [], []
-        d_packed = nt(write, end_low)
         for pair in range(inner // LANES):
             columns = slice(pair * LANES, (pair + 1) * LANES)
             values = act[:, columns]
-            values_f = values.astype(WIDE)
-            dy = d_ssd[:, columns]
-            dys = pair_lanes(dy)
+            dys = pair_lanes(dssd_s[here, columns])
             m00, m10, m11 = [], [], []
             for k in range(2):
                 head = 2 * pair + k
@@ -954,32 +1122,59 @@
             v1 = tn(
                 jnp.concatenate([m11[0], m11[1]], axis=0), jnp.concatenate([dys[0][low], dys[1][low]], axis=0)
             )
-            tail = d_packed[:, columns] * weight_w[:, columns]
-            whole = jnp.concatenate([v0, v1], axis=0) + tail
-            d_conv[slot, :, columns] = conv_grad(
-                whole + through_w[:, columns] * dy.astype(WIDE), conv[:, columns]
-            )
-            value_parts.append(values_f * whole)
-            tails.append(jnp.sum(tail * values_f, axis=0, keepdims=True))
-            packed.append((values_f * weight_w[:, columns]).astype(LOW))
-
-        ds = jnp.concatenate(
+            din_s[here, columns] = jnp.concatenate([v0, v1], axis=0)
+        ds_s[here, :] = jnp.concatenate(
             [
                 jnp.concatenate([jnp.where(lower_mask, ds00, 0.0), jnp.zeros((BLOCK, BLOCK), WIDE)], axis=1),
                 jnp.concatenate([ds10 * second, jnp.where(lower_mask, ds11, 0.0)], axis=1),
             ],
             axis=0,
         ).astype(LOW)
+
+        @pl.when(b == blocks // 2)
+        def _():
+            back_plane.relay()
+
+    back_plane.finish(back_msg)
+    state[...] = fold_states(back_slots, collect, inner, seqs - 1, me, -1, jnp.zeros((inner, STATE), WIDE))
+    taps = jnp.concatenate([kernels[...], filters[...]], axis=1)
+    scale = -jnp.exp(vec[1:2, :])
+    through_w = to_columns(jnp.broadcast_to(vec[2:3, :], (EDGE, LANES)), spread_m)[0:1]
+
+    def scan_back(b, turn):
+        here = group_rows(b)
+        first, second = flags[2 * b], flags[2 * b + 1]
+        act, conv = act_f.at(turn), conv_f.at(turn)
+        cum_v = cum_f.at(turn)[...]
+        steps, sig, ratio = step_terms(raw_f.at(turn)[...], heads)
+        last = cum_v[GROUP - 1 : GROUP, :]
+        write = act[:, inner : inner + STATE]
+        read_v = act[:, inner + STATE :]
+        end = state[...]
+        end_low = end.astype(LOW)
+        start = starts[b]
+        state[...] = carry_columns(carry_of(b, cum_v.T), collect) * end + q[b]
+        weight = steps * jnp.exp(last - cum_v) * jnp.where(row < BLOCK, second, 1.0)
+        weight_w = to_columns(weight, spread_m)
+        d_ssd = dssd_s[here, :]
+        dy_f = d_ssd.astype(WIDE)
+        values_f = act[:, :inner].astype(WIDE)
+        d_query = (dy_f * entry_of(b, cum_v)).astype(LOW)
+        tail = nt(write, end_low) * weight_w
+        whole = din_s[here, :] + tail
+        d_conv[:, :inner] = conv_grad(whole + through_w * dy_f, conv[:, :inner])
+        packed = (values_f * weight_w).astype(LOW)
+        ds = ds_s[here, :]
         d_read = nn(ds, write) + nn(d_query, start.astype(LOW))
-        d_write = tn(ds, read_v) + nn(jnp.concatenate(packed, axis=1), end_low)
-        d_conv[slot, :, inner : inner + STATE] = conv_grad(d_write, conv[:, inner : inner + STATE])
-        d_conv[slot, :, inner + STATE :] = conv_grad(d_read, conv[:, inner + STATE :])
-
-        dy_f = d_ssd.astype(WIDE)
-        own = to_heads(dy_f * act[:, :inner].astype(WIDE), collect)
+        d_write = tn(ds, read_v) + nn(packed, end_low)
+        d_conv[:, inner : inner + STATE] = conv_grad(d_write, conv[:, inner : inner + STATE])
+        d_conv[:, inner + STATE :] = conv_grad(d_read, conv[:, inner + STATE :])
+
+        own = to_heads(dy_f * values_f, collect)
         r1 = to_heads(dy_f * ssd_s[here, :], collect) - vec[2:3, :] * own
-        by_value = to_heads(jnp.concatenate(value_parts, axis=1), collect)
-        tail_row = to_heads(jnp.broadcast_to(jnp.concatenate(tails, axis=1), (EDGE, inner)), collect)[0:1]
+        by_value = to_heads(values_f * whole, collect)
+        tail_sum = jnp.sum(tail * values_f, axis=0, keepdims=True)
+        tail_row = to_heads(jnp.broadcast_to(tail_sum, (EDGE, inner)), collect)[0:1]
         high, rest = halves(end * start)
         ones = jnp.ones((EDGE, STATE), LOW)
         carry_grad = to_heads(nt(ones, high) + nt(ones, rest), collect)[0:1]
@@ -987,33 +1182,36 @@
         d_cum = r1 - by_value + jnp.where(row == GROUP - 1, d_last, 0.0)
         d_rate = sum_after(d_cum)
         d_raw = d_rate * scale * sig + by_value * ratio
-        d_step[slot] = d_raw.astype(LOW)
+        d_step[...] = d_raw.astype(LOW)
         tiny[0:1, :] += jnp.sum(d_raw, axis=0, keepdims=True)
         tiny[1:2, :] += jnp.sum(d_rate * steps, axis=0, keepdims=True) * scale
         tiny[2:3, :] += jnp.sum(own, axis=0, keepdims=True)
 
-    @pl.when(turn == blocks - 1)
-    def _():
-        edge_own[...] = d_conv[jnp.where(turn == 0, 1, 0), 0:EDGE, :]
-        edge_copy(lax.rem(me + seqs - 1, seqs)).start()
-
-    @pl.when(turn == blocks)
-    def _():
-        edge_copy(lax.rem(me + 1, seqs)).wait()
-        after[...] = edge_got[...]
-
-    @pl.when(turn >= 1)
-    def _():
-        final = turn == blocks
-        slot = jnp.where(final, 1, 0)
-        b = jnp.where(final, blocks - 1, blocks - 1 - turn)
-        at_b = group_rows(b)
-        taps = jnp.concatenate([kernels[...], filters[...]], axis=1)
-        grad_c = d_conv[slot]
-        pre_v = pre[...].astype(WIDE)
-        before = jnp.where(b == 0, rim[...], pre_before[HALO - EDGE :, :].astype(WIDE))
+    def conv_back(ref, count):
+        total = taps[TAPS - 1 : TAPS] * ref[pl.ds(0, count), :]
+        for tap in range(TAPS - 1):
+            total = total + taps[tap : tap + 1] * ref[pl.ds(TAPS - 1 - tap, count), :]
+        return total.astype(LOW)
+
+    def input_back(d_pre, step_grad, gate_grad, u_rows):
+        d_normed = (
+            nt(gate_grad, w[:, :inner])
+            + nt(d_pre, w[:, inner : inner + wide])
+            + nt(step_grad, w[:, inner + wide :])
+        )
+        rows_f = u_rows.astype(WIDE)
+        inv = lax.rsqrt(jnp.mean(rows_f * rows_f, axis=1, keepdims=True) + EPS)
+        gained = d_normed * prenorm[...]
+        dot = jnp.sum(gained * rows_f, axis=1, keepdims=True)
+        grad = gained * inv - rows_f * (inv * inv * inv / D * dot)
+        return grad.astype(LOW), d_normed * (rows_f * inv)
+
+    def rows_back(b, turn, final):
+        grad_c = d_conv[...]
+        pre_v = pre_f.at(turn)[...].astype(WIDE)
+        before = jnp.where(b == 0, rim[...], before_f.at(turn)[HALO - EDGE :, :].astype(WIDE))
         bias_g[...] += jnp.sum(grad_c, axis=0, keepdims=True)
-        d_pre = []
+        parts = []
         for half in range(2):
             part_rows = slice(half * BLOCK, (half + 1) * BLOCK)
             tile = grad_c[part_rows]
@@ -1024,126 +1222,160 @@
                     tile * ext[pl.ds(EDGE - (TAPS - 1) + tap, BLOCK), :], axis=0, keepdims=True
                 )
             ext[:BLOCK, :] = tile
-            ext[BLOCK:, :] = (grad_c[BLOCK : BLOCK + EDGE] if half == 0 else after[...]) * flags[2 * b + half + 1]
-            total = taps[TAPS - 1 : TAPS] * ext[:BLOCK, :]
-            for tap in range(TAPS - 1):
-                total = total + taps[tap : tap + 1] * ext[pl.ds(TAPS - 1 - tap, BLOCK), :]
-            d_pre.append(total.astype(LOW))
-        d_pre = jnp.concatenate(d_pre, axis=0)
-        step_grad = d_step[slot]
-        normed_v = normed[...]
+            if half == 0:
+                ext[BLOCK:, :] = grad_c[BLOCK : BLOCK + EDGE] * flags[2 * b + 1]
+            elif final:
+                ext[BLOCK:, :] = jnp.zeros((EDGE, wide), WIDE)
+            else:
+                ext[BLOCK:, :] = after[...] * flags[2 * b + 2]
+            parts.append(conv_back(ext, BLOCK))
+        d_pre = jnp.concatenate(parts, axis=0)
+        step_grad = d_step[...]
+        normed_v = normed_f.at(turn)[...]
+        u_v = u_f.at(turn)
+        done = lax.broadcasted_iota(jnp.int32, (GROUP, 1), 0) < GROUP - HALO
+        if final:
+            d_pre = jnp.where(done, d_pre, jnp.zeros_like(d_pre))
+            keep_conv[:HALO, :] = grad_c[GROUP - HALO :]
+            keep_step[...] = step_grad[GROUP - HALO :]
+            keep_normed[...] = normed_v[GROUP - HALO :]
+            keep_u[...] = u_v[GROUP - HALO :, :]
         dw[:, :wide] += tn(normed_v, d_pre)
         dw[:, wide:] += tn(normed_v, step_grad)
-        d_normed = (
-            nt(dgate_s[at_b, :], w[:, :inner])
-            + nt(d_pre, w[:, inner : inner + wide])
-            + nt(step_grad, w[:, inner + wide :])
-        )
-        u_f = u[...].astype(WIDE)
-        inv = lax.rsqrt(jnp.mean(u_f * u_f, axis=1, keepdims=True) + EPS)
-        gained = d_normed * prenorm[...]
-        dot = jnp.sum(gained * u_f, axis=1, keepdims=True)
-        grad = gained * inv - u_f * (inv * inv * inv / D * dot)
-        pn[...] += jnp.sum(d_normed * (u_f * inv), axis=0, keepdims=True)
-        g_buf[at_b, :] = grad.astype(LOW)
-        all_line(lambda to: dx_copy(to, mine, b).start())
-        result[0, 2 * b] = u[0:BLOCK, pl.ds(pl.multiple_of(mine * width, LANES), width)]
-        result[0, 2 * b + 1] = u[BLOCK:, pl.ds(pl.multiple_of(mine * width, LANES), width)]
-
-    @pl.when((turn >= 0) & (turn < blocks))
-    def _():
-        after[...] = d_conv[jnp.where(turn == 0, 1, 0), 0:EDGE, :]
-
-    @pl.when(turn == blocks)
-    def _():
-        own_copies["dx"].start()
-        dw_low[:, :inner] = dw[:, :inner].astype(LOW)
-        dw_low[:, inner:] = dw[:, wide:].astype(LOW)
-        da_low[...] = dw[:, inner:wide].astype(LOW)
-        w_start(3)
-        w_start(2)
-        own_copies["dw"].start()
-        da_got[me] = da_low[rows_of(me), :]
-
-        for z in range(line):
-            slab = z * size // LANES * LANES
-            zs_send[z] = jnp.zeros(zs_send.shape[1:], WIDE)
-            zs_send[z, 0:1, :] = pn[:, z * width : (z + 1) * width]
-            zs_send[z, EDGE : EDGE + TAPS, :LANES] = taps_g[0:TAPS, inner + slab : inner + slab + LANES]
-            zs_send[z, EDGE + TAPS : EDGE + TAPS + 1, :LANES] = bias_g[:, inner + slab : inner + slab + LANES]
-        zs_got[mine] = zs_send[mine]
-        all_line(lambda to: zs_copy(to, mine).start())
-
-        all_line(lambda other: out_copy(other, other).wait())
-        own_copies["out"].wait()
-
-        def fetch(src, n):
-            return pltpu.make_async_copy(src, out_part, load_sem.at[n])
-
-        fetch(out_got, 0).start()
-        fetch(out_got, 0).wait()
-
-        @pl.loop(0, blocks)
-        def _(b):
-            inv, _ = row_stats(b)
-            total = out_part[0, group_rows(b)].astype(WIDE)
-            for z in range(1, line):
-                total = total + out_part[z, group_rows(b)].astype(WIDE)
-            total = total * inv
-            result[0, 2 * b] = (result[0, 2 * b].astype(WIDE) + total[:BLOCK]).astype(LOW)
-            result[0, 2 * b + 1] = (result[0, 2 * b + 1].astype(WIDE) + total[BLOCK:]).astype(LOW)
-
-        route(0)
-        all_line(lambda other: zs_copy(other, other).wait())
-        from_line = jnp.sum(zs_got[...], axis=0)
-        small[...] = jnp.zeros_like(small)
-        small[0:TAPS, :inner] = taps_g[0:TAPS, :inner]
-        small[0:TAPS, inner:] = from_line[EDGE : EDGE + TAPS, :LANES]
-        small[4:5, :inner] = bias_g[:, :inner]
-        small[4:5, inner:] = from_line[EDGE + TAPS : EDGE + TAPS + 1, :LANES]
-        small[5:6, :inner] = gpost[...]
-        small[6:7, :width] = from_line[0:1]
-        for n in range(3):
-            small[7:8, n * LANES : (n + 1) * LANES] = tiny[n : n + 1, :]
-        own_copies["small"].start()
-        all_seq(lambda to: small_copy(to, me).start())
-
-        w_wait(3)
-        from_plane = da_got[0].astype(WIDE)
-        for n in range(1, seqs):
-            from_plane = from_plane + da_got[n].astype(WIDE)
-        for z in range(line):
-            slab = z * size // LANES * LANES
-            da_send[z] = from_plane[:, slab : slab + LANES]
-        own_copies["addr"].start()
-        all_line(lambda to: da_copy(to, mine).start())
-
-        @pl.loop(0, blocks)
-        def _(b):
-            all_line(lambda other: dx_copy(other, other, b).wait())
-
-        own_copies["dx"].wait()
-        fetch(dx_got, 1).start()
-        fetch(dx_got, 1).wait()
-
-        @pl.loop(0, blocks)
-        def _(b):
-            total = out_part[0, group_rows(b)].astype(WIDE)
-            for z in range(1, line):
-                total = total + out_part[z, group_rows(b)].astype(WIDE)
-            done = (g_own[group_rows(b), :].astype(WIDE) + total).astype(LOW)
-            result[1, 2 * b] = done[:BLOCK]
-            result[1, 2 * b + 1] = done[BLOCK:]
-
-        route(1)
-        for which in range(3):
-            w_wait(which)
-        all_line(lambda other: da_copy(other, other).wait())
-        all_seq(lambda other: small_copy(other, other).wait())
-        all_seq(lambda other: fin_copy(0, other, other).wait())
-        all_seq(lambda other: fin_copy(1, other, other).wait())
-        for name in ("gread", "ggate", "dw", "addr", "small", "fin0", "fin1"):
-            own_copies[name].wait()
+        grad, gain = input_back(d_pre, step_grad, dgate_s[group_rows(b), :], u_v[...])
+        pn[...] += jnp.sum(jnp.where(done, gain, 0.0) if final else gain, axis=0, keepdims=True)
+        g_buf[group_rows(b), :] = grad
+        own_columns = pl.ds(pl.multiple_of(mine * width, LANES), width)
+        result[0, 2 * b] = u_v[0:BLOCK, own_columns]
+        result[0, 2 * b + 1] = u_v[BLOCK:, own_columns]
+        after[...] = grad_c[0:EDGE]
+
+    step(*last_phase, 0, None)
+    scan_back(blocks - 1, 0)
+    rows_back(blocks - 1, 0, True)
+    dx_fold.send(*short_piece)
+
+    @pl.loop(1, blocks)
+    def _(turn):
+        b = blocks - 1 - turn
+        step(*last_phase, turn, None)
+        scan_back(b, turn)
+
+        @pl.when(b == 0)
+        def _():
+            edge_own[...] = d_conv[0:EDGE, :]
+            edge_copy(lax.rem(me + seqs - 1, seqs)).start()
+
+        rows_back(b, turn, False)
+        dx_fold.send(group_rows(b), b)
+
+        @pl.when(turn == 2)
+        def _():
+            dx_fold.merge(*short_piece)
+
+        @pl.when(turn > 2)
+        def _():
+            dx_fold.merge(group_rows(b + 2), b + 2)
+
+    edge_copy(lax.rem(me + 1, seqs)).wait()
+    keep_conv[HALO:, :] = edge_got[...] * flags[2 * blocks]
+    d_edge = conv_back(keep_conv, HALO)
+    dw[:, :wide] += tn(keep_normed[...], d_edge)
+    grad, gain = input_back(d_edge, keep_step[...], dgate_s[pl.ds(rows - HALO, HALO), :], keep_u[...])
+    pn[...] += jnp.sum(gain, axis=0, keepdims=True)
+    g_buf[pl.ds(rows - HALO, HALO), :] = grad
+    dx_fold.send(*edge_piece)
+
+    da_low[...] = dw[:, inner:wide].astype(LOW)
+    w_start(3)
+    dw_low[:, :inner] = dw[:, :inner].astype(LOW)
+    dw_low[:, inner:] = dw[:, wide:].astype(LOW)
+    w_start(2)
+    own_copies["dw"].start()
+    da_got[me] = da_low[rows_of(me), :]
+
+    for z in range(line):
+        slab = z * size // LANES * LANES
+        zs_send[z] = jnp.zeros(zs_send.shape[1:], WIDE)
+        zs_send[z, 0:1, :] = pn[:, z * width : (z + 1) * width]
+        zs_send[z, EDGE : EDGE + TAPS, :LANES] = taps_g[0:TAPS, inner + slab : inner + slab + LANES]
+        zs_send[z, EDGE + TAPS : EDGE + TAPS + 1, :LANES] = bias_g[:, inner + slab : inner + slab + LANES]
+    zs_got[mine] = zs_send[mine]
+    all_line(lambda to: zs_copy(to, mine).start())
+
+    if blocks > 3:
+
+        @pl.loop(0, 2)
+        def _(n):
+            dx_fold.merge(group_rows(1 - n), 1 - n)
+
+    elif blocks == 2:
+        dx_fold.merge(*short_piece)
+        dx_fold.merge(group_rows(0), 0)
+    dx_fold.merge(*edge_piece)
+
+    @pl.loop(0, blocks)
+    def _(b):
+        out_fold.drain(group_rows(b), b)
+
+    fetch(out_far)
+
+    @pl.loop(0, blocks)
+    def _(b):
+        inv, _ = row_stats(b)
+        total = out_fold.total(group_rows(b), out_near if roomy else out_part) * inv
+        result[0, 2 * b] = (result[0, 2 * b].astype(WIDE) + total[:BLOCK]).astype(LOW)
+        result[0, 2 * b + 1] = (result[0, 2 * b + 1].astype(WIDE) + total[BLOCK:]).astype(LOW)
+
+    route(0)
+    own_g = pltpu.make_async_copy(shard_of(g_part, mine), out_part.at[mine], load_sem.at[3])
+    own_g.start()
+
+    w_wait(3)
+    from_plane = da_got[0].astype(WIDE)
+    for n in range(1, seqs):
+        from_plane = from_plane + da_got[n].astype(WIDE)
+    for z in range(line):
+        slab = z * size // LANES * LANES
+        da_send[z] = from_plane[:, slab : slab + LANES]
+    own_copies["addr"].start()
+    all_line(lambda to: da_copy(to, mine).start())
+
+    each_piece(dx_fold.drain)
+    fetch(dx_far)
+    own_g.wait()
+
+    @pl.loop(0, blocks)
+    def _(b):
+        here = group_rows(b)
+        total = dx_fold.total(here, dx_near if roomy else out_part)
+        done = (out_part[mine, here].astype(WIDE) + total).astype(LOW)
+        result[1, 2 * b] = done[:BLOCK]
+        result[1, 2 * b + 1] = done[BLOCK:]
+
+    route(1)
+    all_line(lambda other: zs_copy(other, other).wait())
+    from_line = jnp.sum(zs_got[...], axis=0)
+    small[...] = jnp.zeros_like(small)
+    small[0:TAPS, :inner] = taps_g[0:TAPS, :inner]
+    small[0:TAPS, inner:] = from_line[EDGE : EDGE + TAPS, :LANES]
+    small[4:5, :inner] = bias_g[:, :inner]
+    small[4:5, inner:] = from_line[EDGE + TAPS : EDGE + TAPS + 1, :LANES]
+    small[5:6, :inner] = gpost[...]
+    small[6:7, :width] = from_line[0:1]
+    for n in range(3):
+        small[7:8, n * LANES : (n + 1) * LANES] = tiny[n : n + 1, :]
+    own_copies["small"].start()
+    all_seq(lambda to: small_copy(to, me).start())
+
+    for which in range(3):
+        w_wait(which)
+    all_line(lambda other: da_copy(other, other).wait())
+    all_seq(lambda other: fin_copy(0, other, other).wait())
+    all_seq(lambda other: fin_copy(1, other, other).wait())
+    all_seq(lambda other: small_copy(other, other).wait())
+    for copy in own_copies.values():
+        copy.wait()
 
 
 def core(
@@ -1158,71 +1390,54 @@
     depth = total // seqs
     blocks, tiles = rows // GROUP, rows // BLOCK
     heads = inner // HDIM
-    steps = 4 * blocks + 1
-
-    def scan_block(i):
-        return jnp.clip(4 * blocks - 1 - i, 0, blocks - 1)
-
-    def late_block(i):
-        return jnp.where(i == steps - 1, blocks - 1, jnp.clip(4 * blocks - 1 - i, 0, max(blocks - 2, 0)))
-
-    def place(early, late=None):
-        def at(i):
-            index = jnp.int32(0)
-            for n in range(3):
-                if n in early:
-                    now = i - n * blocks
-                elif any(m > n for m in early):
-                    now = jnp.int32(0)
-                elif late is not None:
-                    now = late(jnp.int32(3 * blocks))
-                else:
-                    now = jnp.int32(blocks - 1)
-                index = jnp.where((i >= n * blocks) & (i < (n + 1) * blocks), now, index)
-            return jnp.where(i >= 3 * blocks, late(i) if late is not None else blocks - 1, index)
-
-        return at
-
-    def by_rows(columns, at, column=0):
-        return blockwise((GROUP, columns), lambda i: (at(i), column))
-
-    local_at = place((0,))
-    pre_at = place((), late_block)
+    pieces = blocks + 1
     message = (inner + HALO, STATE)
     sums = (blocks, EDGE, GROUP)
-    whole = (state_in, r_t, w_all, postnorm, vec, prenorm, kernels, filters, rim)
+    streamed = (gate, part, act, cum, raw, local, conv, pre, normed, u, g_part, r_t, w_all)
+    whole = (state_in, postnorm, vec, prenorm, kernels, filters, rim)
     gather = (line, rows, width)
+    nothing = (line, HALO, width)
+    roomy = rows * total * 2 <= 4 << 20
+    near, far = (gather, nothing) if roomy else (nothing, gather)
+    relay = (2, rows if line == 4 else HALO, width)
     small = (EDGE, inner + LANES)
+    ways = max(line, 3)
+
+    def slots(*dims):
+        return (2,) + dims
+
+    buffers = (
+        (slots(GROUP, inner), WIDE), (slots(GROUP, inner), WIDE), (slots(GROUP, STATE), LOW),
+        (slots(GROUP, LANES), WIDE), (slots(inner, STATE), WIDE), (slots(GROUP, total), LOW),
+        (slots(GROUP, wide), LOW), (slots(GROUP, LANES), WIDE), (slots(GROUP, wide), WIDE),
+        (slots(GROUP, wide), LOW), (slots(HALO, wide), LOW), (slots(GROUP, total), LOW),
+    )
     return pl.pallas_call(
-        functools.partial(core_kernel, seqs, line, heads, blocks),
-        grid=(steps,),
+        functools.partial(core_kernel, seqs, line, heads, blocks, roomy),
+        grid=(1,),
         out_shape=(
-            shape((seqs, BLOCK, width), LOW), shape((seqs, BLOCK, width), LOW), shape(gather, LOW), shape(gather, LOW),
+            shape((seqs, BLOCK, width), LOW), shape((seqs, BLOCK, width), LOW), shape(far, LOW), shape(far, LOW),
             shape((seqs, depth, inner), LOW), shape((seqs, depth, inner), LOW), shape((seqs, depth, inner + LANES), LOW),
             shape((line, depth, LANES), WIDE), shape((seqs,) + small, WIDE),
         ),
-        in_specs=[
-            SMEM_SPEC, SMEM_SPEC,
-            by_rows(inner, place((0, 1, 2))), by_rows(inner, place((0,))),
-            by_rows(STATE, place((0, 2)), (inner + STATE) // STATE), by_rows(wide, place((), scan_block)),
-            by_rows(LANES, place((0, 2), scan_block)), by_rows(LANES, place((), scan_block)),
-            blockwise((1, inner, STATE), lambda i: (local_at(i), 0, 0)), by_rows(wide, place((), scan_block)),
-            by_rows(wide, pre_at),
-            blockwise((HALO, wide), lambda i: (jnp.maximum(pre_at(i) * (GROUP // HALO) - 1, 0), 0)),
-            by_rows(total, place((2,), late_block)), by_rows(total, pre_at), ANY_SPEC,
-        ] + [fixed(a.shape) for a in whole],
+        in_specs=[SMEM_SPEC] * 2 + [ANY_SPEC] * len(streamed) + [fixed(a.shape) for a in whole],
         out_specs=(ANY_SPEC,) * 9,
-        scratch_shapes=[
+        scratch_shapes=[pltpu.VMEM(dims, kind) for dims, kind in buffers] + [
+            DMA((len(buffers), 2)),
+            pltpu.VMEM(r_t.shape, LOW), pltpu.VMEM(w_all.shape, LOW),
             pltpu.VMEM((rows, inner), WIDE), pltpu.VMEM((rows, inner), WIDE), pltpu.VMEM((rows, inner), LOW),
-            pltpu.VMEM((rows, inner), LOW), pltpu.VMEM((blocks, inner, STATE), WIDE),
+            pltpu.VMEM((rows, inner), LOW), pltpu.VMEM((rows, GROUP), LOW), pltpu.VMEM((blocks, inner, STATE), WIDE),
             pltpu.VMEM((blocks, inner, STATE), WIDE), pltpu.VMEM((inner, STATE), WIDE), pltpu.VMEM((LANES, 1), WIDE),
-            pltpu.VMEM((rows, total), LOW), pltpu.VMEM((rows, width), LOW), pltpu.VMEM(gather, LOW),
+            pltpu.VMEM((rows, total), LOW), pltpu.VMEM(gather, LOW),
             pltpu.VMEM((seqs,) + message, LOW), pltpu.VMEM(message, LOW),
+            pltpu.VMEM(relay, LOW), pltpu.VMEM(relay, LOW), pltpu.VMEM(near, LOW), pltpu.VMEM(near, LOW),
             pltpu.VMEM((line,) + sums, WIDE), pltpu.VMEM(sums, WIDE),
             pltpu.VMEM((total, inner), WIDE), pltpu.VMEM((total, inner), WIDE), pltpu.VMEM((total, inner), LOW),
             pltpu.VMEM((total, inner), LOW), pltpu.VMEM((1, inner), WIDE), pltpu.VMEM((EDGE, LANES), WIDE),
-            pltpu.VMEM((2, GROUP, wide), WIDE), pltpu.VMEM((2, GROUP, LANES), LOW), pltpu.VMEM((EDGE, wide), WIDE),
+            pltpu.VMEM((GROUP, wide), WIDE), pltpu.VMEM((GROUP, LANES), LOW), pltpu.VMEM((EDGE, wide), WIDE),
             pltpu.VMEM((EDGE, wide), WIDE), pltpu.VMEM((EDGE, wide), WIDE), pltpu.VMEM((BLOCK + EDGE, wide), WIDE),
+            pltpu.VMEM((HALO + EDGE, wide), WIDE), pltpu.VMEM((HALO, LANES), LOW), pltpu.VMEM((HALO, total), LOW),
+            pltpu.VMEM((HALO, total), LOW),
             pltpu.VMEM((EDGE, wide), WIDE), pltpu.VMEM((1, wide), WIDE), pltpu.VMEM((total, wide + LANES), WIDE),
             pltpu.VMEM((total, inner + LANES), LOW), pltpu.VMEM((total, wide - inner), LOW),
             pltpu.VMEM((seqs, depth, wide - inner), LOW), pltpu.VMEM((line, depth, LANES), WIDE),
@@ -1230,17 +1445,16 @@
             pltpu.VMEM((line, 2 * EDGE, width), WIDE), pltpu.VMEM(small, WIDE),
             pltpu.VMEM((2, tiles, BLOCK, width), LOW), pltpu.VMEM((2, seqs, BLOCK, width), LOW),
             DMA((seqs,)), DMA((seqs,)), DMA((seqs,)), DMA((line,)), DMA((line,)), DMA((2, line)), DMA((line,)), DMA((4,)),
-            DMA((line,)), DMA((line,)), DMA((4, seqs)), DMA((4, seqs)), DMA((line, blocks)), DMA((line, blocks)), DMA, DMA,
+            DMA((ways, blocks)), DMA((line, blocks)), DMA((2, blocks)), DMA((4, seqs)), DMA((4, seqs)),
+            DMA((ways, pieces)), DMA((line, pieces)), DMA((2, pieces)), DMA, DMA,
             DMA((line,)), DMA((line,)), DMA((line,)), DMA((line,)), DMA((seqs,)), DMA((seqs,)), DMA((2, seqs)),
-            DMA((2, seqs)), DMA((9,)),
+            DMA((2, seqs)), DMA((7,)), DMA((2,)),
         ],
         compiler_params=pltpu.CompilerParams(
             collective_id=1, has_side_effects=True, vmem_limit_bytes=VMEM_LIMIT, dimension_semantics=("arbitrary",)
         ),
         name="core",
-    )(
-        flags, give, gate, part, act, act, cum, raw, local, conv, pre, pre, normed, u, g_part, *whole
-    )
+    )(flags, give, *streamed, *whole)
 
 
 def finish_kernel(
@@ -1248,7 +1462,7 @@
     out_o, dx_o, prenorm_o, gate_o, pay_o, addr_o, step_o, kernels_o, offsets_o, filters_o, shifts_o,
     stepbias_o, decays_o, through_o, post_o, read_o,
 ):
-    inner, size, heads, width = gate_o.shape[1], addr_o.shape[1], step_o.shape[0], prenorm_o.shape[1]
+    inner, size, heads, width = gate_o.shape[1], addr_o.shape[0], step_o.shape[0], prenorm_o.shape[1]
     offset = lax.rem(lax.axis_index("head") * size, LANES)
     back_turn = lax.rem(LANES - offset, LANES)
     for k in range(out_o.shape[0]):
@@ -1266,7 +1480,7 @@
     grads = summed(dw_got)
     pay_o[...] = grads[:, :inner]
     step_o[...] = grads[:, inner:].T[:heads]
-    addr_o[...] = pltpu.roll(summed(addr_got), back_turn, 1)[:, :size]
+    addr_o[...] = pltpu.roll(summed(addr_got), back_turn, 1).T[:size]
     totals = jnp.sum(small_got[...], axis=0)
     kernels_o[...] = totals[0:TAPS, :inner]
     offsets_o[...] = totals[4:5, :inner]
@@ -1288,7 +1502,7 @@
     operands = (out_recv, grad_recv, gread_got, ggate_got, dw_got, addr_got, small_got)
     outs = (
         shape((tiles, BLOCK, width), LOW), shape((tiles, BLOCK, width), LOW), shape((1, width), WIDE),
-        shape((depth, inner), WIDE), shape((depth, inner), WIDE), shape((depth, size), WIDE),
+        shape((depth, inner), WIDE), shape((depth, inner), WIDE), shape((size, depth), WIDE),
         shape((heads, depth), WIDE), shape((TAPS, inner), WIDE), shape((1, inner), WIDE),
         shape((TAPS, size), WIDE), shape((1, size), WIDE), shape((1, heads), WIDE), shape((1, heads), WIDE),
         shape((1, heads), WIDE), shape((1, inner), WIDE), shape((inner, depth), WIDE),
@@ -1349,7 +1563,7 @@
         prenorm_g.reshape(-1),
         gate_g,
         pay_g,
-        addr_g,
+        addr_g.T,
         step_g.T,
         kernels_g,
         offsets_g.reshape(-1),

time: 226 us -> 198 us (0.88); the launches traced: 226 us -> 195 us
  Pallas kernels: 224 us -> 194 us
    pallas_call x1, Pallas kernels: 145 us -> 121 us  [core(): pl.pallas_call(functools.partial(core_kernel, seqs, line, heads, blocks,...]
    pallas_call x1, Pallas kernels: 73 us -> 66.8 us  [front(): pl.pallas_call(functools.partial(front_kernel, seqs, line, heads, blocks,...]
where the time goes in v6:
time: 198 us; the launch traced here: 195 us
  Pallas kernels  194 us (98%)
    pallas_call x1, Pallas kernels, core(): pl.pallas_call(functools.partial(core_kernel, seqs, line, heads, blocks,...  121 us
    pallas_call x1, Pallas kernels, front(): pl.pallas_call(functools.partial(front_kernel, seqs, line, heads, blocks,...  66.8 us
    pallas_call x1, Pallas kernels, finish(): pl.pallas_call(finish_kernel, grid=(1,), out_shape=outs, in_specs=[SMEM_S...  4.04 us

profile of v6, /device:TPU:1, one launch (start us, length us, event | category | flops | bytes accessed | tf_op | source)
XLA Modules:
  0.0 195.0 jit_solution(14268275435813617279)
XLA Ops:
  0.6 2.3 %index.1 = (s32[8]{0:T(128)}, s32[8]{0:T(128)}, s32[8]{0:T(128)}, s32[8]{0:T(128)}, f32[9]{0:T(128)}, /*index=5*/f32[8,128]{1,0:T(8,128)}) custom-call(s32[64]{0:T(128)} %place.1, s32[4]{0:T(128)} %lengths.1, f32[1,8]{1,0:T(1,128)} %bitcast.29, f32[1,8]{1,0:T(1,128)} %bitcast.30, f32[1,8]{1,0:T(1,128)} %bitcast.31), custom_call_target="tpu_custom_call" | custom-call | tf_op jit(solution)/shard_map/index/pallas_call | solution.py:326
  2.9 66.8 %front.1 = (bf16[1024,1024]{1,0:T(8,128)(2,1)}, bf16[1024,1024]{1,0:T(8,128)(2,1)}, f32[1024,512]{1,0:T(8,128)}, bf16[1024,768]{1,0:T(8,128)(2,1)}, f32[1024,768...) custom-call(s32[8]{0:T(128)} %get-tuple-element.63.give, ...), custom_call_target="tpu_custom_call" | custom-call | tf_op jit(solution)/shard_map/front/pallas_call | solution.py:643
  69.7 121.1 %core.1 = (bf16[8,128,256]{2,1,0:T(8,128)(2,1)}, bf16[8,128,256]{2,1,0:T(8,128)(2,1)}, bf16[4,16,256]{2,1,0:T(8,128)(2,1)}, bf16[4,16,256]{2,1,0:T(8,128)(2,1)},...) custom-call(f32[9]{0:T(128)} %get-tuple-element.61.flags, ...), custom_call_target="tpu_custom_call" | custom-call | tf_op jit(solution)/shard_map/core/pallas_call | solution.py:1415
  190.8 4.0 %finish.1 = (bf16[8,128,256]{2,1,0:T(8,128)(2,1)}, bf16[8,128,256]{2,1,0:T(8,128)(2,1)}, f32[1,256]{1,0:T(1,128)}, f32[128,512]{1,0:T(8,128)}, f32[128,512]{1,0:...) custom-call(s32[8]{0:T(128)} %get-tuple-element.60.take, ...), custom_call_target="tpu_custom_call" | custom-call | tf_op jit(solution)/shard_map/finish/pallas_call | solution.py:1510

commit v7 on v6

--- a/solution.py
+++ b/solution.py
@@ -484,6 +484,9 @@
         def _(n):
             rim_copy(n, n).wait_recv()
 
+        arrange(1, recv_g, work_g)
+        g_line.first(work_g)
+        own_g.start()
         w_plane.finish(w_own)
         save_w.start()
 
@@ -492,12 +495,6 @@
         @pl.when(lax.rem(i, per) == 0)
         def _():
             u_line(lax.div(i, per)).hop(line - 1)
-
-    @pl.when(i == blocks - 1)
-    def _():
-        arrange(1, recv_g, work_g)
-        g_line.first(work_g)
-        own_g.start()
 
     taps = jnp.concatenate([kernels[...], filters[...]], axis=1)
     bias = jnp.concatenate([offsets[...], shifts[...]], axis=1)
@@ -732,7 +729,7 @@
         slot = self.got.at[source, rows]
         return remote(slot, slot, self.sent.at[0, piece], self.arrived.at[source, piece], {"head": source})
 
-    def send(self, rows, piece):
+    def send_far(self, rows, piece):
         if not self.merges:
             if self.line > 1:
                 self.others(lambda to: self.chunk(rows, piece, to, to, to).start())
@@ -742,11 +739,11 @@
         def _():
             self.hand(rows, piece, self.far, 1).start()
             self.hand(rows, piece, self.next, 0).start()
-            self.chunk(rows, piece, self.mid, self.mid, 0).start()
-
-        @pl.when(jnp.logical_not(self.is_end))
-        def _():
-            self.chunk(rows, piece, self.end, self.end, 0).start()
+
+    def send_near(self, rows, piece):
+        if self.merges:
+            near = jnp.where(self.is_end, self.mid, self.end)
+            self.chunk(rows, piece, near, near, 0).start()
 
     def merge(self, rows, piece):
         if self.merges:
@@ -780,26 +777,83 @@
         return sum_
 
 
+class Halved:
+    def __init__(self, seqs, src, pair, got, sems):
+        self.chips, self.src, self.pair, self.got = seqs // 2, src, pair, got
+        self.depth = pair.shape[1]
+        self.pair_sent, self.pair_got, self.sent, self.arrived = [sems.at[n] for n in range(4)]
+        self.me = lax.axis_index("seq")
+        self.core = lax.rem(self.me, 2)
+        self.chip = lax.div(self.me, 2)
+
+    def rows(self, chip, core):
+        return pl.ds(pl.multiple_of((2 * chip + core) * self.depth, self.depth), self.depth)
+
+    def give(self, chip):
+        return remote(
+            self.src.at[self.rows(chip, 1 - self.core)], self.pair.at[chip], self.pair_sent.at[chip],
+            self.pair_got.at[chip], {"seq": 2 * self.chip + 1 - self.core},
+        )
+
+    def send(self, chip, slot):
+        return remote(
+            self.src.at[self.rows(chip, self.core)], self.got.at[slot], self.sent.at[chip], self.arrived.at[slot],
+            {"seq": 2 * chip + self.core},
+        )
+
+    def kept(self):
+        return pltpu.make_async_copy(
+            self.src.at[self.rows(self.chip, self.core)], self.got.at[self.chip], self.sent.at[self.chip]
+        )
+
+    def begin(self):
+        pl.loop(0, self.chips)(lambda chip: self.give(chip).start())
+
+    def combine(self):
+        def add(chip):
+            rows = self.rows(chip, self.core)
+            self.give(chip).wait_recv()
+            self.src[rows, :] = (self.src[rows, :].astype(WIDE) + self.pair[chip].astype(WIDE)).astype(LOW)
+
+        @pl.loop(1, self.chips)
+        def _(n):
+            chip = lax.rem(self.chip + n, self.chips)
+            add(chip)
+            self.send(chip, self.chip).start()
+
+        add(self.chip)
+        self.kept().start()
+
+    def drain(self):
+        @pl.loop(1, self.chips)
+        def _(n):
+            other = lax.rem(self.chip + n, self.chips)
+            self.send(other, other).wait()
+
+        self.kept().wait()
+        pl.loop(0, self.chips)(lambda chip: self.give(chip).wait_send())
+
+
 def core_kernel(
     seqs, line, heads, blocks, roomy, flags, give,
     gate_in, part_in, act_in, cum_in, raw_in, local_in, conv_in, pre_in, normed_in, u_in, g_part, r_in, w_in,
     state_in, postnorm, vec, prenorm, kernels, filters, rim,
-    out_recv, grad_recv, out_far, dx_far, gread_got, ggate_got, dw_got, addr_got, small_got,
+    out_recv, grad_recv, out_far, dx_far, early_got, dw_got, addr_got, small_got,
     gate_b, part_b, read_b, cum_b, local_b, normed_b, act_b, raw_b, conv_b, pre_b, before_b, u_b, stream_sems,
     r_t, w, ssd_s, din_s, dssd_s, dgate_s, ds_s, starts, q, state, prod, g_buf, out_part, back_slots, back_msg,
     relay, dx_relay, out_near, dx_near, sums,
-    totals, gread, ggate, gread_low, ggate_low, gpost, tiny, d_conv, d_step, after, edge_own, edge_got, ext,
+    totals, gread, ggate, early_low, early_pair, gpost, tiny, d_conv, d_step, after, edge_own, edge_got, ext,
     keep_conv, keep_step, keep_normed, keep_u,
-    taps_g, bias_g, dw, dw_low, da_low, da_got, da_send, pn, zs_send, zs_got, small, result, fin_send,
+    taps_g, bias_g, dw, dw_low, dw_pair, da_low, da_pair, da_got, da_send, pn, zs_send, zs_got, small, result, fin_send,
     back_sent, back_sem, back_passed, sum_sent, sum_sem, line_sent, line_sem, load_sem, out_sent, out_sem, out_relayed,
-    w_sent, w_sem, dx_sent, dx_sem, dx_relayed, edge_sent, edge_sem, zs_sent, zs_sem, da_sent, da_sem, small_sent,
-    small_sem, fin_sent, fin_sem, own_sem, weight_sem,
+    early_sems, dw_sems, da_sems, dx_sent, dx_sem, dx_relayed, edge_sent, edge_sem, zs_sent, zs_sem, da_sent, da_sem, small_sent,
+    small_sem, fin_sent, fin_sem, own_sem, weight_sem, residual_sem,
 ):
     me, mine = lax.axis_index("seq"), lax.axis_index("head")
     inner = r_t.shape[1]
     wide = act_b.shape[2]
     width = out_part.shape[2]
-    depth = gread_got.shape[1]
+    depth = early_got.shape[1]
     rows = ssd_s.shape[0]
     size = 2 * STATE // line
     g_line = Line(line, g_buf, width, line_sent, line_sem)
@@ -869,8 +923,8 @@
 
     first_phase = ((gate_f, part_f, read_f, cum_f, local_f), forwards)
     norm_phase = ((gate_f,), forwards)
-    gate_phase = ((gate_f, normed_f, read_f, cum_f), forwards)
-    scan_phase = ((act_f, cum_f, raw_f), forwards)
+    gate_phase = ((gate_f, read_f, cum_f), forwards)
+    scan_phase = ((gate_f, normed_f, act_f, cum_f, raw_f), forwards)
     last_phase = ((act_f, cum_f, raw_f, conv_f, pre_f, before_f, normed_f, u_f), backwards)
 
     def each_load(body):
@@ -885,18 +939,9 @@
     def sum_copy(to, slot):
         return remote(sums.at[mine], sums.at[slot], sum_sent.at[to], sum_sem.at[slot], {"head": to})
 
-    weights = ((gread_low, gread_got), (ggate_low, ggate_got), (dw_low, dw_got), (da_low, da_got))
-
-    def w_copy(which, to, slot):
-        src, dst = weights[which]
-        return remote(src.at[rows_of(to)], dst.at[slot], w_sent.at[which, to], w_sem.at[which, slot], {"seq": to})
-
-    def w_start(which):
-        all_seq(lambda to: w_copy(which, to, me).start())
-
-    def w_wait(which):
-        all_seq(lambda other: w_copy(which, other, other).wait())
-
+    early_sum = Halved(seqs, early_low, early_pair, early_got, early_sems)
+    dw_sum = Halved(seqs, dw_low, dw_pair, dw_got, dw_sems)
+    da_sum = Halved(seqs, da_low, da_pair, da_got, da_sems)
     out_fold = Fold(
         line, lambda z, at: out_part.at[z, at], out_got, relay, out_sent, out_sem, out_relayed
     )
@@ -932,27 +977,24 @@
 
     def fin_copy(which, to, slot):
         return remote(
-            fin_send.at[which, to], arrivals[which].at[slot], fin_sent.at[which, to], fin_sem.at[which, slot],
+            fin_send.at[to], arrivals[which].at[slot], fin_sent.at[which, to], fin_sem.at[which, slot],
             {"seq": to},
         )
 
     own_copies = {
-        "gread": pltpu.make_async_copy(gread_low.at[rows_of(me)], gread_got.at[me], own_sem.at[0]),
-        "ggate": pltpu.make_async_copy(ggate_low.at[rows_of(me)], ggate_got.at[me], own_sem.at[1]),
-        "dw": pltpu.make_async_copy(dw_low.at[rows_of(me)], dw_got.at[me], own_sem.at[2]),
-        "addr": pltpu.make_async_copy(da_send.at[mine], addr_got.at[mine], own_sem.at[3]),
-        "small": pltpu.make_async_copy(small, small_got.at[me], own_sem.at[4]),
-        "fin0": pltpu.make_async_copy(fin_send.at[0, me], out_recv.at[me], own_sem.at[5]),
-        "fin1": pltpu.make_async_copy(fin_send.at[1, me], grad_recv.at[me], own_sem.at[6]),
+        "addr": pltpu.make_async_copy(da_send.at[mine], addr_got.at[mine], own_sem.at[0]),
+        "small": pltpu.make_async_copy(small, small_got.at[me], own_sem.at[1]),
+        "fin0": pltpu.make_async_copy(fin_send.at[me], out_recv.at[me], own_sem.at[2]),
+        "fin1": pltpu.make_async_copy(fin_send.at[me], grad_recv.at[me], own_sem.at[3]),
     }
 
     def route(which):
         def send(to):
-            fin_send[which, to] = result[which, give[to]]
+            fin_send[to] = result[give[to]]
             fin_copy(which, to, me).start()
 
         all_seq(send)
-        fin_send[which, me] = result[which, give[me]]
+        fin_send[me] = result[give[me]]
         own_copies["fin%d" % which].start()
 
     def fetch(src):
@@ -991,6 +1033,10 @@
     fetch_w.start()
     state[...] = state_in[...]
     fetch_r.wait()
+
+    def out_part_done(b):
+        if out_fold.merges:
+            out_fold.send_far(group_rows(b), b)
 
     @pl.loop(0, blocks)
     def _(b):
@@ -1005,8 +1051,13 @@
         out = nt((gated_of(ssd, b) * postnorm[...]).astype(LOW), r_t[...])
         for z in range(line):
             out_part[z, here] = out[:, z * width : (z + 1) * width].astype(LOW)
-        if out_fold.merges:
-            pl.when(out_fold.is_end)(lambda: out_fold.send(here, b))
+        out_part_done(b)
+
+    if out_fold.merges:
+
+        @pl.when(out_fold.is_end)
+        def _():
+            pl.loop(0, blocks)(lambda b: out_fold.send_near(group_rows(b), b))
 
     for hop in range(2, line):
         g_line.hop(hop)
@@ -1033,36 +1084,46 @@
     all_line(lambda other: sum_copy(other, other).wait())
     totals[...] = jnp.sum(sums[...], axis=0)
 
-    @pl.loop(0, blocks)
-    def _(b):
+    if out_fold.merges:
+
+        @pl.when(jnp.logical_not(out_fold.is_end))
+        def _():
+            @pl.loop(0, blocks)
+            def _(b):
+                out_fold.merge(group_rows(b), b)
+
+            pl.loop(0, blocks)(lambda b: out_fold.send_near(group_rows(b), b))
+
+    else:
+        pl.loop(0, blocks)(lambda b: out_fold.send_far(group_rows(b), b))
+
+    def residual(n):
+        at = pl.ds(pl.multiple_of(n * BLOCK, BLOCK), BLOCK)
+        columns = pl.ds(pl.multiple_of(mine * width, LANES), width)
+        return pltpu.make_async_copy(u_in.at[at, columns], result.at[n], residual_sem.at[n])
+
+    pl.loop(0, 2 * blocks)(lambda n: residual(n).start())
+
+    def norm_back(b, turn):
         here = group_rows(b)
-        if out_fold.merges:
-            pl.when(jnp.logical_not(out_fold.is_end))(lambda: out_fold.send(here, b))
-        else:
-            out_fold.send(here, b)
-        out_fold.merge(here, b)
+        inv, dot = row_stats(b)
+        gate_v = gate_f.at(turn)[...]
+        sig = sigmoid(gate_v)
+        ssd = ssd_s[here, :]
+        return gate_v, sig, ssd, ssd * (gate_v * sig), inv, dot
 
     @pl.loop(0, blocks)
     def _(b):
         step(*gate_phase, b, scan_phase)
         here = group_rows(b)
         cum_v = cum_f.at(b)[...]
-        inv, dot = row_stats(b)
-        gate_v = gate_f.at(b)[...]
-        sig = sigmoid(gate_v)
-        ssd = ssd_s[here, :]
+        gate_v, sig, ssd, gated, inv, dot = norm_back(b, b)
         d_inner = din_s[here, :]
-        gated = ssd * (gate_v * sig)
-        gated_inv = gated * inv
-        inner_normed = (gated_inv * postnorm[...]).astype(LOW)
         d_gated = (inv * postnorm[...]) * d_inner - gated * (inv * inv * inv / INNER * dot)
-        gpost[...] += jnp.sum(d_inner * gated_inv, axis=0, keepdims=True)
+        gpost[...] += jnp.sum(d_inner * (gated * inv), axis=0, keepdims=True)
         d_ssd = (d_gated * (gate_v * sig)).astype(LOW)
-        d_gate = (d_gated * ssd * sig * (1.0 + gate_v * (1.0 - sig))).astype(LOW)
         dssd_s[here, :] = d_ssd
-        dgate_s[here, :] = d_gate
-        gread[...] += tn(g_buf[here, :], inner_normed)
-        ggate[...] += tn(normed_f.at(b)[...], d_gate)
+        dgate_s[here, :] = (d_gated * ssd * sig * (1.0 + gate_v * (1.0 - sig))).astype(LOW)
         query_grad = (d_ssd.astype(WIDE) * entry_of(b, cum_v)).astype(LOW)
         found = tn(query_grad, read_f.at(b)[...])
         q[b] = found
@@ -1072,12 +1133,6 @@
     back_msg[:inner, :] = state[...].astype(LOW)
     back_msg[inner:, :] = jnp.broadcast_to(prod[:HALO], (HALO, STATE)).astype(LOW)
     back_plane.start(back_msg)
-    gread_low[...] = gread[...].astype(LOW)
-    ggate_low[...] = ggate[...].astype(LOW)
-    w_start(0)
-    w_start(1)
-    own_copies["gread"].start()
-    own_copies["ggate"].start()
 
     @pl.loop(0, blocks)
     def _(b):
@@ -1131,12 +1186,22 @@
             axis=0,
         ).astype(LOW)
 
+        gated, inv = norm_back(b, b)[3:5]
+        inner_normed = (gated * inv * postnorm[...]).astype(LOW)
+        gread[...] += tn(g_buf[here, :], inner_normed)
+        ggate[...] += tn(normed_f.at(b)[...], dgate_s[here, :])
+
         @pl.when(b == blocks // 2)
         def _():
             back_plane.relay()
 
+    early_low[:, :inner] = gread[...].astype(LOW)
+    early_low[:, inner:] = ggate[...].astype(LOW)
+    early_sum.begin()
     back_plane.finish(back_msg)
     state[...] = fold_states(back_slots, collect, inner, seqs - 1, me, -1, jnp.zeros((inner, STATE), WIDE))
+
+    early_sum.combine()
     taps = jnp.concatenate([kernels[...], filters[...]], axis=1)
     scale = -jnp.exp(vec[1:2, :])
     through_w = to_columns(jnp.broadcast_to(vec[2:3, :], (EDGE, LANES)), spread_m)[0:1]
@@ -1245,15 +1310,29 @@
         grad, gain = input_back(d_pre, step_grad, dgate_s[group_rows(b), :], u_v[...])
         pn[...] += jnp.sum(jnp.where(done, gain, 0.0) if final else gain, axis=0, keepdims=True)
         g_buf[group_rows(b), :] = grad
-        own_columns = pl.ds(pl.multiple_of(mine * width, LANES), width)
-        result[0, 2 * b] = u_v[0:BLOCK, own_columns]
-        result[0, 2 * b + 1] = u_v[BLOCK:, own_columns]
         after[...] = grad_c[0:EDGE]
+
+    def outputs_home():
+        pl.loop(0, 2 * blocks)(lambda n: residual(n).wait())
+        pl.loop(0, blocks)(lambda b: out_fold.drain(group_rows(b), b))
+        fetch(out_far)
+
+        @pl.loop(0, blocks)
+        def _(b):
+            inv, _ = row_stats(b)
+            total = out_fold.total(group_rows(b), out_near if roomy else out_part) * inv
+            result[2 * b] = (result[2 * b].astype(WIDE) + total[:BLOCK]).astype(LOW)
+            result[2 * b + 1] = (result[2 * b + 1].astype(WIDE) + total[BLOCK:]).astype(LOW)
+
+        route(0)
+        own_g.start()
+
+    own_g = pltpu.make_async_copy(shard_of(g_part, mine), out_part.at[mine], load_sem.at[3])
 
     step(*last_phase, 0, None)
     scan_back(blocks - 1, 0)
     rows_back(blocks - 1, 0, True)
-    dx_fold.send(*short_piece)
+    dx_fold.send_far(*short_piece)
 
     @pl.loop(1, blocks)
     def _(turn):
@@ -1267,11 +1346,13 @@
             edge_copy(lax.rem(me + seqs - 1, seqs)).start()
 
         rows_back(b, turn, False)
-        dx_fold.send(group_rows(b), b)
+        dx_fold.send_far(group_rows(b), b)
 
         @pl.when(turn == 2)
         def _():
             dx_fold.merge(*short_piece)
+
+        pl.when(turn == max(blocks // 2, 1))(outputs_home)
 
         @pl.when(turn > 2)
         def _():
@@ -1284,15 +1365,17 @@
     grad, gain = input_back(d_edge, keep_step[...], dgate_s[pl.ds(rows - HALO, HALO), :], keep_u[...])
     pn[...] += jnp.sum(gain, axis=0, keepdims=True)
     g_buf[pl.ds(rows - HALO, HALO), :] = grad
-    dx_fold.send(*edge_piece)
+    dx_fold.send_far(*edge_piece)
+    each_piece(dx_fold.send_near)
+
+    if blocks > 3:
+        dx_fold.merge(group_rows(1), 1)
 
     da_low[...] = dw[:, inner:wide].astype(LOW)
-    w_start(3)
+    da_sum.begin()
     dw_low[:, :inner] = dw[:, :inner].astype(LOW)
     dw_low[:, inner:] = dw[:, wide:].astype(LOW)
-    w_start(2)
-    own_copies["dw"].start()
-    da_got[me] = da_low[rows_of(me), :]
+    dw_sum.begin()
 
     for z in range(line):
         slab = z * size // LANES * LANES
@@ -1304,36 +1387,17 @@
     all_line(lambda to: zs_copy(to, mine).start())
 
     if blocks > 3:
-
-        @pl.loop(0, 2)
-        def _(n):
-            dx_fold.merge(group_rows(1 - n), 1 - n)
-
+        dx_fold.merge(group_rows(0), 0)
     elif blocks == 2:
         dx_fold.merge(*short_piece)
         dx_fold.merge(group_rows(0), 0)
     dx_fold.merge(*edge_piece)
-
-    @pl.loop(0, blocks)
-    def _(b):
-        out_fold.drain(group_rows(b), b)
-
-    fetch(out_far)
-
-    @pl.loop(0, blocks)
-    def _(b):
-        inv, _ = row_stats(b)
-        total = out_fold.total(group_rows(b), out_near if roomy else out_part) * inv
-        result[0, 2 * b] = (result[0, 2 * b].astype(WIDE) + total[:BLOCK]).astype(LOW)
-        result[0, 2 * b + 1] = (result[0, 2 * b + 1].astype(WIDE) + total[BLOCK:]).astype(LOW)
-
-    route(0)
-    own_g = pltpu.make_async_copy(shard_of(g_part, mine), out_part.at[mine], load_sem.at[3])
-    own_g.start()
-
-    w_wait(3)
+    da_sum.combine()
+    dw_sum.combine()
+
+    da_sum.drain()
     from_plane = da_got[0].astype(WIDE)
-    for n in range(1, seqs):
+    for n in range(1, seqs // 2):
         from_plane = from_plane + da_got[n].astype(WIDE)
     for z in range(line):
         slab = z * size // LANES * LANES
@@ -1341,6 +1405,8 @@
     own_copies["addr"].start()
     all_line(lambda to: da_copy(to, mine).start())
 
+    all_seq(lambda other: fin_copy(0, other, other).wait())
+    own_copies["fin0"].wait()
     each_piece(dx_fold.drain)
     fetch(dx_far)
     own_g.wait()
@@ -1350,8 +1416,8 @@
         here = group_rows(b)
         total = dx_fold.total(here, dx_near if roomy else out_part)
         done = (out_part[mine, here].astype(WIDE) + total).astype(LOW)
-        result[1, 2 * b] = done[:BLOCK]
-        result[1, 2 * b + 1] = done[BLOCK:]
+        result[2 * b] = done[:BLOCK]
+        result[2 * b + 1] = done[BLOCK:]
 
     route(1)
     all_line(lambda other: zs_copy(other, other).wait())
@@ -1368,14 +1434,13 @@
     own_copies["small"].start()
     all_seq(lambda to: small_copy(to, me).start())
 
-    for which in range(3):
-        w_wait(which)
+    early_sum.drain()
+    dw_sum.drain()
     all_line(lambda other: da_copy(other, other).wait())
-    all_seq(lambda other: fin_copy(0, other, other).wait())
     all_seq(lambda other: fin_copy(1, other, other).wait())
     all_seq(lambda other: small_copy(other, other).wait())
-    for copy in own_copies.values():
-        copy.wait()
+    for name in ("addr", "small", "fin1"):
+        own_copies[name].wait()
 
 
 def core(
@@ -1417,11 +1482,11 @@
         grid=(1,),
         out_shape=(
             shape((seqs, BLOCK, width), LOW), shape((seqs, BLOCK, width), LOW), shape(far, LOW), shape(far, LOW),
-            shape((seqs, depth, inner), LOW), shape((seqs, depth, inner), LOW), shape((seqs, depth, inner + LANES), LOW),
+            shape((seqs // 2, depth, 2 * inner), LOW), shape((seqs // 2, depth, inner + LANES), LOW),
             shape((line, depth, LANES), WIDE), shape((seqs,) + small, WIDE),
         ),
         in_specs=[SMEM_SPEC] * 2 + [ANY_SPEC] * len(streamed) + [fixed(a.shape) for a in whole],
-        out_specs=(ANY_SPEC,) * 9,
+        out_specs=(ANY_SPEC,) * 8,
         scratch_shapes=[pltpu.VMEM(dims, kind) for dims, kind in buffers] + [
             DMA((len(buffers), 2)),
             pltpu.VMEM(r_t.shape, LOW), pltpu.VMEM(w_all.shape, LOW),
@@ -1432,23 +1497,24 @@
             pltpu.VMEM((seqs,) + message, LOW), pltpu.VMEM(message, LOW),
             pltpu.VMEM(relay, LOW), pltpu.VMEM(relay, LOW), pltpu.VMEM(near, LOW), pltpu.VMEM(near, LOW),
             pltpu.VMEM((line,) + sums, WIDE), pltpu.VMEM(sums, WIDE),
-            pltpu.VMEM((total, inner), WIDE), pltpu.VMEM((total, inner), WIDE), pltpu.VMEM((total, inner), LOW),
-            pltpu.VMEM((total, inner), LOW), pltpu.VMEM((1, inner), WIDE), pltpu.VMEM((EDGE, LANES), WIDE),
+            pltpu.VMEM((total, inner), WIDE), pltpu.VMEM((total, inner), WIDE), pltpu.VMEM((total, 2 * inner), LOW),
+            pltpu.VMEM((seqs // 2, depth, 2 * inner), LOW), pltpu.VMEM((1, inner), WIDE), pltpu.VMEM((EDGE, LANES), WIDE),
             pltpu.VMEM((GROUP, wide), WIDE), pltpu.VMEM((GROUP, LANES), LOW), pltpu.VMEM((EDGE, wide), WIDE),
             pltpu.VMEM((EDGE, wide), WIDE), pltpu.VMEM((EDGE, wide), WIDE), pltpu.VMEM((BLOCK + EDGE, wide), WIDE),
             pltpu.VMEM((HALO + EDGE, wide), WIDE), pltpu.VMEM((HALO, LANES), LOW), pltpu.VMEM((HALO, total), LOW),
             pltpu.VMEM((HALO, total), LOW),
             pltpu.VMEM((EDGE, wide), WIDE), pltpu.VMEM((1, wide), WIDE), pltpu.VMEM((total, wide + LANES), WIDE),
-            pltpu.VMEM((total, inner + LANES), LOW), pltpu.VMEM((total, wide - inner), LOW),
-            pltpu.VMEM((seqs, depth, wide - inner), LOW), pltpu.VMEM((line, depth, LANES), WIDE),
+            pltpu.VMEM((total, inner + LANES), LOW), pltpu.VMEM((seqs // 2, depth, inner + LANES), LOW),
+            pltpu.VMEM((total, wide - inner), LOW), pltpu.VMEM((seqs // 2, depth, wide - inner), LOW),
+            pltpu.VMEM((seqs // 2, depth, wide - inner), LOW), pltpu.VMEM((line, depth, LANES), WIDE),
             pltpu.VMEM((1, total), WIDE), pltpu.VMEM((line, 2 * EDGE, width), WIDE),
             pltpu.VMEM((line, 2 * EDGE, width), WIDE), pltpu.VMEM(small, WIDE),
-            pltpu.VMEM((2, tiles, BLOCK, width), LOW), pltpu.VMEM((2, seqs, BLOCK, width), LOW),
+            pltpu.VMEM((tiles, BLOCK, width), LOW), pltpu.VMEM((seqs, BLOCK, width), LOW),
             DMA((seqs,)), DMA((seqs,)), DMA((seqs,)), DMA((line,)), DMA((line,)), DMA((2, line)), DMA((line,)), DMA((4,)),
-            DMA((ways, blocks)), DMA((line, blocks)), DMA((2, blocks)), DMA((4, seqs)), DMA((4, seqs)),
+            DMA((ways, blocks)), DMA((line, blocks)), DMA((2, blocks)), DMA((4, seqs // 2)), DMA((4, seqs // 2)), DMA((4, seqs // 2)),
             DMA((ways, pieces)), DMA((line, pieces)), DMA((2, pieces)), DMA, DMA,
             DMA((line,)), DMA((line,)), DMA((line,)), DMA((line,)), DMA((seqs,)), DMA((seqs,)), DMA((2, seqs)),
-            DMA((2, seqs)), DMA((7,)), DMA((2,)),
+            DMA((2, seqs)), DMA((4,)), DMA((2,)), DMA((tiles,)),
         ],
         compiler_params=pltpu.CompilerParams(
             collective_id=1, has_side_effects=True, vmem_limit_bytes=VMEM_LIMIT, dimension_semantics=("arbitrary",)
@@ -1458,7 +1524,7 @@
 
 
 def finish_kernel(
-    take, out_recv, grad_recv, gread_got, ggate_got, dw_got, addr_got, small_got,
+    take, out_recv, grad_recv, early_got, dw_got, addr_got, small_got,
     out_o, dx_o, prenorm_o, gate_o, pay_o, addr_o, step_o, kernels_o, offsets_o, filters_o, shifts_o,
     stepbias_o, decays_o, through_o, post_o, read_o,
 ):
@@ -1475,8 +1541,9 @@
             total = total + ref[n].astype(WIDE)
         return total
 
-    read_o[...] = summed(gread_got).T
-    gate_o[...] = summed(ggate_got)
+    early = summed(early_got)
+    read_o[...] = early[:, :inner].T
+    gate_o[...] = early[:, inner:]
     grads = summed(dw_got)
     pay_o[...] = grads[:, :inner]
     step_o[...] = grads[:, inner:].T[:heads]
@@ -1493,13 +1560,14 @@
         ref[...] = totals[7:8, n * LANES : n * LANES + heads]
 
 
-def finish(take, out_recv, grad_recv, gread_got, ggate_got, dw_got, addr_got, small_got):
+def finish(take, out_recv, grad_recv, early_got, dw_got, addr_got, small_got):
     seqs, _, width = out_recv.shape
     tiles = take.shape[0]
-    _, depth, inner = gread_got.shape
+    _, depth, inner = early_got.shape
+    inner = inner // 2
     heads = inner // HDIM
     size = 2 * STATE // addr_got.shape[0]
-    operands = (out_recv, grad_recv, gread_got, ggate_got, dw_got, addr_got, small_got)
+    operands = (out_recv, grad_recv, early_got, dw_got, addr_got, small_got)
     outs = (
         shape((tiles, BLOCK, width), LOW), shape((tiles, BLOCK, width), LOW), shape((1, width), WIDE),
         shape((depth, inner), WIDE), shape((depth, inner), WIDE), shape((size, depth), WIDE),
@@ -1549,14 +1617,14 @@
         give_in, take_in, flags, inputs, cotangent, gating, payload, address, stepping, readout, vec, gain, kernels,
         filters, offsets[None, :], shifts[None, :]
     )
-    out_recv, grad_recv, _, _, gread_got, ggate_got, dw_got, addr_got, small_got = core(
+    out_recv, grad_recv, _, _, early_got, dw_got, addr_got, small_got = core(
         flags, give_out, gate, part, act, cum, raw, local, conv, pre, normed, u, g_part, state_in, r_t, w_all, post, vec,
         gain, kernels, filters, rim
     )
     (
         out, dx, prenorm_g, gate_g, pay_g, addr_g, step_g, kernels_g, offsets_g, filters_g, shifts_g, stepbias_g,
         decays_g, through_g, post_g, read_g,
-    ) = finish(take_out, out_recv, grad_recv, gread_got, ggate_got, dw_got, addr_got, small_got)
+    ) = finish(take_out, out_recv, grad_recv, early_got, dw_got, addr_got, small_got)
     return (
         out.reshape(rows, width),
         dx.reshape(rows, width),

time: 198 us -> 194 us (0.980); the launches traced: 195 us -> 193 us
  no operation moved by 1% of the time
where the time goes in v7:
time: 194 us; the launch traced here: 193 us
  Pallas kernels  193 us (99%)
    pallas_call x1, Pallas kernels, core(): pl.pallas_call(functools.partial(core_kernel, seqs, line, heads, blocks,...  121 us
    pallas_call x1, Pallas kernels, front(): pl.pallas_call(functools.partial(front_kernel, seqs, line, heads, blocks,...  66 us

profile of v7, /device:TPU:1, one launch (start us, length us, event | category | flops | bytes accessed | tf_op | source)
XLA Modules:
  0.0 193.4 jit_solution(1587935922030825448)
XLA Ops:
  0.6 2.3 %index.1 = (s32[8]{0:T(128)}, s32[8]{0:T(128)}, s32[8]{0:T(128)}, s32[8]{0:T(128)}, f32[9]{0:T(128)}, /*index=5*/f32[8,128]{1,0:T(8,128)}) custom-call(s32[64]{0:T(128)} %place.1, s32[4]{0:T(128)} %lengths.1, f32[1,8]{1,0:T(1,128)} %bitcast.29, f32[1,8]{1,0:T(1,128)} %bitcast.30, f32[1,8]{1,0:T(1,128)} %bitcast.31), custom_call_target="tpu_custom_call" | custom-call | tf_op jit(solution)/shard_map/index/pallas_call | solution.py:326
  2.9 66.0 %front.1 = (bf16[1024,1024]{1,0:T(8,128)(2,1)}, bf16[1024,1024]{1,0:T(8,128)(2,1)}, f32[1024,512]{1,0:T(8,128)}, bf16[1024,768]{1,0:T(8,128)(2,1)}, f32[1024,768...) custom-call(s32[8]{0:T(128)} %get-tuple-element.62.give, ...), custom_call_target="tpu_custom_call" | custom-call | tf_op jit(solution)/shard_map/front/pallas_call | solution.py:640
  68.9 121.0 %core.1 = (bf16[8,128,256]{2,1,0:T(8,128)(2,1)}, bf16[8,128,256]{2,1,0:T(8,128)(2,1)}, bf16[4,16,256]{2,1,0:T(8,128)(2,1)}, bf16[4,16,256]{2,1,0:T(8,128)(2,1)},...) custom-call(f32[9]{0:T(128)} %get-tuple-element.60.flags, ...), custom_call_target="tpu_custom_call" | custom-call | tf_op jit(solution)/shard_map/core/pallas_call | solution.py:1480
  189.9 3.3 %finish.1 = (bf16[8,128,256]{2,1,0:T(8,128)(2,1)}, bf16[8,128,256]{2,1,0:T(8,128)(2,1)}, f32[1,256]{1,0:T(1,128)}, f32[128,512]{1,0:T(8,128)}, f32[128,512]{1,0:...) custom-call(s32[8]{0:T(128)} %get-tuple-element.59.take, ...), custom_call_target="tpu_custom_call" | custom-call | tf_op jit(solution)/shard_map/finish/pallas_call | solution.py:1578

commit v8 on v7

--- a/solution.py
+++ b/solution.py
@@ -931,10 +931,10 @@
         def load(shard, n):
             return pltpu.make_async_copy(shard_of(g_part, shard), shard_of(g_buf, shard), load_sem.at[n])
 
-        body(load(mine, 0))
-        if line > 1:
-            pl.when(mine > 0)(lambda: body(load(mine - 1, 1)))
-            pl.when(mine < line - 1)(lambda: body(load(mine + 1, 2)))
+        for n, away in enumerate((0, -1, 1)):
+            if abs(away) < line:
+                there = (mine + away >= 0) & (mine + away < line)
+                pl.when(there)(lambda: body(load(mine + away, n)))
 
     def sum_copy(to, slot):
         return remote(sums.at[mine], sums.at[slot], sum_sent.at[to], sum_sem.at[slot], {"head": to})
@@ -1053,12 +1053,6 @@
             out_part[z, here] = out[:, z * width : (z + 1) * width].astype(LOW)
         out_part_done(b)
 
-    if out_fold.merges:
-
-        @pl.when(out_fold.is_end)
-        def _():
-            pl.loop(0, blocks)(lambda b: out_fold.send_near(group_rows(b), b))
-
     for hop in range(2, line):
         g_line.hop(hop)
     each_load(lambda copy: copy.wait())
@@ -1085,17 +1079,7 @@
     totals[...] = jnp.sum(sums[...], axis=0)
 
     if out_fold.merges:
-
-        @pl.when(jnp.logical_not(out_fold.is_end))
-        def _():
-            @pl.loop(0, blocks)
-            def _(b):
-                out_fold.merge(group_rows(b), b)
-
-            pl.loop(0, blocks)(lambda b: out_fold.send_near(group_rows(b), b))
-
-    else:
-        pl.loop(0, blocks)(lambda b: out_fold.send_far(group_rows(b), b))
+        pl.loop(0, blocks)(lambda b: out_fold.send_near(group_rows(b), b))
 
     def residual(n):
         at = pl.ds(pl.multiple_of(n * BLOCK, BLOCK), BLOCK)
@@ -1133,6 +1117,17 @@
     back_msg[:inner, :] = state[...].astype(LOW)
     back_msg[inner:, :] = jnp.broadcast_to(prod[:HALO], (HALO, STATE)).astype(LOW)
     back_plane.start(back_msg)
+
+    if out_fold.merges:
+
+        @pl.when(jnp.logical_not(out_fold.is_end))
+        def _():
+            @pl.loop(0, blocks)
+            def _(b):
+                out_fold.merge(group_rows(b), b)
+
+    else:
+        pl.loop(0, blocks)(lambda b: out_fold.send_far(group_rows(b), b))
 
     @pl.loop(0, blocks)
     def _(b):
@@ -1327,7 +1322,7 @@
         route(0)
         own_g.start()
 
-    own_g = pltpu.make_async_copy(shard_of(g_part, mine), out_part.at[mine], load_sem.at[3])
+    own_g = pltpu.make_async_copy(shard_of(g_part, mine), out_part.at[mine], load_sem.at[5])
 
     step(*last_phase, 0, None)
     scan_back(blocks - 1, 0)
@@ -1366,16 +1361,6 @@
     pn[...] += jnp.sum(gain, axis=0, keepdims=True)
     g_buf[pl.ds(rows - HALO, HALO), :] = grad
     dx_fold.send_far(*edge_piece)
-    each_piece(dx_fold.send_near)
-
-    if blocks > 3:
-        dx_fold.merge(group_rows(1), 1)
-
-    da_low[...] = dw[:, inner:wide].astype(LOW)
-    da_sum.begin()
-    dw_low[:, :inner] = dw[:, :inner].astype(LOW)
-    dw_low[:, inner:] = dw[:, wide:].astype(LOW)
-    dw_sum.begin()
 
     for z in range(line):
         slab = z * size // LANES * LANES
@@ -1386,6 +1371,17 @@
     zs_got[mine] = zs_send[mine]
     all_line(lambda to: zs_copy(to, mine).start())
 
+    each_piece(dx_fold.send_near)
+
+    if blocks > 3:
+        dx_fold.merge(group_rows(1), 1)
+
+    da_low[...] = dw[:, inner:wide].astype(LOW)
+    da_sum.begin()
+    dw_low[:, :inner] = dw[:, :inner].astype(LOW)
+    dw_low[:, inner:] = dw[:, wide:].astype(LOW)
+    dw_sum.begin()
+
     if blocks > 3:
         dx_fold.merge(group_rows(0), 0)
     elif blocks == 2:
@@ -1395,31 +1391,6 @@
     da_sum.combine()
     dw_sum.combine()
 
-    da_sum.drain()
-    from_plane = da_got[0].astype(WIDE)
-    for n in range(1, seqs // 2):
-        from_plane = from_plane + da_got[n].astype(WIDE)
-    for z in range(line):
-        slab = z * size // LANES * LANES
-        da_send[z] = from_plane[:, slab : slab + LANES]
-    own_copies["addr"].start()
-    all_line(lambda to: da_copy(to, mine).start())
-
-    all_seq(lambda other: fin_copy(0, other, other).wait())
-    own_copies["fin0"].wait()
-    each_piece(dx_fold.drain)
-    fetch(dx_far)
-    own_g.wait()
-
-    @pl.loop(0, blocks)
-    def _(b):
-        here = group_rows(b)
-        total = dx_fold.total(here, dx_near if roomy else out_part)
-        done = (out_part[mine, here].astype(WIDE) + total).astype(LOW)
-        result[2 * b] = done[:BLOCK]
-        result[2 * b + 1] = done[BLOCK:]
-
-    route(1)
     all_line(lambda other: zs_copy(other, other).wait())
     from_line = jnp.sum(zs_got[...], axis=0)
     small[...] = jnp.zeros_like(small)
@@ -1434,6 +1405,31 @@
     own_copies["small"].start()
     all_seq(lambda to: small_copy(to, me).start())
 
+    da_sum.drain()
+    from_plane = da_got[0].astype(WIDE)
+    for n in range(1, seqs // 2):
+        from_plane = from_plane + da_got[n].astype(WIDE)
+    for z in range(line):
+        slab = z * size // LANES * LANES
+        da_send[z] = from_plane[:, slab : slab + LANES]
+    own_copies["addr"].start()
+    all_line(lambda to: da_copy(to, mine).start())
+
+    all_seq(lambda other: fin_copy(0, other, other).wait())
+    own_copies["fin0"].wait()
+    each_piece(dx_fold.drain)
+    fetch(dx_far)
+    own_g.wait()
+
+    @pl.loop(0, blocks)
+    def _(b):
+        here = group_rows(b)
+        total = dx_fold.total(here, dx_near if roomy else out_part)
+        done = (out_part[mine, here].astype(WIDE) + total).astype(LOW)
+        result[2 * b] = done[:BLOCK]
+        result[2 * b + 1] = done[BLOCK:]
+
+    route(1)
     early_sum.drain()
     dw_sum.drain()
     all_line(lambda other: da_copy(other, other).wait())
@@ -1510,7 +1506,7 @@
             pltpu.VMEM((1, total), WIDE), pltpu.VMEM((line, 2 * EDGE, width), WIDE),
             pltpu.VMEM((line, 2 * EDGE, width), WIDE), pltpu.VMEM(small, WIDE),
             pltpu.VMEM((tiles, BLOCK, width), LOW), pltpu.VMEM((seqs, BLOCK, width), LOW),
-            DMA((seqs,)), DMA((seqs,)), DMA((seqs,)), DMA((line,)), DMA((line,)), DMA((2, line)), DMA((line,)), DMA((4,)),
+            DMA((seqs,)), DMA((seqs,)), DMA((seqs,)), DMA((line,)), DMA((line,)), DMA((2, line)), DMA((line,)), DMA((6,)),
             DMA((ways, blocks)), DMA((line, blocks)), DMA((2, blocks)), DMA((4, seqs // 2)), DMA((4, seqs // 2)), DMA((4, seqs // 2)),
             DMA((ways, pieces)), DMA((line, pieces)), DMA((2, pieces)), DMA, DMA,
             DMA((line,)), DMA((line,)), DMA((line,)), DMA((line,)), DMA((seqs,)), DMA((seqs,)), DMA((2, seqs)),

time: 194 us -> 183 us (0.943)
  Pallas kernels: 193 us -> 182 us
    pallas_call x1, Pallas kernels: 121 us -> 111 us  [core(): pl.pallas_call(functools.partial(core_kernel, seqs, line, heads, blocks,...]
where the time goes in v8:
time: 183 us
  Pallas kernels  182 us (99%)
    pallas_call x1, Pallas kernels, core(): pl.pallas_call(functools.partial(core_kernel, seqs, line, heads, blocks,...  111 us
    pallas_call x1, Pallas kernels, front(): pl.pallas_call(functools.partial(front_kernel, seqs, line, heads, blocks,...  66 us

profile of v8, /device:TPU:1, one launch (start us, length us, event | category | flops | bytes accessed | tf_op | source)
XLA Modules:
  0.0 183.1 jit_solution(5638703661526266163)
XLA Ops:
  0.6 2.3 %index.1 = (s32[8]{0:T(128)}, s32[8]{0:T(128)}, s32[8]{0:T(128)}, s32[8]{0:T(128)}, f32[9]{0:T(128)}, /*index=5*/f32[8,128]{1,0:T(8,128)}) custom-call(s32[64]{0:T(128)} %place.1, s32[4]{0:T(128)} %lengths.1, f32[1,8]{1,0:T(1,128)} %bitcast.29, f32[1,8]{1,0:T(1,128)} %bitcast.30, f32[1,8]{1,0:T(1,128)} %bitcast.31), custom_call_target="tpu_custom_call" | custom-call | tf_op jit(solution)/shard_map/index/pallas_call | solution.py:326
  2.9 66.0 %front.1 = (bf16[1024,1024]{1,0:T(8,128)(2,1)}, bf16[1024,1024]{1,0:T(8,128)(2,1)}, f32[1024,512]{1,0:T(8,128)}, bf16[1024,768]{1,0:T(8,128)(2,1)}, f32[1024,768...) custom-call(s32[8]{0:T(128)} %get-tuple-element.62.give, ...), custom_call_target="tpu_custom_call" | custom-call | tf_op jit(solution)/shard_map/front/pallas_call | solution.py:640
  68.9 110.7 %core.1 = (bf16[8,128,256]{2,1,0:T(8,128)(2,1)}, bf16[8,128,256]{2,1,0:T(8,128)(2,1)}, bf16[4,16,256]{2,1,0:T(8,128)(2,1)}, bf16[4,16,256]{2,1,0:T(8,128)(2,1)},...) custom-call(f32[9]{0:T(128)} %get-tuple-element.60.flags, ...), custom_call_target="tpu_custom_call" | custom-call | tf_op jit(solution)/shard_map/core/pallas_call | solution.py:1476
  179.6 3.3 %finish.1 = (bf16[8,128,256]{2,1,0:T(8,128)(2,1)}, bf16[8,128,256]{2,1,0:T(8,128)(2,1)}, f32[1,256]{1,0:T(1,128)}, f32[128,512]{1,0:T(8,128)}, f32[128,512]{1,0:...) custom-call(s32[8]{0:T(128)} %get-tuple-element.59.take, ...), custom_call_target="tpu_custom_call" | custom-call | tf_op jit(solution)/shard_map/finish/pallas_call | solution.py:1574

commit v9 on v8

--- a/solution.py
+++ b/solution.py
@@ -395,6 +395,10 @@
     def u_line(n):
         return Line(line, u.at[piece(n)], width, line_sent.at[n], line_got.at[n])
 
+    hops = sorted(((step, n) for step in range(1, line - 1) for n in range(chunks)), key=lambda hop: (sum(hop), hop))
+    late_hops = [(step, n) for step, n in hops if step == line - 2 and n >= 2]
+    early_hops = [hop for hop in hops if hop not in late_hops]
+
     def own_columns(ref):
         return ref.at[:, pl.ds(pl.multiple_of(mine * width, LANES), width)]
 
@@ -473,22 +477,29 @@
         own.start()
         post(1, g, send_g, recv_g)
         r_plane.start(r_own)
-        for step in range(1, line - 1):
-            for n in range(chunks):
-                u_line(n).hop(step)
-            if step == 1:
-                w_plane.relay()
+        for step, n in early_hops:
+            u_line(n).hop(step)
+        w_plane.relay()
         own.wait()
 
         @pl.loop(0, line)
         def _(n):
             rim_copy(n, n).wait_recv()
 
+        w_plane.finish(w_own)
+        save_w.start()
+
+    for step, n in late_hops:
+
+        @pl.when(i == (n - 1) * per)
+        def _():
+            u_line(n).hop(step)
+
+    @pl.when(i == blocks // 2)
+    def _():
         arrange(1, recv_g, work_g)
         g_line.first(work_g)
         own_g.start()
-        w_plane.finish(w_own)
-        save_w.start()
 
     if line > 1:
 
@@ -856,7 +867,8 @@
     depth = early_got.shape[1]
     rows = ssd_s.shape[0]
     size = 2 * STATE // line
-    g_line = Line(line, g_buf, width, line_sent, line_sem)
+    chunks = line_sem.shape[0]
+    per = blocks // chunks
     back_plane = Plane(seqs, lambda s: back_slots.at[s], back_sent, back_sem, back_passed, way=-1)
     out_got, dx_got = (out_near, dx_near) if roomy else (out_far, dx_far)
 
@@ -868,6 +880,12 @@
 
     def shard_of(ref, shard):
         return ref.at[:, pl.ds(pl.multiple_of(shard * width, LANES), width)]
+
+    def chunk_rows(n):
+        return pl.ds(pl.multiple_of(n * (rows // chunks), rows // chunks), rows // chunks)
+
+    def g_line(n):
+        return Line(line, g_buf.at[chunk_rows(n)], width, line_sent.at[n], line_sem.at[n])
 
     def by_group(ref, first=0, columns=None):
         if columns is None:
@@ -1028,7 +1046,8 @@
     fetch_w = pltpu.make_async_copy(w_in, w, weight_sem.at[1])
     fetch_r.start()
     greet(seqs, line)
-    g_line.hop(1, take=False, source=lambda shard: shard_of(g_part, shard))
+    for n in range(chunks):
+        g_line(n).hop(1, take=False, source=lambda shard: shard_of(g_part.at[chunk_rows(n)], shard))
     each_load(lambda copy: copy.start())
     fetch_w.start()
     state[...] = state_in[...]
@@ -1036,7 +1055,7 @@
 
     def out_part_done(b):
         if out_fold.merges:
-            out_fold.send_far(group_rows(b), b)
+            pl.when(b < blocks - 1)(lambda: out_fold.send_far(group_rows(b), b))
 
     @pl.loop(0, blocks)
     def _(b):
@@ -1053,16 +1072,18 @@
             out_part[z, here] = out[:, z * width : (z + 1) * width].astype(LOW)
         out_part_done(b)
 
-    for hop in range(2, line):
-        g_line.hop(hop)
+    for hop in range(2, line - 1):
+        for n in range(chunks):
+            g_line(n).hop(hop)
     each_load(lambda copy: copy.wait())
-    g_line.finish(None, range(1, line - 1))
     fetch_w.wait()
 
     @pl.loop(0, blocks)
     def _(b):
         step(*norm_phase, b, gate_phase)
         here = group_rows(b)
+        if line > 1:
+            pl.when(lax.rem(b, per) == 0)(lambda: g_line(lax.div(b, per)).hop(line - 1))
         gated = gated_of(ssd_s[here, :], b)
         d_inner = nn(g_buf[here, :], r_t[...])
         din_s[here, :] = d_inner
@@ -1072,6 +1093,8 @@
         sums[mine, b] = both[:EDGE]
 
     all_line(lambda to: sum_copy(to, mine).start())
+    for n in range(chunks):
+        g_line(n).finish(None, range(1, line - 1))
     for ref in (gread, ggate, gpost, state, tiny, taps_g, bias_g, dw, pn):
         ref[...] = jnp.zeros_like(ref)
     prod[...] = jnp.ones_like(prod)
@@ -1079,6 +1102,7 @@
     totals[...] = jnp.sum(sums[...], axis=0)
 
     if out_fold.merges:
+        out_fold.send_far(group_rows(blocks - 1), blocks - 1)
         pl.loop(0, blocks)(lambda b: out_fold.send_near(group_rows(b), b))
 
     def residual(n):
@@ -1122,7 +1146,7 @@
 
         @pl.when(jnp.logical_not(out_fold.is_end))
         def _():
-            @pl.loop(0, blocks)
+            @pl.loop(0, blocks - 1)
             def _(b):
                 out_fold.merge(group_rows(b), b)
 
@@ -1193,10 +1217,10 @@
     early_low[:, :inner] = gread[...].astype(LOW)
     early_low[:, inner:] = ggate[...].astype(LOW)
     early_sum.begin()
+    out_fold.merge(group_rows(blocks - 1), blocks - 1)
     back_plane.finish(back_msg)
     state[...] = fold_states(back_slots, collect, inner, seqs - 1, me, -1, jnp.zeros((inner, STATE), WIDE))
 
-    early_sum.combine()
     taps = jnp.concatenate([kernels[...], filters[...]], axis=1)
     scale = -jnp.exp(vec[1:2, :])
     through_w = to_columns(jnp.broadcast_to(vec[2:3, :], (EDGE, LANES)), spread_m)[0:1]
@@ -1328,6 +1352,7 @@
     scan_back(blocks - 1, 0)
     rows_back(blocks - 1, 0, True)
     dx_fold.send_far(*short_piece)
+    early_sum.combine()
 
     @pl.loop(1, blocks)
     def _(turn):
@@ -1452,6 +1477,7 @@
     blocks, tiles = rows // GROUP, rows // BLOCK
     heads = inner // HDIM
     pieces = blocks + 1
+    chunks = min(blocks, 4)
     message = (inner + HALO, STATE)
     sums = (blocks, EDGE, GROUP)
     streamed = (gate, part, act, cum, raw, local, conv, pre, normed, u, g_part, r_t, w_all)
@@ -1506,7 +1532,8 @@
             pltpu.VMEM((1, total), WIDE), pltpu.VMEM((line, 2 * EDGE, width), WIDE),
             pltpu.VMEM((line, 2 * EDGE, width), WIDE), pltpu.VMEM(small, WIDE),
             pltpu.VMEM((tiles, BLOCK, width), LOW), pltpu.VMEM((seqs, BLOCK, width), LOW),
-            DMA((seqs,)), DMA((seqs,)), DMA((seqs,)), DMA((line,)), DMA((line,)), DMA((2, line)), DMA((line,)), DMA((6,)),
+            DMA((seqs,)), DMA((seqs,)), DMA((seqs,)), DMA((line,)), DMA((line,)), DMA((chunks, 2, line)), DMA((chunks, line)),
+            DMA((6,)),
             DMA((ways, blocks)), DMA((line, blocks)), DMA((2, blocks)), DMA((4, seqs // 2)), DMA((4, seqs // 2)), DMA((4, seqs // 2)),
             DMA((ways, pieces)), DMA((line, pieces)), DMA((2, pieces)), DMA, DMA,
             DMA((line,)), DMA((line,)), DMA((line,)), DMA((line,)), DMA((seqs,)), DMA((seqs,)), DMA((2, seqs)),

time: 183 us -> 180 us (0.984)
  Pallas kernels: 182 us -> 179 us
    pallas_call x1, Pallas kernels: 111 us -> 108 us  [core(): pl.pallas_call(functools.partial(core_kernel, seqs, line, heads, blocks,...]
where the time goes in v9:
time: 180 us
  Pallas kernels  179 us (99%)
    pallas_call x1, Pallas kernels, core(): pl.pallas_call(functools.partial(core_kernel, seqs, line, heads, blocks,...  108 us
    pallas_call x1, Pallas kernels, front(): pl.pallas_call(functools.partial(front_kernel, seqs, line, heads, blocks,...  65.5 us

profile of v9, /device:TPU:1, one launch (start us, length us, event | category | flops | bytes accessed | tf_op | source)
XLA Modules:
  0.0 179.9 jit_solution(421619684447792436)
XLA Ops:
  0.6 2.3 %index.1 = (s32[8]{0:T(128)}, s32[8]{0:T(128)}, s32[8]{0:T(128)}, s32[8]{0:T(128)}, f32[9]{0:T(128)}, /*index=5*/f32[8,128]{1,0:T(8,128)}) custom-call(s32[64]{0:T(128)} %place.1, s32[4]{0:T(128)} %lengths.1, f32[1,8]{1,0:T(1,128)} %bitcast.29, f32[1,8]{1,0:T(1,128)} %bitcast.30, f32[1,8]{1,0:T(1,128)} %bitcast.31), custom_call_target="tpu_custom_call" | custom-call | tf_op jit(solution)/shard_map/index/pallas_call | solution.py:326
  2.9 65.5 %front.1 = (bf16[1024,1024]{1,0:T(8,128)(2,1)}, bf16[1024,1024]{1,0:T(8,128)(2,1)}, f32[1024,512]{1,0:T(8,128)}, bf16[1024,768]{1,0:T(8,128)(2,1)}, f32[1024,768...) custom-call(s32[8]{0:T(128)} %get-tuple-element.62.give, ...), custom_call_target="tpu_custom_call" | custom-call | tf_op jit(solution)/shard_map/front/pallas_call | solution.py:651
  68.4 107.9 %core.1 = (bf16[8,128,256]{2,1,0:T(8,128)(2,1)}, bf16[8,128,256]{2,1,0:T(8,128)(2,1)}, bf16[4,16,256]{2,1,0:T(8,128)(2,1)}, bf16[4,16,256]{2,1,0:T(8,128)(2,1)},...) custom-call(f32[9]{0:T(128)} %get-tuple-element.60.flags, ...), custom_call_target="tpu_custom_call" | custom-call | tf_op jit(solution)/shard_map/core/pallas_call | solution.py:1502
  176.4 3.3 %finish.1 = (bf16[8,128,256]{2,1,0:T(8,128)(2,1)}, bf16[8,128,256]{2,1,0:T(8,128)(2,1)}, f32[1,256]{1,0:T(1,128)}, f32[128,512]{1,0:T(8,128)}, f32[128,512]{1,0:...) custom-call(s32[8]{0:T(128)} %get-tuple-element.59.take, ...), custom_call_target="tpu_custom_call" | custom-call | tf_op jit(solution)/shard_map/finish/pallas_call | solution.py:1601

commit v10 on v9

--- a/solution.py
+++ b/solution.py
@@ -1372,7 +1372,7 @@
         def _():
             dx_fold.merge(*short_piece)
 
-        pl.when(turn == max(blocks // 2, 1))(outputs_home)
+        pl.when(turn == blocks - 1)(outputs_home)
 
         @pl.when(turn > 2)
         def _():

time: 180 us -> 177 us (0.983)
  Pallas kernels: 179 us -> 176 us
    pallas_call x1, Pallas kernels: 108 us -> 105 us  [core(): pl.pallas_call(functools.partial(core_kernel, seqs, line, heads, blocks,...]
where the time goes in v10:
time: 177 us
  Pallas kernels  176 us (99%)
    pallas_call x1, Pallas kernels, core(): pl.pallas_call(functools.partial(core_kernel, seqs, line, heads, blocks,...  105 us
    pallas_call x1, Pallas kernels, front(): pl.pallas_call(functools.partial(front_kernel, seqs, line, heads, blocks,...  65.5 us

profile of v10, /device:TPU:1, one launch (start us, length us, event | category | flops | bytes accessed | tf_op | source)
XLA Modules:
  0.0 177.1 jit_solution(1102487197510802463)
XLA Ops:
  0.6 2.3 %index.1 = (s32[8]{0:T(128)}, s32[8]{0:T(128)}, s32[8]{0:T(128)}, s32[8]{0:T(128)}, f32[9]{0:T(128)}, /*index=5*/f32[8,128]{1,0:T(8,128)}) custom-call(s32[64]{0:T(128)} %place.1, s32[4]{0:T(128)} %lengths.1, f32[1,8]{1,0:T(1,128)} %bitcast.29, f32[1,8]{1,0:T(1,128)} %bitcast.30, f32[1,8]{1,0:T(1,128)} %bitcast.31), custom_call_target="tpu_custom_call" | custom-call | tf_op jit(solution)/shard_map/index/pallas_call | solution.py:326
  2.9 65.5 %front.1 = (bf16[1024,1024]{1,0:T(8,128)(2,1)}, bf16[1024,1024]{1,0:T(8,128)(2,1)}, f32[1024,512]{1,0:T(8,128)}, bf16[1024,768]{1,0:T(8,128)(2,1)}, f32[1024,768...) custom-call(s32[8]{0:T(128)} %get-tuple-element.62.give, ...), custom_call_target="tpu_custom_call" | custom-call | tf_op jit(solution)/shard_map/front/pallas_call | solution.py:651
  68.4 105.1 %core.1 = (bf16[8,128,256]{2,1,0:T(8,128)(2,1)}, bf16[8,128,256]{2,1,0:T(8,128)(2,1)}, bf16[4,16,256]{2,1,0:T(8,128)(2,1)}, bf16[4,16,256]{2,1,0:T(8,128)(2,1)},...) custom-call(f32[9]{0:T(128)} %get-tuple-element.60.flags, ...), custom_call_target="tpu_custom_call" | custom-call | tf_op jit(solution)/shard_map/core/pallas_call | solution.py:1502
  173.6 3.3 %finish.1 = (bf16[8,128,256]{2,1,0:T(8,128)(2,1)}, bf16[8,128,256]{2,1,0:T(8,128)(2,1)}, f32[1,256]{1,0:T(1,128)}, f32[128,512]{1,0:T(8,128)}, f32[128,512]{1,0:...) custom-call(s32[8]{0:T(128)} %get-tuple-element.59.take, ...), custom_call_target="tpu_custom_call" | custom-call | tf_op jit(solution)/shard_map/finish/pallas_call | solution.py:1601
